TPU v7x, 256 devices: a whole 4x4x8 slice. The times are simulated.
256 devices in a mesh: slab: 32 (over z_lo, y, core), head: 8 (over z_hi, x).
Axes of the slice: x: 4, y: 4, z: 8 (z_hi: 2, z_lo: 4; z = z_hi * 4 + z_lo), core: 2. Of those that a mesh axis runs over, the one named last changes fastest.
Arguments:
- queries: bfloat16 [4096, 3072], P('slab', 'head'), may hold values from -20 to 20
- keys: bfloat16 [4096, 3072], P('slab', 'head'), may hold values from -20 to 20
- values: bfloat16 [4096, 3072], P('slab', 'head'), may hold values from -6 to 6
- w_out: bfloat16 [3072, 3072], P('head'), may hold values from -0.109375 to 0.109375
- d_out: bfloat16 [4096, 3072], P('slab', 'head'), may hold values from -6 to 6
- far_ids: int32 [64, 4], P('slab'), may hold values from 0 to 63, as said below
- far_counts: int32 [64], P('slab'), may hold values from 0 to 4, as said below
Outputs:
- mixed: bfloat16 [4096, 3072], P('slab', 'head')
- query_grad: bfloat16 [4096, 3072], P('slab', 'head')
- key_grad: bfloat16 [4096, 3072], P('slab', 'head')
- value_grad: bfloat16 [4096, 3072], P('slab', 'head')
- weight_grad: float32 [3072, 3072], P(('head', 'slab'))
Inputs may be any that keep to these rules, and one draw needn't show every extreme that they name: `far_ids`: within each aligned block of 2 rows, the 8 values id // 2 are all different. `far_counts`: each aligned block of 2 entries holds 4 at least once.
All inputs are finite; a program needn't handle non-finite values.
Results may differ from a plain program's by a relative error of at most 0.028.
Values may be sent and summed in bfloat16 or wider, within the bound.
No kernel may reach another device: no remote copies, remote signals or barrier semaphores. Data moves between devices by JAX's collectives and lax.ppermute only.
A program may use at most 192 MiB of HBM per device.

v0:
```python
import functools
import math

import jax
import jax.numpy as jnp
from jax import lax
from jax.experimental import pallas as pl
from jax.experimental.pallas import tpu as pltpu
from jax.sharding import PartitionSpec as P

HD = 128
TILE = 64
HEADS = 3
ROWS = 128
COLS = 384
WIDE = 3072
NT_DEV = 4
NY_DEV = 4
DEAD = -1e30
SCALE = 1.0 / math.sqrt(HD)
ORDER = (0, 4, 1, 5, 2, 6, 3, 7)
BF = jnp.bfloat16
F32 = jnp.float32


def swap(block, axis, distance):
    devices = range(lax.axis_size(axis))
    return lax.ppermute(block, axis, [(i, i ^ distance) for i in devices])


def gathered(block, axis, unit):
    near = swap(block, axis, unit)
    rows = block.shape[0]
    far = swap(jnp.concatenate([block, near], axis=0), axis, 2 * unit)
    return [block, near, far[:rows], far[rows:]]


def dot(lhs, rhs, left, right):
    return lax.dot_general(lhs, rhs, (((left,), (right,)), ((), ())), preferred_element_type=F32)


def call(kernel, outs, *args, flops, moved, scratch=()):
    vmem = pl.BlockSpec(memory_space=pltpu.VMEM)
    smem = pl.BlockSpec(memory_space=pltpu.SMEM)
    return pl.pallas_call(
        kernel,
        out_shape=[jax.ShapeDtypeStruct(shape, dtype) for shape, dtype in outs],
        in_specs=[smem if a.dtype == jnp.int32 else vmem for a in args],
        out_specs=[vmem] * len(outs),
        scratch_shapes=list(scratch),
        compiler_params=pltpu.CompilerParams(vmem_limit_bytes=40 * 1024 * 1024),
        cost_estimate=pl.CostEstimate(flops=flops, bytes_accessed=moved, transcendentals=0),
    )(*args)


def pack_kernel(ids_ref, counts_ref, q_ref, k_ref, v_ref, q_out, kv_out):
    q_out[0:ROWS, :] = q_ref[...]
    row = lax.broadcasted_iota(jnp.int32, (16, COLS), 0)
    col = lax.broadcasted_iota(jnp.int32, (16, COLS), 1)
    named = jnp.full((16, COLS), -1.0, F32)
    for tile in range(2):
        for f in range(4):
            one = jnp.where(f < counts_ref[tile], ids_ref[tile, f], -1).astype(F32)
            named = jnp.where((row == tile) & (col == f), one, named)
    q_out[ROWS : ROWS + 16, :] = named.astype(BF)
    kv_out[0:ROWS, :] = k_ref[...]
    kv_out[ROWS : 2 * ROWS, :] = v_ref[...]


def log_counts(rank_ref, q_refs):
    t, y, c = rank_ref[0], rank_ref[1], rank_ref[2]
    row = lax.broadcasted_iota(jnp.int32, (16, ROWS), 0)
    lane = lax.broadcasted_iota(jnp.int32, (16, ROWS), 1)
    block = row // 2
    height = (y ^ (block % 4)) * 2 + (c ^ (block // 4))
    tile = (((t * 8 + height) * 2) + row % 2).astype(F32)
    near_height = jnp.abs(height - (y * 2 + c)) <= 1
    parts = []
    for j, q in enumerate(q_refs):
        near_time = jnp.abs((t ^ j) - t) <= 1
        count = jnp.where(near_height & near_time, 1.0, 0.0)
        named = q[ROWS : ROWS + 16, 0:HD].astype(F32)
        for f in range(4):
            one = jnp.where(lane < TILE, named[0:1, f : f + 1], named[1:2, f : f + 1])
            count = count + jnp.where(one == tile, 1.0, 0.0)
        parts.append(jnp.where(count > 0, jnp.log(jnp.maximum(count, 1.0)), DEAD))
    return jnp.concatenate(parts, axis=1)


def forward_kernel(*refs):
    rank_ref, q_refs, kv_refs = refs[0], refs[1:5], refs[5:13]
    out_refs, s_ref, bias_ref = refs[13:17], refs[17], refs[18]
    bias_ref[...] = log_counts(rank_ref, q_refs)
    row = lax.broadcasted_iota(jnp.int32, (16, 4 * ROWS), 0)
    stats = jnp.zeros((16, 4 * ROWS), F32)
    for h in range(HEADS):
        cols = slice(h * HD, (h + 1) * HD)
        q = jnp.concatenate([r[0:ROWS, cols] for r in q_refs], axis=0)
        top = jnp.full((1, 4 * ROWS), 2 * DEAD, F32)
        for b, kv in enumerate(kv_refs):
            s = dot(kv[0:ROWS, cols], q, 1, 1) * SCALE
            for half in range(2):
                part = s[half * TILE : (half + 1) * TILE] + bias_ref[2 * b + half : 2 * b + half + 1, :]
                start = b * ROWS + half * TILE
                s_ref[start : start + TILE, :] = part
                top = jnp.maximum(top, jnp.max(part, axis=0, keepdims=True))
        total = jnp.zeros((1, 4 * ROWS), F32)
        out = jnp.zeros((HD, 4 * ROWS), F32)
        for b, kv in enumerate(kv_refs):
            e = jnp.exp(s_ref[b * ROWS : (b + 1) * ROWS, :] - top)
            total = total + jnp.sum(e, axis=0, keepdims=True)
            out = out + dot(kv[ROWS : 2 * ROWS, cols], e.astype(BF), 0, 0)
        out = (out / total).astype(BF)
        for j, r in enumerate(out_refs):
            r[cols, :] = out[:, j * ROWS : (j + 1) * ROWS]
        rest = top + jnp.log(total)
        for piece in range(3):
            high = rest.astype(BF).astype(F32)
            stats = jnp.where(row == 3 * h + piece, high, stats)
            rest = rest - high
    stats = stats.astype(BF)
    for j, r in enumerate(out_refs):
        r[COLS : COLS + 16, :] = stats[:, j * ROWS : (j + 1) * ROWS]


def merge_kernel(*refs):
    parts, grad_ref, att_ref, stats_ref = refs[:4], refs[4], refs[5], refs[6]
    row = lax.broadcasted_iota(jnp.int32, (8, ROWS), 0)
    stats = jnp.zeros((8, ROWS), F32)
    pieces = [r[COLS : COLS + 16, :].astype(F32) for r in parts]
    for h in range(HEADS):
        cols = slice(h * HD, (h + 1) * HD)
        logs = [(p[3 * h : 3 * h + 1] + p[3 * h + 1 : 3 * h + 2]) + p[3 * h + 2 : 3 * h + 3] for p in pieces]
        top = functools.reduce(jnp.maximum, logs)
        shares = [jnp.exp(l - top) for l in logs]
        total = functools.reduce(jnp.add, shares)
        out = sum((r[cols, :].astype(F32) * (w / total) for r, w in zip(parts, shares)), jnp.zeros((HD, ROWS), F32))
        out = out.astype(BF)
        att_ref[cols, :] = out
        delta = jnp.sum(out.astype(F32) * grad_ref[cols, :].astype(F32), axis=0, keepdims=True)
        stats = jnp.where(row == h, top + jnp.log(total), stats)
        stats = jnp.where(row == 3 + h, delta, stats)
    stats_ref[...] = stats


def grad_kernel(rank_ref, w_ref, d_ref, out_ref):
    total = jnp.zeros((COLS, ROWS), F32)
    for p in range(8):
        start = pl.multiple_of((rank_ref[3] ^ ORDER[p]) * COLS, 128)
        total = total + dot(w_ref[:, pl.ds(start, COLS)], d_ref[p * ROWS : (p + 1) * ROWS, :], 1, 1)
    out_ref[...] = total.astype(BF)


def mix_kernel(rank_ref, att_ref, w_ref, own_ref, other_ref):
    att = att_ref[...].T
    for i, p in enumerate(ORDER):
        start = pl.multiple_of((rank_ref[3] ^ p) * COLS, 128)
        part = jnp.dot(att, w_ref[:, pl.ds(start, COLS)], preferred_element_type=F32)
        target = own_ref if i < 4 else other_ref
        target[(i % 4) * ROWS : (i % 4 + 1) * ROWS, :] = part.astype(target.dtype)


def weight_kernel(rank_ref, att_ref, att2_ref, d_ref, d2_ref, own_ref, *out_refs):
    t, y, c = rank_ref[0], rank_ref[1], rank_ref[2]
    row = lax.broadcasted_iota(jnp.int32, (192, COLS), 0)
    col = lax.broadcasted_iota(jnp.int32, (192, COLS), 1)
    source = row * 0
    for jy in range(4):
        for jt in range(4):
            low = jy * 48 + jt * 12
            base = (t ^ jt) * 96 + (y ^ jy) * 24 + c * 12 - low
            source = jnp.where((row >= low) & (row < low + 12), row + base, source)
    pick = jnp.where(source == col, 1.0, 0.0).astype(BF)
    first = jnp.dot(pick, att_ref[...], preferred_element_type=F32).astype(BF)
    second = jnp.dot(pick, att2_ref[...], preferred_element_type=F32).astype(BF)
    both = jnp.concatenate([first, second], axis=1)
    for p in range(8):
        start = pl.multiple_of((rank_ref[3] ^ ORDER[p]) * COLS, 128)
        rows = slice(p * ROWS, (p + 1) * ROWS)
        rhs = jnp.concatenate([d_ref[rows, :], d2_ref[rows, :]], axis=0)
        part = jnp.dot(both, rhs, preferred_element_type=F32)
        own_ref[:, pl.ds(start, COLS)] = part[0:48]
        for j in range(3):
            out_refs[j][:, pl.ds(start, COLS)] = part[48 * (j + 1) : 48 * (j + 2)].astype(BF)


def backward_kernel(*refs):
    rank_ref, q_refs, kv_refs = refs[0], refs[1:5], refs[5:13]
    g_refs, stat_refs = refs[13:17], refs[17:21]
    dq_own, dq_other, own_ref, other_ref, bias_ref = refs[21:26]
    bias_ref[...] = log_counts(rank_ref, q_refs)
    for h in range(HEADS):
        cols = slice(h * HD, (h + 1) * HD)
        q = jnp.concatenate([r[0:ROWS, cols] for r in q_refs], axis=0)
        g = jnp.concatenate([r[cols, :] for r in g_refs], axis=1)
        log_total = jnp.concatenate([r[h : h + 1, :] for r in stat_refs], axis=1)
        delta = jnp.concatenate([r[3 + h : 4 + h, :] for r in stat_refs], axis=1)
        dq = jnp.zeros((HD, 4 * ROWS), F32)
        for b, kv in enumerate(kv_refs):
            k, v = kv[0:ROWS, cols], kv[ROWS : 2 * ROWS, cols]
            s = dot(k, q, 1, 1) * SCALE
            bias = [
                jnp.broadcast_to(bias_ref[2 * b + half : 2 * b + half + 1, :], (TILE, 4 * ROWS)) for half in range(2)
            ]
            p = jnp.exp(s + jnp.concatenate(bias, axis=0) - log_total)
            ds = (p * (jnp.dot(v, g, preferred_element_type=F32) - delta)).astype(BF)
            dv = dot(p.astype(BF), g, 1, 1)
            dk = jnp.dot(ds, q, preferred_element_type=F32) * SCALE
            dq = dq + dot(k, ds, 0, 0)
            place = (b % 4) * 2 * ROWS
            target = own_ref if b < 4 else other_ref
            target[place : place + ROWS, cols] = dk.astype(target.dtype)
            target[place + ROWS : place + 2 * ROWS, cols] = dv.astype(target.dtype)
        dq = dq * SCALE
        for j in range(4):
            target = dq_own if j < 2 else dq_other
            start = (j % 2) * COLS + h * HD
            target[start : start + HD, :] = dq[:, j * ROWS : (j + 1) * ROWS].astype(target.dtype)


def on_device(queries, keys, values, w_out, d_out, far_ids, far_counts):
    slab = lax.axis_index("slab")
    head = lax.axis_index("head")
    t, y, c = slab // 8, slab // 2 % 4, slab % 2
    ranks = jnp.stack([t, y, c, head]).astype(jnp.int32)

    q_ext, kv = call(
        pack_kernel,
        [((ROWS + 16, COLS), BF), ((2 * ROWS, COLS), BF)],
        far_ids,
        far_counts,
        queries,
        keys,
        values,
        flops=0,
        moved=10**6,
    )
    kv_near = [kv] + [swap(kv, "slab", 2 * e) for e in (1, 2, 3)]
    q_all = gathered(q_ext, "slab", 8)
    kv_all = kv_near + [swap(block, "slab", 1) for block in kv_near]

    d_out, _ = lax.optimization_barrier((d_out, kv_near[1]))
    d_full = jnp.concatenate([d_out, swap(d_out, "head", 4)], axis=0)
    d_full = jnp.concatenate([d_full, swap(d_full, "head", 1)], axis=0)
    d_full = jnp.concatenate([d_full, swap(d_full, "head", 2)], axis=0)
    d_other = swap(d_full, "slab", 1)

    grad = call(grad_kernel, [((COLS, ROWS), BF)], ranks, w_out, d_full, flops=3 * 10**8, moved=3 * 10**6)[0]
    g_all = gathered(grad, "slab", 8)

    bias_scratch = pltpu.VMEM((16, 4 * ROWS), F32)
    parts = call(
        forward_kernel,
        [((COLS + 16, ROWS), BF)] * 4,
        ranks,
        *q_all,
        *kv_all,
        flops=3 * 10**9,
        moved=3 * 10**6,
        scratch=[pltpu.VMEM((8 * ROWS, 4 * ROWS), F32), bias_scratch],
    )
    parts = [parts[0]] + [swap(parts[j], "slab", 8 * j) for j in (1, 2, 3)]
    att, stats = call(
        merge_kernel, [((COLS, ROWS), BF), ((8, ROWS), F32)], *parts, grad, flops=10**8, moved=10**6
    )
    stat_all = [stats] + [swap(stats, "slab", 8 * j) for j in (1, 2, 3)]
    att_other = swap(att, "slab", 1)

    mix = call(
        mix_kernel,
        [((4 * ROWS, COLS), F32), ((4 * ROWS, COLS), BF)],
        ranks,
        att,
        w_out,
        flops=3 * 10**8,
        moved=4 * 10**6,
    )
    mixed = mix[0] + swap(mix[1], "head", 2).astype(F32)
    mixed = mixed[: 2 * ROWS] + swap(mixed[2 * ROWS :].astype(BF), "head", 1).astype(F32)
    mixed = mixed[:ROWS] + swap(mixed[ROWS:].astype(BF), "head", 4).astype(F32)

    weight = call(
        weight_kernel,
        [((48, WIDE), F32)] + [((48, WIDE), BF)] * 3,
        ranks,
        att,
        att_other,
        d_full,
        d_other,
        flops=6 * 10**8,
        moved=4 * 10**6,
    )
    weight = weight[0] + sum((swap(weight[j], "slab", 2 * j).astype(F32) for j in (1, 2, 3)), 0.0)
    weight = weight[:24] + swap(weight[24:].astype(BF), "slab", 16).astype(F32)
    weight_grad = weight[:12] + swap(weight[12:].astype(BF), "slab", 8).astype(F32)

    dq_own, dq_other, own, other = call(
        backward_kernel,
        [((2 * COLS, ROWS), F32), ((2 * COLS, ROWS), BF), ((8 * ROWS, COLS), F32), ((8 * ROWS, COLS), BF)],
        ranks,
        *q_all,
        *kv_all,
        *g_all,
        *stat_all,
        flops=6 * 10**9,
        moved=6 * 10**6,
        scratch=[bias_scratch],
    )
    dq = dq_own + swap(dq_other, "slab", 16).astype(F32)
    dq = dq[:COLS] + swap(dq[COLS:].astype(BF), "slab", 8).astype(F32)
    query_grad = dq.astype(BF).T
    pair = (own + swap(other, "slab", 1).astype(F32)).reshape(4, 2 * ROWS, COLS)
    total = pair[0] + sum((swap(pair[e].astype(BF), "slab", 2 * e).astype(F32) for e in (1, 2, 3)), 0.0)
    total = total.astype(BF)
    return mixed.astype(BF), query_grad, total[:ROWS], total[ROWS:], weight_grad


def solution(mesh):
    placed = (
        P("slab", "head"),
        P("slab", "head"),
        P("slab", "head"),
        P("head", None),
        P("slab", "head"),
        P("slab", None),
        P("slab"),
    )
    return jax.shard_map(
        on_device,
        mesh=mesh,
        in_specs=placed,
        out_specs=(
            P("slab", "head"),
            P("slab", "head"),
            P("slab", "head"),
            P("slab", "head"),
            P(("head", "slab"), None),
        ),
        check_vma=False,
    )
```

profile of v0, /device:TPU:2, one launch (start us, length us, event | category | flops | bytes accessed | tf_op | source)
XLA Modules:
  0.0 144.7 jit_solution(2621346714997193786)
XLA Ops:
  5.3 1.7 %collective-permute-start.2 = (bf16[256,384]{1,0:T(8,128)(2,1)S(1)}, bf16[256,384]{1,0:T(8,128)(2,1)S(1)}, u32[]{:S(2)}, u32[]{:S(2)}) collective-permute-start(bf16[256,384]{1,0:T(8,128)(2,1)S(1)} %get-tuple-element.25.refs_5_), channel_id=1, source_target_pairs={{0,16},{8,24},{16,0},{24,8},{32,48},{40,56},{48,32},{56,40},{64,80... | collective-permute-start | bytes 589832 | tf_op jit(solution)/shard_map/ppermute | solution.py:28
  6.9 5.1 %collective-permute-done.2.refs_6_ = bf16[256,384]{1,0:T(8,128)(2,1)S(1)} collective-permute-done((bf16[256,384]{1,0:T(8,128)(2,1)S(1)}, bf16[256,384]{1,0:T(8,128)(2,1)S(1)}, u32[]{:S(2)}, u32[]{:S(2)}) %collective-permute-start.2) | collective-permute-done | bytes 196640 | tf_op jit(solution)/shard_map/ppermute | solution.py:28
  12.0 7.2 %collective-permute-start.12 = (bf16[128,384]{1,0:T(8,128)(2,1)}, bf16[128,384]{1,0:T(8,128)(2,1)S(1)}, u32[]{:S(2)}, u32[]{:S(2)}) collective-permute-start(bf16[128,384]{1,0:T(8,128)(2,1)} %param.11), channel_id=1, source_target_pairs={{0,4},{1,5},{2,6},{3,7},{4,0},{5,1},{6,2},{7,3},{8,12},{9,13},{10,... | collective-permute-start | bytes 294920 | tf_op jit(solution)/shard_map/ppermute | solution.py:28
  19.2 3.2 %collective-permute-done.12 = bf16[128,384]{1,0:T(8,128)(2,1)S(1)} collective-permute-done((bf16[128,384]{1,0:T(8,128)(2,1)}, bf16[128,384]{1,0:T(8,128)(2,1)S(1)}, u32[]{:S(2)}, u32[]{:S(2)}) %collective-permute-start.12) | collective-permute-done | bytes 98336 | tf_op jit(solution)/shard_map/ppermute | solution.py:28
  24.5 3.2 %collective-permute-start.3 = (bf16[256,384]{1,0:T(8,128)(2,1)S(1)}, bf16[256,384]{1,0:T(8,128)(2,1)S(1)}, u32[]{:S(2)}, u32[]{:S(2)}) collective-permute-start(bf16[256,384]{1,0:T(8,128)(2,1)S(1)} %get-tuple-element.25.refs_5_), channel_id=1, source_target_pairs={{0,32},{8,40},{16,48},{24,56},{32,0},{40,8},{48,16},{56,24},{64,96... | collective-permute-start | bytes 589832 | tf_op jit(solution)/shard_map/ppermute | solution.py:28
  28.8 1.8 %collective-permute-start = (bf16[144,384]{1,0:T(8,128)(2,1)S(1)}, bf16[144,384]{1,0:T(8,128)(2,1)S(1)}, u32[]{:S(2)}, u32[]{:S(2)}) collective-permute-start(bf16[144,384]{1,0:T(8,128)(2,1)S(1)} %get-tuple-element.24.refs_1_), channel_id=1, source_target_pairs={{0,64},{8,72},{16,80},{24,88},{32,96},{40,104},{48,112},{56,120},{... | collective-permute-start | bytes 331784 | tf_op jit(solution)/shard_map/ppermute | solution.py:28
  31.7 2.5 %collective-permute-start.14 = (bf16[512,384]{1,0:T(8,128)(2,1)S(1)}, bf16[512,384]{1,0:T(8,128)(2,1)S(1)}, u32[]{:S(2)}, u32[]{:S(2)}) collective-permute-start(bf16[512,384]{1,0:T(8,128)(2,1)S(1)} %pad_maximum_fusion), channel_id=1, source_target_pairs={{0,2},{1,3},{2,0},{3,1},{4,6},{5,7},{6,4},{7,5},{8,10},{9,11},{10,... | collective-permute-start | bytes 1179656 | tf_op jit(solution)/shard_map/ppermute | solution.py:28
  34.3 2.9 %collective-permute-start.1 = (bf16[288,384]{1,0:T(8,128)(2,1)S(1)}, bf16[288,384]{1,0:T(8,128)(2,1)S(1)}, u32[]{:S(2)}, u32[]{:S(2)}) collective-permute-start(bf16[288,384]{1,0:T(8,128)(2,1)S(1)} %pad_maximum_fusion.1), channel_id=1, source_target_pairs={{0,128},{8,136},{16,144},{24,152},{32,160},{40,168},{48,176},{56,1... | collective-permute-start | bytes 663560 | tf_op jit(solution)/shard_map/ppermute | solution.py:28
  39.8 4.8 %collective-permute-done.14 = bf16[512,384]{1,0:T(8,128)(2,1)S(1)} collective-permute-done((bf16[512,384]{1,0:T(8,128)(2,1)S(1)}, bf16[512,384]{1,0:T(8,128)(2,1)S(1)}, u32[]{:S(2)}, u32[]{:S(2)}) %collective-permute-start.14) | collective-permute-done | bytes 393248 | tf_op jit(solution)/shard_map/ppermute | solution.py:28
  47.3 4.6 %collective-permute-done.18.refs_14_ = bf16[384,128]{1,0:T(8,128)(2,1)S(1)} collective-permute-done((bf16[384,128]{1,0:T(8,128)(2,1)S(1)}, bf16[384,128]{1,0:T(8,128)(2,1)S(1)}, u32[]{:S(2)}, u32[]{:S(2)}) %collective-permute-start.18) | collective-permute-done | bytes 98336 | tf_op jit(solution)/shard_map/ppermute | solution.py:28
  53.4 4.3 %shard_map.111 = (bf16[400,128]{1,0:T(8,128)(2,1)S(1)}, bf16[400,128]{1,0:T(8,128)(2,1)S(1)}, bf16[400,128]{1,0:T(8,128)(2,1)S(1)}, bf16[400,128]{1,0:T(8,128)(2,1)S(1)}) custom-call(s32[4]{0:T(128)S(1)} %pad_add_fusion.refs_0_.rank_ref, bf16[144,384]{1,0:T(8,128)(2,1)S(1)} %get-tuple-element.24.refs_1_, bf16[144,384]{1,0:T(8,128)(2,1)S(1)} %collective-permute-done.refs_2_, ...), custom_call_target="tpu_custom_call" | custom-call | flops 3000000000 | bytes 3000000 | tf_op jit(solution)/shard_map/pallas_call | solution.py:45
  57.7 1.9 %collective-permute-start.10 = (bf16[400,128]{1,0:T(8,128)(2,1)S(1)}, bf16[400,128]{1,0:T(8,128)(2,1)S(1)}, u32[]{:S(2)}, u32[]{:S(2)}) collective-permute-start(bf16[400,128]{1,0:T(8,128)(2,1)S(1)} %get-tuple-element.28), channel_id=1, source_target_pairs={{0,128},{8,136},{16,144},{24,152},{32,160},{40,168},{48,176},{56,1... | collective-permute-start | bytes 307208 | tf_op jit(solution)/shard_map/ppermute | solution.py:28
  59.6 2.8 %collective-permute-start.11 = (bf16[400,128]{1,0:T(8,128)(2,1)S(1)}, bf16[400,128]{1,0:T(8,128)(2,1)S(1)}, u32[]{:S(2)}, u32[]{:S(2)}) collective-permute-start(bf16[400,128]{1,0:T(8,128)(2,1)S(1)} %get-tuple-element.29), channel_id=1, source_target_pairs={{0,192},{8,200},{16,208},{24,216},{32,224},{40,232},{48,240},{56,2... | collective-permute-start | bytes 307208 | tf_op jit(solution)/shard_map/ppermute | solution.py:28
  62.4 7.0 %collective-permute-done.10.refs_2_ = bf16[400,128]{1,0:T(8,128)(2,1)S(1)} collective-permute-done((bf16[400,128]{1,0:T(8,128)(2,1)S(1)}, bf16[400,128]{1,0:T(8,128)(2,1)S(1)}, u32[]{:S(2)}, u32[]{:S(2)}) %collective-permute-start.10) | collective-permute-done | bytes 102432 | tf_op jit(solution)/shard_map/ppermute | solution.py:28
  70.0 1.8 %collective-permute-start.20 = (f32[8,128]{1,0:T(8,128)S(1)}, f32[8,128]{1,0:T(8,128)S(1)}, u32[]{:S(2)}, u32[]{:S(2)}) collective-permute-start(f32[8,128]{1,0:T(8,128)S(1)} %get-tuple-element.34.refs_17_), channel_id=1, source_target_pairs={{0,64},{8,72},{16,80},{24,88},{32,96},{40,104},{48,112},{56,120},{... | collective-permute-start | bytes 12296 | tf_op jit(solution)/shard_map/ppermute | solution.py:28
  75.9 2.5 %collective-permute-start.15 = (bf16[512,384]{1,0:T(8,128)(2,1)S(1)}, bf16[512,384]{1,0:T(8,128)(2,1)S(1)}, u32[]{:S(2)}, u32[]{:S(2)}) collective-permute-start(bf16[512,384]{1,0:T(8,128)(2,1)S(1)} %get-tuple-element.33), channel_id=1, source_target_pairs={{0,2},{1,3},{2,0},{3,1},{4,6},{5,7},{6,4},{7,5},{8,10},{9,11},{10,... | collective-permute-start | bytes 1179656 | tf_op jit(solution)/shard_map/ppermute | solution.py:28
  78.4 1.7 %collective-permute-done.22.refs_20_ = f32[8,128]{1,0:T(8,128)S(1)} collective-permute-done((f32[8,128]{1,0:T(8,128)S(1)}, f32[8,128]{1,0:T(8,128)S(1)}, u32[]{:S(2)}, u32[]{:S(2)}) %collective-permute-start.22) | collective-permute-done | bytes 4128 | tf_op jit(solution)/shard_map/ppermute | solution.py:28
  80.0 7.3 %shard_map.115 = (f32[768,128]{1,0:T(8,128)S(1)}, bf16[768,128]{1,0:T(8,128)(2,1)S(1)}, f32[1024,384]{1,0:T(8,128)S(1)}, bf16[1024,384]{1,0:T(8,128)(2,1)S(1)}) custom-call(s32[4]{0:T(128)S(1)} %pad_add_fusion.refs_0_.rank_ref, bf16[144,384]{1,0:T(8,128)(2,1)S(1)} %get-tuple-element.24.refs_1_, bf16[144,384]{1,0:T(8,128)(2,1)S(1)} %collective-permute-done.refs_2_, ...), custom_call_target="tpu_custom_call" | custom-call | flops 6000000000 | bytes 6000000 | tf_op jit(solution)/shard_map/pallas_call | solution.py:45
  88.8 2.0 %collective-permute-start.16 = (bf16[256,384]{1,0:T(8,128)(2,1)S(1)}, bf16[256,384]{1,0:T(8,128)(2,1)S(1)}, u32[]{:S(2)}, u32[]{:S(2)}) collective-permute-start(bf16[256,384]{1,0:T(8,128)(2,1)S(1)} %slice.131), channel_id=1, source_target_pairs={{0,1},{1,0},{2,3},{3,2},{4,5},{5,4},{6,7},{7,6},{8,9},{9,8},{10,11... | collective-permute-start | bytes 589832 | tf_op jit(solution)/shard_map/ppermute | solution.py:28
  90.8 8.4 %collective-permute-done.23 = bf16[768,128]{1,0:T(8,128)(2,1)S(1)} collective-permute-done((bf16[768,128]{1,0:T(8,128)(2,1)S(1)}, bf16[768,128]{1,0:T(8,128)(2,1)S(1)}, u32[]{:S(2)}, u32[]{:S(2)}) %collective-permute-start.23) | collective-permute-done | bytes 196640 | tf_op jit(solution)/shard_map/ppermute | solution.py:28
  99.4 5.7 %collective-permute-start.17 = (bf16[128,384]{1,0:T(8,128)(2,1)S(1)}, bf16[128,384]{1,0:T(8,128)(2,1)}, u32[]{:S(2)}, u32[]{:S(2)}) collective-permute-start(bf16[128,384]{1,0:T(8,128)(2,1)S(1)} %slice.135), channel_id=1, source_target_pairs={{0,4},{1,5},{2,6},{3,7},{4,0},{5,1},{6,2},{7,3},{8,12},{9,13},{10,... | collective-permute-start | bytes 294920 | tf_op jit(solution)/shard_map/ppermute | solution.py:28
  105.2 2.1 %shard_map.116 = (f32[48,3072]{1,0:T(8,128)S(1)}, bf16[48,3072]{1,0:T(8,128)(2,1)}, bf16[48,3072]{1,0:T(8,128)(2,1)}, bf16[48,3072]{1,0:T(8,128)(2,1)S(1)}) custom-call(s32[4]{0:T(128)S(1)} %pad_add_fusion.refs_0_.rank_ref, bf16[384,128]{1,0:T(8,128)(2,1)S(1)} %get-tuple-element.31.att_ref, bf16[384,128]{1,0:T(8,128)(2,1)S(1)} %collective-permute-done.29.att2_ref, ...), custom_call_target="tpu_custom_call" | custom-call | flops 600000000 | bytes 4000000 | tf_op jit(solution)/shard_map/pallas_call | solution.py:45
  107.3 3.6 %collective-permute-start.32 = (bf16[48,3072]{1,0:T(8,128)(2,1)}, bf16[48,3072]{1,0:T(8,128)(2,1)}, u32[]{:S(2)}, u32[]{:S(2)}) collective-permute-start(bf16[48,3072]{1,0:T(8,128)(2,1)} %get-tuple-element.41), channel_id=1, source_target_pairs={{0,32},{8,40},{16,48},{24,56},{32,0},{40,8},{48,16},{56,24},{64,96... | collective-permute-start | bytes 884744 | tf_op jit(solution)/shard_map/ppermute | solution.py:28
  112.8 1.7 %fusion.2 = bf16[128,384]{1,0:T(8,128)(2,1)} fusion(f32[256,384]{1,0:T(8,128)} %copy-done.14, bf16[128,384]{1,0:T(8,128)(2,1)} %collective-permute-done.17), kind=kLoop, calls=%fused_computation.19 | loop fusion | flops 147456 | bytes 393216 | tf_op jit(solution)/shard_map/convert_element_type | solution.py:315
  114.4 3.1 %collective-permute-done.31 = bf16[48,3072]{1,0:T(8,128)(2,1)} collective-permute-done((bf16[48,3072]{1,0:T(8,128)(2,1)}, bf16[48,3072]{1,0:T(8,128)(2,1)}, u32[]{:S(2)}, u32[]{:S(2)}) %collective-permute-start.31) | collective-permute-done | bytes 294944 | tf_op jit(solution)/shard_map/ppermute | solution.py:28
  117.5 6.8 %collective-permute-done.32 = bf16[48,3072]{1,0:T(8,128)(2,1)} collective-permute-done((bf16[48,3072]{1,0:T(8,128)(2,1)}, bf16[48,3072]{1,0:T(8,128)(2,1)}, u32[]{:S(2)}, u32[]{:S(2)}) %collective-permute-start.32) | collective-permute-done | bytes 294944 | tf_op jit(solution)/shard_map/ppermute | solution.py:28
  124.3 2.4 %collective-permute-done.33 = bf16[48,3072]{1,0:T(8,128)(2,1)} collective-permute-done((bf16[48,3072]{1,0:T(8,128)(2,1)S(1)}, bf16[48,3072]{1,0:T(8,128)(2,1)}, u32[]{:S(2)}, u32[]{:S(2)}) %collective-permute-start.33) | collective-permute-done | bytes 294944 | tf_op jit(solution)/shard_map/ppermute | solution.py:28
  128.0 2.3 %collective-permute-start.34 = (bf16[24,3072]{1,0:T(8,128)(2,1)S(1)}, bf16[24,3072]{1,0:T(8,128)(2,1)S(1)}, u32[]{:S(2)}, u32[]{:S(2)}) collective-permute-start(bf16[24,3072]{1,0:T(8,128)(2,1)S(1)} %slice.132), channel_id=1, source_target_pairs={{0,128},{8,136},{16,144},{24,152},{32,160},{40,168},{48,176},{56,1... | collective-permute-start | bytes 442376 | tf_op jit(solution)/shard_map/ppermute | solution.py:28
  131.9 2.5 %collective-permute-start.27 = (bf16[256,384]{1,0:T(8,128)(2,1)S(1)}, bf16[256,384]{1,0:T(8,128)(2,1)S(1)}, u32[]{:S(2)}, u32[]{:S(2)}) collective-permute-start(bf16[256,384]{1,0:T(8,128)(2,1)S(1)} %get-tuple-element.52), channel_id=1, source_target_pairs={{0,32},{8,40},{16,48},{24,56},{32,0},{40,8},{48,16},{56,24},{64,96... | collective-permute-start | bytes 589832 | tf_op jit(solution)/shard_map/ppermute | solution.py:28
  134.4 2.2 %collective-permute-start.28 = (bf16[256,384]{1,0:T(8,128)(2,1)S(1)}, bf16[256,384]{1,0:T(8,128)(2,1)S(1)}, u32[]{:S(2)}, u32[]{:S(2)}) collective-permute-start(bf16[256,384]{1,0:T(8,128)(2,1)S(1)} %get-tuple-element.51), channel_id=1, source_target_pairs={{0,48},{8,56},{16,32},{24,40},{32,16},{40,24},{48,0},{56,8},{64,11... | collective-permute-start | bytes 589832 | tf_op jit(solution)/shard_map/ppermute | solution.py:28
  138.5 2.7 %collective-permute-done.27 = bf16[256,384]{1,0:T(8,128)(2,1)S(1)} collective-permute-done((bf16[256,384]{1,0:T(8,128)(2,1)S(1)}, bf16[256,384]{1,0:T(8,128)(2,1)S(1)}, u32[]{:S(2)}, u32[]{:S(2)}) %collective-permute-start.27) | collective-permute-done | bytes 196640 | tf_op jit(solution)/shard_map/ppermute | solution.py:28
  141.2 2.0 %collective-permute-done.28 = bf16[256,384]{1,0:T(8,128)(2,1)S(1)} collective-permute-done((bf16[256,384]{1,0:T(8,128)(2,1)S(1)}, bf16[256,384]{1,0:T(8,128)(2,1)S(1)}, u32[]{:S(2)}, u32[]{:S(2)}) %collective-permute-start.28) | collective-permute-done | bytes 196640 | tf_op jit(solution)/shard_map/ppermute | solution.py:28
  (110 shorter events, 30.1 us)
Async XLA Ops:
  5.3 6.7 %collective-permute-start.2 = (bf16[256,384]{1,0:T(8,128)(2,1)S(1)}, bf16[256,384]{1,0:T(8,128)(2,1)S(1)}, u32[]{:S(2)}, u32[]{:S(2)}) collective-permute-start(bf16[256,384]{1,0:T(8,128)(2,1)S(1)} %get-tuple-element.25.refs_5_), channel_id=1, source_target_pairs={{0,16},{8,24},{16,0},{24,8},{32,48},{40,56},{48,32},{56,40},{64,80... | collective-permute-start | bytes 589832 | tf_op jit(solution)/shard_map/ppermute | solution.py:28
  12.0 10.4 %collective-permute-start.12 = (bf16[128,384]{1,0:T(8,128)(2,1)}, bf16[128,384]{1,0:T(8,128)(2,1)S(1)}, u32[]{:S(2)}, u32[]{:S(2)}) collective-permute-start(bf16[128,384]{1,0:T(8,128)(2,1)} %param.11), channel_id=1, source_target_pairs={{0,4},{1,5},{2,6},{3,7},{4,0},{5,1},{6,2},{7,3},{8,12},{9,13},{10,... | collective-permute-start | bytes 294920 | tf_op jit(solution)/shard_map/ppermute | solution.py:28
  24.0 6.7 %collective-permute-start.13 = (bf16[256,384]{1,0:T(8,128)(2,1)}, bf16[256,384]{1,0:T(8,128)(2,1)}, u32[]{:S(2)}, u32[]{:S(2)}) collective-permute-start(bf16[256,384]{1,0:T(8,128)(2,1)} %pad_maximum_fusion.2), channel_id=1, source_target_pairs={{0,1},{1,0},{2,3},{3,2},{4,5},{5,4},{6,7},{7,6},{8,9},{9,8},{10,11... | collective-permute-start | bytes 589832 | tf_op jit(solution)/shard_map/ppermute | solution.py:28
  24.5 14.6 %collective-permute-start.3 = (bf16[256,384]{1,0:T(8,128)(2,1)S(1)}, bf16[256,384]{1,0:T(8,128)(2,1)S(1)}, u32[]{:S(2)}, u32[]{:S(2)}) collective-permute-start(bf16[256,384]{1,0:T(8,128)(2,1)S(1)} %get-tuple-element.25.refs_5_), channel_id=1, source_target_pairs={{0,32},{8,40},{16,48},{24,56},{32,0},{40,8},{48,16},{56,24},{64,96... | collective-permute-start | bytes 589832 | tf_op jit(solution)/shard_map/ppermute | solution.py:28
  27.7 11.6 %collective-permute-start.4 = (bf16[256,384]{1,0:T(8,128)(2,1)S(1)}, bf16[256,384]{1,0:T(8,128)(2,1)S(1)}, u32[]{:S(2)}, u32[]{:S(2)}) collective-permute-start(bf16[256,384]{1,0:T(8,128)(2,1)S(1)} %get-tuple-element.25.refs_5_), channel_id=1, source_target_pairs={{0,48},{8,56},{16,32},{24,40},{32,16},{40,24},{48,0},{56,8},{64,11... | collective-permute-start | bytes 589832 | tf_op jit(solution)/shard_map/ppermute | solution.py:28
  28.8 24.5 %collective-permute-start.5 = (bf16[256,384]{1,0:T(8,128)(2,1)S(1)}, bf16[256,384]{1,0:T(8,128)(2,1)}, u32[]{:S(2)}, u32[]{:S(2)}) collective-permute-start(bf16[256,384]{1,0:T(8,128)(2,1)S(1)} %get-tuple-element.25.refs_5_), channel_id=1, source_target_pairs={{0,8},{8,0},{16,24},{24,16},{32,40},{40,32},{48,56},{56,48},{64,72... | collective-permute-start | bytes 589832 | tf_op jit(solution)/shard_map/ppermute | solution.py:28
  31.7 12.8 %collective-permute-start.14 = (bf16[512,384]{1,0:T(8,128)(2,1)S(1)}, bf16[512,384]{1,0:T(8,128)(2,1)S(1)}, u32[]{:S(2)}, u32[]{:S(2)}) collective-permute-start(bf16[512,384]{1,0:T(8,128)(2,1)S(1)} %pad_maximum_fusion), channel_id=1, source_target_pairs={{0,2},{1,3},{2,0},{3,1},{4,6},{5,7},{6,4},{7,5},{8,10},{9,11},{10,... | collective-permute-start | bytes 1179656 | tf_op jit(solution)/shard_map/ppermute | solution.py:28
  34.3 13.0 %collective-permute-start.1 = (bf16[288,384]{1,0:T(8,128)(2,1)S(1)}, bf16[288,384]{1,0:T(8,128)(2,1)S(1)}, u32[]{:S(2)}, u32[]{:S(2)}) collective-permute-start(bf16[288,384]{1,0:T(8,128)(2,1)S(1)} %pad_maximum_fusion.1), channel_id=1, source_target_pairs={{0,128},{8,136},{16,144},{24,152},{32,160},{40,168},{48,176},{56,1... | collective-permute-start | bytes 663560 | tf_op jit(solution)/shard_map/ppermute | solution.py:28
  39.2 14.2 %collective-permute-start.6 = (bf16[256,384]{1,0:T(8,128)(2,1)S(1)}, bf16[256,384]{1,0:T(8,128)(2,1)S(1)}, u32[]{:S(2)}, u32[]{:S(2)}) collective-permute-start(bf16[256,384]{1,0:T(8,128)(2,1)S(1)} %collective-permute-done.2.refs_6_), channel_id=1, source_target_pairs={{0,8},{8,0},{16,24},{24,16},{32,40},{40,32},{48,56},{56,48},{64,72... | collective-permute-start | bytes 589832 | tf_op jit(solution)/shard_map/ppermute | solution.py:28
  39.3 14.0 %collective-permute-start.7 = (bf16[256,384]{1,0:T(8,128)(2,1)S(1)}, bf16[256,384]{1,0:T(8,128)(2,1)S(1)}, u32[]{:S(2)}, u32[]{:S(2)}) collective-permute-start(bf16[256,384]{1,0:T(8,128)(2,1)S(1)} %collective-permute-done.3.refs_7_), channel_id=1, source_target_pairs={{0,8},{8,0},{16,24},{24,16},{32,40},{40,32},{48,56},{56,48},{64,72... | collective-permute-start | bytes 589832 | tf_op jit(solution)/shard_map/ppermute | solution.py:28
  44.6 8.8 %collective-permute-start.8 = (bf16[256,384]{1,0:T(8,128)(2,1)S(1)}, bf16[256,384]{1,0:T(8,128)(2,1)S(1)}, u32[]{:S(2)}, u32[]{:S(2)}) collective-permute-start(bf16[256,384]{1,0:T(8,128)(2,1)S(1)} %collective-permute-done.4.refs_8_), channel_id=1, source_target_pairs={{0,8},{8,0},{16,24},{24,16},{32,40},{40,32},{48,56},{56,48},{64,72... | collective-permute-start | bytes 589832 | tf_op jit(solution)/shard_map/ppermute | solution.py:28
  52.0 22.6 %collective-permute-start.19 = (bf16[768,128]{1,0:T(8,128)(2,1)S(1)}, bf16[768,128]{1,0:T(8,128)(2,1)S(1)}, u32[]{:S(2)}, u32[]{:S(2)}) collective-permute-start(bf16[768,128]{1,0:T(8,128)(2,1)S(1)} %pad_maximum_fusion.3), channel_id=1, source_target_pairs={{0,128},{8,136},{16,144},{24,152},{32,160},{40,168},{48,176},{56,1... | collective-permute-start | bytes 589832 | tf_op jit(solution)/shard_map/ppermute | solution.py:28
  57.7 11.7 %collective-permute-start.10 = (bf16[400,128]{1,0:T(8,128)(2,1)S(1)}, bf16[400,128]{1,0:T(8,128)(2,1)S(1)}, u32[]{:S(2)}, u32[]{:S(2)}) collective-permute-start(bf16[400,128]{1,0:T(8,128)(2,1)S(1)} %get-tuple-element.28), channel_id=1, source_target_pairs={{0,128},{8,136},{16,144},{24,152},{32,160},{40,168},{48,176},{56,1... | collective-permute-start | bytes 307208 | tf_op jit(solution)/shard_map/ppermute | solution.py:28
  59.6 9.8 %collective-permute-start.11 = (bf16[400,128]{1,0:T(8,128)(2,1)S(1)}, bf16[400,128]{1,0:T(8,128)(2,1)S(1)}, u32[]{:S(2)}, u32[]{:S(2)}) collective-permute-start(bf16[400,128]{1,0:T(8,128)(2,1)S(1)} %get-tuple-element.29), channel_id=1, source_target_pairs={{0,192},{8,200},{16,208},{24,216},{32,224},{40,232},{48,240},{56,2... | collective-permute-start | bytes 307208 | tf_op jit(solution)/shard_map/ppermute | solution.py:28
  62.4 7.5 %collective-permute-start.9 = (bf16[400,128]{1,0:T(8,128)(2,1)S(1)}, bf16[400,128]{1,0:T(8,128)(2,1)S(1)}, u32[]{:S(2)}, u32[]{:S(2)}) collective-permute-start(bf16[400,128]{1,0:T(8,128)(2,1)S(1)} %get-tuple-element.27), channel_id=1, source_target_pairs={{0,64},{8,72},{16,80},{24,88},{32,96},{40,104},{48,112},{56,120},{... | collective-permute-start | bytes 307208 | tf_op jit(solution)/shard_map/ppermute | solution.py:28
  62.4 42.8 %collective-permute-start.30 = (bf16[1024,384]{1,0:T(8,128)(2,1)S(1)}, bf16[1024,384]{1,0:T(8,128)(2,1)S(1)}, u32[]{:S(2)}, u32[]{:S(2)}) collective-permute-start(bf16[1024,384]{1,0:T(8,128)(2,1)S(1)} %constant_dynamic-update-slice_fusion.d_ref), channel_id=1, source_target_pairs={{0,8},{8,0},{16,24},{24,16},{32,40},{40,32},{48,56},{56,48},{64,72... | collective-permute-start | bytes 2359304 | tf_op jit(solution)/shard_map/ppermute | solution.py:28
  71.8 6.6 %collective-permute-start.21 = (f32[8,128]{1,0:T(8,128)S(1)}, f32[8,128]{1,0:T(8,128)S(1)}, u32[]{:S(2)}, u32[]{:S(2)}) collective-permute-start(f32[8,128]{1,0:T(8,128)S(1)} %get-tuple-element.34.refs_17_), channel_id=1, source_target_pairs={{0,128},{8,136},{16,144},{24,152},{32,160},{40,168},{48,176},{56,1... | collective-permute-start | bytes 12296 | tf_op jit(solution)/shard_map/ppermute | solution.py:28
  73.3 31.9 %collective-permute-start.29 = (bf16[384,128]{1,0:T(8,128)(2,1)S(1)}, bf16[384,128]{1,0:T(8,128)(2,1)S(1)}, u32[]{:S(2)}, u32[]{:S(2)}) collective-permute-start(bf16[384,128]{1,0:T(8,128)(2,1)S(1)} %get-tuple-element.31.att_ref), channel_id=1, source_target_pairs={{0,8},{8,0},{16,24},{24,16},{32,40},{40,32},{48,56},{56,48},{64,72... | collective-permute-start | bytes 294920 | tf_op jit(solution)/shard_map/ppermute | solution.py:28
  75.9 12.8 %collective-permute-start.15 = (bf16[512,384]{1,0:T(8,128)(2,1)S(1)}, bf16[512,384]{1,0:T(8,128)(2,1)S(1)}, u32[]{:S(2)}, u32[]{:S(2)}) collective-permute-start(bf16[512,384]{1,0:T(8,128)(2,1)S(1)} %get-tuple-element.33), channel_id=1, source_target_pairs={{0,2},{1,3},{2,0},{3,1},{4,6},{5,7},{6,4},{7,5},{8,10},{9,11},{10,... | collective-permute-start | bytes 1179656 | tf_op jit(solution)/shard_map/ppermute | solution.py:28
  87.3 43.0 %collective-permute-start.25 = (bf16[1024,384]{1,0:T(8,128)(2,1)S(1)}, bf16[1024,384]{1,0:T(8,128)(2,1)}, u32[]{:S(2)}, u32[]{:S(2)}) collective-permute-start(bf16[1024,384]{1,0:T(8,128)(2,1)S(1)} %get-tuple-element.38), channel_id=1, source_target_pairs={{0,8},{8,0},{16,24},{24,16},{32,40},{40,32},{48,56},{56,48},{64,72... | collective-permute-start | bytes 2359304 | tf_op jit(solution)/shard_map/ppermute | solution.py:28
  87.4 11.8 %collective-permute-start.23 = (bf16[768,128]{1,0:T(8,128)(2,1)S(1)}, bf16[768,128]{1,0:T(8,128)(2,1)S(1)}, u32[]{:S(2)}, u32[]{:S(2)}) collective-permute-start(bf16[768,128]{1,0:T(8,128)(2,1)S(1)} %get-tuple-element.36), channel_id=1, source_target_pairs={{0,128},{8,136},{16,144},{24,152},{32,160},{40,168},{48,176},{56,1... | collective-permute-start | bytes 589832 | tf_op jit(solution)/shard_map/ppermute | solution.py:28
  88.8 10.5 %collective-permute-start.16 = (bf16[256,384]{1,0:T(8,128)(2,1)S(1)}, bf16[256,384]{1,0:T(8,128)(2,1)S(1)}, u32[]{:S(2)}, u32[]{:S(2)}) collective-permute-start(bf16[256,384]{1,0:T(8,128)(2,1)S(1)} %slice.131), channel_id=1, source_target_pairs={{0,1},{1,0},{2,3},{3,2},{4,5},{5,4},{6,7},{7,6},{8,9},{9,8},{10,11... | collective-permute-start | bytes 589832 | tf_op jit(solution)/shard_map/ppermute | solution.py:28
  99.2 11.7 %collective-permute-start.24 = (bf16[384,128]{1,0:T(8,128)(2,1)S(1)}, bf16[384,128]{1,0:T(8,128)(2,1)S(1)}, u32[]{:S(2)}, u32[]{:S(2)}) collective-permute-start(bf16[384,128]{1,0:T(8,128)(2,1)S(1)} %slice.134), channel_id=1, source_target_pairs={{0,64},{8,72},{16,80},{24,88},{32,96},{40,104},{48,112},{56,120},{... | collective-permute-start | bytes 294920 | tf_op jit(solution)/shard_map/ppermute | solution.py:28
  99.4 13.3 %collective-permute-start.17 = (bf16[128,384]{1,0:T(8,128)(2,1)S(1)}, bf16[128,384]{1,0:T(8,128)(2,1)}, u32[]{:S(2)}, u32[]{:S(2)}) collective-permute-start(bf16[128,384]{1,0:T(8,128)(2,1)S(1)} %slice.135), channel_id=1, source_target_pairs={{0,4},{1,5},{2,6},{3,7},{4,0},{5,1},{6,2},{7,3},{8,12},{9,13},{10,... | collective-permute-start | bytes 294920 | tf_op jit(solution)/shard_map/ppermute | solution.py:28
  107.3 10.2 %collective-permute-start.31 = (bf16[48,3072]{1,0:T(8,128)(2,1)}, bf16[48,3072]{1,0:T(8,128)(2,1)}, u32[]{:S(2)}, u32[]{:S(2)}) collective-permute-start(bf16[48,3072]{1,0:T(8,128)(2,1)} %get-tuple-element.40), channel_id=1, source_target_pairs={{0,16},{8,24},{16,0},{24,8},{32,48},{40,56},{48,32},{56,40},{64,80... | collective-permute-start | bytes 884744 | tf_op jit(solution)/shard_map/ppermute | solution.py:28
  107.3 17.1 %collective-permute-start.32 = (bf16[48,3072]{1,0:T(8,128)(2,1)}, bf16[48,3072]{1,0:T(8,128)(2,1)}, u32[]{:S(2)}, u32[]{:S(2)}) collective-permute-start(bf16[48,3072]{1,0:T(8,128)(2,1)} %get-tuple-element.41), channel_id=1, source_target_pairs={{0,32},{8,40},{16,48},{24,56},{32,0},{40,8},{48,16},{56,24},{64,96... | collective-permute-start | bytes 884744 | tf_op jit(solution)/shard_map/ppermute | solution.py:28
  110.9 15.8 %collective-permute-start.33 = (bf16[48,3072]{1,0:T(8,128)(2,1)S(1)}, bf16[48,3072]{1,0:T(8,128)(2,1)}, u32[]{:S(2)}, u32[]{:S(2)}) collective-permute-start(bf16[48,3072]{1,0:T(8,128)(2,1)S(1)} %get-tuple-element.42), channel_id=1, source_target_pairs={{0,48},{8,56},{16,32},{24,40},{32,16},{40,24},{48,0},{56,8},{64,11... | collective-permute-start | bytes 884744 | tf_op jit(solution)/shard_map/ppermute | solution.py:28
  128.0 8.5 %collective-permute-start.34 = (bf16[24,3072]{1,0:T(8,128)(2,1)S(1)}, bf16[24,3072]{1,0:T(8,128)(2,1)S(1)}, u32[]{:S(2)}, u32[]{:S(2)}) collective-permute-start(bf16[24,3072]{1,0:T(8,128)(2,1)S(1)} %slice.132), channel_id=1, source_target_pairs={{0,128},{8,136},{16,144},{24,152},{32,160},{40,168},{48,176},{56,1... | collective-permute-start | bytes 442376 | tf_op jit(solution)/shard_map/ppermute | solution.py:28
  131.8 6.7 %collective-permute-start.26 = (bf16[256,384]{1,0:T(8,128)(2,1)S(1)}, bf16[256,384]{1,0:T(8,128)(2,1)S(1)}, u32[]{:S(2)}, u32[]{:S(2)}) collective-permute-start(bf16[256,384]{1,0:T(8,128)(2,1)S(1)} %get-tuple-element.50), channel_id=1, source_target_pairs={{0,16},{8,24},{16,0},{24,8},{32,48},{40,56},{48,32},{56,40},{64,80... | collective-permute-start | bytes 589832 | tf_op jit(solution)/shard_map/ppermute | solution.py:28
  131.9 9.3 %collective-permute-start.27 = (bf16[256,384]{1,0:T(8,128)(2,1)S(1)}, bf16[256,384]{1,0:T(8,128)(2,1)S(1)}, u32[]{:S(2)}, u32[]{:S(2)}) collective-permute-start(bf16[256,384]{1,0:T(8,128)(2,1)S(1)} %get-tuple-element.52), channel_id=1, source_target_pairs={{0,32},{8,40},{16,48},{24,56},{32,0},{40,8},{48,16},{56,24},{64,96... | collective-permute-start | bytes 589832 | tf_op jit(solution)/shard_map/ppermute | solution.py:28
  134.4 8.8 %collective-permute-start.28 = (bf16[256,384]{1,0:T(8,128)(2,1)S(1)}, bf16[256,384]{1,0:T(8,128)(2,1)S(1)}, u32[]{:S(2)}, u32[]{:S(2)}) collective-permute-start(bf16[256,384]{1,0:T(8,128)(2,1)S(1)} %get-tuple-element.51), channel_id=1, source_target_pairs={{0,48},{8,56},{16,32},{24,40},{32,16},{40,24},{48,0},{56,8},{64,11... | collective-permute-start | bytes 589832 | tf_op jit(solution)/shard_map/ppermute | solution.py:28
  136.6 7.4 %collective-permute-start.35 = (bf16[12,3072]{1,0:T(8,128)(2,1)S(1)}, bf16[12,3072]{1,0:T(8,128)(2,1)S(1)}, u32[]{:S(2)}, u32[]{:S(2)}) collective-permute-start(bf16[12,3072]{1,0:T(8,128)(2,1)S(1)} %slice.133), channel_id=1, source_target_pairs={{0,64},{8,72},{16,80},{24,88},{32,96},{40,104},{48,112},{56,120},{... | collective-permute-start | bytes 221192 | tf_op jit(solution)/shard_map/ppermute | solution.py:28
  (21 other events, 268.3 us)
where the time goes:
time: 146 us; the launch traced here: 145 us
  waiting for transfers between devices  55.9 us (38%)
  starting transfers between devices  55 us (38%)
  Pallas kernels  17 us (12%)
  other arithmetic  8.12 us (6%)
  local copies, waits for them, and re-layouts  7.64 us (5%)
    ppermute x36, waiting for transfers between devices, swap(): return lax.ppermute(block, axis, [(i, i ^ distance) for i in devices])  55.9 us
    ppermute x36, starting transfers between devices, swap(): return lax.ppermute(block, axis, [(i, i ^ distance) for i in devices])  55 us
    pallas_call x7, Pallas kernels, call(): pl.pallas_call(kernel, out_shape=[jax.ShapeDtypeStruct(shape, dtype) for...  17 us
    unnamed x38, local copies, waits for them, and re-layouts  6.69 us
  transfers between devices with their start and end apart: 36, of which 17 were waited for; matrix products, arithmetic and copies ran while one was open for 6% of the time, Pallas kernels for 11%

commit v1 on v0

--- a/solution.py
+++ b/solution.py
@@ -39,22 +39,33 @@
     return lax.dot_general(lhs, rhs, (((left,), (right,)), ((), ())), preferred_element_type=F32)
 
 
-def call(kernel, outs, *args, flops, moved, scratch=()):
+def call(kernel, outs, *args, flops, moved, scratch=(), limit=24, by_hand=False):
+    anywhere = pl.BlockSpec(memory_space=pl.ANY)
     vmem = pl.BlockSpec(memory_space=pltpu.VMEM)
     smem = pl.BlockSpec(memory_space=pltpu.SMEM)
     return pl.pallas_call(
         kernel,
         out_shape=[jax.ShapeDtypeStruct(shape, dtype) for shape, dtype in outs],
-        in_specs=[smem if a.dtype == jnp.int32 else vmem for a in args],
+        in_specs=[anywhere if by_hand else smem if a.dtype == jnp.int32 else vmem for a in args],
         out_specs=[vmem] * len(outs),
         scratch_shapes=list(scratch),
-        compiler_params=pltpu.CompilerParams(vmem_limit_bytes=40 * 1024 * 1024),
-        cost_estimate=pl.CostEstimate(flops=flops, bytes_accessed=moved, transcendentals=0),
+        compiler_params=pltpu.CompilerParams(vmem_limit_bytes=limit * 1024 * 1024),
+        cost_estimate=pl.CostEstimate(flops=1000, bytes_accessed=1000, transcendentals=0),
     )(*args)
 
 
-def pack_kernel(ids_ref, counts_ref, q_ref, k_ref, v_ref, q_out, kv_out):
-    q_out[0:ROWS, :] = q_ref[...]
+def pack_kernel(ids_hbm, counts_hbm, q_hbm, k_hbm, v_hbm, q_out, kv_out, ids_ref, counts_ref, sems):
+    copies = [
+        pltpu.make_async_copy(ids_hbm, ids_ref, sems.at[0]),
+        pltpu.make_async_copy(counts_hbm, counts_ref, sems.at[1]),
+        pltpu.make_async_copy(k_hbm, kv_out.at[0:ROWS], sems.at[2]),
+        pltpu.make_async_copy(v_hbm, kv_out.at[ROWS : 2 * ROWS], sems.at[3]),
+        pltpu.make_async_copy(q_hbm, q_out.at[0:ROWS], sems.at[4]),
+    ]
+    for copy in copies:
+        copy.start()
+    copies[0].wait()
+    copies[1].wait()
     row = lax.broadcasted_iota(jnp.int32, (16, COLS), 0)
     col = lax.broadcasted_iota(jnp.int32, (16, COLS), 1)
     named = jnp.full((16, COLS), -1.0, F32)
@@ -63,8 +74,12 @@
             one = jnp.where(f < counts_ref[tile], ids_ref[tile, f], -1).astype(F32)
             named = jnp.where((row == tile) & (col == f), one, named)
     q_out[ROWS : ROWS + 16, :] = named.astype(BF)
-    kv_out[0:ROWS, :] = k_ref[...]
-    kv_out[ROWS : 2 * ROWS, :] = v_ref[...]
+    for copy in copies[2:]:
+        copy.wait()
+
+
+def after(value, *others):
+    return lax.optimization_barrier((value, others))[0]
 
 
 def log_counts(rank_ref, q_refs):
@@ -124,9 +139,9 @@
 
 
 def merge_kernel(*refs):
-    parts, grad_ref, att_ref, stats_ref = refs[:4], refs[4], refs[5], refs[6]
+    parts, att_ref, logs_ref = refs[:4], refs[4], refs[5]
     row = lax.broadcasted_iota(jnp.int32, (8, ROWS), 0)
-    stats = jnp.zeros((8, ROWS), F32)
+    merged = jnp.zeros((8, ROWS), F32)
     pieces = [r[COLS : COLS + 16, :].astype(F32) for r in parts]
     for h in range(HEADS):
         cols = slice(h * HD, (h + 1) * HD)
@@ -135,10 +150,17 @@
         shares = [jnp.exp(l - top) for l in logs]
         total = functools.reduce(jnp.add, shares)
         out = sum((r[cols, :].astype(F32) * (w / total) for r, w in zip(parts, shares)), jnp.zeros((HD, ROWS), F32))
-        out = out.astype(BF)
-        att_ref[cols, :] = out
-        delta = jnp.sum(out.astype(F32) * grad_ref[cols, :].astype(F32), axis=0, keepdims=True)
-        stats = jnp.where(row == h, top + jnp.log(total), stats)
+        att_ref[cols, :] = out.astype(BF)
+        merged = jnp.where(row == h, top + jnp.log(total), merged)
+    logs_ref[...] = merged
+
+
+def delta_kernel(logs_ref, att_ref, grad_ref, stats_ref):
+    row = lax.broadcasted_iota(jnp.int32, (8, ROWS), 0)
+    stats = logs_ref[...]
+    for h in range(HEADS):
+        cols = slice(h * HD, (h + 1) * HD)
+        delta = jnp.sum(att_ref[cols, :].astype(F32) * grad_ref[cols, :].astype(F32), axis=0, keepdims=True)
         stats = jnp.where(row == 3 + h, delta, stats)
     stats_ref[...] = stats
 
@@ -224,6 +246,7 @@
     t, y, c = slab // 8, slab // 2 % 4, slab % 2
     ranks = jnp.stack([t, y, c, head]).astype(jnp.int32)
 
+    d_across = swap(d_out, "head", 4)
     q_ext, kv = call(
         pack_kernel,
         [((ROWS + 16, COLS), BF), ((2 * ROWS, COLS), BF)],
@@ -234,19 +257,16 @@
         values,
         flops=0,
         moved=10**6,
+        scratch=[pltpu.SMEM((2, 4), jnp.int32), pltpu.SMEM((2,), jnp.int32), pltpu.SemaphoreType.DMA((5,))],
+        by_hand=True,
     )
     kv_near = [kv] + [swap(kv, "slab", 2 * e) for e in (1, 2, 3)]
     q_all = gathered(q_ext, "slab", 8)
     kv_all = kv_near + [swap(block, "slab", 1) for block in kv_near]
 
-    d_out, _ = lax.optimization_barrier((d_out, kv_near[1]))
-    d_full = jnp.concatenate([d_out, swap(d_out, "head", 4)], axis=0)
+    d_full = after(jnp.concatenate([d_out, d_across], axis=0), *kv_near)
     d_full = jnp.concatenate([d_full, swap(d_full, "head", 1)], axis=0)
     d_full = jnp.concatenate([d_full, swap(d_full, "head", 2)], axis=0)
-    d_other = swap(d_full, "slab", 1)
-
-    grad = call(grad_kernel, [((COLS, ROWS), BF)], ranks, w_out, d_full, flops=3 * 10**8, moved=3 * 10**6)[0]
-    g_all = gathered(grad, "slab", 8)
 
     bias_scratch = pltpu.VMEM((16, 4 * ROWS), F32)
     parts = call(
@@ -260,9 +280,13 @@
         scratch=[pltpu.VMEM((8 * ROWS, 4 * ROWS), F32), bias_scratch],
     )
     parts = [parts[0]] + [swap(parts[j], "slab", 8 * j) for j in (1, 2, 3)]
-    att, stats = call(
-        merge_kernel, [((COLS, ROWS), BF), ((8, ROWS), F32)], *parts, grad, flops=10**8, moved=10**6
-    )
+    d_full = after(d_full, parts[1])
+    d_other = swap(d_full, "slab", 1)
+    grad = call(grad_kernel, [((COLS, ROWS), BF)], ranks, w_out, d_full, flops=3 * 10**8, moved=3 * 10**6)[0]
+    g_all = gathered(grad, "slab", 8)
+    parts[0] = after(parts[0], g_all[1])
+    att, logs = call(merge_kernel, [((COLS, ROWS), BF), ((8, ROWS), F32)], *parts, flops=10**8, moved=10**6)
+    stats = call(delta_kernel, [((8, ROWS), F32)], logs, att, grad, flops=10**6, moved=10**6)[0]
     stat_all = [stats] + [swap(stats, "slab", 8 * j) for j in (1, 2, 3)]
     att_other = swap(att, "slab", 1)
 
@@ -275,10 +299,7 @@
         flops=3 * 10**8,
         moved=4 * 10**6,
     )
-    mixed = mix[0] + swap(mix[1], "head", 2).astype(F32)
-    mixed = mixed[: 2 * ROWS] + swap(mixed[2 * ROWS :].astype(BF), "head", 1).astype(F32)
-    mixed = mixed[:ROWS] + swap(mixed[ROWS:].astype(BF), "head", 4).astype(F32)
-
+    mix_in = swap(mix[1], "head", 2)
     weight = call(
         weight_kernel,
         [((48, WIDE), F32)] + [((48, WIDE), BF)] * 3,
@@ -290,9 +311,8 @@
         flops=6 * 10**8,
         moved=4 * 10**6,
     )
-    weight = weight[0] + sum((swap(weight[j], "slab", 2 * j).astype(F32) for j in (1, 2, 3)), 0.0)
-    weight = weight[:24] + swap(weight[24:].astype(BF), "slab", 16).astype(F32)
-    weight_grad = weight[:12] + swap(weight[12:].astype(BF), "slab", 8).astype(F32)
+    weight_in = [swap(weight[j], "slab", 2 * j) for j in (1, 2, 3)]
+    stat_all[0] = after(stat_all[0], weight[1])
 
     dq_own, dq_other, own, other = call(
         backward_kernel,
@@ -306,12 +326,25 @@
         moved=6 * 10**6,
         scratch=[bias_scratch],
     )
-    dq = dq_own + swap(dq_other, "slab", 16).astype(F32)
+    weight = after(weight[0], other) + sum((w.astype(F32) for w in weight_in), 0.0)
+    weight_away = weight[24:].astype(BF)
+    mixed = after(mix[0], other) + mix_in.astype(F32)
+    mixed_away = mixed[2 * ROWS :].astype(BF)
+
+    other = swap(other, "slab", 1)
+    pair = (after(own, weight_away, mixed_away) + other.astype(F32)).reshape(4, 2 * ROWS, COLS)
+    away = [pair[e].astype(BF) for e in (1, 2, 3)]
+    total = pair[0] + sum((swap(away[e - 1], "slab", 2 * e).astype(F32) for e in (1, 2, 3)), 0.0)
+    total = total.astype(BF)
+
+    weight = after(weight[:24], away[0]) + swap(weight_away, "slab", 16).astype(F32)
+    weight_grad = weight[:12] + swap(weight[12:].astype(BF), "slab", 8).astype(F32)
+    mixed = after(mixed[: 2 * ROWS], away[0]) + swap(mixed_away, "head", 1).astype(F32)
+    mixed = mixed[:ROWS] + swap(mixed[ROWS:].astype(BF), "head", 4).astype(F32)
+
+    dq = dq_own + swap(after(dq_other, away[0]), "slab", 16).astype(F32)
     dq = dq[:COLS] + swap(dq[COLS:].astype(BF), "slab", 8).astype(F32)
     query_grad = dq.astype(BF).T
-    pair = (own + swap(other, "slab", 1).astype(F32)).reshape(4, 2 * ROWS, COLS)
-    total = pair[0] + sum((swap(pair[e].astype(BF), "slab", 2 * e).astype(F32) for e in (1, 2, 3)), 0.0)
-    total = total.astype(BF)
     return mixed.astype(BF), query_grad, total[:ROWS], total[ROWS:], weight_grad
 
 

time: 146 us -> 124 us (0.85)
  starting transfers between devices: 55 us -> 46.9 us
  other arithmetic: 8.12 us -> 3.17 us
  waiting for transfers between devices: 55.9 us -> 51.4 us
  local copies, waits for them, and re-layouts: 7.64 us -> 5.68 us
  Pallas kernels: 17 us -> 15.4 us
    ppermute x36, starting transfers between devices: 55 us -> 46.9 us  [swap(): return lax.ppermute(block, axis, [(i, i ^ distance) for i in devices])]
    ppermute x36, waiting for transfers between devices: 55.9 us -> 51.4 us  [swap(): return lax.ppermute(block, axis, [(i, i ^ distance) for i in devices])]
    unnamed x38 -> x15, local copies, waits for them, and re-layouts: 6.69 us -> 4.77 us
    pallas_call x7 -> x8, Pallas kernels: 17 us -> 15.4 us  [call(): pl.pallas_call(kernel, out_shape=[jax.ShapeDtypeStruct(shape, dtype) for...]
  transfers between devices with their start and end apart: 36 -> 36, of which waited for: 17 -> 14; matrix products, arithmetic and copies ran while one was open for 6% -> 3% of each run, Pallas kernels for 11% -> 12%
where the time goes in v1:
time: 124 us
  waiting for transfers between devices  51.4 us (41%)
  starting transfers between devices  46.9 us (38%)
  Pallas kernels  15.4 us (12%)
  local copies, waits for them, and re-layouts  5.68 us (5%)
  other arithmetic  3.17 us (3%)
    ppermute x36, waiting for transfers between devices, swap(): return lax.ppermute(block, axis, [(i, i ^ distance) for i in devices])  51.4 us
    ppermute x36, starting transfers between devices, swap(): return lax.ppermute(block, axis, [(i, i ^ distance) for i in devices])  46.9 us
    pallas_call x8, Pallas kernels, call(): pl.pallas_call(kernel, out_shape=[jax.ShapeDtypeStruct(shape, dtype) for...  15.4 us
    unnamed x15, local copies, waits for them, and re-layouts  4.77 us
  transfers between devices with their start and end apart: 36, of which 14 were waited for; matrix products, arithmetic and copies ran while one was open for 3% of the time, Pallas kernels for 12%

profile of v1, /device:TPU:2, one launch (start us, length us, event | category | flops | bytes accessed | tf_op | source)
XLA Modules:
  0.0 123.6 jit_solution(9547081341402972763)
XLA Ops:
  0.6 7.3 %collective-permute-start.9 = (bf16[128,384]{1,0:T(8,128)(2,1)}, bf16[128,384]{1,0:T(8,128)(2,1)S(1)}, u32[]{:S(2)}, u32[]{:S(2)}) collective-permute-start(bf16[128,384]{1,0:T(8,128)(2,1)} %param.11), channel_id=1, source_target_pairs={{0,4},{1,5},{2,6},{3,7},{4,0},{5,1},{6,2},{7,3},{8,12},{9,13},{10,... | collective-permute-start | bytes 294920 | tf_op jit(solution)/shard_map/ppermute | solution.py:28
  12.6 3.1 %collective-permute-start.4 = (bf16[256,384]{1,0:T(8,128)(2,1)S(1)}, bf16[256,384]{1,0:T(8,128)(2,1)S(1)}, u32[]{:S(2)}, u32[]{:S(2)}) collective-permute-start(bf16[256,384]{1,0:T(8,128)(2,1)S(1)} %get-tuple-element.34.refs_5_), channel_id=1, source_target_pairs={{0,48},{8,56},{16,32},{24,40},{32,16},{40,24},{48,0},{56,8},{64,11... | collective-permute-start | bytes 589832 | tf_op jit(solution)/shard_map/ppermute | solution.py:28
  18.7 5.3 %collective-permute-done.4.refs_8_ = bf16[256,384]{1,0:T(8,128)(2,1)S(1)} collective-permute-done((bf16[256,384]{1,0:T(8,128)(2,1)S(1)}, bf16[256,384]{1,0:T(8,128)(2,1)S(1)}, u32[]{:S(2)}, u32[]{:S(2)}) %collective-permute-start.4) | collective-permute-done | bytes 196640 | tf_op jit(solution)/shard_map/ppermute | solution.py:28
  25.8 1.6 %collective-permute-start.1 = (bf16[288,384]{1,0:T(8,128)(2,1)S(1)}, bf16[288,384]{1,0:T(8,128)(2,1)S(1)}, u32[]{:S(2)}, u32[]{:S(2)}) collective-permute-start(bf16[288,384]{1,0:T(8,128)(2,1)S(1)} %pad_maximum_fusion.2), channel_id=1, source_target_pairs={{0,128},{8,136},{16,144},{24,152},{32,160},{40,168},{48,176},{56,1... | collective-permute-start | bytes 663560 | tf_op jit(solution)/shard_map/ppermute | solution.py:28
  27.3 3.5 %collective-permute-done.10 = bf16[256,384]{1,0:T(8,128)(2,1)S(1)} collective-permute-done((bf16[256,384]{1,0:T(8,128)(2,1)S(1)}, bf16[256,384]{1,0:T(8,128)(2,1)S(1)}, u32[]{:S(2)}, u32[]{:S(2)}) %collective-permute-start.10) | collective-permute-done | bytes 196640 | tf_op jit(solution)/shard_map/ppermute | solution.py:28
  30.9 2.7 %collective-permute-start.11 = (bf16[512,384]{1,0:T(8,128)(2,1)S(1)}, bf16[512,384]{1,0:T(8,128)(2,1)S(1)}, u32[]{:S(2)}, u32[]{:S(2)}) collective-permute-start(bf16[512,384]{1,0:T(8,128)(2,1)S(1)} %pad_maximum_fusion.1), channel_id=1, source_target_pairs={{0,2},{1,3},{2,0},{3,1},{4,6},{5,7},{6,4},{7,5},{8,10},{9,11},{10,... | collective-permute-start | bytes 1179656 | tf_op jit(solution)/shard_map/ppermute | solution.py:28
  34.3 2.8 %collective-permute-done.1 = bf16[288,384]{1,0:T(8,128)(2,1)S(1)} collective-permute-done((bf16[288,384]{1,0:T(8,128)(2,1)S(1)}, bf16[288,384]{1,0:T(8,128)(2,1)S(1)}, u32[]{:S(2)}, u32[]{:S(2)}) %collective-permute-start.1) | collective-permute-done | bytes 221216 | tf_op jit(solution)/shard_map/ppermute | solution.py:28
  37.2 1.4 %collective-permute-done.6.refs_10_ = bf16[256,384]{1,0:T(8,128)(2,1)S(1)} collective-permute-done((bf16[256,384]{1,0:T(8,128)(2,1)S(1)}, bf16[256,384]{1,0:T(8,128)(2,1)S(1)}, u32[]{:S(2)}, u32[]{:S(2)}) %collective-permute-start.6) | collective-permute-done | bytes 196640 | tf_op jit(solution)/shard_map/ppermute | solution.py:28
  38.5 3.9 %shard_map.111 = (bf16[400,128]{1,0:T(8,128)(2,1)S(1)}, bf16[400,128]{1,0:T(8,128)(2,1)S(1)}, bf16[400,128]{1,0:T(8,128)(2,1)S(1)}, bf16[400,128]{1,0:T(8,128)(2,1)S(1)}) custom-call(s32[4]{0:T(128)S(1)} %pad_add_fusion.refs_0_.rank_ref, bf16[144,384]{1,0:T(8,128)(2,1)S(1)} %get-tuple-element.33.refs_1_, bf16[144,384]{1,0:T(8,128)(2,1)S(1)} %collective-permute-done.refs_2_, ...), custom_call_target="tpu_custom_call" | custom-call | flops 1000 | bytes 1000 | tf_op jit(solution)/shard_map/pallas_call | solution.py:46
  42.7 4.8 %collective-permute-done.12.refs_1_ = bf16[400,128]{1,0:T(8,128)(2,1)S(1)} collective-permute-done((bf16[400,128]{1,0:T(8,128)(2,1)S(1)}, bf16[400,128]{1,0:T(8,128)(2,1)S(1)}, u32[]{:S(2)}, u32[]{:S(2)}) %collective-permute-start.12) | collective-permute-done | bytes 102432 | tf_op jit(solution)/shard_map/ppermute | solution.py:28
  47.5 1.3 %shard_map.112.grad_ref.refs_13_ = bf16[384,128]{1,0:T(8,128)(2,1)S(1)} custom-call(s32[4]{0:T(128)S(1)} %pad_add_fusion.refs_0_.rank_ref, bf16[384,3072]{1,0:T(8,128)(2,1)S(1)} %copy-done, bf16[1024,384]{1,0:T(8,128)(2,1)S(1)} %pad_maximum_fusion.d_ref), custom_call_target="tpu_custom_call" | custom-call | flops 1000 | bytes 1000 | tf_op jit(solution)/shard_map/pallas_call | solution.py:46
  49.4 2.2 %collective-permute-start.14 = (bf16[400,128]{1,0:T(8,128)(2,1)S(1)}, bf16[400,128]{1,0:T(8,128)(2,1)S(1)}, u32[]{:S(2)}, u32[]{:S(2)}) collective-permute-start(bf16[400,128]{1,0:T(8,128)(2,1)S(1)} %get-tuple-element.40), channel_id=1, source_target_pairs={{0,128},{8,136},{16,144},{24,152},{32,160},{40,168},{48,176},{56,1... | collective-permute-start | bytes 307208 | tf_op jit(solution)/shard_map/ppermute | solution.py:28
  51.6 1.9 %collective-permute-start.15 = (bf16[400,128]{1,0:T(8,128)(2,1)S(1)}, bf16[400,128]{1,0:T(8,128)(2,1)S(1)}, u32[]{:S(2)}, u32[]{:S(2)}) collective-permute-start(bf16[400,128]{1,0:T(8,128)(2,1)S(1)} %get-tuple-element.41), channel_id=1, source_target_pairs={{0,192},{8,200},{16,208},{24,216},{32,224},{40,232},{48,240},{56,2... | collective-permute-start | bytes 307208 | tf_op jit(solution)/shard_map/ppermute | solution.py:28
  53.5 2.2 %collective-permute-done.13.refs_14_ = bf16[384,128]{1,0:T(8,128)(2,1)S(1)} collective-permute-done((bf16[384,128]{1,0:T(8,128)(2,1)S(1)}, bf16[384,128]{1,0:T(8,128)(2,1)S(1)}, u32[]{:S(2)}, u32[]{:S(2)}) %collective-permute-start.13) | collective-permute-done | bytes 98336 | tf_op jit(solution)/shard_map/ppermute | solution.py:28
  55.8 8.9 %collective-permute-done.14.refs_2_ = bf16[400,128]{1,0:T(8,128)(2,1)S(1)} collective-permute-done((bf16[400,128]{1,0:T(8,128)(2,1)S(1)}, bf16[400,128]{1,0:T(8,128)(2,1)S(1)}, u32[]{:S(2)}, u32[]{:S(2)}) %collective-permute-start.14) | collective-permute-done | bytes 102432 | tf_op jit(solution)/shard_map/ppermute | solution.py:28
  64.8 1.2 %shard_map.114 = (f32[512,384]{1,0:T(8,128)S(1)}, bf16[512,384]{1,0:T(8,128)(2,1)S(1)}) custom-call(s32[4]{0:T(128)S(1)} %pad_add_fusion.refs_0_.rank_ref, bf16[384,128]{1,0:T(8,128)(2,1)S(1)} %get-tuple-element.42.att_ref, bf16[384,3072]{1,0:T(8,128)(2,1)S(1)} %copy-done), custom_call_target="tpu_custom_call" | custom-call | flops 1000 | bytes 1000 | tf_op jit(solution)/shard_map/pallas_call | solution.py:46
  66.0 2.5 %collective-permute-start.22 = (bf16[512,384]{1,0:T(8,128)(2,1)S(1)}, bf16[512,384]{1,0:T(8,128)(2,1)S(1)}, u32[]{:S(2)}, u32[]{:S(2)}) collective-permute-start(bf16[512,384]{1,0:T(8,128)(2,1)S(1)} %get-tuple-element.49), channel_id=1, source_target_pairs={{0,2},{1,3},{2,0},{3,1},{4,6},{5,7},{6,4},{7,5},{8,10},{9,11},{10,... | collective-permute-start | bytes 1179656 | tf_op jit(solution)/shard_map/ppermute | solution.py:28
  68.6 2.0 %collective-permute-start.21 = (f32[8,128]{1,0:T(8,128)S(1)}, f32[8,128]{1,0:T(8,128)S(1)}, u32[]{:S(2)}, u32[]{:S(2)}) collective-permute-start(f32[8,128]{1,0:T(8,128)S(1)} %shard_map.115.refs_17_), channel_id=1, source_target_pairs={{0,192},{8,200},{16,208},{24,216},{32,224},{40,232},{48,240},{56,2... | collective-permute-start | bytes 12296 | tf_op jit(solution)/shard_map/ppermute | solution.py:28
  70.6 2.4 %collective-permute-start.20 = (f32[8,128]{1,0:T(8,128)S(1)}, f32[8,128]{1,0:T(8,128)S(1)}, u32[]{:S(2)}, u32[]{:S(2)}) collective-permute-start(f32[8,128]{1,0:T(8,128)S(1)} %shard_map.115.refs_17_), channel_id=1, source_target_pairs={{0,128},{8,136},{16,144},{24,152},{32,160},{40,168},{48,176},{56,1... | collective-permute-start | bytes 12296 | tf_op jit(solution)/shard_map/ppermute | solution.py:28
  73.1 1.3 %shard_map.116 = (f32[48,3072]{1,0:T(8,128)S(1)}, bf16[48,3072]{1,0:T(8,128)(2,1)S(1)}, bf16[48,3072]{1,0:T(8,128)(2,1)S(1)}, bf16[48,3072]{1,0:T(8,128)(2,1)S(1)}) custom-call(s32[4]{0:T(128)S(1)} %pad_add_fusion.refs_0_.rank_ref, bf16[384,128]{1,0:T(8,128)(2,1)S(1)} %get-tuple-element.42.att_ref, bf16[384,128]{1,0:T(8,128)(2,1)S(1)} %collective-permute-done.17.att2_ref, ...), custom_call_target="tpu_custom_call" | custom-call | flops 1000 | bytes 1000 | tf_op jit(solution)/shard_map/pallas_call | solution.py:46
  74.4 3.0 %collective-permute-start.24 = (bf16[48,3072]{1,0:T(8,128)(2,1)S(1)}, bf16[48,3072]{1,0:T(8,128)(2,1)S(1)}, u32[]{:S(2)}, u32[]{:S(2)}) collective-permute-start(bf16[48,3072]{1,0:T(8,128)(2,1)S(1)} %get-tuple-element.53), channel_id=1, source_target_pairs={{0,32},{8,40},{16,48},{24,56},{32,0},{40,8},{48,16},{56,24},{64,96... | collective-permute-start | bytes 884744 | tf_op jit(solution)/shard_map/ppermute | solution.py:28
  77.3 1.1 collective-permute-start.25
  78.9 6.9 %shard_map.117 = (f32[768,128]{1,0:T(8,128)S(1)}, bf16[768,128]{1,0:T(8,128)(2,1)S(1)}, f32[1024,384]{1,0:T(8,128)S(1)}, bf16[1024,384]{1,0:T(8,128)(2,1)S(1)}) custom-call(s32[4]{0:T(128)S(1)} %pad_add_fusion.refs_0_.rank_ref, bf16[144,384]{1,0:T(8,128)(2,1)S(1)} %get-tuple-element.33.refs_1_, bf16[144,384]{1,0:T(8,128)(2,1)S(1)} %collective-permute-done.refs_2_, ...), custom_call_target="tpu_custom_call" | custom-call | flops 1000 | bytes 1000 | tf_op jit(solution)/shard_map/pallas_call | solution.py:46
  86.0 1.9 %collective-permute-start.27 = (bf16[256,384]{1,0:T(8,128)(2,1)S(1)}, bf16[256,384]{1,0:T(8,128)(2,1)S(1)}, u32[]{:S(2)}, u32[]{:S(2)}) collective-permute-start(bf16[256,384]{1,0:T(8,128)(2,1)S(1)} %slice.129), channel_id=1, source_target_pairs={{0,1},{1,0},{2,3},{3,2},{4,5},{5,4},{6,7},{7,6},{8,9},{9,8},{10,11... | collective-permute-start | bytes 589832 | tf_op jit(solution)/shard_map/ppermute | solution.py:28
  87.9 3.2 %collective-permute-done.25 = bf16[48,3072]{1,0:T(8,128)(2,1)S(1)} collective-permute-done((bf16[48,3072]{1,0:T(8,128)(2,1)S(1)}, bf16[48,3072]{1,0:T(8,128)(2,1)S(1)}, u32[]{:S(2)}, u32[]{:S(2)}) %collective-permute-start.25) | collective-permute-done | bytes 294944 | tf_op jit(solution)/shard_map/ppermute | solution.py:28
  91.9 2.2 %collective-permute-start.34 = (bf16[24,3072]{1,0:T(8,128)(2,1)S(1)}, bf16[24,3072]{1,0:T(8,128)(2,1)S(1)}, u32[]{:S(2)}, u32[]{:S(2)}) collective-permute-start(bf16[24,3072]{1,0:T(8,128)(2,1)S(1)} %slice.130), channel_id=1, source_target_pairs={{0,128},{8,136},{16,144},{24,152},{32,160},{40,168},{48,176},{56,1... | collective-permute-start | bytes 442376 | tf_op jit(solution)/shard_map/ppermute | solution.py:28
  95.3 5.8 %collective-permute-done.34 = bf16[24,3072]{1,0:T(8,128)(2,1)S(1)} collective-permute-done((bf16[24,3072]{1,0:T(8,128)(2,1)S(1)}, bf16[24,3072]{1,0:T(8,128)(2,1)S(1)}, u32[]{:S(2)}, u32[]{:S(2)}) %collective-permute-start.34) | collective-permute-done | bytes 147488 | tf_op jit(solution)/shard_map/ppermute | solution.py:28
  101.4 2.4 %collective-permute-start.29 = (bf16[768,128]{1,0:T(8,128)(2,1)S(1)}, bf16[768,128]{1,0:T(8,128)(2,1)S(1)}, u32[]{:S(2)}, u32[]{:S(2)}) collective-permute-start(bf16[768,128]{1,0:T(8,128)(2,1)S(1)} %get-tuple-element.59), channel_id=1, source_target_pairs={{0,128},{8,136},{16,144},{24,152},{32,160},{40,168},{48,176},{56,1... | collective-permute-start | bytes 589832 | tf_op jit(solution)/shard_map/ppermute | solution.py:28
  103.8 2.4 %collective-permute-start.32 = (bf16[256,384]{1,0:T(8,128)(2,1)S(1)}, bf16[256,384]{1,0:T(8,128)(2,1)S(1)}, u32[]{:S(2)}, u32[]{:S(2)}) collective-permute-start(bf16[256,384]{1,0:T(8,128)(2,1)S(1)} %get-tuple-element.68), channel_id=1, source_target_pairs={{0,32},{8,40},{16,48},{24,56},{32,0},{40,8},{48,16},{56,24},{64,96... | collective-permute-start | bytes 589832 | tf_op jit(solution)/shard_map/ppermute | solution.py:28
  106.2 1.5 %collective-permute-start.33 = (bf16[256,384]{1,0:T(8,128)(2,1)S(1)}, bf16[256,384]{1,0:T(8,128)(2,1)S(1)}, u32[]{:S(2)}, u32[]{:S(2)}) collective-permute-start(bf16[256,384]{1,0:T(8,128)(2,1)S(1)} %get-tuple-element.69), channel_id=1, source_target_pairs={{0,48},{8,56},{16,32},{24,40},{32,16},{40,24},{48,0},{56,8},{64,11... | collective-permute-start | bytes 589832 | tf_op jit(solution)/shard_map/ppermute | solution.py:28
  109.5 7.8 %collective-permute-done.28 = bf16[128,384]{1,0:T(8,128)(2,1)S(1)} collective-permute-done((bf16[128,384]{1,0:T(8,128)(2,1)S(1)}, bf16[128,384]{1,0:T(8,128)(2,1)S(1)}, u32[]{:S(2)}, u32[]{:S(2)}) %collective-permute-start.28) | collective-permute-done | bytes 98336 | tf_op jit(solution)/shard_map/ppermute | solution.py:28
  119.0 3.8 %collective-permute-done.30 = bf16[384,128]{1,0:T(8,128)(2,1)S(1)} collective-permute-done((bf16[384,128]{1,0:T(8,128)(2,1)S(1)}, bf16[384,128]{1,0:T(8,128)(2,1)S(1)}, u32[]{:S(2)}, u32[]{:S(2)}) %collective-permute-start.30) | collective-permute-done | bytes 98336 | tf_op jit(solution)/shard_map/ppermute | solution.py:28
  (91 shorter events, 18.2 us)
Async XLA Ops:
  0.6 17.1 %collective-permute-start.9 = (bf16[128,384]{1,0:T(8,128)(2,1)}, bf16[128,384]{1,0:T(8,128)(2,1)S(1)}, u32[]{:S(2)}, u32[]{:S(2)}) collective-permute-start(bf16[128,384]{1,0:T(8,128)(2,1)} %param.11), channel_id=1, source_target_pairs={{0,4},{1,5},{2,6},{3,7},{4,0},{5,1},{6,2},{7,3},{8,12},{9,13},{10,... | collective-permute-start | bytes 294920 | tf_op jit(solution)/shard_map/ppermute | solution.py:28
  12.6 11.4 %collective-permute-start.4 = (bf16[256,384]{1,0:T(8,128)(2,1)S(1)}, bf16[256,384]{1,0:T(8,128)(2,1)S(1)}, u32[]{:S(2)}, u32[]{:S(2)}) collective-permute-start(bf16[256,384]{1,0:T(8,128)(2,1)S(1)} %get-tuple-element.34.refs_5_), channel_id=1, source_target_pairs={{0,48},{8,56},{16,32},{24,40},{32,16},{40,24},{48,0},{56,8},{64,11... | collective-permute-start | bytes 589832 | tf_op jit(solution)/shard_map/ppermute | solution.py:28
  15.7 9.3 %collective-permute-start.3 = (bf16[256,384]{1,0:T(8,128)(2,1)S(1)}, bf16[256,384]{1,0:T(8,128)(2,1)S(1)}, u32[]{:S(2)}, u32[]{:S(2)}) collective-permute-start(bf16[256,384]{1,0:T(8,128)(2,1)S(1)} %get-tuple-element.34.refs_5_), channel_id=1, source_target_pairs={{0,32},{8,40},{16,48},{24,56},{32,0},{40,8},{48,16},{56,24},{64,96... | collective-permute-start | bytes 589832 | tf_op jit(solution)/shard_map/ppermute | solution.py:28
  16.3 8.9 %collective-permute-start.2 = (bf16[256,384]{1,0:T(8,128)(2,1)S(1)}, bf16[256,384]{1,0:T(8,128)(2,1)S(1)}, u32[]{:S(2)}, u32[]{:S(2)}) collective-permute-start(bf16[256,384]{1,0:T(8,128)(2,1)S(1)} %get-tuple-element.34.refs_5_), channel_id=1, source_target_pairs={{0,16},{8,24},{16,0},{24,8},{32,48},{40,56},{48,32},{56,40},{64,80... | collective-permute-start | bytes 589832 | tf_op jit(solution)/shard_map/ppermute | solution.py:28
  16.7 9.0 %collective-permute-start = (bf16[144,384]{1,0:T(8,128)(2,1)S(1)}, bf16[144,384]{1,0:T(8,128)(2,1)S(1)}, u32[]{:S(2)}, u32[]{:S(2)}) collective-permute-start(bf16[144,384]{1,0:T(8,128)(2,1)S(1)} %get-tuple-element.33.refs_1_), channel_id=1, source_target_pairs={{0,64},{8,72},{16,80},{24,88},{32,96},{40,104},{48,112},{56,120},{... | collective-permute-start | bytes 331784 | tf_op jit(solution)/shard_map/ppermute | solution.py:28
  25.2 5.7 %collective-permute-start.10 = (bf16[256,384]{1,0:T(8,128)(2,1)S(1)}, bf16[256,384]{1,0:T(8,128)(2,1)S(1)}, u32[]{:S(2)}, u32[]{:S(2)}) collective-permute-start(bf16[256,384]{1,0:T(8,128)(2,1)S(1)} %pad_maximum_fusion.3), channel_id=1, source_target_pairs={{0,1},{1,0},{2,3},{3,2},{4,5},{5,4},{6,7},{7,6},{8,9},{9,8},{10,11... | collective-permute-start | bytes 589832 | tf_op jit(solution)/shard_map/ppermute | solution.py:28
  25.8 11.3 %collective-permute-start.1 = (bf16[288,384]{1,0:T(8,128)(2,1)S(1)}, bf16[288,384]{1,0:T(8,128)(2,1)S(1)}, u32[]{:S(2)}, u32[]{:S(2)}) collective-permute-start(bf16[288,384]{1,0:T(8,128)(2,1)S(1)} %pad_maximum_fusion.2), channel_id=1, source_target_pairs={{0,128},{8,136},{16,144},{24,152},{32,160},{40,168},{48,176},{56,1... | collective-permute-start | bytes 663560 | tf_op jit(solution)/shard_map/ppermute | solution.py:28
  30.9 11.6 %collective-permute-start.11 = (bf16[512,384]{1,0:T(8,128)(2,1)S(1)}, bf16[512,384]{1,0:T(8,128)(2,1)S(1)}, u32[]{:S(2)}, u32[]{:S(2)}) collective-permute-start(bf16[512,384]{1,0:T(8,128)(2,1)S(1)} %pad_maximum_fusion.1), channel_id=1, source_target_pairs={{0,2},{1,3},{2,0},{3,1},{4,6},{5,7},{6,4},{7,5},{8,10},{9,11},{10,... | collective-permute-start | bytes 1179656 | tf_op jit(solution)/shard_map/ppermute | solution.py:28
  33.6 3.5 %collective-permute-start.5 = (bf16[256,384]{1,0:T(8,128)(2,1)S(1)}, bf16[256,384]{1,0:T(8,128)(2,1)S(1)}, u32[]{:S(2)}, u32[]{:S(2)}) collective-permute-start(bf16[256,384]{1,0:T(8,128)(2,1)S(1)} %get-tuple-element.34.refs_5_), channel_id=1, source_target_pairs={{0,8},{8,0},{16,24},{24,16},{32,40},{40,32},{48,56},{56,48},{64,72... | collective-permute-start | bytes 589832 | tf_op jit(solution)/shard_map/ppermute | solution.py:28
  42.5 5.0 %collective-permute-start.12 = (bf16[400,128]{1,0:T(8,128)(2,1)S(1)}, bf16[400,128]{1,0:T(8,128)(2,1)S(1)}, u32[]{:S(2)}, u32[]{:S(2)}) collective-permute-start(bf16[400,128]{1,0:T(8,128)(2,1)S(1)} %get-tuple-element.37), channel_id=1, source_target_pairs={{0,64},{8,72},{16,80},{24,88},{32,96},{40,104},{48,112},{56,120},{... | collective-permute-start | bytes 307208 | tf_op jit(solution)/shard_map/ppermute | solution.py:28
  47.5 25.6 %collective-permute-start.18 = (bf16[1024,384]{1,0:T(8,128)(2,1)S(1)}, bf16[1024,384]{1,0:T(8,128)(2,1)S(1)}, u32[]{:S(2)}, u32[]{:S(2)}) collective-permute-start(bf16[1024,384]{1,0:T(8,128)(2,1)S(1)} %pad_maximum_fusion.d_ref), channel_id=1, source_target_pairs={{0,8},{8,0},{16,24},{24,16},{32,40},{40,32},{48,56},{56,48},{64,72... | collective-permute-start | bytes 2359304 | tf_op jit(solution)/shard_map/ppermute | solution.py:28
  48.8 6.8 %collective-permute-start.13 = (bf16[384,128]{1,0:T(8,128)(2,1)S(1)}, bf16[384,128]{1,0:T(8,128)(2,1)S(1)}, u32[]{:S(2)}, u32[]{:S(2)}) collective-permute-start(bf16[384,128]{1,0:T(8,128)(2,1)S(1)} %shard_map.112.grad_ref.refs_13_), channel_id=1, source_target_pairs={{0,64},{8,72},{16,80},{24,88},{32,96},{40,104},{48,112},{56,120},{... | collective-permute-start | bytes 294920 | tf_op jit(solution)/shard_map/ppermute | solution.py:28
  49.4 15.3 %collective-permute-start.14 = (bf16[400,128]{1,0:T(8,128)(2,1)S(1)}, bf16[400,128]{1,0:T(8,128)(2,1)S(1)}, u32[]{:S(2)}, u32[]{:S(2)}) collective-permute-start(bf16[400,128]{1,0:T(8,128)(2,1)S(1)} %get-tuple-element.40), channel_id=1, source_target_pairs={{0,128},{8,136},{16,144},{24,152},{32,160},{40,168},{48,176},{56,1... | collective-permute-start | bytes 307208 | tf_op jit(solution)/shard_map/ppermute | solution.py:28
  51.6 13.1 %collective-permute-start.15 = (bf16[400,128]{1,0:T(8,128)(2,1)S(1)}, bf16[400,128]{1,0:T(8,128)(2,1)S(1)}, u32[]{:S(2)}, u32[]{:S(2)}) collective-permute-start(bf16[400,128]{1,0:T(8,128)(2,1)S(1)} %get-tuple-element.41), channel_id=1, source_target_pairs={{0,192},{8,200},{16,208},{24,216},{32,224},{40,232},{48,240},{56,2... | collective-permute-start | bytes 307208 | tf_op jit(solution)/shard_map/ppermute | solution.py:28
  55.7 22.8 %collective-permute-start.16 = (bf16[768,128]{1,0:T(8,128)(2,1)S(1)}, bf16[768,128]{1,0:T(8,128)(2,1)S(1)}, u32[]{:S(2)}, u32[]{:S(2)}) collective-permute-start(bf16[768,128]{1,0:T(8,128)(2,1)S(1)} %pad_maximum_fusion.4), channel_id=1, source_target_pairs={{0,128},{8,136},{16,144},{24,152},{32,160},{40,168},{48,176},{56,1... | collective-permute-start | bytes 589832 | tf_op jit(solution)/shard_map/ppermute | solution.py:28
  66.0 19.9 %collective-permute-start.22 = (bf16[512,384]{1,0:T(8,128)(2,1)S(1)}, bf16[512,384]{1,0:T(8,128)(2,1)S(1)}, u32[]{:S(2)}, u32[]{:S(2)}) collective-permute-start(bf16[512,384]{1,0:T(8,128)(2,1)S(1)} %get-tuple-element.49), channel_id=1, source_target_pairs={{0,2},{1,3},{2,0},{3,1},{4,6},{5,7},{6,4},{7,5},{8,10},{9,11},{10,... | collective-permute-start | bytes 1179656 | tf_op jit(solution)/shard_map/ppermute | solution.py:28
  68.6 5.8 %collective-permute-start.21 = (f32[8,128]{1,0:T(8,128)S(1)}, f32[8,128]{1,0:T(8,128)S(1)}, u32[]{:S(2)}, u32[]{:S(2)}) collective-permute-start(f32[8,128]{1,0:T(8,128)S(1)} %shard_map.115.refs_17_), channel_id=1, source_target_pairs={{0,192},{8,200},{16,208},{24,216},{32,224},{40,232},{48,240},{56,2... | collective-permute-start | bytes 12296 | tf_op jit(solution)/shard_map/ppermute | solution.py:28
  70.6 6.7 %collective-permute-start.20 = (f32[8,128]{1,0:T(8,128)S(1)}, f32[8,128]{1,0:T(8,128)S(1)}, u32[]{:S(2)}, u32[]{:S(2)}) collective-permute-start(f32[8,128]{1,0:T(8,128)S(1)} %shard_map.115.refs_17_), channel_id=1, source_target_pairs={{0,128},{8,136},{16,144},{24,152},{32,160},{40,168},{48,176},{56,1... | collective-permute-start | bytes 12296 | tf_op jit(solution)/shard_map/ppermute | solution.py:28
  73.1 5.9 %collective-permute-start.19 = (f32[8,128]{1,0:T(8,128)S(1)}, f32[8,128]{1,0:T(8,128)S(1)}, u32[]{:S(2)}, u32[]{:S(2)}) collective-permute-start(f32[8,128]{1,0:T(8,128)S(1)} %shard_map.115.refs_17_), channel_id=1, source_target_pairs={{0,64},{8,72},{16,80},{24,88},{32,96},{40,104},{48,112},{56,120},{... | collective-permute-start | bytes 12296 | tf_op jit(solution)/shard_map/ppermute | solution.py:28
  74.4 13.5 %collective-permute-start.24 = (bf16[48,3072]{1,0:T(8,128)(2,1)S(1)}, bf16[48,3072]{1,0:T(8,128)(2,1)S(1)}, u32[]{:S(2)}, u32[]{:S(2)}) collective-permute-start(bf16[48,3072]{1,0:T(8,128)(2,1)S(1)} %get-tuple-element.53), channel_id=1, source_target_pairs={{0,32},{8,40},{16,48},{24,56},{32,0},{40,8},{48,16},{56,24},{64,96... | collective-permute-start | bytes 884744 | tf_op jit(solution)/shard_map/ppermute | solution.py:28
  77.3 13.7 %collective-permute-start.25 = (bf16[48,3072]{1,0:T(8,128)(2,1)S(1)}, bf16[48,3072]{1,0:T(8,128)(2,1)S(1)}, u32[]{:S(2)}, u32[]{:S(2)}) collective-permute-start(bf16[48,3072]{1,0:T(8,128)(2,1)S(1)} %get-tuple-element.54), channel_id=1, source_target_pairs={{0,48},{8,56},{16,32},{24,40},{32,16},{40,24},{48,0},{56,8},{64,11... | collective-permute-start | bytes 884744 | tf_op jit(solution)/shard_map/ppermute | solution.py:28
  78.4 13.3 %collective-permute-start.23 = (bf16[48,3072]{1,0:T(8,128)(2,1)S(1)}, bf16[48,3072]{1,0:T(8,128)(2,1)S(1)}, u32[]{:S(2)}, u32[]{:S(2)}) collective-permute-start(bf16[48,3072]{1,0:T(8,128)(2,1)S(1)} %get-tuple-element.45), channel_id=1, source_target_pairs={{0,16},{8,24},{16,0},{24,8},{32,48},{40,56},{48,32},{56,40},{64,80... | collective-permute-start | bytes 884744 | tf_op jit(solution)/shard_map/ppermute | solution.py:28
  85.8 8.4 %collective-permute-start.26 = (bf16[1024,384]{1,0:T(8,128)(2,1)S(1)}, bf16[1024,384]{1,0:T(8,128)(2,1)S(1)}, u32[]{:S(2)}, u32[]{:S(2)}) collective-permute-start(bf16[1024,384]{1,0:T(8,128)(2,1)S(1)} %get-tuple-element.47), channel_id=1, source_target_pairs={{0,8},{8,0},{16,24},{24,16},{32,40},{40,32},{48,56},{56,48},{64,72... | collective-permute-start | bytes 2359304 | tf_op jit(solution)/shard_map/ppermute | solution.py:28
  86.0 20.2 %collective-permute-start.27 = (bf16[256,384]{1,0:T(8,128)(2,1)S(1)}, bf16[256,384]{1,0:T(8,128)(2,1)S(1)}, u32[]{:S(2)}, u32[]{:S(2)}) collective-permute-start(bf16[256,384]{1,0:T(8,128)(2,1)S(1)} %slice.129), channel_id=1, source_target_pairs={{0,1},{1,0},{2,3},{3,2},{4,5},{5,4},{6,7},{7,6},{8,9},{9,8},{10,11... | collective-permute-start | bytes 589832 | tf_op jit(solution)/shard_map/ppermute | solution.py:28
  91.9 9.3 %collective-permute-start.34 = (bf16[24,3072]{1,0:T(8,128)(2,1)S(1)}, bf16[24,3072]{1,0:T(8,128)(2,1)S(1)}, u32[]{:S(2)}, u32[]{:S(2)}) collective-permute-start(bf16[24,3072]{1,0:T(8,128)(2,1)S(1)} %slice.130), channel_id=1, source_target_pairs={{0,128},{8,136},{16,144},{24,152},{32,160},{40,168},{48,176},{56,1... | collective-permute-start | bytes 442376 | tf_op jit(solution)/shard_map/ppermute | solution.py:28
  94.4 23.8 %collective-permute-start.31 = (bf16[256,384]{1,0:T(8,128)(2,1)S(1)}, bf16[256,384]{1,0:T(8,128)(2,1)S(1)}, u32[]{:S(2)}, u32[]{:S(2)}) collective-permute-start(bf16[256,384]{1,0:T(8,128)(2,1)S(1)} %get-tuple-element.70), channel_id=1, source_target_pairs={{0,16},{8,24},{16,0},{24,8},{32,48},{40,56},{48,32},{56,40},{64,80... | collective-permute-start | bytes 589832 | tf_op jit(solution)/shard_map/ppermute | solution.py:28
  101.3 6.6 %collective-permute-start.35 = (bf16[12,3072]{1,0:T(8,128)(2,1)S(1)}, bf16[12,3072]{1,0:T(8,128)(2,1)S(1)}, u32[]{:S(2)}, u32[]{:S(2)}) collective-permute-start(bf16[12,3072]{1,0:T(8,128)(2,1)S(1)} %slice.131), channel_id=1, source_target_pairs={{0,64},{8,72},{16,80},{24,88},{32,96},{40,104},{48,112},{56,120},{... | collective-permute-start | bytes 221192 | tf_op jit(solution)/shard_map/ppermute | solution.py:28
  101.4 16.7 %collective-permute-start.29 = (bf16[768,128]{1,0:T(8,128)(2,1)S(1)}, bf16[768,128]{1,0:T(8,128)(2,1)S(1)}, u32[]{:S(2)}, u32[]{:S(2)}) collective-permute-start(bf16[768,128]{1,0:T(8,128)(2,1)S(1)} %get-tuple-element.59), channel_id=1, source_target_pairs={{0,128},{8,136},{16,144},{24,152},{32,160},{40,168},{48,176},{56,1... | collective-permute-start | bytes 589832 | tf_op jit(solution)/shard_map/ppermute | solution.py:28
  103.8 14.4 %collective-permute-start.32 = (bf16[256,384]{1,0:T(8,128)(2,1)S(1)}, bf16[256,384]{1,0:T(8,128)(2,1)S(1)}, u32[]{:S(2)}, u32[]{:S(2)}) collective-permute-start(bf16[256,384]{1,0:T(8,128)(2,1)S(1)} %get-tuple-element.68), channel_id=1, source_target_pairs={{0,32},{8,40},{16,48},{24,56},{32,0},{40,8},{48,16},{56,24},{64,96... | collective-permute-start | bytes 589832 | tf_op jit(solution)/shard_map/ppermute | solution.py:28
  106.2 12.0 %collective-permute-start.33 = (bf16[256,384]{1,0:T(8,128)(2,1)S(1)}, bf16[256,384]{1,0:T(8,128)(2,1)S(1)}, u32[]{:S(2)}, u32[]{:S(2)}) collective-permute-start(bf16[256,384]{1,0:T(8,128)(2,1)S(1)} %get-tuple-element.69), channel_id=1, source_target_pairs={{0,48},{8,56},{16,32},{24,40},{32,16},{40,24},{48,0},{56,8},{64,11... | collective-permute-start | bytes 589832 | tf_op jit(solution)/shard_map/ppermute | solution.py:28
  107.8 9.5 %collective-permute-start.28 = (bf16[128,384]{1,0:T(8,128)(2,1)S(1)}, bf16[128,384]{1,0:T(8,128)(2,1)S(1)}, u32[]{:S(2)}, u32[]{:S(2)}) collective-permute-start(bf16[128,384]{1,0:T(8,128)(2,1)S(1)} %slice.133), channel_id=1, source_target_pairs={{0,4},{1,5},{2,6},{3,7},{4,0},{5,1},{6,2},{7,3},{8,12},{9,13},{10,... | collective-permute-start | bytes 294920 | tf_op jit(solution)/shard_map/ppermute | solution.py:28
  118.1 4.7 %collective-permute-start.30 = (bf16[384,128]{1,0:T(8,128)(2,1)S(1)}, bf16[384,128]{1,0:T(8,128)(2,1)S(1)}, u32[]{:S(2)}, u32[]{:S(2)}) collective-permute-start(bf16[384,128]{1,0:T(8,128)(2,1)S(1)} %slice.132), channel_id=1, source_target_pairs={{0,64},{8,72},{16,80},{24,88},{32,96},{40,104},{48,112},{56,120},{... | collective-permute-start | bytes 294920 | tf_op jit(solution)/shard_map/ppermute | solution.py:28
  (12 other events, 42.1 us)

commit v2 on v1

--- a/solution.py
+++ b/solution.py
@@ -40,7 +40,7 @@
 
 
 def call(kernel, outs, *args, flops, moved, scratch=(), limit=24, by_hand=False):
-    anywhere = pl.BlockSpec(memory_space=pl.ANY)
+    anywhere = pl.BlockSpec(memory_space=pltpu.HBM)
     vmem = pl.BlockSpec(memory_space=pltpu.VMEM)
     smem = pl.BlockSpec(memory_space=pltpu.SMEM)
     return pl.pallas_call(
@@ -246,7 +246,6 @@
     t, y, c = slab // 8, slab // 2 % 4, slab % 2
     ranks = jnp.stack([t, y, c, head]).astype(jnp.int32)
 
-    d_across = swap(d_out, "head", 4)
     q_ext, kv = call(
         pack_kernel,
         [((ROWS + 16, COLS), BF), ((2 * ROWS, COLS), BF)],
@@ -259,12 +258,14 @@
         moved=10**6,
         scratch=[pltpu.SMEM((2, 4), jnp.int32), pltpu.SMEM((2,), jnp.int32), pltpu.SemaphoreType.DMA((5,))],
         by_hand=True,
+        limit=58,
     )
     kv_near = [kv] + [swap(kv, "slab", 2 * e) for e in (1, 2, 3)]
     q_all = gathered(q_ext, "slab", 8)
     kv_all = kv_near + [swap(block, "slab", 1) for block in kv_near]
 
-    d_full = after(jnp.concatenate([d_out, d_across], axis=0), *kv_near)
+    d_across = after(swap(after(d_out, q_all[1]), "head", 4), *kv_near)
+    d_full = jnp.concatenate([d_out, d_across], axis=0)
     d_full = jnp.concatenate([d_full, swap(d_full, "head", 1)], axis=0)
     d_full = jnp.concatenate([d_full, swap(d_full, "head", 2)], axis=0)
 
@@ -280,7 +281,7 @@
         scratch=[pltpu.VMEM((8 * ROWS, 4 * ROWS), F32), bias_scratch],
     )
     parts = [parts[0]] + [swap(parts[j], "slab", 8 * j) for j in (1, 2, 3)]
-    d_full = after(d_full, parts[1])
+    d_full = after(d_full, *parts[1:])
     d_other = swap(d_full, "slab", 1)
     grad = call(grad_kernel, [((COLS, ROWS), BF)], ranks, w_out, d_full, flops=3 * 10**8, moved=3 * 10**6)[0]
     g_all = gathered(grad, "slab", 8)
@@ -334,16 +335,21 @@
     other = swap(other, "slab", 1)
     pair = (after(own, weight_away, mixed_away) + other.astype(F32)).reshape(4, 2 * ROWS, COLS)
     away = [pair[e].astype(BF) for e in (1, 2, 3)]
-    total = pair[0] + sum((swap(away[e - 1], "slab", 2 * e).astype(F32) for e in (1, 2, 3)), 0.0)
+    arrived = [swap(away[e - 1], "slab", 2 * e) for e in (1, 2, 3)]
+    dq_in = swap(after(dq_other, other), "slab", 16)
+
+    weight = after(weight[:24], arrived[1]) + swap(weight_away, "slab", 16).astype(F32)
+    weight_away = weight[12:].astype(BF)
+    mixed = after(mixed[: 2 * ROWS], arrived[1]) + swap(mixed_away, "head", 1).astype(F32)
+    mixed_away = mixed[ROWS:].astype(BF)
+    dq = after(dq_own, arrived[1]) + dq_in.astype(F32)
+    dq_away = dq[COLS:].astype(BF)
+
+    total = after(pair[0], weight_away, mixed_away, dq_away) + sum((a.astype(F32) for a in arrived), 0.0)
     total = total.astype(BF)
-
-    weight = after(weight[:24], away[0]) + swap(weight_away, "slab", 16).astype(F32)
-    weight_grad = weight[:12] + swap(weight[12:].astype(BF), "slab", 8).astype(F32)
-    mixed = after(mixed[: 2 * ROWS], away[0]) + swap(mixed_away, "head", 1).astype(F32)
-    mixed = mixed[:ROWS] + swap(mixed[ROWS:].astype(BF), "head", 4).astype(F32)
-
-    dq = dq_own + swap(after(dq_other, away[0]), "slab", 16).astype(F32)
-    dq = dq[:COLS] + swap(dq[COLS:].astype(BF), "slab", 8).astype(F32)
+    weight_grad = weight[:12] + swap(weight_away, "slab", 8).astype(F32)
+    mixed = mixed[:ROWS] + swap(mixed_away, "head", 4).astype(F32)
+    dq = dq[:COLS] + swap(dq_away, "slab", 8).astype(F32)
     query_grad = dq.astype(BF).T
     return mixed.astype(BF), query_grad, total[:ROWS], total[ROWS:], weight_grad
 

time: 124 us -> 122 us (0.984); the launches traced: 124 us -> 120 us
  waiting for transfers between devices: 51.4 us -> 37.7 us
  starting transfers between devices: 46.9 us -> 58.2 us
  local copies, waits for them, and re-layouts: 5.68 us -> 1.71 us
  other arithmetic: 3.17 us -> 4.93 us
    ppermute x36, waiting for transfers between devices: 51.4 us -> 37.7 us  [swap(): return lax.ppermute(block, axis, [(i, i ^ distance) for i in devices])]
    ppermute x36, starting transfers between devices: 46.9 us -> 58.2 us  [swap(): return lax.ppermute(block, axis, [(i, i ^ distance) for i in devices])]
    unnamed x15 -> x11, local copies, waits for them, and re-layouts: 4.77 us -> 0.78 us
  transfers between devices with their start and end apart: 36 -> 36, of which waited for: 14 -> 16; matrix products, arithmetic and copies ran while one was open for 3% -> 4% of each run, Pallas kernels for 12% -> 12%
where the time goes in v2:
time: 122 us; the launch traced here: 120 us
  starting transfers between devices  58.2 us (48%)
  waiting for transfers between devices  37.7 us (31%)
  Pallas kernels  16.6 us (14%)
  other arithmetic  4.93 us (4%)
  local copies, waits for them, and re-layouts  1.71 us (1%)
    ppermute x36, starting transfers between devices, swap(): return lax.ppermute(block, axis, [(i, i ^ distance) for i in devices])  58.2 us
    ppermute x36, waiting for transfers between devices, swap(): return lax.ppermute(block, axis, [(i, i ^ distance) for i in devices])  37.7 us
    pallas_call x8, Pallas kernels, call(): pl.pallas_call(kernel, out_shape=[jax.ShapeDtypeStruct(shape, dtype) for...  16.6 us
  transfers between devices with their start and end apart: 36, of which 16 were waited for; matrix products, arithmetic and copies ran while one was open for 4% of the time, Pallas kernels for 12%

profile of v2, /device:TPU:2, one launch (start us, length us, event | category | flops | bytes accessed | tf_op | source)
XLA Modules:
  0.0 120.1 jit_solution(17005354062393738869)
XLA Ops:
  0.6 1.7 %shard_map.110 = (bf16[144,384]{1,0:T(8,128)(2,1)}, bf16[256,384]{1,0:T(8,128)(2,1)}) custom-call(s32[2,4]{1,0:T(2,128)} %ids_hbm.1, s32[2]{0:T(128)} %counts_hbm.1, bf16[128,384]{1,0:T(8,128)(2,1)} %q_hbm.1, bf16[128,384]{1,0:T(8,128)(2,1)} %k_hbm.1, bf16[128,384]{1,0:T(8,128)(2,1)} %v_hbm.1), custom_call_target="tpu_custom_call" | custom-call | flops 1000 | bytes 1000 | tf_op jit(solution)/shard_map/pallas_call | solution.py:46
  2.4 2.0 %collective-permute-start = (bf16[144,384]{1,0:T(8,128)(2,1)}, bf16[144,384]{1,0:T(8,128)(2,1)S(1)}, u32[]{:S(2)}, u32[]{:S(2)}) collective-permute-start(bf16[144,384]{1,0:T(8,128)(2,1)} %get-tuple-element.36.refs_1_), channel_id=1, source_target_pairs={{0,64},{8,72},{16,80},{24,88},{32,96},{40,104},{48,112},{56,120},{... | collective-permute-start | bytes 331784 | tf_op jit(solution)/shard_map/ppermute | solution.py:28
  4.4 3.0 %collective-permute-start.4 = (bf16[256,384]{1,0:T(8,128)(2,1)}, bf16[256,384]{1,0:T(8,128)(2,1)S(1)}, u32[]{:S(2)}, u32[]{:S(2)}) collective-permute-start(bf16[256,384]{1,0:T(8,128)(2,1)} %get-tuple-element.37.refs_5_), channel_id=1, source_target_pairs={{0,48},{8,56},{16,32},{24,40},{32,16},{40,24},{48,0},{56,8},{64,11... | collective-permute-start | bytes 589832 | tf_op jit(solution)/shard_map/ppermute | solution.py:28
  8.5 6.3 %collective-permute-start.9 = (bf16[128,384]{1,0:T(8,128)(2,1)}, bf16[128,384]{1,0:T(8,128)(2,1)S(1)}, u32[]{:S(2)}, u32[]{:S(2)}) collective-permute-start(bf16[128,384]{1,0:T(8,128)(2,1)} %param.11), channel_id=1, source_target_pairs={{0,4},{1,5},{2,6},{3,7},{4,0},{5,1},{6,2},{7,3},{8,12},{9,13},{10,... | collective-permute-start | bytes 294920 | tf_op jit(solution)/shard_map/ppermute | solution.py:28
  17.1 1.4 %collective-permute-done.9 = bf16[128,384]{1,0:T(8,128)(2,1)S(1)} collective-permute-done((bf16[128,384]{1,0:T(8,128)(2,1)}, bf16[128,384]{1,0:T(8,128)(2,1)S(1)}, u32[]{:S(2)}, u32[]{:S(2)}) %collective-permute-start.9) | collective-permute-done | bytes 98336 | tf_op jit(solution)/shard_map/ppermute | solution.py:28
  20.8 3.1 %collective-permute-start.1 = (bf16[288,384]{1,0:T(8,128)(2,1)S(1)}, bf16[288,384]{1,0:T(8,128)(2,1)S(1)}, u32[]{:S(2)}, u32[]{:S(2)}) collective-permute-start(bf16[288,384]{1,0:T(8,128)(2,1)S(1)} %pad_maximum_fusion.2), channel_id=1, source_target_pairs={{0,128},{8,136},{16,144},{24,152},{32,160},{40,168},{48,176},{56,1... | collective-permute-start | bytes 663560 | tf_op jit(solution)/shard_map/ppermute | solution.py:28
  26.1 2.2 %collective-permute-start.11 = (bf16[512,384]{1,0:T(8,128)(2,1)S(1)}, bf16[512,384]{1,0:T(8,128)(2,1)S(1)}, u32[]{:S(2)}, u32[]{:S(2)}) collective-permute-start(bf16[512,384]{1,0:T(8,128)(2,1)S(1)} %pad_maximum_fusion.1), channel_id=1, source_target_pairs={{0,2},{1,3},{2,0},{3,1},{4,6},{5,7},{6,4},{7,5},{8,10},{9,11},{10,... | collective-permute-start | bytes 1179656 | tf_op jit(solution)/shard_map/ppermute | solution.py:28
  29.0 2.7 %collective-permute-done.1 = bf16[288,384]{1,0:T(8,128)(2,1)S(1)} collective-permute-done((bf16[288,384]{1,0:T(8,128)(2,1)S(1)}, bf16[288,384]{1,0:T(8,128)(2,1)S(1)}, u32[]{:S(2)}, u32[]{:S(2)}) %collective-permute-start.1) | collective-permute-done | bytes 221216 | tf_op jit(solution)/shard_map/ppermute | solution.py:28
  31.8 1.4 %collective-permute-done.6.refs_10_ = bf16[256,384]{1,0:T(8,128)(2,1)S(1)} collective-permute-done((bf16[256,384]{1,0:T(8,128)(2,1)S(1)}, bf16[256,384]{1,0:T(8,128)(2,1)S(1)}, u32[]{:S(2)}, u32[]{:S(2)}) %collective-permute-start.6) | collective-permute-done | bytes 196640 | tf_op jit(solution)/shard_map/ppermute | solution.py:28
  33.2 3.9 %shard_map.111 = (bf16[400,128]{1,0:T(8,128)(2,1)S(1)}, bf16[400,128]{1,0:T(8,128)(2,1)S(1)}, bf16[400,128]{1,0:T(8,128)(2,1)S(1)}, bf16[400,128]{1,0:T(8,128)(2,1)S(1)}) custom-call(s32[4]{0:T(128)S(1)} %pad_add_fusion.refs_0_.rank_ref, bf16[144,384]{1,0:T(8,128)(2,1)S(1)} %copy-done.1, bf16[144,384]{1,0:T(8,128)(2,1)S(1)} %collective-permute-done.refs_2_, ...), custom_call_target="tpu_custom_call" | custom-call | flops 1000 | bytes 1000 | tf_op jit(solution)/shard_map/pallas_call | solution.py:46
  37.2 3.2 %collective-permute-start.13 = (bf16[400,128]{1,0:T(8,128)(2,1)S(1)}, bf16[400,128]{1,0:T(8,128)(2,1)S(1)}, u32[]{:S(2)}, u32[]{:S(2)}) collective-permute-start(bf16[400,128]{1,0:T(8,128)(2,1)S(1)} %get-tuple-element.42), channel_id=1, source_target_pairs={{0,128},{8,136},{16,144},{24,152},{32,160},{40,168},{48,176},{56,1... | collective-permute-start | bytes 307208 | tf_op jit(solution)/shard_map/ppermute | solution.py:28
  41.7 2.1 %collective-permute-done.12.refs_1_ = bf16[400,128]{1,0:T(8,128)(2,1)S(1)} collective-permute-done((bf16[400,128]{1,0:T(8,128)(2,1)S(1)}, bf16[400,128]{1,0:T(8,128)(2,1)S(1)}, u32[]{:S(2)}, u32[]{:S(2)}) %collective-permute-start.12) | collective-permute-done | bytes 102432 | tf_op jit(solution)/shard_map/ppermute | solution.py:28
  43.8 4.7 %collective-permute-done.13.refs_2_ = bf16[400,128]{1,0:T(8,128)(2,1)S(1)} collective-permute-done((bf16[400,128]{1,0:T(8,128)(2,1)S(1)}, bf16[400,128]{1,0:T(8,128)(2,1)S(1)}, u32[]{:S(2)}, u32[]{:S(2)}) %collective-permute-start.13) | collective-permute-done | bytes 102432 | tf_op jit(solution)/shard_map/ppermute | solution.py:28
  49.9 2.0 %collective-permute-start.15 = (bf16[384,128]{1,0:T(8,128)(2,1)S(1)}, bf16[384,128]{1,0:T(8,128)(2,1)S(1)}, u32[]{:S(2)}, u32[]{:S(2)}) collective-permute-start(bf16[384,128]{1,0:T(8,128)(2,1)S(1)} %shard_map.112.grad_ref.refs_13_), channel_id=1, source_target_pairs={{0,64},{8,72},{16,80},{24,88},{32,96},{40,104},{48,112},{56,120},{... | collective-permute-start | bytes 294920 | tf_op jit(solution)/shard_map/ppermute | solution.py:28
  51.9 3.5 %collective-permute-done.15.refs_14_ = bf16[384,128]{1,0:T(8,128)(2,1)S(1)} collective-permute-done((bf16[384,128]{1,0:T(8,128)(2,1)S(1)}, bf16[384,128]{1,0:T(8,128)(2,1)S(1)}, u32[]{:S(2)}, u32[]{:S(2)}) %collective-permute-start.15) | collective-permute-done | bytes 98336 | tf_op jit(solution)/shard_map/ppermute | solution.py:28
  55.4 2.8 %collective-permute-start.16 = (bf16[768,128]{1,0:T(8,128)(2,1)S(1)}, bf16[768,128]{1,0:T(8,128)(2,1)S(1)}, u32[]{:S(2)}, u32[]{:S(2)}) collective-permute-start(bf16[768,128]{1,0:T(8,128)(2,1)S(1)} %pad_maximum_fusion.4), channel_id=1, source_target_pairs={{0,128},{8,136},{16,144},{24,152},{32,160},{40,168},{48,176},{56,1... | collective-permute-start | bytes 589832 | tf_op jit(solution)/shard_map/ppermute | solution.py:28
  59.6 2.5 %collective-permute-start.22 = (bf16[512,384]{1,0:T(8,128)(2,1)S(1)}, bf16[512,384]{1,0:T(8,128)(2,1)S(1)}, u32[]{:S(2)}, u32[]{:S(2)}) collective-permute-start(bf16[512,384]{1,0:T(8,128)(2,1)S(1)} %get-tuple-element.53), channel_id=1, source_target_pairs={{0,2},{1,3},{2,0},{3,1},{4,6},{5,7},{6,4},{7,5},{8,10},{9,11},{10,... | collective-permute-start | bytes 1179656 | tf_op jit(solution)/shard_map/ppermute | solution.py:28
  62.2 1.4 %collective-permute-start.21 = (f32[8,128]{1,0:T(8,128)S(1)}, f32[8,128]{1,0:T(8,128)S(1)}, u32[]{:S(2)}, u32[]{:S(2)}) collective-permute-start(f32[8,128]{1,0:T(8,128)S(1)} %shard_map.115.refs_17_), channel_id=1, source_target_pairs={{0,192},{8,200},{16,208},{24,216},{32,224},{40,232},{48,240},{56,2... | collective-permute-start | bytes 12296 | tf_op jit(solution)/shard_map/ppermute | solution.py:28
  64.0 2.6 %collective-permute-start.19 = (f32[8,128]{1,0:T(8,128)S(1)}, f32[8,128]{1,0:T(8,128)S(1)}, u32[]{:S(2)}, u32[]{:S(2)}) collective-permute-start(f32[8,128]{1,0:T(8,128)S(1)} %shard_map.115.refs_17_), channel_id=1, source_target_pairs={{0,64},{8,72},{16,80},{24,88},{32,96},{40,104},{48,112},{56,120},{... | collective-permute-start | bytes 12296 | tf_op jit(solution)/shard_map/ppermute | solution.py:28
  68.0 3.1 %collective-permute-start.24 = (bf16[48,3072]{1,0:T(8,128)(2,1)S(1)}, bf16[48,3072]{1,0:T(8,128)(2,1)S(1)}, u32[]{:S(2)}, u32[]{:S(2)}) collective-permute-start(bf16[48,3072]{1,0:T(8,128)(2,1)S(1)} %get-tuple-element.57), channel_id=1, source_target_pairs={{0,32},{8,40},{16,48},{24,56},{32,0},{40,8},{48,16},{56,24},{64,96... | collective-permute-start | bytes 884744 | tf_op jit(solution)/shard_map/ppermute | solution.py:28
  72.2 6.9 %shard_map.117 = (f32[768,128]{1,0:T(8,128)S(1)}, bf16[768,128]{1,0:T(8,128)(2,1)S(1)}, f32[1024,384]{1,0:T(8,128)S(1)}, bf16[1024,384]{1,0:T(8,128)(2,1)S(1)}) custom-call(s32[4]{0:T(128)S(1)} %pad_add_fusion.refs_0_.rank_ref, bf16[144,384]{1,0:T(8,128)(2,1)S(1)} %copy-done.1, bf16[144,384]{1,0:T(8,128)(2,1)S(1)} %collective-permute-done.refs_2_, ...), custom_call_target="tpu_custom_call" | custom-call | flops 1000 | bytes 1000 | tf_op jit(solution)/shard_map/pallas_call | solution.py:46
  79.5 4.9 %collective-permute-done.25 = bf16[48,3072]{1,0:T(8,128)(2,1)S(1)} collective-permute-done((bf16[48,3072]{1,0:T(8,128)(2,1)S(1)}, bf16[48,3072]{1,0:T(8,128)(2,1)S(1)}, u32[]{:S(2)}, u32[]{:S(2)}) %collective-permute-start.25) | collective-permute-done | bytes 294944 | tf_op jit(solution)/shard_map/ppermute | solution.py:28
  85.3 2.1 %collective-permute-start.27 = (bf16[256,384]{1,0:T(8,128)(2,1)S(1)}, bf16[256,384]{1,0:T(8,128)(2,1)S(1)}, u32[]{:S(2)}, u32[]{:S(2)}) collective-permute-start(bf16[256,384]{1,0:T(8,128)(2,1)S(1)} %get-tuple-element.76), channel_id=1, source_target_pairs={{0,32},{8,40},{16,48},{24,56},{32,0},{40,8},{48,16},{56,24},{64,96... | collective-permute-start | bytes 589832 | tf_op jit(solution)/shard_map/ppermute | solution.py:28
  87.8 1.8 %collective-permute-start.28 = (bf16[256,384]{1,0:T(8,128)(2,1)S(1)}, bf16[256,384]{1,0:T(8,128)(2,1)S(1)}, u32[]{:S(2)}, u32[]{:S(2)}) collective-permute-start(bf16[256,384]{1,0:T(8,128)(2,1)S(1)} %slice.126), channel_id=1, source_target_pairs={{0,1},{1,0},{2,3},{3,2},{4,5},{5,4},{6,7},{7,6},{8,9},{9,8},{10,11... | collective-permute-start | bytes 589832 | tf_op jit(solution)/shard_map/ppermute | solution.py:28
  89.6 2.6 %collective-permute-start.30 = (bf16[768,128]{1,0:T(8,128)(2,1)S(1)}, bf16[768,128]{1,0:T(8,128)(2,1)S(1)}, u32[]{:S(2)}, u32[]{:S(2)}) collective-permute-start(bf16[768,128]{1,0:T(8,128)(2,1)S(1)} %get-tuple-element.64), channel_id=1, source_target_pairs={{0,128},{8,136},{16,144},{24,152},{32,160},{40,168},{48,176},{56,1... | collective-permute-start | bytes 589832 | tf_op jit(solution)/shard_map/ppermute | solution.py:28
  92.3 1.5 %collective-permute-start.33 = (bf16[256,384]{1,0:T(8,128)(2,1)S(1)}, bf16[256,384]{1,0:T(8,128)(2,1)S(1)}, u32[]{:S(2)}, u32[]{:S(2)}) collective-permute-start(bf16[256,384]{1,0:T(8,128)(2,1)S(1)} %get-tuple-element.74), channel_id=1, source_target_pairs={{0,16},{8,24},{16,0},{24,8},{32,48},{40,56},{48,32},{56,40},{64,80... | collective-permute-start | bytes 589832 | tf_op jit(solution)/shard_map/ppermute | solution.py:28
  93.8 2.7 %collective-permute-start.34 = (bf16[256,384]{1,0:T(8,128)(2,1)S(1)}, bf16[256,384]{1,0:T(8,128)(2,1)S(1)}, u32[]{:S(2)}, u32[]{:S(2)}) collective-permute-start(bf16[256,384]{1,0:T(8,128)(2,1)S(1)} %get-tuple-element.75), channel_id=1, source_target_pairs={{0,48},{8,56},{16,32},{24,40},{32,16},{40,24},{48,0},{56,8},{64,11... | collective-permute-start | bytes 589832 | tf_op jit(solution)/shard_map/ppermute | solution.py:28
  96.5 4.1 %collective-permute-done.32 = bf16[24,3072]{1,0:T(8,128)(2,1)S(1)} collective-permute-done((bf16[24,3072]{1,0:T(8,128)(2,1)S(1)}, bf16[24,3072]{1,0:T(8,128)(2,1)S(1)}, u32[]{:S(2)}, u32[]{:S(2)}) %collective-permute-start.32) | collective-permute-done | bytes 147488 | tf_op jit(solution)/shard_map/ppermute | solution.py:28
  100.6 3.9 %collective-permute-done.30 = bf16[768,128]{1,0:T(8,128)(2,1)S(1)} collective-permute-done((bf16[768,128]{1,0:T(8,128)(2,1)S(1)}, bf16[768,128]{1,0:T(8,128)(2,1)S(1)}, u32[]{:S(2)}, u32[]{:S(2)}) %collective-permute-start.30) | collective-permute-done | bytes 196640 | tf_op jit(solution)/shard_map/ppermute | solution.py:28
  104.6 2.0 %collective-permute-start.31 = (bf16[384,128]{1,0:T(8,128)(2,1)S(1)}, bf16[384,128]{1,0:T(8,128)(2,1)S(1)}, u32[]{:S(2)}, u32[]{:S(2)}) collective-permute-start(bf16[384,128]{1,0:T(8,128)(2,1)S(1)} %slice.129), channel_id=1, source_target_pairs={{0,64},{8,72},{16,80},{24,88},{32,96},{40,104},{48,112},{56,120},{... | collective-permute-start | bytes 294920 | tf_op jit(solution)/shard_map/ppermute | solution.py:28
  106.7 5.6 %collective-permute-start.29 = (bf16[128,384]{1,0:T(8,128)(2,1)S(1)}, bf16[128,384]{1,0:T(8,128)(2,1)S(1)}, u32[]{:S(2)}, u32[]{:S(2)}) collective-permute-start(bf16[128,384]{1,0:T(8,128)(2,1)S(1)} %slice.130), channel_id=1, source_target_pairs={{0,4},{1,5},{2,6},{3,7},{4,0},{5,1},{6,2},{7,3},{8,12},{9,13},{10,... | collective-permute-start | bytes 294920 | tf_op jit(solution)/shard_map/ppermute | solution.py:28
  114.6 4.8 %collective-permute-done.29 = bf16[128,384]{1,0:T(8,128)(2,1)S(1)} collective-permute-done((bf16[128,384]{1,0:T(8,128)(2,1)S(1)}, bf16[128,384]{1,0:T(8,128)(2,1)S(1)}, u32[]{:S(2)}, u32[]{:S(2)}) %collective-permute-start.29) | collective-permute-done | bytes 98336 | tf_op jit(solution)/shard_map/ppermute | solution.py:28
  (88 shorter events, 20.4 us)
Async XLA Ops:
  2.4 6.1 %collective-permute-start = (bf16[144,384]{1,0:T(8,128)(2,1)}, bf16[144,384]{1,0:T(8,128)(2,1)S(1)}, u32[]{:S(2)}, u32[]{:S(2)}) collective-permute-start(bf16[144,384]{1,0:T(8,128)(2,1)} %get-tuple-element.36.refs_1_), channel_id=1, source_target_pairs={{0,64},{8,72},{16,80},{24,88},{32,96},{40,104},{48,112},{56,120},{... | collective-permute-start | bytes 331784 | tf_op jit(solution)/shard_map/ppermute | solution.py:28
  4.4 11.5 %collective-permute-start.4 = (bf16[256,384]{1,0:T(8,128)(2,1)}, bf16[256,384]{1,0:T(8,128)(2,1)S(1)}, u32[]{:S(2)}, u32[]{:S(2)}) collective-permute-start(bf16[256,384]{1,0:T(8,128)(2,1)} %get-tuple-element.37.refs_5_), channel_id=1, source_target_pairs={{0,48},{8,56},{16,32},{24,40},{32,16},{40,24},{48,0},{56,8},{64,11... | collective-permute-start | bytes 589832 | tf_op jit(solution)/shard_map/ppermute | solution.py:28
  7.4 9.6 %collective-permute-start.3 = (bf16[256,384]{1,0:T(8,128)(2,1)}, bf16[256,384]{1,0:T(8,128)(2,1)S(1)}, u32[]{:S(2)}, u32[]{:S(2)}) collective-permute-start(bf16[256,384]{1,0:T(8,128)(2,1)} %get-tuple-element.37.refs_5_), channel_id=1, source_target_pairs={{0,32},{8,40},{16,48},{24,56},{32,0},{40,8},{48,16},{56,24},{64,96... | collective-permute-start | bytes 589832 | tf_op jit(solution)/shard_map/ppermute | solution.py:28
  8.1 9.0 %collective-permute-start.2 = (bf16[256,384]{1,0:T(8,128)(2,1)}, bf16[256,384]{1,0:T(8,128)(2,1)S(1)}, u32[]{:S(2)}, u32[]{:S(2)}) collective-permute-start(bf16[256,384]{1,0:T(8,128)(2,1)} %get-tuple-element.37.refs_5_), channel_id=1, source_target_pairs={{0,16},{8,24},{16,0},{24,8},{32,48},{40,56},{48,32},{56,40},{64,80... | collective-permute-start | bytes 589832 | tf_op jit(solution)/shard_map/ppermute | solution.py:28
  8.5 10.0 %collective-permute-start.9 = (bf16[128,384]{1,0:T(8,128)(2,1)}, bf16[128,384]{1,0:T(8,128)(2,1)S(1)}, u32[]{:S(2)}, u32[]{:S(2)}) collective-permute-start(bf16[128,384]{1,0:T(8,128)(2,1)} %param.11), channel_id=1, source_target_pairs={{0,4},{1,5},{2,6},{3,7},{4,0},{5,1},{6,2},{7,3},{8,12},{9,13},{10,... | collective-permute-start | bytes 294920 | tf_op jit(solution)/shard_map/ppermute | solution.py:28
  19.4 5.8 %collective-permute-start.10 = (bf16[256,384]{1,0:T(8,128)(2,1)S(1)}, bf16[256,384]{1,0:T(8,128)(2,1)S(1)}, u32[]{:S(2)}, u32[]{:S(2)}) collective-permute-start(bf16[256,384]{1,0:T(8,128)(2,1)S(1)} %pad_maximum_fusion.3), channel_id=1, source_target_pairs={{0,1},{1,0},{2,3},{3,2},{4,5},{5,4},{6,7},{7,6},{8,9},{9,8},{10,11... | collective-permute-start | bytes 589832 | tf_op jit(solution)/shard_map/ppermute | solution.py:28
  20.8 10.9 %collective-permute-start.1 = (bf16[288,384]{1,0:T(8,128)(2,1)S(1)}, bf16[288,384]{1,0:T(8,128)(2,1)S(1)}, u32[]{:S(2)}, u32[]{:S(2)}) collective-permute-start(bf16[288,384]{1,0:T(8,128)(2,1)S(1)} %pad_maximum_fusion.2), channel_id=1, source_target_pairs={{0,128},{8,136},{16,144},{24,152},{32,160},{40,168},{48,176},{56,1... | collective-permute-start | bytes 663560 | tf_op jit(solution)/shard_map/ppermute | solution.py:28
  26.1 15.5 %collective-permute-start.11 = (bf16[512,384]{1,0:T(8,128)(2,1)S(1)}, bf16[512,384]{1,0:T(8,128)(2,1)S(1)}, u32[]{:S(2)}, u32[]{:S(2)}) collective-permute-start(bf16[512,384]{1,0:T(8,128)(2,1)S(1)} %pad_maximum_fusion.1), channel_id=1, source_target_pairs={{0,2},{1,3},{2,0},{3,1},{4,6},{5,7},{6,4},{7,5},{8,10},{9,11},{10,... | collective-permute-start | bytes 1179656 | tf_op jit(solution)/shard_map/ppermute | solution.py:28
  28.3 3.4 %collective-permute-start.5 = (bf16[256,384]{1,0:T(8,128)(2,1)S(1)}, bf16[256,384]{1,0:T(8,128)(2,1)S(1)}, u32[]{:S(2)}, u32[]{:S(2)}) collective-permute-start(bf16[256,384]{1,0:T(8,128)(2,1)S(1)} %copy-done.2), channel_id=1, source_target_pairs={{0,8},{8,0},{16,24},{24,16},{32,40},{40,32},{48,56},{56,48},{64,72... | collective-permute-start | bytes 589832 | tf_op jit(solution)/shard_map/ppermute | solution.py:28
  37.1 6.7 %collective-permute-start.12 = (bf16[400,128]{1,0:T(8,128)(2,1)S(1)}, bf16[400,128]{1,0:T(8,128)(2,1)S(1)}, u32[]{:S(2)}, u32[]{:S(2)}) collective-permute-start(bf16[400,128]{1,0:T(8,128)(2,1)S(1)} %get-tuple-element.41), channel_id=1, source_target_pairs={{0,64},{8,72},{16,80},{24,88},{32,96},{40,104},{48,112},{56,120},{... | collective-permute-start | bytes 307208 | tf_op jit(solution)/shard_map/ppermute | solution.py:28
  37.2 11.3 %collective-permute-start.13 = (bf16[400,128]{1,0:T(8,128)(2,1)S(1)}, bf16[400,128]{1,0:T(8,128)(2,1)S(1)}, u32[]{:S(2)}, u32[]{:S(2)}) collective-permute-start(bf16[400,128]{1,0:T(8,128)(2,1)S(1)} %get-tuple-element.42), channel_id=1, source_target_pairs={{0,128},{8,136},{16,144},{24,152},{32,160},{40,168},{48,176},{56,1... | collective-permute-start | bytes 307208 | tf_op jit(solution)/shard_map/ppermute | solution.py:28
  40.4 8.1 %collective-permute-start.14 = (bf16[400,128]{1,0:T(8,128)(2,1)S(1)}, bf16[400,128]{1,0:T(8,128)(2,1)S(1)}, u32[]{:S(2)}, u32[]{:S(2)}) collective-permute-start(bf16[400,128]{1,0:T(8,128)(2,1)S(1)} %get-tuple-element.43), channel_id=1, source_target_pairs={{0,192},{8,200},{16,208},{24,216},{32,224},{40,232},{48,240},{56,2... | collective-permute-start | bytes 307208 | tf_op jit(solution)/shard_map/ppermute | solution.py:28
  48.5 15.5 %collective-permute-start.18 = (bf16[1024,384]{1,0:T(8,128)(2,1)S(1)}, bf16[1024,384]{1,0:T(8,128)(2,1)S(1)}, u32[]{:S(2)}, u32[]{:S(2)}) collective-permute-start(bf16[1024,384]{1,0:T(8,128)(2,1)S(1)} %pad_maximum_fusion.d_ref), channel_id=1, source_target_pairs={{0,8},{8,0},{16,24},{24,16},{32,40},{40,32},{48,56},{56,48},{64,72... | collective-permute-start | bytes 2359304 | tf_op jit(solution)/shard_map/ppermute | solution.py:28
  49.9 5.5 %collective-permute-start.15 = (bf16[384,128]{1,0:T(8,128)(2,1)S(1)}, bf16[384,128]{1,0:T(8,128)(2,1)S(1)}, u32[]{:S(2)}, u32[]{:S(2)}) collective-permute-start(bf16[384,128]{1,0:T(8,128)(2,1)S(1)} %shard_map.112.grad_ref.refs_13_), channel_id=1, source_target_pairs={{0,64},{8,72},{16,80},{24,88},{32,96},{40,104},{48,112},{56,120},{... | collective-permute-start | bytes 294920 | tf_op jit(solution)/shard_map/ppermute | solution.py:28
  55.4 16.7 %collective-permute-start.16 = (bf16[768,128]{1,0:T(8,128)(2,1)S(1)}, bf16[768,128]{1,0:T(8,128)(2,1)S(1)}, u32[]{:S(2)}, u32[]{:S(2)}) collective-permute-start(bf16[768,128]{1,0:T(8,128)(2,1)S(1)} %pad_maximum_fusion.4), channel_id=1, source_target_pairs={{0,128},{8,136},{16,144},{24,152},{32,160},{40,168},{48,176},{56,1... | collective-permute-start | bytes 589832 | tf_op jit(solution)/shard_map/ppermute | solution.py:28
  59.6 19.6 %collective-permute-start.22 = (bf16[512,384]{1,0:T(8,128)(2,1)S(1)}, bf16[512,384]{1,0:T(8,128)(2,1)S(1)}, u32[]{:S(2)}, u32[]{:S(2)}) collective-permute-start(bf16[512,384]{1,0:T(8,128)(2,1)S(1)} %get-tuple-element.53), channel_id=1, source_target_pairs={{0,2},{1,3},{2,0},{3,1},{4,6},{5,7},{6,4},{7,5},{8,10},{9,11},{10,... | collective-permute-start | bytes 1179656 | tf_op jit(solution)/shard_map/ppermute | solution.py:28
  62.2 5.8 %collective-permute-start.21 = (f32[8,128]{1,0:T(8,128)S(1)}, f32[8,128]{1,0:T(8,128)S(1)}, u32[]{:S(2)}, u32[]{:S(2)}) collective-permute-start(f32[8,128]{1,0:T(8,128)S(1)} %shard_map.115.refs_17_), channel_id=1, source_target_pairs={{0,192},{8,200},{16,208},{24,216},{32,224},{40,232},{48,240},{56,2... | collective-permute-start | bytes 12296 | tf_op jit(solution)/shard_map/ppermute | solution.py:28
  63.6 7.5 %collective-permute-start.20 = (f32[8,128]{1,0:T(8,128)S(1)}, f32[8,128]{1,0:T(8,128)S(1)}, u32[]{:S(2)}, u32[]{:S(2)}) collective-permute-start(f32[8,128]{1,0:T(8,128)S(1)} %shard_map.115.refs_17_), channel_id=1, source_target_pairs={{0,128},{8,136},{16,144},{24,152},{32,160},{40,168},{48,176},{56,1... | collective-permute-start | bytes 12296 | tf_op jit(solution)/shard_map/ppermute | solution.py:28
  64.0 8.2 %collective-permute-start.19 = (f32[8,128]{1,0:T(8,128)S(1)}, f32[8,128]{1,0:T(8,128)S(1)}, u32[]{:S(2)}, u32[]{:S(2)}) collective-permute-start(f32[8,128]{1,0:T(8,128)S(1)} %shard_map.115.refs_17_), channel_id=1, source_target_pairs={{0,64},{8,72},{16,80},{24,88},{32,96},{40,104},{48,112},{56,120},{... | collective-permute-start | bytes 12296 | tf_op jit(solution)/shard_map/ppermute | solution.py:28
  68.0 11.6 %collective-permute-start.24 = (bf16[48,3072]{1,0:T(8,128)(2,1)S(1)}, bf16[48,3072]{1,0:T(8,128)(2,1)S(1)}, u32[]{:S(2)}, u32[]{:S(2)}) collective-permute-start(bf16[48,3072]{1,0:T(8,128)(2,1)S(1)} %get-tuple-element.57), channel_id=1, source_target_pairs={{0,32},{8,40},{16,48},{24,56},{32,0},{40,8},{48,16},{56,24},{64,96... | collective-permute-start | bytes 884744 | tf_op jit(solution)/shard_map/ppermute | solution.py:28
  71.1 13.4 %collective-permute-start.25 = (bf16[48,3072]{1,0:T(8,128)(2,1)S(1)}, bf16[48,3072]{1,0:T(8,128)(2,1)S(1)}, u32[]{:S(2)}, u32[]{:S(2)}) collective-permute-start(bf16[48,3072]{1,0:T(8,128)(2,1)S(1)} %get-tuple-element.58), channel_id=1, source_target_pairs={{0,48},{8,56},{16,32},{24,40},{32,16},{40,24},{48,0},{56,8},{64,11... | collective-permute-start | bytes 884744 | tf_op jit(solution)/shard_map/ppermute | solution.py:28
  72.2 12.7 %collective-permute-start.23 = (bf16[48,3072]{1,0:T(8,128)(2,1)S(1)}, bf16[48,3072]{1,0:T(8,128)(2,1)S(1)}, u32[]{:S(2)}, u32[]{:S(2)}) collective-permute-start(bf16[48,3072]{1,0:T(8,128)(2,1)S(1)} %get-tuple-element.49), channel_id=1, source_target_pairs={{0,16},{8,24},{16,0},{24,8},{32,48},{40,56},{48,32},{56,40},{64,80... | collective-permute-start | bytes 884744 | tf_op jit(solution)/shard_map/ppermute | solution.py:28
  79.1 5.9 %collective-permute-start.26 = (bf16[1024,384]{1,0:T(8,128)(2,1)S(1)}, bf16[1024,384]{1,0:T(8,128)(2,1)S(1)}, u32[]{:S(2)}, u32[]{:S(2)}) collective-permute-start(bf16[1024,384]{1,0:T(8,128)(2,1)S(1)} %get-tuple-element.51), channel_id=1, source_target_pairs={{0,8},{8,0},{16,24},{24,16},{32,40},{40,32},{48,56},{56,48},{64,72... | collective-permute-start | bytes 2359304 | tf_op jit(solution)/shard_map/ppermute | solution.py:28
  85.3 8.5 %collective-permute-start.27 = (bf16[256,384]{1,0:T(8,128)(2,1)S(1)}, bf16[256,384]{1,0:T(8,128)(2,1)S(1)}, u32[]{:S(2)}, u32[]{:S(2)}) collective-permute-start(bf16[256,384]{1,0:T(8,128)(2,1)S(1)} %get-tuple-element.76), channel_id=1, source_target_pairs={{0,32},{8,40},{16,48},{24,56},{32,0},{40,8},{48,16},{56,24},{64,96... | collective-permute-start | bytes 589832 | tf_op jit(solution)/shard_map/ppermute | solution.py:28
  87.4 13.1 %collective-permute-start.32 = (bf16[24,3072]{1,0:T(8,128)(2,1)S(1)}, bf16[24,3072]{1,0:T(8,128)(2,1)S(1)}, u32[]{:S(2)}, u32[]{:S(2)}) collective-permute-start(bf16[24,3072]{1,0:T(8,128)(2,1)S(1)} %slice.127), channel_id=1, source_target_pairs={{0,128},{8,136},{16,144},{24,152},{32,160},{40,168},{48,176},{56,1... | collective-permute-start | bytes 442376 | tf_op jit(solution)/shard_map/ppermute | solution.py:28
  87.8 18.9 %collective-permute-start.28 = (bf16[256,384]{1,0:T(8,128)(2,1)S(1)}, bf16[256,384]{1,0:T(8,128)(2,1)S(1)}, u32[]{:S(2)}, u32[]{:S(2)}) collective-permute-start(bf16[256,384]{1,0:T(8,128)(2,1)S(1)} %slice.126), channel_id=1, source_target_pairs={{0,1},{1,0},{2,3},{3,2},{4,5},{5,4},{6,7},{7,6},{8,9},{9,8},{10,11... | collective-permute-start | bytes 589832 | tf_op jit(solution)/shard_map/ppermute | solution.py:28
  89.6 14.8 %collective-permute-start.30 = (bf16[768,128]{1,0:T(8,128)(2,1)S(1)}, bf16[768,128]{1,0:T(8,128)(2,1)S(1)}, u32[]{:S(2)}, u32[]{:S(2)}) collective-permute-start(bf16[768,128]{1,0:T(8,128)(2,1)S(1)} %get-tuple-element.64), channel_id=1, source_target_pairs={{0,128},{8,136},{16,144},{24,152},{32,160},{40,168},{48,176},{56,1... | collective-permute-start | bytes 589832 | tf_op jit(solution)/shard_map/ppermute | solution.py:28
  92.3 20.0 %collective-permute-start.33 = (bf16[256,384]{1,0:T(8,128)(2,1)S(1)}, bf16[256,384]{1,0:T(8,128)(2,1)S(1)}, u32[]{:S(2)}, u32[]{:S(2)}) collective-permute-start(bf16[256,384]{1,0:T(8,128)(2,1)S(1)} %get-tuple-element.74), channel_id=1, source_target_pairs={{0,16},{8,24},{16,0},{24,8},{32,48},{40,56},{48,32},{56,40},{64,80... | collective-permute-start | bytes 589832 | tf_op jit(solution)/shard_map/ppermute | solution.py:28
  93.8 18.6 %collective-permute-start.34 = (bf16[256,384]{1,0:T(8,128)(2,1)S(1)}, bf16[256,384]{1,0:T(8,128)(2,1)S(1)}, u32[]{:S(2)}, u32[]{:S(2)}) collective-permute-start(bf16[256,384]{1,0:T(8,128)(2,1)S(1)} %get-tuple-element.75), channel_id=1, source_target_pairs={{0,48},{8,56},{16,32},{24,40},{32,16},{40,24},{48,0},{56,8},{64,11... | collective-permute-start | bytes 589832 | tf_op jit(solution)/shard_map/ppermute | solution.py:28
  104.5 8.6 %collective-permute-start.35 = (bf16[12,3072]{1,0:T(8,128)(2,1)S(1)}, bf16[12,3072]{1,0:T(8,128)(2,1)S(1)}, u32[]{:S(2)}, u32[]{:S(2)}) collective-permute-start(bf16[12,3072]{1,0:T(8,128)(2,1)S(1)} %slice.128), channel_id=1, source_target_pairs={{0,64},{8,72},{16,80},{24,88},{32,96},{40,104},{48,112},{56,120},{... | collective-permute-start | bytes 221192 | tf_op jit(solution)/shard_map/ppermute | solution.py:28
  104.6 9.2 %collective-permute-start.31 = (bf16[384,128]{1,0:T(8,128)(2,1)S(1)}, bf16[384,128]{1,0:T(8,128)(2,1)S(1)}, u32[]{:S(2)}, u32[]{:S(2)}) collective-permute-start(bf16[384,128]{1,0:T(8,128)(2,1)S(1)} %slice.129), channel_id=1, source_target_pairs={{0,64},{8,72},{16,80},{24,88},{32,96},{40,104},{48,112},{56,120},{... | collective-permute-start | bytes 294920 | tf_op jit(solution)/shard_map/ppermute | solution.py:28
  106.7 12.7 %collective-permute-start.29 = (bf16[128,384]{1,0:T(8,128)(2,1)S(1)}, bf16[128,384]{1,0:T(8,128)(2,1)S(1)}, u32[]{:S(2)}, u32[]{:S(2)}) collective-permute-start(bf16[128,384]{1,0:T(8,128)(2,1)S(1)} %slice.130), channel_id=1, source_target_pairs={{0,4},{1,5},{2,6},{3,7},{4,0},{5,1},{6,2},{7,3},{8,12},{9,13},{10,... | collective-permute-start | bytes 294920 | tf_op jit(solution)/shard_map/ppermute | solution.py:28
  (10 other events, 127.5 us)

commit v3 on v2

--- a/solution.py
+++ b/solution.py
@@ -26,13 +26,6 @@
 def swap(block, axis, distance):
     devices = range(lax.axis_size(axis))
     return lax.ppermute(block, axis, [(i, i ^ distance) for i in devices])
-
-
-def gathered(block, axis, unit):
-    near = swap(block, axis, unit)
-    rows = block.shape[0]
-    far = swap(jnp.concatenate([block, near], axis=0), axis, 2 * unit)
-    return [block, near, far[:rows], far[rows:]]
 
 
 def dot(lhs, rhs, left, right):
@@ -261,13 +254,12 @@
         limit=58,
     )
     kv_near = [kv] + [swap(kv, "slab", 2 * e) for e in (1, 2, 3)]
-    q_all = gathered(q_ext, "slab", 8)
+    q_all = [q_ext] + [swap(q_ext, "slab", 8 * j) for j in (1, 2, 3)]
     kv_all = kv_near + [swap(block, "slab", 1) for block in kv_near]
 
-    d_across = after(swap(after(d_out, q_all[1]), "head", 4), *kv_near)
+    d_across = after(swap(after(d_out, q_all[1]), "head", 4), *kv_near, *q_all)
     d_full = jnp.concatenate([d_out, d_across], axis=0)
-    d_full = jnp.concatenate([d_full, swap(d_full, "head", 1)], axis=0)
-    d_full = jnp.concatenate([d_full, swap(d_full, "head", 2)], axis=0)
+    d_near = swap(d_full, "head", 1)
 
     bias_scratch = pltpu.VMEM((16, 4 * ROWS), F32)
     parts = call(
@@ -280,12 +272,13 @@
         moved=3 * 10**6,
         scratch=[pltpu.VMEM((8 * ROWS, 4 * ROWS), F32), bias_scratch],
     )
+    d_full = jnp.concatenate([d_full, after(d_near, parts[0])], axis=0)
+    d_full = jnp.concatenate([d_full, swap(d_full, "head", 2)], axis=0)
     parts = [parts[0]] + [swap(parts[j], "slab", 8 * j) for j in (1, 2, 3)]
     d_full = after(d_full, *parts[1:])
     d_other = swap(d_full, "slab", 1)
     grad = call(grad_kernel, [((COLS, ROWS), BF)], ranks, w_out, d_full, flops=3 * 10**8, moved=3 * 10**6)[0]
-    g_all = gathered(grad, "slab", 8)
-    parts[0] = after(parts[0], g_all[1])
+    g_near = swap(grad, "slab", 8)
     att, logs = call(merge_kernel, [((COLS, ROWS), BF), ((8, ROWS), F32)], *parts, flops=10**8, moved=10**6)
     stats = call(delta_kernel, [((8, ROWS), F32)], logs, att, grad, flops=10**6, moved=10**6)[0]
     stat_all = [stats] + [swap(stats, "slab", 8 * j) for j in (1, 2, 3)]
@@ -295,12 +288,14 @@
         mix_kernel,
         [((4 * ROWS, COLS), F32), ((4 * ROWS, COLS), BF)],
         ranks,
-        att,
+        after(att, grad),
         w_out,
         flops=3 * 10**8,
         moved=4 * 10**6,
     )
     mix_in = swap(mix[1], "head", 2)
+    g_far = swap(jnp.concatenate([grad, after(g_near, mix[1])], axis=0), "slab", 16)
+    g_all = [grad, g_near, g_far[:COLS], g_far[COLS:]]
     weight = call(
         weight_kernel,
         [((48, WIDE), F32)] + [((48, WIDE), BF)] * 3,
@@ -313,7 +308,9 @@
         moved=4 * 10**6,
     )
     weight_in = [swap(weight[j], "slab", 2 * j) for j in (1, 2, 3)]
-    stat_all[0] = after(stat_all[0], weight[1])
+    mixed = mix[0] + mix_in.astype(F32)
+    mixed_away = mixed[2 * ROWS :].astype(BF)
+    stat_all[0] = after(stat_all[0], weight[1], mixed_away)
 
     dq_own, dq_other, own, other = call(
         backward_kernel,
@@ -329,20 +326,18 @@
     )
     weight = after(weight[0], other) + sum((w.astype(F32) for w in weight_in), 0.0)
     weight_away = weight[24:].astype(BF)
-    mixed = after(mix[0], other) + mix_in.astype(F32)
-    mixed_away = mixed[2 * ROWS :].astype(BF)
 
     other = swap(other, "slab", 1)
-    pair = (after(own, weight_away, mixed_away) + other.astype(F32)).reshape(4, 2 * ROWS, COLS)
+    pair = (after(own, weight_away) + other.astype(F32)).reshape(4, 2 * ROWS, COLS)
     away = [pair[e].astype(BF) for e in (1, 2, 3)]
     arrived = [swap(away[e - 1], "slab", 2 * e) for e in (1, 2, 3)]
     dq_in = swap(after(dq_other, other), "slab", 16)
 
-    weight = after(weight[:24], arrived[1]) + swap(weight_away, "slab", 16).astype(F32)
-    weight_away = weight[12:].astype(BF)
     mixed = after(mixed[: 2 * ROWS], arrived[1]) + swap(mixed_away, "head", 1).astype(F32)
     mixed_away = mixed[ROWS:].astype(BF)
-    dq = after(dq_own, arrived[1]) + dq_in.astype(F32)
+    weight = after(weight[:24], mixed_away) + swap(weight_away, "slab", 16).astype(F32)
+    weight_away = weight[12:].astype(BF)
+    dq = after(dq_own, mixed_away) + dq_in.astype(F32)
     dq_away = dq[COLS:].astype(BF)
 
     total = after(pair[0], weight_away, mixed_away, dq_away) + sum((a.astype(F32) for a in arrived), 0.0)

time: 122 us -> 115 us (0.943); the launches traced: 120 us -> 114 us
  waiting for transfers between devices: 37.7 us -> 32.6 us
  local copies, waits for them, and re-layouts: 1.71 us -> 3.49 us
  other arithmetic: 4.93 us -> 3.16 us
    ppermute x36 -> x37, waiting for transfers between devices: 37.7 us -> 32.6 us  [swap(): return lax.ppermute(block, axis, [(i, i ^ distance) for i in devices])]
    unnamed x11 -> x17, local copies, waits for them, and re-layouts: 0.78 us -> 2.6 us
    concatenate x3 -> x2, other arithmetic: 1.87 us -> 0.06 us  [the longest x1 0.04 us: on_device(): d_full = jnp.concatenate([d_full, after(d_near, parts[0])], axis=0)]
    ppermute x36 -> x37, starting transfers between devices: 58.2 us -> 57.6 us  [swap(): return lax.ppermute(block, axis, [(i, i ^ distance) for i in devices])]
  transfers between devices with their start and end apart: 36 -> 37, of which waited for: 16 -> 13; matrix products, arithmetic and copies ran while one was open for 4% -> 3% of each run, Pallas kernels for 12% -> 13%
where the time goes in v3:
time: 115 us; the launch traced here: 114 us
  starting transfers between devices  57.6 us (50%)
  waiting for transfers between devices  32.6 us (28%)
  Pallas kernels  16.5 us (14%)
  local copies, waits for them, and re-layouts  3.49 us (3%)
  other arithmetic  3.16 us (3%)
    ppermute x37, starting transfers between devices, swap(): return lax.ppermute(block, axis, [(i, i ^ distance) for i in devices])  57.6 us
    ppermute x37, waiting for transfers between devices, swap(): return lax.ppermute(block, axis, [(i, i ^ distance) for i in devices])  32.6 us
    pallas_call x8, Pallas kernels, call(): pl.pallas_call(kernel, out_shape=[jax.ShapeDtypeStruct(shape, dtype) for...  16.5 us
    unnamed x17, local copies, waits for them, and re-layouts  2.6 us
  transfers between devices with their start and end apart: 37, of which 13 were waited for; matrix products, arithmetic and copies ran while one was open for 3% of the time, Pallas kernels for 13%

profile of v3, /device:TPU:2, one launch (start us, length us, event | category | flops | bytes accessed | tf_op | source)
XLA Modules:
  0.0 114.4 jit_solution(3207556226195938889)
XLA Ops:
  0.6 1.8 %shard_map.110 = (bf16[144,384]{1,0:T(8,128)(2,1)}, bf16[256,384]{1,0:T(8,128)(2,1)}) custom-call(s32[2,4]{1,0:T(2,128)} %ids_hbm.1, s32[2]{0:T(128)} %counts_hbm.1, bf16[128,384]{1,0:T(8,128)(2,1)} %q_hbm.1, bf16[128,384]{1,0:T(8,128)(2,1)} %k_hbm.1, bf16[128,384]{1,0:T(8,128)(2,1)} %v_hbm.1), custom_call_target="tpu_custom_call" | custom-call | flops 1000 | bytes 1000 | tf_op jit(solution)/shard_map/pallas_call | solution.py:39
  2.4 2.0 %collective-permute-start = (bf16[144,384]{1,0:T(8,128)(2,1)}, bf16[144,384]{1,0:T(8,128)(2,1)S(1)}, u32[]{:S(2)}, u32[]{:S(2)}) collective-permute-start(bf16[144,384]{1,0:T(8,128)(2,1)} %get-tuple-element.37.refs_1_), channel_id=1, source_target_pairs={{0,64},{8,72},{16,80},{24,88},{32,96},{40,104},{48,112},{56,120},{... | collective-permute-start | bytes 331784 | tf_op jit(solution)/shard_map/ppermute | solution.py:28
  4.4 2.8 %collective-permute-start.2 = (bf16[144,384]{1,0:T(8,128)(2,1)}, bf16[144,384]{1,0:T(8,128)(2,1)S(1)}, u32[]{:S(2)}, u32[]{:S(2)}) collective-permute-start(bf16[144,384]{1,0:T(8,128)(2,1)} %get-tuple-element.37.refs_1_), channel_id=1, source_target_pairs={{0,192},{8,200},{16,208},{24,216},{32,224},{40,232},{48,240},{56,2... | collective-permute-start | bytes 331784 | tf_op jit(solution)/shard_map/ppermute | solution.py:28
  7.3 3.0 %collective-permute-start.5 = (bf16[256,384]{1,0:T(8,128)(2,1)}, bf16[256,384]{1,0:T(8,128)(2,1)S(1)}, u32[]{:S(2)}, u32[]{:S(2)}) collective-permute-start(bf16[256,384]{1,0:T(8,128)(2,1)} %get-tuple-element.38.refs_5_), channel_id=1, source_target_pairs={{0,48},{8,56},{16,32},{24,40},{32,16},{40,24},{48,0},{56,8},{64,11... | collective-permute-start | bytes 589832 | tf_op jit(solution)/shard_map/ppermute | solution.py:28
  12.9 5.2 %collective-permute-start.13 = (bf16[128,384]{1,0:T(8,128)(2,1)}, bf16[128,384]{1,0:T(8,128)(2,1)S(1)}, u32[]{:S(2)}, u32[]{:S(2)}) collective-permute-start(bf16[128,384]{1,0:T(8,128)(2,1)} %param.11), channel_id=1, source_target_pairs={{0,4},{1,5},{2,6},{3,7},{4,0},{5,1},{6,2},{7,3},{8,12},{9,13},{10,... | collective-permute-start | bytes 294920 | tf_op jit(solution)/shard_map/ppermute | solution.py:28
  18.1 1.6 %collective-permute-done.1.refs_3_ = bf16[144,384]{1,0:T(8,128)(2,1)S(1)} collective-permute-done((bf16[144,384]{1,0:T(8,128)(2,1)}, bf16[144,384]{1,0:T(8,128)(2,1)S(1)}, u32[]{:S(2)}, u32[]{:S(2)}) %collective-permute-start.1) | collective-permute-done | bytes 110624 | tf_op jit(solution)/shard_map/ppermute | solution.py:28
  20.6 1.4 %collective-permute-done.13 = bf16[128,384]{1,0:T(8,128)(2,1)S(1)} collective-permute-done((bf16[128,384]{1,0:T(8,128)(2,1)}, bf16[128,384]{1,0:T(8,128)(2,1)S(1)}, u32[]{:S(2)}, u32[]{:S(2)}) %collective-permute-start.13) | collective-permute-done | bytes 98336 | tf_op jit(solution)/shard_map/ppermute | solution.py:28
  25.5 3.9 %shard_map.111 = (bf16[400,128]{1,0:T(8,128)(2,1)S(1)}, bf16[400,128]{1,0:T(8,128)(2,1)S(1)}, bf16[400,128]{1,0:T(8,128)(2,1)S(1)}, bf16[400,128]{1,0:T(8,128)(2,1)S(1)}) custom-call(s32[4]{0:T(128)S(1)} %pad_add_fusion.refs_0_.rank_ref, bf16[144,384]{1,0:T(8,128)(2,1)S(1)} %copy-done.3, bf16[144,384]{1,0:T(8,128)(2,1)S(1)} %collective-permute-done.refs_2_, ...), custom_call_target="tpu_custom_call" | custom-call | flops 1000 | bytes 1000 | tf_op jit(solution)/shard_map/pallas_call | solution.py:39
  29.5 2.5 %collective-permute-start.15 = (bf16[512,384]{1,0:T(8,128)(2,1)S(1)}, bf16[512,384]{1,0:T(8,128)(2,1)S(1)}, u32[]{:S(2)}, u32[]{:S(2)}) collective-permute-start(bf16[512,384]{1,0:T(8,128)(2,1)S(1)} %pad_maximum_fusion.1), channel_id=1, source_target_pairs={{0,2},{1,3},{2,0},{3,1},{4,6},{5,7},{6,4},{7,5},{8,10},{9,11},{10,... | collective-permute-start | bytes 1179656 | tf_op jit(solution)/shard_map/ppermute | solution.py:28
  32.0 2.7 %collective-permute-start.10 = (bf16[400,128]{1,0:T(8,128)(2,1)S(1)}, bf16[400,128]{1,0:T(8,128)(2,1)S(1)}, u32[]{:S(2)}, u32[]{:S(2)}) collective-permute-start(bf16[400,128]{1,0:T(8,128)(2,1)S(1)} %get-tuple-element.40), channel_id=1, source_target_pairs={{0,64},{8,72},{16,80},{24,88},{32,96},{40,104},{48,112},{56,120},{... | collective-permute-start | bytes 307208 | tf_op jit(solution)/shard_map/ppermute | solution.py:28
  35.6 1.5 %collective-permute-start.12 = (bf16[400,128]{1,0:T(8,128)(2,1)S(1)}, bf16[400,128]{1,0:T(8,128)(2,1)S(1)}, u32[]{:S(2)}, u32[]{:S(2)}) collective-permute-start(bf16[400,128]{1,0:T(8,128)(2,1)S(1)} %get-tuple-element.42), channel_id=1, source_target_pairs={{0,192},{8,200},{16,208},{24,216},{32,224},{40,232},{48,240},{56,2... | collective-permute-start | bytes 307208 | tf_op jit(solution)/shard_map/ppermute | solution.py:28
  37.1 3.4 %collective-permute-done.15 = bf16[512,384]{1,0:T(8,128)(2,1)S(1)} collective-permute-done((bf16[512,384]{1,0:T(8,128)(2,1)S(1)}, bf16[512,384]{1,0:T(8,128)(2,1)S(1)}, u32[]{:S(2)}, u32[]{:S(2)}) %collective-permute-start.15) | collective-permute-done | bytes 393248 | tf_op jit(solution)/shard_map/ppermute | solution.py:28
  40.6 1.8 %collective-permute-done.11.refs_2_ = bf16[400,128]{1,0:T(8,128)(2,1)S(1)} collective-permute-done((bf16[400,128]{1,0:T(8,128)(2,1)S(1)}, bf16[400,128]{1,0:T(8,128)(2,1)S(1)}, u32[]{:S(2)}, u32[]{:S(2)}) %collective-permute-start.11) | collective-permute-done | bytes 102432 | tf_op jit(solution)/shard_map/ppermute | solution.py:28
  43.8 1.7 %collective-permute-start.17 = (bf16[384,128]{1,0:T(8,128)(2,1)S(1)}, bf16[384,128]{1,0:T(8,128)(2,1)S(1)}, u32[]{:S(2)}, u32[]{:S(2)}) collective-permute-start(bf16[384,128]{1,0:T(8,128)(2,1)S(1)} %shard_map.113.grad_ref.refs_13_), channel_id=1, source_target_pairs={{0,64},{8,72},{16,80},{24,88},{32,96},{40,104},{48,112},{56,120},{... | collective-permute-start | bytes 294920 | tf_op jit(solution)/shard_map/ppermute | solution.py:28
  46.9 2.2 %collective-permute-done.17.refs_14_ = bf16[384,128]{1,0:T(8,128)(2,1)S(1)} collective-permute-done((bf16[384,128]{1,0:T(8,128)(2,1)S(1)}, bf16[384,128]{1,0:T(8,128)(2,1)S(1)}, u32[]{:S(2)}, u32[]{:S(2)}) %collective-permute-start.17) | collective-permute-done | bytes 98336 | tf_op jit(solution)/shard_map/ppermute | solution.py:28
  49.1 2.3 %collective-permute-start.18 = (bf16[768,128]{1,0:T(8,128)(2,1)S(1)}, bf16[768,128]{1,0:T(8,128)(2,1)S(1)}, u32[]{:S(2)}, u32[]{:S(2)}) collective-permute-start(bf16[768,128]{1,0:T(8,128)(2,1)S(1)} %pad_maximum_fusion.3), channel_id=1, source_target_pairs={{0,128},{8,136},{16,144},{24,152},{32,160},{40,168},{48,176},{56,1... | collective-permute-start | bytes 589832 | tf_op jit(solution)/shard_map/ppermute | solution.py:28
  52.6 1.9 %collective-permute-start.23 = (f32[8,128]{1,0:T(8,128)S(1)}, f32[8,128]{1,0:T(8,128)S(1)}, u32[]{:S(2)}, u32[]{:S(2)}) collective-permute-start(f32[8,128]{1,0:T(8,128)S(1)} %shard_map.115.refs_17_), channel_id=1, source_target_pairs={{0,192},{8,200},{16,208},{24,216},{32,224},{40,232},{48,240},{56,2... | collective-permute-start | bytes 12296 | tf_op jit(solution)/shard_map/ppermute | solution.py:28
  54.5 6.5 %collective-permute-done.18 = bf16[768,128]{1,0:T(8,128)(2,1)S(1)} collective-permute-done((bf16[768,128]{1,0:T(8,128)(2,1)S(1)}, bf16[768,128]{1,0:T(8,128)(2,1)S(1)}, u32[]{:S(2)}, u32[]{:S(2)}) %collective-permute-start.18) | collective-permute-done | bytes 196640 | tf_op jit(solution)/shard_map/ppermute | solution.py:28
  61.0 2.7 %collective-permute-start.21 = (f32[8,128]{1,0:T(8,128)S(1)}, f32[8,128]{1,0:T(8,128)S(1)}, u32[]{:S(2)}, u32[]{:S(2)}) collective-permute-start(f32[8,128]{1,0:T(8,128)S(1)} %shard_map.115.refs_17_), channel_id=1, source_target_pairs={{0,64},{8,72},{16,80},{24,88},{32,96},{40,104},{48,112},{56,120},{... | collective-permute-start | bytes 12296 | tf_op jit(solution)/shard_map/ppermute | solution.py:28
  65.0 3.4 %collective-permute-start.25 = (bf16[48,3072]{1,0:T(8,128)(2,1)S(1)}, bf16[48,3072]{1,0:T(8,128)(2,1)S(1)}, u32[]{:S(2)}, u32[]{:S(2)}) collective-permute-start(bf16[48,3072]{1,0:T(8,128)(2,1)S(1)} %get-tuple-element.59), channel_id=1, source_target_pairs={{0,32},{8,40},{16,48},{24,56},{32,0},{40,8},{48,16},{56,24},{64,96... | collective-permute-start | bytes 884744 | tf_op jit(solution)/shard_map/ppermute | solution.py:28
  69.7 6.8 %shard_map.117 = (f32[768,128]{1,0:T(8,128)S(1)}, bf16[768,128]{1,0:T(8,128)(2,1)S(1)}, f32[1024,384]{1,0:T(8,128)S(1)}, bf16[1024,384]{1,0:T(8,128)(2,1)S(1)}) custom-call(s32[4]{0:T(128)S(1)} %pad_add_fusion.refs_0_.rank_ref, bf16[144,384]{1,0:T(8,128)(2,1)S(1)} %copy-done.4, bf16[144,384]{1,0:T(8,128)(2,1)S(1)} %collective-permute-done.refs_2_, ...), custom_call_target="tpu_custom_call" | custom-call | flops 1000 | bytes 1000 | tf_op jit(solution)/shard_map/pallas_call | solution.py:39
  76.6 3.6 %collective-permute-done.26 = bf16[48,3072]{1,0:T(8,128)(2,1)S(1)} collective-permute-done((bf16[48,3072]{1,0:T(8,128)(2,1)S(1)}, bf16[48,3072]{1,0:T(8,128)(2,1)S(1)}, u32[]{:S(2)}, u32[]{:S(2)}) %collective-permute-start.26) | collective-permute-done | bytes 294944 | tf_op jit(solution)/shard_map/ppermute | solution.py:28
  81.1 2.1 %collective-permute-start.28 = (bf16[256,384]{1,0:T(8,128)(2,1)S(1)}, bf16[256,384]{1,0:T(8,128)(2,1)S(1)}, u32[]{:S(2)}, u32[]{:S(2)}) collective-permute-start(bf16[256,384]{1,0:T(8,128)(2,1)S(1)} %get-tuple-element.78), channel_id=1, source_target_pairs={{0,32},{8,40},{16,48},{24,56},{32,0},{40,8},{48,16},{56,24},{64,96... | collective-permute-start | bytes 589832 | tf_op jit(solution)/shard_map/ppermute | solution.py:28
  83.2 1.8 %collective-permute-start.29 = (bf16[256,384]{1,0:T(8,128)(2,1)S(1)}, bf16[256,384]{1,0:T(8,128)(2,1)S(1)}, u32[]{:S(2)}, u32[]{:S(2)}) collective-permute-start(bf16[256,384]{1,0:T(8,128)(2,1)S(1)} %slice.116), channel_id=1, source_target_pairs={{0,1},{1,0},{2,3},{3,2},{4,5},{5,4},{6,7},{7,6},{8,9},{9,8},{10,11... | collective-permute-start | bytes 589832 | tf_op jit(solution)/shard_map/ppermute | solution.py:28
  85.8 2.2 %collective-permute-start.31 = (bf16[768,128]{1,0:T(8,128)(2,1)S(1)}, bf16[768,128]{1,0:T(8,128)(2,1)S(1)}, u32[]{:S(2)}, u32[]{:S(2)}) collective-permute-start(bf16[768,128]{1,0:T(8,128)(2,1)S(1)} %get-tuple-element.66), channel_id=1, source_target_pairs={{0,128},{8,136},{16,144},{24,152},{32,160},{40,168},{48,176},{56,1... | collective-permute-start | bytes 589832 | tf_op jit(solution)/shard_map/ppermute | solution.py:28
  88.0 1.5 %collective-permute-start.34 = (bf16[256,384]{1,0:T(8,128)(2,1)S(1)}, bf16[256,384]{1,0:T(8,128)(2,1)S(1)}, u32[]{:S(2)}, u32[]{:S(2)}) collective-permute-start(bf16[256,384]{1,0:T(8,128)(2,1)S(1)} %get-tuple-element.76), channel_id=1, source_target_pairs={{0,16},{8,24},{16,0},{24,8},{32,48},{40,56},{48,32},{56,40},{64,80... | collective-permute-start | bytes 589832 | tf_op jit(solution)/shard_map/ppermute | solution.py:28
  89.5 2.7 %collective-permute-start.35 = (bf16[256,384]{1,0:T(8,128)(2,1)S(1)}, bf16[256,384]{1,0:T(8,128)(2,1)S(1)}, u32[]{:S(2)}, u32[]{:S(2)}) collective-permute-start(bf16[256,384]{1,0:T(8,128)(2,1)S(1)} %get-tuple-element.77), channel_id=1, source_target_pairs={{0,48},{8,56},{16,32},{24,40},{32,16},{40,24},{48,0},{56,8},{64,11... | collective-permute-start | bytes 589832 | tf_op jit(solution)/shard_map/ppermute | solution.py:28
  92.3 5.5 %collective-permute-start.30 = (bf16[128,384]{1,0:T(8,128)(2,1)S(1)}, bf16[128,384]{1,0:T(8,128)(2,1)S(1)}, u32[]{:S(2)}, u32[]{:S(2)}) collective-permute-start(bf16[128,384]{1,0:T(8,128)(2,1)S(1)} %slice.120), channel_id=1, source_target_pairs={{0,4},{1,5},{2,6},{3,7},{4,0},{5,1},{6,2},{7,3},{8,12},{9,13},{10,... | collective-permute-start | bytes 294920 | tf_op jit(solution)/shard_map/ppermute | solution.py:28
  97.8 3.5 %collective-permute-done.33 = bf16[24,3072]{1,0:T(8,128)(2,1)S(1)} collective-permute-done((bf16[24,3072]{1,0:T(8,128)(2,1)S(1)}, bf16[24,3072]{1,0:T(8,128)(2,1)S(1)}, u32[]{:S(2)}, u32[]{:S(2)}) %collective-permute-start.33) | collective-permute-done | bytes 147488 | tf_op jit(solution)/shard_map/ppermute | solution.py:28
  101.3 5.1 %collective-permute-done.31 = bf16[768,128]{1,0:T(8,128)(2,1)S(1)} collective-permute-done((bf16[768,128]{1,0:T(8,128)(2,1)S(1)}, bf16[768,128]{1,0:T(8,128)(2,1)S(1)}, u32[]{:S(2)}, u32[]{:S(2)}) %collective-permute-start.31) | collective-permute-done | bytes 196640 | tf_op jit(solution)/shard_map/ppermute | solution.py:28
  106.5 2.0 %collective-permute-start.32 = (bf16[384,128]{1,0:T(8,128)(2,1)S(1)}, bf16[384,128]{1,0:T(8,128)(2,1)S(1)}, u32[]{:S(2)}, u32[]{:S(2)}) collective-permute-start(bf16[384,128]{1,0:T(8,128)(2,1)S(1)} %slice.119), channel_id=1, source_target_pairs={{0,64},{8,72},{16,80},{24,88},{32,96},{40,104},{48,112},{56,120},{... | collective-permute-start | bytes 294920 | tf_op jit(solution)/shard_map/ppermute | solution.py:28
  109.3 2.6 %collective-permute-done.36 = bf16[12,3072]{1,0:T(8,128)(2,1)S(1)} collective-permute-done((bf16[12,3072]{1,0:T(8,128)(2,1)S(1)}, bf16[12,3072]{1,0:T(8,128)(2,1)S(1)}, u32[]{:S(2)}, u32[]{:S(2)}) %collective-permute-start.36) | collective-permute-done | bytes 73760 | tf_op jit(solution)/shard_map/ppermute | solution.py:28
  (95 shorter events, 19.9 us)
Async XLA Ops:
  2.4 8.9 %collective-permute-start = (bf16[144,384]{1,0:T(8,128)(2,1)}, bf16[144,384]{1,0:T(8,128)(2,1)S(1)}, u32[]{:S(2)}, u32[]{:S(2)}) collective-permute-start(bf16[144,384]{1,0:T(8,128)(2,1)} %get-tuple-element.37.refs_1_), channel_id=1, source_target_pairs={{0,64},{8,72},{16,80},{24,88},{32,96},{40,104},{48,112},{56,120},{... | collective-permute-start | bytes 331784 | tf_op jit(solution)/shard_map/ppermute | solution.py:28
  4.4 8.4 %collective-permute-start.2 = (bf16[144,384]{1,0:T(8,128)(2,1)}, bf16[144,384]{1,0:T(8,128)(2,1)S(1)}, u32[]{:S(2)}, u32[]{:S(2)}) collective-permute-start(bf16[144,384]{1,0:T(8,128)(2,1)} %get-tuple-element.37.refs_1_), channel_id=1, source_target_pairs={{0,192},{8,200},{16,208},{24,216},{32,224},{40,232},{48,240},{56,2... | collective-permute-start | bytes 331784 | tf_op jit(solution)/shard_map/ppermute | solution.py:28
  7.3 12.4 %collective-permute-start.5 = (bf16[256,384]{1,0:T(8,128)(2,1)}, bf16[256,384]{1,0:T(8,128)(2,1)S(1)}, u32[]{:S(2)}, u32[]{:S(2)}) collective-permute-start(bf16[256,384]{1,0:T(8,128)(2,1)} %get-tuple-element.38.refs_5_), channel_id=1, source_target_pairs={{0,48},{8,56},{16,32},{24,40},{32,16},{40,24},{48,0},{56,8},{64,11... | collective-permute-start | bytes 589832 | tf_op jit(solution)/shard_map/ppermute | solution.py:28
  10.3 9.9 %collective-permute-start.4 = (bf16[256,384]{1,0:T(8,128)(2,1)}, bf16[256,384]{1,0:T(8,128)(2,1)S(1)}, u32[]{:S(2)}, u32[]{:S(2)}) collective-permute-start(bf16[256,384]{1,0:T(8,128)(2,1)} %get-tuple-element.38.refs_5_), channel_id=1, source_target_pairs={{0,32},{8,40},{16,48},{24,56},{32,0},{40,8},{48,16},{56,24},{64,96... | collective-permute-start | bytes 589832 | tf_op jit(solution)/shard_map/ppermute | solution.py:28
  10.9 9.3 %collective-permute-start.3 = (bf16[256,384]{1,0:T(8,128)(2,1)}, bf16[256,384]{1,0:T(8,128)(2,1)S(1)}, u32[]{:S(2)}, u32[]{:S(2)}) collective-permute-start(bf16[256,384]{1,0:T(8,128)(2,1)} %get-tuple-element.38.refs_5_), channel_id=1, source_target_pairs={{0,16},{8,24},{16,0},{24,8},{32,48},{40,56},{48,32},{56,40},{64,80... | collective-permute-start | bytes 589832 | tf_op jit(solution)/shard_map/ppermute | solution.py:28
  11.4 8.3 %collective-permute-start.1 = (bf16[144,384]{1,0:T(8,128)(2,1)}, bf16[144,384]{1,0:T(8,128)(2,1)S(1)}, u32[]{:S(2)}, u32[]{:S(2)}) collective-permute-start(bf16[144,384]{1,0:T(8,128)(2,1)} %get-tuple-element.37.refs_1_), channel_id=1, source_target_pairs={{0,128},{8,136},{16,144},{24,152},{32,160},{40,168},{48,176},{56,1... | collective-permute-start | bytes 331784 | tf_op jit(solution)/shard_map/ppermute | solution.py:28
  12.9 9.2 %collective-permute-start.13 = (bf16[128,384]{1,0:T(8,128)(2,1)}, bf16[128,384]{1,0:T(8,128)(2,1)S(1)}, u32[]{:S(2)}, u32[]{:S(2)}) collective-permute-start(bf16[128,384]{1,0:T(8,128)(2,1)} %param.11), channel_id=1, source_target_pairs={{0,4},{1,5},{2,6},{3,7},{4,0},{5,1},{6,2},{7,3},{8,12},{9,13},{10,... | collective-permute-start | bytes 294920 | tf_op jit(solution)/shard_map/ppermute | solution.py:28
  23.0 6.4 %collective-permute-start.14 = (bf16[256,384]{1,0:T(8,128)(2,1)S(1)}, bf16[256,384]{1,0:T(8,128)(2,1)S(1)}, u32[]{:S(2)}, u32[]{:S(2)}) collective-permute-start(bf16[256,384]{1,0:T(8,128)(2,1)S(1)} %pad_maximum_fusion.2), channel_id=1, source_target_pairs={{0,1},{1,0},{2,3},{3,2},{4,5},{5,4},{6,7},{7,6},{8,9},{9,8},{10,11... | collective-permute-start | bytes 589832 | tf_op jit(solution)/shard_map/ppermute | solution.py:28
  29.5 11.0 %collective-permute-start.15 = (bf16[512,384]{1,0:T(8,128)(2,1)S(1)}, bf16[512,384]{1,0:T(8,128)(2,1)S(1)}, u32[]{:S(2)}, u32[]{:S(2)}) collective-permute-start(bf16[512,384]{1,0:T(8,128)(2,1)S(1)} %pad_maximum_fusion.1), channel_id=1, source_target_pairs={{0,2},{1,3},{2,0},{3,1},{4,6},{5,7},{6,4},{7,5},{8,10},{9,11},{10,... | collective-permute-start | bytes 1179656 | tf_op jit(solution)/shard_map/ppermute | solution.py:28
  32.0 8.6 %collective-permute-start.10 = (bf16[400,128]{1,0:T(8,128)(2,1)S(1)}, bf16[400,128]{1,0:T(8,128)(2,1)S(1)}, u32[]{:S(2)}, u32[]{:S(2)}) collective-permute-start(bf16[400,128]{1,0:T(8,128)(2,1)S(1)} %get-tuple-element.40), channel_id=1, source_target_pairs={{0,64},{8,72},{16,80},{24,88},{32,96},{40,104},{48,112},{56,120},{... | collective-permute-start | bytes 307208 | tf_op jit(solution)/shard_map/ppermute | solution.py:28
  34.7 7.8 %collective-permute-start.11 = (bf16[400,128]{1,0:T(8,128)(2,1)S(1)}, bf16[400,128]{1,0:T(8,128)(2,1)S(1)}, u32[]{:S(2)}, u32[]{:S(2)}) collective-permute-start(bf16[400,128]{1,0:T(8,128)(2,1)S(1)} %get-tuple-element.41), channel_id=1, source_target_pairs={{0,128},{8,136},{16,144},{24,152},{32,160},{40,168},{48,176},{56,1... | collective-permute-start | bytes 307208 | tf_op jit(solution)/shard_map/ppermute | solution.py:28
  35.6 6.8 %collective-permute-start.12 = (bf16[400,128]{1,0:T(8,128)(2,1)S(1)}, bf16[400,128]{1,0:T(8,128)(2,1)S(1)}, u32[]{:S(2)}, u32[]{:S(2)}) collective-permute-start(bf16[400,128]{1,0:T(8,128)(2,1)S(1)} %get-tuple-element.42), channel_id=1, source_target_pairs={{0,192},{8,200},{16,208},{24,216},{32,224},{40,232},{48,240},{56,2... | collective-permute-start | bytes 307208 | tf_op jit(solution)/shard_map/ppermute | solution.py:28
  42.5 21.2 %collective-permute-start.20 = (bf16[1024,384]{1,0:T(8,128)(2,1)S(1)}, bf16[1024,384]{1,0:T(8,128)(2,1)S(1)}, u32[]{:S(2)}, u32[]{:S(2)}) collective-permute-start(bf16[1024,384]{1,0:T(8,128)(2,1)S(1)} %pad_maximum_fusion.d_ref), channel_id=1, source_target_pairs={{0,8},{8,0},{16,24},{24,16},{32,40},{40,32},{48,56},{56,48},{64,72... | collective-permute-start | bytes 2359304 | tf_op jit(solution)/shard_map/ppermute | solution.py:28
  43.8 5.3 %collective-permute-start.17 = (bf16[384,128]{1,0:T(8,128)(2,1)S(1)}, bf16[384,128]{1,0:T(8,128)(2,1)S(1)}, u32[]{:S(2)}, u32[]{:S(2)}) collective-permute-start(bf16[384,128]{1,0:T(8,128)(2,1)S(1)} %shard_map.113.grad_ref.refs_13_), channel_id=1, source_target_pairs={{0,64},{8,72},{16,80},{24,88},{32,96},{40,104},{48,112},{56,120},{... | collective-permute-start | bytes 294920 | tf_op jit(solution)/shard_map/ppermute | solution.py:28
  49.1 11.9 %collective-permute-start.18 = (bf16[768,128]{1,0:T(8,128)(2,1)S(1)}, bf16[768,128]{1,0:T(8,128)(2,1)S(1)}, u32[]{:S(2)}, u32[]{:S(2)}) collective-permute-start(bf16[768,128]{1,0:T(8,128)(2,1)S(1)} %pad_maximum_fusion.3), channel_id=1, source_target_pairs={{0,128},{8,136},{16,144},{24,152},{32,160},{40,168},{48,176},{56,1... | collective-permute-start | bytes 589832 | tf_op jit(solution)/shard_map/ppermute | solution.py:28
  51.4 18.0 %collective-permute-start.16 = (bf16[512,384]{1,0:T(8,128)(2,1)S(1)}, bf16[512,384]{1,0:T(8,128)(2,1)S(1)}, u32[]{:S(2)}, u32[]{:S(2)}) collective-permute-start(bf16[512,384]{1,0:T(8,128)(2,1)S(1)} %get-tuple-element.50), channel_id=1, source_target_pairs={{0,2},{1,3},{2,0},{3,1},{4,6},{5,7},{6,4},{7,5},{8,10},{9,11},{10,... | collective-permute-start | bytes 1179656 | tf_op jit(solution)/shard_map/ppermute | solution.py:28
  52.5 8.5 %collective-permute-start.19 = (bf16[384,128]{1,0:T(8,128)(2,1)S(1)}, bf16[384,128]{1,0:T(8,128)(2,1)S(1)}, u32[]{:S(2)}, u32[]{:S(2)}) collective-permute-start(bf16[384,128]{1,0:T(8,128)(2,1)S(1)} %get-tuple-element.48.att_ref), channel_id=1, source_target_pairs={{0,8},{8,0},{16,24},{24,16},{32,40},{40,32},{48,56},{56,48},{64,72... | collective-permute-start | bytes 294920 | tf_op jit(solution)/shard_map/ppermute | solution.py:28
  52.6 15.8 %collective-permute-start.23 = (f32[8,128]{1,0:T(8,128)S(1)}, f32[8,128]{1,0:T(8,128)S(1)}, u32[]{:S(2)}, u32[]{:S(2)}) collective-permute-start(f32[8,128]{1,0:T(8,128)S(1)} %shard_map.115.refs_17_), channel_id=1, source_target_pairs={{0,192},{8,200},{16,208},{24,216},{32,224},{40,232},{48,240},{56,2... | collective-permute-start | bytes 12296 | tf_op jit(solution)/shard_map/ppermute | solution.py:28
  61.0 8.6 %collective-permute-start.22 = (f32[8,128]{1,0:T(8,128)S(1)}, f32[8,128]{1,0:T(8,128)S(1)}, u32[]{:S(2)}, u32[]{:S(2)}) collective-permute-start(f32[8,128]{1,0:T(8,128)S(1)} %shard_map.115.refs_17_), channel_id=1, source_target_pairs={{0,128},{8,136},{16,144},{24,152},{32,160},{40,168},{48,176},{56,1... | collective-permute-start | bytes 12296 | tf_op jit(solution)/shard_map/ppermute | solution.py:28
  61.0 8.6 %collective-permute-start.21 = (f32[8,128]{1,0:T(8,128)S(1)}, f32[8,128]{1,0:T(8,128)S(1)}, u32[]{:S(2)}, u32[]{:S(2)}) collective-permute-start(f32[8,128]{1,0:T(8,128)S(1)} %shard_map.115.refs_17_), channel_id=1, source_target_pairs={{0,64},{8,72},{16,80},{24,88},{32,96},{40,104},{48,112},{56,120},{... | collective-permute-start | bytes 12296 | tf_op jit(solution)/shard_map/ppermute | solution.py:28
  65.0 11.6 %collective-permute-start.25 = (bf16[48,3072]{1,0:T(8,128)(2,1)S(1)}, bf16[48,3072]{1,0:T(8,128)(2,1)S(1)}, u32[]{:S(2)}, u32[]{:S(2)}) collective-permute-start(bf16[48,3072]{1,0:T(8,128)(2,1)S(1)} %get-tuple-element.59), channel_id=1, source_target_pairs={{0,32},{8,40},{16,48},{24,56},{32,0},{40,8},{48,16},{56,24},{64,96... | collective-permute-start | bytes 884744 | tf_op jit(solution)/shard_map/ppermute | solution.py:28
  68.4 11.8 %collective-permute-start.26 = (bf16[48,3072]{1,0:T(8,128)(2,1)S(1)}, bf16[48,3072]{1,0:T(8,128)(2,1)S(1)}, u32[]{:S(2)}, u32[]{:S(2)}) collective-permute-start(bf16[48,3072]{1,0:T(8,128)(2,1)S(1)} %get-tuple-element.60), channel_id=1, source_target_pairs={{0,48},{8,56},{16,32},{24,40},{32,16},{40,24},{48,0},{56,8},{64,11... | collective-permute-start | bytes 884744 | tf_op jit(solution)/shard_map/ppermute | solution.py:28
  69.5 11.1 %collective-permute-start.24 = (bf16[48,3072]{1,0:T(8,128)(2,1)S(1)}, bf16[48,3072]{1,0:T(8,128)(2,1)S(1)}, u32[]{:S(2)}, u32[]{:S(2)}) collective-permute-start(bf16[48,3072]{1,0:T(8,128)(2,1)S(1)} %get-tuple-element.53), channel_id=1, source_target_pairs={{0,16},{8,24},{16,0},{24,8},{32,48},{40,56},{48,32},{56,40},{64,80... | collective-permute-start | bytes 884744 | tf_op jit(solution)/shard_map/ppermute | solution.py:28
  81.1 8.4 %collective-permute-start.28 = (bf16[256,384]{1,0:T(8,128)(2,1)S(1)}, bf16[256,384]{1,0:T(8,128)(2,1)S(1)}, u32[]{:S(2)}, u32[]{:S(2)}) collective-permute-start(bf16[256,384]{1,0:T(8,128)(2,1)S(1)} %get-tuple-element.78), channel_id=1, source_target_pairs={{0,32},{8,40},{16,48},{24,56},{32,0},{40,8},{48,16},{56,24},{64,96... | collective-permute-start | bytes 589832 | tf_op jit(solution)/shard_map/ppermute | solution.py:28
  83.2 9.0 %collective-permute-start.29 = (bf16[256,384]{1,0:T(8,128)(2,1)S(1)}, bf16[256,384]{1,0:T(8,128)(2,1)S(1)}, u32[]{:S(2)}, u32[]{:S(2)}) collective-permute-start(bf16[256,384]{1,0:T(8,128)(2,1)S(1)} %slice.116), channel_id=1, source_target_pairs={{0,1},{1,0},{2,3},{3,2},{4,5},{5,4},{6,7},{7,6},{8,9},{9,8},{10,11... | collective-permute-start | bytes 589832 | tf_op jit(solution)/shard_map/ppermute | solution.py:28
  85.0 16.2 %collective-permute-start.33 = (bf16[24,3072]{1,0:T(8,128)(2,1)S(1)}, bf16[24,3072]{1,0:T(8,128)(2,1)S(1)}, u32[]{:S(2)}, u32[]{:S(2)}) collective-permute-start(bf16[24,3072]{1,0:T(8,128)(2,1)S(1)} %slice.117), channel_id=1, source_target_pairs={{0,128},{8,136},{16,144},{24,152},{32,160},{40,168},{48,176},{56,1... | collective-permute-start | bytes 442376 | tf_op jit(solution)/shard_map/ppermute | solution.py:28
  85.8 20.5 %collective-permute-start.31 = (bf16[768,128]{1,0:T(8,128)(2,1)S(1)}, bf16[768,128]{1,0:T(8,128)(2,1)S(1)}, u32[]{:S(2)}, u32[]{:S(2)}) collective-permute-start(bf16[768,128]{1,0:T(8,128)(2,1)S(1)} %get-tuple-element.66), channel_id=1, source_target_pairs={{0,128},{8,136},{16,144},{24,152},{32,160},{40,168},{48,176},{56,1... | collective-permute-start | bytes 589832 | tf_op jit(solution)/shard_map/ppermute | solution.py:28
  88.0 20.5 %collective-permute-start.34 = (bf16[256,384]{1,0:T(8,128)(2,1)S(1)}, bf16[256,384]{1,0:T(8,128)(2,1)S(1)}, u32[]{:S(2)}, u32[]{:S(2)}) collective-permute-start(bf16[256,384]{1,0:T(8,128)(2,1)S(1)} %get-tuple-element.76), channel_id=1, source_target_pairs={{0,16},{8,24},{16,0},{24,8},{32,48},{40,56},{48,32},{56,40},{64,80... | collective-permute-start | bytes 589832 | tf_op jit(solution)/shard_map/ppermute | solution.py:28
  89.5 19.0 %collective-permute-start.35 = (bf16[256,384]{1,0:T(8,128)(2,1)S(1)}, bf16[256,384]{1,0:T(8,128)(2,1)S(1)}, u32[]{:S(2)}, u32[]{:S(2)}) collective-permute-start(bf16[256,384]{1,0:T(8,128)(2,1)S(1)} %get-tuple-element.77), channel_id=1, source_target_pairs={{0,48},{8,56},{16,32},{24,40},{32,16},{40,24},{48,0},{56,8},{64,11... | collective-permute-start | bytes 589832 | tf_op jit(solution)/shard_map/ppermute | solution.py:28
  92.3 21.5 %collective-permute-start.30 = (bf16[128,384]{1,0:T(8,128)(2,1)S(1)}, bf16[128,384]{1,0:T(8,128)(2,1)S(1)}, u32[]{:S(2)}, u32[]{:S(2)}) collective-permute-start(bf16[128,384]{1,0:T(8,128)(2,1)S(1)} %slice.120), channel_id=1, source_target_pairs={{0,4},{1,5},{2,6},{3,7},{4,0},{5,1},{6,2},{7,3},{8,12},{9,13},{10,... | collective-permute-start | bytes 294920 | tf_op jit(solution)/shard_map/ppermute | solution.py:28
  106.4 5.5 %collective-permute-start.36 = (bf16[12,3072]{1,0:T(8,128)(2,1)S(1)}, bf16[12,3072]{1,0:T(8,128)(2,1)S(1)}, u32[]{:S(2)}, u32[]{:S(2)}) collective-permute-start(bf16[12,3072]{1,0:T(8,128)(2,1)S(1)} %slice.118), channel_id=1, source_target_pairs={{0,64},{8,72},{16,80},{24,88},{32,96},{40,104},{48,112},{56,120},{... | collective-permute-start | bytes 221192 | tf_op jit(solution)/shard_map/ppermute | solution.py:28
  106.5 6.4 %collective-permute-start.32 = (bf16[384,128]{1,0:T(8,128)(2,1)S(1)}, bf16[384,128]{1,0:T(8,128)(2,1)S(1)}, u32[]{:S(2)}, u32[]{:S(2)}) collective-permute-start(bf16[384,128]{1,0:T(8,128)(2,1)S(1)} %slice.119), channel_id=1, source_target_pairs={{0,64},{8,72},{16,80},{24,88},{32,96},{40,104},{48,112},{56,120},{... | collective-permute-start | bytes 294920 | tf_op jit(solution)/shard_map/ppermute | solution.py:28
  (15 other events, 115.6 us)

commit v4 on v3

--- a/solution.py
+++ b/solution.py
@@ -276,10 +276,11 @@
     d_full = jnp.concatenate([d_full, swap(d_full, "head", 2)], axis=0)
     parts = [parts[0]] + [swap(parts[j], "slab", 8 * j) for j in (1, 2, 3)]
     d_full = after(d_full, *parts[1:])
-    d_other = swap(d_full, "slab", 1)
     grad = call(grad_kernel, [((COLS, ROWS), BF)], ranks, w_out, d_full, flops=3 * 10**8, moved=3 * 10**6)[0]
     g_near = swap(grad, "slab", 8)
     att, logs = call(merge_kernel, [((COLS, ROWS), BF), ((8, ROWS), F32)], *parts, flops=10**8, moved=10**6)
+    g_far = swap(jnp.concatenate([grad, after(g_near, att)], axis=0), "slab", 16)
+    g_all = [grad, g_near, g_far[:COLS], g_far[COLS:]]
     stats = call(delta_kernel, [((8, ROWS), F32)], logs, att, grad, flops=10**6, moved=10**6)[0]
     stat_all = [stats] + [swap(stats, "slab", 8 * j) for j in (1, 2, 3)]
     att_other = swap(att, "slab", 1)
@@ -288,14 +289,13 @@
         mix_kernel,
         [((4 * ROWS, COLS), F32), ((4 * ROWS, COLS), BF)],
         ranks,
-        after(att, grad),
+        after(att, g_near, *stat_all[1:]),
         w_out,
         flops=3 * 10**8,
         moved=4 * 10**6,
     )
     mix_in = swap(mix[1], "head", 2)
-    g_far = swap(jnp.concatenate([grad, after(g_near, mix[1])], axis=0), "slab", 16)
-    g_all = [grad, g_near, g_far[:COLS], g_far[COLS:]]
+    d_other = swap(after(d_full, g_near), "slab", 1)
     weight = call(
         weight_kernel,
         [((48, WIDE), F32)] + [((48, WIDE), BF)] * 3,
@@ -308,9 +308,10 @@
         moved=4 * 10**6,
     )
     weight_in = [swap(weight[j], "slab", 2 * j) for j in (1, 2, 3)]
-    mixed = mix[0] + mix_in.astype(F32)
+    mixed = after(mix[0], weight[1]) + mix_in.astype(F32)
     mixed_away = mixed[2 * ROWS :].astype(BF)
-    stat_all[0] = after(stat_all[0], weight[1], mixed_away)
+    mix_near = swap(mixed_away, "head", 1)
+    stat_all[0] = after(stat_all[0], weight[1])
 
     dq_own, dq_other, own, other = call(
         backward_kernel,
@@ -328,14 +329,15 @@
     weight_away = weight[24:].astype(BF)
 
     other = swap(other, "slab", 1)
-    pair = (after(own, weight_away) + other.astype(F32)).reshape(4, 2 * ROWS, COLS)
+    pair = (after(own, weight_away, mixed_away) + other.astype(F32)).reshape(4, 2 * ROWS, COLS)
     away = [pair[e].astype(BF) for e in (1, 2, 3)]
     arrived = [swap(away[e - 1], "slab", 2 * e) for e in (1, 2, 3)]
+    weight_far = swap(weight_away, "slab", 16)
     dq_in = swap(after(dq_other, other), "slab", 16)
 
-    mixed = after(mixed[: 2 * ROWS], arrived[1]) + swap(mixed_away, "head", 1).astype(F32)
+    mixed = after(mixed[: 2 * ROWS], arrived[1]) + mix_near.astype(F32)
     mixed_away = mixed[ROWS:].astype(BF)
-    weight = after(weight[:24], mixed_away) + swap(weight_away, "slab", 16).astype(F32)
+    weight = after(weight[:24], mixed_away) + weight_far.astype(F32)
     weight_away = weight[12:].astype(BF)
     dq = after(dq_own, mixed_away) + dq_in.astype(F32)
     dq_away = dq[COLS:].astype(BF)

time: 115 us -> 119 us (1.035)
  waiting for transfers between devices: 32.6 us -> 41.9 us
  starting transfers between devices: 57.6 us -> 52.8 us
    ppermute x37, waiting for transfers between devices: 32.6 us -> 41.9 us  [swap(): return lax.ppermute(block, axis, [(i, i ^ distance) for i in devices])]
    ppermute x37, starting transfers between devices: 57.6 us -> 52.8 us  [swap(): return lax.ppermute(block, axis, [(i, i ^ distance) for i in devices])]
  transfers between devices with their start and end apart: 37 -> 37, of which waited for: 13 -> 17; matrix products, arithmetic and copies ran while one was open for 3% -> 3% of each run, Pallas kernels for 13% -> 11%
where the time goes in v4:
time: 119 us
  starting transfers between devices  52.8 us (44%)
  waiting for transfers between devices  41.9 us (35%)
  Pallas kernels  16.6 us (14%)
  local copies, waits for them, and re-layouts  3.49 us (3%)
  other arithmetic  3.12 us (3%)
    ppermute x37, starting transfers between devices, swap(): return lax.ppermute(block, axis, [(i, i ^ distance) for i in devices])  52.8 us
    ppermute x37, waiting for transfers between devices, swap(): return lax.ppermute(block, axis, [(i, i ^ distance) for i in devices])  41.9 us
    pallas_call x8, Pallas kernels, call(): pl.pallas_call(kernel, out_shape=[jax.ShapeDtypeStruct(shape, dtype) for...  16.6 us
    unnamed x17, local copies, waits for them, and re-layouts  2.6 us
  transfers between devices with their start and end apart: 37, of which 17 were waited for; matrix products, arithmetic and copies ran while one was open for 3% of the time, Pallas kernels for 11%

profile of v4, /device:TPU:2, one launch (start us, length us, event | category | flops | bytes accessed | tf_op | source)
XLA Modules:
  0.0 118.8 jit_solution(4769148229803814142)
XLA Ops:
  0.6 1.8 %shard_map.110 = (bf16[144,384]{1,0:T(8,128)(2,1)}, bf16[256,384]{1,0:T(8,128)(2,1)}) custom-call(s32[2,4]{1,0:T(2,128)} %ids_hbm.1, s32[2]{0:T(128)} %counts_hbm.1, bf16[128,384]{1,0:T(8,128)(2,1)} %q_hbm.1, bf16[128,384]{1,0:T(8,128)(2,1)} %k_hbm.1, bf16[128,384]{1,0:T(8,128)(2,1)} %v_hbm.1), custom_call_target="tpu_custom_call" | custom-call | flops 1000 | bytes 1000 | tf_op jit(solution)/shard_map/pallas_call | solution.py:39
  2.4 2.0 %collective-permute-start = (bf16[144,384]{1,0:T(8,128)(2,1)}, bf16[144,384]{1,0:T(8,128)(2,1)S(1)}, u32[]{:S(2)}, u32[]{:S(2)}) collective-permute-start(bf16[144,384]{1,0:T(8,128)(2,1)} %get-tuple-element.39.refs_1_), channel_id=1, source_target_pairs={{0,64},{8,72},{16,80},{24,88},{32,96},{40,104},{48,112},{56,120},{... | collective-permute-start | bytes 331784 | tf_op jit(solution)/shard_map/ppermute | solution.py:28
  4.4 3.3 %collective-permute-start.1 = (bf16[144,384]{1,0:T(8,128)(2,1)}, bf16[144,384]{1,0:T(8,128)(2,1)S(1)}, u32[]{:S(2)}, u32[]{:S(2)}) collective-permute-start(bf16[144,384]{1,0:T(8,128)(2,1)} %get-tuple-element.39.refs_1_), channel_id=1, source_target_pairs={{0,128},{8,136},{16,144},{24,152},{32,160},{40,168},{48,176},{56,1... | collective-permute-start | bytes 331784 | tf_op jit(solution)/shard_map/ppermute | solution.py:28
  7.7 1.6 %collective-permute-start.3 = (bf16[256,384]{1,0:T(8,128)(2,1)}, bf16[256,384]{1,0:T(8,128)(2,1)S(1)}, u32[]{:S(2)}, u32[]{:S(2)}) collective-permute-start(bf16[256,384]{1,0:T(8,128)(2,1)} %get-tuple-element.40.refs_5_), channel_id=1, source_target_pairs={{0,16},{8,24},{16,0},{24,8},{32,48},{40,56},{48,32},{56,40},{64,80... | collective-permute-start | bytes 589832 | tf_op jit(solution)/shard_map/ppermute | solution.py:28
  9.3 2.9 %collective-permute-start.4 = (bf16[256,384]{1,0:T(8,128)(2,1)}, bf16[256,384]{1,0:T(8,128)(2,1)S(1)}, u32[]{:S(2)}, u32[]{:S(2)}) collective-permute-start(bf16[256,384]{1,0:T(8,128)(2,1)} %get-tuple-element.40.refs_5_), channel_id=1, source_target_pairs={{0,32},{8,40},{16,48},{24,56},{32,0},{40,8},{48,16},{56,24},{64,96... | collective-permute-start | bytes 589832 | tf_op jit(solution)/shard_map/ppermute | solution.py:28
  13.4 5.4 %collective-permute-start.13 = (bf16[128,384]{1,0:T(8,128)(2,1)}, bf16[128,384]{1,0:T(8,128)(2,1)S(1)}, u32[]{:S(2)}, u32[]{:S(2)}) collective-permute-start(bf16[128,384]{1,0:T(8,128)(2,1)} %param.11), channel_id=1, source_target_pairs={{0,4},{1,5},{2,6},{3,7},{4,0},{5,1},{6,2},{7,3},{8,12},{9,13},{10,... | collective-permute-start | bytes 294920 | tf_op jit(solution)/shard_map/ppermute | solution.py:28
  18.8 1.6 %collective-permute-done.2.refs_4_ = bf16[144,384]{1,0:T(8,128)(2,1)S(1)} collective-permute-done((bf16[144,384]{1,0:T(8,128)(2,1)}, bf16[144,384]{1,0:T(8,128)(2,1)S(1)}, u32[]{:S(2)}, u32[]{:S(2)}) %collective-permute-start.2) | collective-permute-done | bytes 110624 | tf_op jit(solution)/shard_map/ppermute | solution.py:28
  21.0 2.2 %collective-permute-done.5.refs_8_ = bf16[256,384]{1,0:T(8,128)(2,1)S(1)} collective-permute-done((bf16[256,384]{1,0:T(8,128)(2,1)}, bf16[256,384]{1,0:T(8,128)(2,1)S(1)}, u32[]{:S(2)}, u32[]{:S(2)}) %collective-permute-start.5) | collective-permute-done | bytes 196640 | tf_op jit(solution)/shard_map/ppermute | solution.py:28
  27.4 3.9 %shard_map.111 = (bf16[400,128]{1,0:T(8,128)(2,1)S(1)}, bf16[400,128]{1,0:T(8,128)(2,1)S(1)}, bf16[400,128]{1,0:T(8,128)(2,1)S(1)}, bf16[400,128]{1,0:T(8,128)(2,1)S(1)}) custom-call(s32[4]{0:T(128)S(1)} %pad_add_fusion.refs_0_.rank_ref, bf16[144,384]{1,0:T(8,128)(2,1)S(1)} %copy-done.3, bf16[144,384]{1,0:T(8,128)(2,1)S(1)} %collective-permute-done.refs_2_, ...), custom_call_target="tpu_custom_call" | custom-call | flops 1000 | bytes 1000 | tf_op jit(solution)/shard_map/pallas_call | solution.py:39
  31.6 2.2 %collective-permute-start.15 = (bf16[512,384]{1,0:T(8,128)(2,1)S(1)}, bf16[512,384]{1,0:T(8,128)(2,1)S(1)}, u32[]{:S(2)}, u32[]{:S(2)}) collective-permute-start(bf16[512,384]{1,0:T(8,128)(2,1)S(1)} %pad_maximum_fusion.1), channel_id=1, source_target_pairs={{0,2},{1,3},{2,0},{3,1},{4,6},{5,7},{6,4},{7,5},{8,10},{9,11},{10,... | collective-permute-start | bytes 1179656 | tf_op jit(solution)/shard_map/ppermute | solution.py:28
  35.0 1.5 %collective-permute-start.11 = (bf16[400,128]{1,0:T(8,128)(2,1)S(1)}, bf16[400,128]{1,0:T(8,128)(2,1)S(1)}, u32[]{:S(2)}, u32[]{:S(2)}) collective-permute-start(bf16[400,128]{1,0:T(8,128)(2,1)S(1)} %get-tuple-element.43), channel_id=1, source_target_pairs={{0,128},{8,136},{16,144},{24,152},{32,160},{40,168},{48,176},{56,1... | collective-permute-start | bytes 307208 | tf_op jit(solution)/shard_map/ppermute | solution.py:28
  36.5 1.7 %collective-permute-start.12 = (bf16[400,128]{1,0:T(8,128)(2,1)S(1)}, bf16[400,128]{1,0:T(8,128)(2,1)S(1)}, u32[]{:S(2)}, u32[]{:S(2)}) collective-permute-start(bf16[400,128]{1,0:T(8,128)(2,1)S(1)} %get-tuple-element.44), channel_id=1, source_target_pairs={{0,192},{8,200},{16,208},{24,216},{32,224},{40,232},{48,240},{56,2... | collective-permute-start | bytes 307208 | tf_op jit(solution)/shard_map/ppermute | solution.py:28
  38.2 5.3 %collective-permute-done.15 = bf16[512,384]{1,0:T(8,128)(2,1)S(1)} collective-permute-done((bf16[512,384]{1,0:T(8,128)(2,1)S(1)}, bf16[512,384]{1,0:T(8,128)(2,1)S(1)}, u32[]{:S(2)}, u32[]{:S(2)}) %collective-permute-start.15) | collective-permute-done | bytes 393248 | tf_op jit(solution)/shard_map/ppermute | solution.py:28
  45.8 1.7 %collective-permute-start.16 = (bf16[384,128]{1,0:T(8,128)(2,1)S(1)}, bf16[384,128]{1,0:T(8,128)(2,1)S(1)}, u32[]{:S(2)}, u32[]{:S(2)}) collective-permute-start(bf16[384,128]{1,0:T(8,128)(2,1)S(1)} %shard_map.113.grad_ref.refs_13_), channel_id=1, source_target_pairs={{0,64},{8,72},{16,80},{24,88},{32,96},{40,104},{48,112},{56,120},{... | collective-permute-start | bytes 294920 | tf_op jit(solution)/shard_map/ppermute | solution.py:28
  47.6 3.0 %collective-permute-done.16.refs_14_ = bf16[384,128]{1,0:T(8,128)(2,1)S(1)} collective-permute-done((bf16[384,128]{1,0:T(8,128)(2,1)S(1)}, bf16[384,128]{1,0:T(8,128)(2,1)S(1)}, u32[]{:S(2)}, u32[]{:S(2)}) %collective-permute-start.16) | collective-permute-done | bytes 98336 | tf_op jit(solution)/shard_map/ppermute | solution.py:28
  50.7 1.6 %collective-permute-start.23 = (bf16[768,128]{1,0:T(8,128)(2,1)S(1)}, bf16[768,128]{1,0:T(8,128)(2,1)S(1)}, u32[]{:S(2)}, u32[]{:S(2)}) collective-permute-start(bf16[768,128]{1,0:T(8,128)(2,1)S(1)} %pad_maximum_fusion.3), channel_id=1, source_target_pairs={{0,128},{8,136},{16,144},{24,152},{32,160},{40,168},{48,176},{56,1... | collective-permute-start | bytes 589832 | tf_op jit(solution)/shard_map/ppermute | solution.py:28
  52.8 2.7 %collective-permute-start.18 = (f32[8,128]{1,0:T(8,128)S(1)}, f32[8,128]{1,0:T(8,128)S(1)}, u32[]{:S(2)}, u32[]{:S(2)}) collective-permute-start(f32[8,128]{1,0:T(8,128)S(1)} %shard_map.114.refs_17_), channel_id=1, source_target_pairs={{0,128},{8,136},{16,144},{24,152},{32,160},{40,168},{48,176},{56,1... | collective-permute-start | bytes 12296 | tf_op jit(solution)/shard_map/ppermute | solution.py:28
  57.4 6.1 %collective-permute-done.18.refs_19_ = f32[8,128]{1,0:T(8,128)S(1)} collective-permute-done((f32[8,128]{1,0:T(8,128)S(1)}, f32[8,128]{1,0:T(8,128)S(1)}, u32[]{:S(2)}, u32[]{:S(2)}) %collective-permute-start.18) | collective-permute-done | bytes 4128 | tf_op jit(solution)/shard_map/ppermute | solution.py:28
  64.8 1.6 %collective-permute-start.22 = (bf16[512,384]{1,0:T(8,128)(2,1)S(1)}, bf16[512,384]{1,0:T(8,128)(2,1)S(1)}, u32[]{:S(2)}, u32[]{:S(2)}) collective-permute-start(bf16[512,384]{1,0:T(8,128)(2,1)S(1)} %get-tuple-element.56), channel_id=1, source_target_pairs={{0,2},{1,3},{2,0},{3,1},{4,6},{5,7},{6,4},{7,5},{8,10},{9,11},{10,... | collective-permute-start | bytes 1179656 | tf_op jit(solution)/shard_map/ppermute | solution.py:28
  69.0 1.8 %collective-permute-start.24 = (bf16[48,3072]{1,0:T(8,128)(2,1)S(1)}, bf16[48,3072]{1,0:T(8,128)(2,1)S(1)}, u32[]{:S(2)}, u32[]{:S(2)}) collective-permute-start(bf16[48,3072]{1,0:T(8,128)(2,1)S(1)} %get-tuple-element.54), channel_id=1, source_target_pairs={{0,16},{8,24},{16,0},{24,8},{32,48},{40,56},{48,32},{56,40},{64,80... | collective-permute-start | bytes 884744 | tf_op jit(solution)/shard_map/ppermute | solution.py:28
  70.8 1.8 %collective-permute-start.25 = (bf16[48,3072]{1,0:T(8,128)(2,1)S(1)}, bf16[48,3072]{1,0:T(8,128)(2,1)S(1)}, u32[]{:S(2)}, u32[]{:S(2)}) collective-permute-start(bf16[48,3072]{1,0:T(8,128)(2,1)S(1)} %get-tuple-element.63), channel_id=1, source_target_pairs={{0,32},{8,40},{16,48},{24,56},{32,0},{40,8},{48,16},{56,24},{64,96... | collective-permute-start | bytes 884744 | tf_op jit(solution)/shard_map/ppermute | solution.py:28
  73.9 6.9 %shard_map.117 = (f32[768,128]{1,0:T(8,128)S(1)}, bf16[768,128]{1,0:T(8,128)(2,1)S(1)}, f32[1024,384]{1,0:T(8,128)S(1)}, bf16[1024,384]{1,0:T(8,128)(2,1)S(1)}) custom-call(s32[4]{0:T(128)S(1)} %pad_add_fusion.refs_0_.rank_ref, bf16[144,384]{1,0:T(8,128)(2,1)S(1)} %copy-done.4, bf16[144,384]{1,0:T(8,128)(2,1)S(1)} %collective-permute-done.refs_2_, ...), custom_call_target="tpu_custom_call" | custom-call | flops 1000 | bytes 1000 | tf_op jit(solution)/shard_map/pallas_call | solution.py:39
  81.0 5.2 %collective-permute-done.25 = bf16[48,3072]{1,0:T(8,128)(2,1)S(1)} collective-permute-done((bf16[48,3072]{1,0:T(8,128)(2,1)S(1)}, bf16[48,3072]{1,0:T(8,128)(2,1)S(1)}, u32[]{:S(2)}, u32[]{:S(2)}) %collective-permute-start.25) | collective-permute-done | bytes 294944 | tf_op jit(solution)/shard_map/ppermute | solution.py:28
  86.2 2.7 %collective-permute-done.26 = bf16[48,3072]{1,0:T(8,128)(2,1)S(1)} collective-permute-done((bf16[48,3072]{1,0:T(8,128)(2,1)S(1)}, bf16[48,3072]{1,0:T(8,128)(2,1)S(1)}, u32[]{:S(2)}, u32[]{:S(2)}) %collective-permute-start.26) | collective-permute-done | bytes 294944 | tf_op jit(solution)/shard_map/ppermute | solution.py:28
  89.7 1.8 %collective-permute-start.29 = (bf16[256,384]{1,0:T(8,128)(2,1)S(1)}, bf16[256,384]{1,0:T(8,128)(2,1)S(1)}, u32[]{:S(2)}, u32[]{:S(2)}) collective-permute-start(bf16[256,384]{1,0:T(8,128)(2,1)S(1)} %slice.116), channel_id=1, source_target_pairs={{0,1},{1,0},{2,3},{3,2},{4,5},{5,4},{6,7},{7,6},{8,9},{9,8},{10,11... | collective-permute-start | bytes 589832 | tf_op jit(solution)/shard_map/ppermute | solution.py:28
  91.8 2.7 %collective-permute-start.31 = (bf16[768,128]{1,0:T(8,128)(2,1)S(1)}, bf16[768,128]{1,0:T(8,128)(2,1)S(1)}, u32[]{:S(2)}, u32[]{:S(2)}) collective-permute-start(bf16[768,128]{1,0:T(8,128)(2,1)S(1)} %get-tuple-element.70), channel_id=1, source_target_pairs={{0,128},{8,136},{16,144},{24,152},{32,160},{40,168},{48,176},{56,1... | collective-permute-start | bytes 589832 | tf_op jit(solution)/shard_map/ppermute | solution.py:28
  94.6 1.7 %collective-permute-start.34 = (bf16[256,384]{1,0:T(8,128)(2,1)S(1)}, bf16[256,384]{1,0:T(8,128)(2,1)S(1)}, u32[]{:S(2)}, u32[]{:S(2)}) collective-permute-start(bf16[256,384]{1,0:T(8,128)(2,1)S(1)} %get-tuple-element.80), channel_id=1, source_target_pairs={{0,16},{8,24},{16,0},{24,8},{32,48},{40,56},{48,32},{56,40},{64,80... | collective-permute-start | bytes 589832 | tf_op jit(solution)/shard_map/ppermute | solution.py:28
  96.6 1.8 %collective-permute-start.35 = (bf16[256,384]{1,0:T(8,128)(2,1)S(1)}, bf16[256,384]{1,0:T(8,128)(2,1)S(1)}, u32[]{:S(2)}, u32[]{:S(2)}) collective-permute-start(bf16[256,384]{1,0:T(8,128)(2,1)S(1)} %get-tuple-element.81), channel_id=1, source_target_pairs={{0,48},{8,56},{16,32},{24,40},{32,16},{40,24},{48,0},{56,8},{64,11... | collective-permute-start | bytes 589832 | tf_op jit(solution)/shard_map/ppermute | solution.py:28
  98.5 5.3 %collective-permute-start.30 = (bf16[128,384]{1,0:T(8,128)(2,1)S(1)}, bf16[128,384]{1,0:T(8,128)(2,1)S(1)}, u32[]{:S(2)}, u32[]{:S(2)}) collective-permute-start(bf16[128,384]{1,0:T(8,128)(2,1)S(1)} %slice.120), channel_id=1, source_target_pairs={{0,4},{1,5},{2,6},{3,7},{4,0},{5,1},{6,2},{7,3},{8,12},{9,13},{10,... | collective-permute-start | bytes 294920 | tf_op jit(solution)/shard_map/ppermute | solution.py:28
  103.8 3.4 %collective-permute-done.33 = bf16[24,3072]{1,0:T(8,128)(2,1)S(1)} collective-permute-done((bf16[24,3072]{1,0:T(8,128)(2,1)S(1)}, bf16[24,3072]{1,0:T(8,128)(2,1)S(1)}, u32[]{:S(2)}, u32[]{:S(2)}) %collective-permute-start.33) | collective-permute-done | bytes 147488 | tf_op jit(solution)/shard_map/ppermute | solution.py:28
  107.3 5.3 %collective-permute-done.31 = bf16[768,128]{1,0:T(8,128)(2,1)S(1)} collective-permute-done((bf16[768,128]{1,0:T(8,128)(2,1)S(1)}, bf16[768,128]{1,0:T(8,128)(2,1)S(1)}, u32[]{:S(2)}, u32[]{:S(2)}) %collective-permute-start.31) | collective-permute-done | bytes 196640 | tf_op jit(solution)/shard_map/ppermute | solution.py:28
  115.4 2.0 %collective-permute-done.32 = bf16[384,128]{1,0:T(8,128)(2,1)S(1)} collective-permute-done((bf16[384,128]{1,0:T(8,128)(2,1)S(1)}, bf16[384,128]{1,0:T(8,128)(2,1)S(1)}, u32[]{:S(2)}, u32[]{:S(2)}) %collective-permute-start.32) | collective-permute-done | bytes 98336 | tf_op jit(solution)/shard_map/ppermute | solution.py:28
  (95 shorter events, 23.5 us)
Async XLA Ops:
  2.4 10.0 %collective-permute-start = (bf16[144,384]{1,0:T(8,128)(2,1)}, bf16[144,384]{1,0:T(8,128)(2,1)S(1)}, u32[]{:S(2)}, u32[]{:S(2)}) collective-permute-start(bf16[144,384]{1,0:T(8,128)(2,1)} %get-tuple-element.39.refs_1_), channel_id=1, source_target_pairs={{0,64},{8,72},{16,80},{24,88},{32,96},{40,104},{48,112},{56,120},{... | collective-permute-start | bytes 331784 | tf_op jit(solution)/shard_map/ppermute | solution.py:28
  4.4 9.0 %collective-permute-start.1 = (bf16[144,384]{1,0:T(8,128)(2,1)}, bf16[144,384]{1,0:T(8,128)(2,1)S(1)}, u32[]{:S(2)}, u32[]{:S(2)}) collective-permute-start(bf16[144,384]{1,0:T(8,128)(2,1)} %get-tuple-element.39.refs_1_), channel_id=1, source_target_pairs={{0,128},{8,136},{16,144},{24,152},{32,160},{40,168},{48,176},{56,1... | collective-permute-start | bytes 331784 | tf_op jit(solution)/shard_map/ppermute | solution.py:28
  7.7 12.7 %collective-permute-start.3 = (bf16[256,384]{1,0:T(8,128)(2,1)}, bf16[256,384]{1,0:T(8,128)(2,1)S(1)}, u32[]{:S(2)}, u32[]{:S(2)}) collective-permute-start(bf16[256,384]{1,0:T(8,128)(2,1)} %get-tuple-element.40.refs_5_), channel_id=1, source_target_pairs={{0,16},{8,24},{16,0},{24,8},{32,48},{40,56},{48,32},{56,40},{64,80... | collective-permute-start | bytes 589832 | tf_op jit(solution)/shard_map/ppermute | solution.py:28
  9.3 11.6 %collective-permute-start.4 = (bf16[256,384]{1,0:T(8,128)(2,1)}, bf16[256,384]{1,0:T(8,128)(2,1)S(1)}, u32[]{:S(2)}, u32[]{:S(2)}) collective-permute-start(bf16[256,384]{1,0:T(8,128)(2,1)} %get-tuple-element.40.refs_5_), channel_id=1, source_target_pairs={{0,32},{8,40},{16,48},{24,56},{32,0},{40,8},{48,16},{56,24},{64,96... | collective-permute-start | bytes 589832 | tf_op jit(solution)/shard_map/ppermute | solution.py:28
  12.2 11.0 %collective-permute-start.5 = (bf16[256,384]{1,0:T(8,128)(2,1)}, bf16[256,384]{1,0:T(8,128)(2,1)S(1)}, u32[]{:S(2)}, u32[]{:S(2)}) collective-permute-start(bf16[256,384]{1,0:T(8,128)(2,1)} %get-tuple-element.40.refs_5_), channel_id=1, source_target_pairs={{0,48},{8,56},{16,32},{24,40},{32,16},{40,24},{48,0},{56,8},{64,11... | collective-permute-start | bytes 589832 | tf_op jit(solution)/shard_map/ppermute | solution.py:28
  12.4 8.0 %collective-permute-start.2 = (bf16[144,384]{1,0:T(8,128)(2,1)}, bf16[144,384]{1,0:T(8,128)(2,1)S(1)}, u32[]{:S(2)}, u32[]{:S(2)}) collective-permute-start(bf16[144,384]{1,0:T(8,128)(2,1)} %get-tuple-element.39.refs_1_), channel_id=1, source_target_pairs={{0,192},{8,200},{16,208},{24,216},{32,224},{40,232},{48,240},{56,2... | collective-permute-start | bytes 331784 | tf_op jit(solution)/shard_map/ppermute | solution.py:28
  13.4 10.5 %collective-permute-start.13 = (bf16[128,384]{1,0:T(8,128)(2,1)}, bf16[128,384]{1,0:T(8,128)(2,1)S(1)}, u32[]{:S(2)}, u32[]{:S(2)}) collective-permute-start(bf16[128,384]{1,0:T(8,128)(2,1)} %param.11), channel_id=1, source_target_pairs={{0,4},{1,5},{2,6},{3,7},{4,0},{5,1},{6,2},{7,3},{8,12},{9,13},{10,... | collective-permute-start | bytes 294920 | tf_op jit(solution)/shard_map/ppermute | solution.py:28
  20.4 5.1 %collective-permute-start.6 = (bf16[256,384]{1,0:T(8,128)(2,1)}, bf16[256,384]{1,0:T(8,128)(2,1)S(1)}, u32[]{:S(2)}, u32[]{:S(2)}) collective-permute-start(bf16[256,384]{1,0:T(8,128)(2,1)} %get-tuple-element.40.refs_5_), channel_id=1, source_target_pairs={{0,8},{8,0},{16,24},{24,16},{32,40},{40,32},{48,56},{56,48},{64,72... | collective-permute-start | bytes 589832 | tf_op jit(solution)/shard_map/ppermute | solution.py:28
  20.4 5.1 %collective-permute-start.7 = (bf16[256,384]{1,0:T(8,128)(2,1)S(1)}, bf16[256,384]{1,0:T(8,128)(2,1)S(1)}, u32[]{:S(2)}, u32[]{:S(2)}) collective-permute-start(bf16[256,384]{1,0:T(8,128)(2,1)S(1)} %collective-permute-done.3.refs_6_), channel_id=1, source_target_pairs={{0,8},{8,0},{16,24},{24,16},{32,40},{40,32},{48,56},{56,48},{64,72... | collective-permute-start | bytes 589832 | tf_op jit(solution)/shard_map/ppermute | solution.py:28
  24.8 6.7 %collective-permute-start.14 = (bf16[256,384]{1,0:T(8,128)(2,1)S(1)}, bf16[256,384]{1,0:T(8,128)(2,1)S(1)}, u32[]{:S(2)}, u32[]{:S(2)}) collective-permute-start(bf16[256,384]{1,0:T(8,128)(2,1)S(1)} %pad_maximum_fusion.2), channel_id=1, source_target_pairs={{0,1},{1,0},{2,3},{3,2},{4,5},{5,4},{6,7},{7,6},{8,9},{9,8},{10,11... | collective-permute-start | bytes 589832 | tf_op jit(solution)/shard_map/ppermute | solution.py:28
  31.6 11.9 %collective-permute-start.15 = (bf16[512,384]{1,0:T(8,128)(2,1)S(1)}, bf16[512,384]{1,0:T(8,128)(2,1)S(1)}, u32[]{:S(2)}, u32[]{:S(2)}) collective-permute-start(bf16[512,384]{1,0:T(8,128)(2,1)S(1)} %pad_maximum_fusion.1), channel_id=1, source_target_pairs={{0,2},{1,3},{2,0},{3,1},{4,6},{5,7},{6,4},{7,5},{8,10},{9,11},{10,... | collective-permute-start | bytes 1179656 | tf_op jit(solution)/shard_map/ppermute | solution.py:28
  33.8 9.8 %collective-permute-start.10 = (bf16[400,128]{1,0:T(8,128)(2,1)S(1)}, bf16[400,128]{1,0:T(8,128)(2,1)S(1)}, u32[]{:S(2)}, u32[]{:S(2)}) collective-permute-start(bf16[400,128]{1,0:T(8,128)(2,1)S(1)} %get-tuple-element.42), channel_id=1, source_target_pairs={{0,64},{8,72},{16,80},{24,88},{32,96},{40,104},{48,112},{56,120},{... | collective-permute-start | bytes 307208 | tf_op jit(solution)/shard_map/ppermute | solution.py:28
  35.0 9.5 %collective-permute-start.11 = (bf16[400,128]{1,0:T(8,128)(2,1)S(1)}, bf16[400,128]{1,0:T(8,128)(2,1)S(1)}, u32[]{:S(2)}, u32[]{:S(2)}) collective-permute-start(bf16[400,128]{1,0:T(8,128)(2,1)S(1)} %get-tuple-element.43), channel_id=1, source_target_pairs={{0,128},{8,136},{16,144},{24,152},{32,160},{40,168},{48,176},{56,1... | collective-permute-start | bytes 307208 | tf_op jit(solution)/shard_map/ppermute | solution.py:28
  36.5 8.0 %collective-permute-start.12 = (bf16[400,128]{1,0:T(8,128)(2,1)S(1)}, bf16[400,128]{1,0:T(8,128)(2,1)S(1)}, u32[]{:S(2)}, u32[]{:S(2)}) collective-permute-start(bf16[400,128]{1,0:T(8,128)(2,1)S(1)} %get-tuple-element.44), channel_id=1, source_target_pairs={{0,192},{8,200},{16,208},{24,216},{32,224},{40,232},{48,240},{56,2... | collective-permute-start | bytes 307208 | tf_op jit(solution)/shard_map/ppermute | solution.py:28
  50.5 17.2 %collective-permute-start.21 = (bf16[1024,384]{1,0:T(8,128)(2,1)S(1)}, bf16[1024,384]{1,0:T(8,128)(2,1)S(1)}, u32[]{:S(2)}, u32[]{:S(2)}) collective-permute-start(bf16[1024,384]{1,0:T(8,128)(2,1)S(1)} %pad_maximum_fusion.d_ref), channel_id=1, source_target_pairs={{0,8},{8,0},{16,24},{24,16},{32,40},{40,32},{48,56},{56,48},{64,72... | collective-permute-start | bytes 2359304 | tf_op jit(solution)/shard_map/ppermute | solution.py:28
  50.7 23.1 %collective-permute-start.23 = (bf16[768,128]{1,0:T(8,128)(2,1)S(1)}, bf16[768,128]{1,0:T(8,128)(2,1)S(1)}, u32[]{:S(2)}, u32[]{:S(2)}) collective-permute-start(bf16[768,128]{1,0:T(8,128)(2,1)S(1)} %pad_maximum_fusion.3), channel_id=1, source_target_pairs={{0,128},{8,136},{16,144},{24,152},{32,160},{40,168},{48,176},{56,1... | collective-permute-start | bytes 589832 | tf_op jit(solution)/shard_map/ppermute | solution.py:28
  52.4 5.0 %collective-permute-start.17 = (f32[8,128]{1,0:T(8,128)S(1)}, f32[8,128]{1,0:T(8,128)S(1)}, u32[]{:S(2)}, u32[]{:S(2)}) collective-permute-start(f32[8,128]{1,0:T(8,128)S(1)} %shard_map.114.refs_17_), channel_id=1, source_target_pairs={{0,64},{8,72},{16,80},{24,88},{32,96},{40,104},{48,112},{56,120},{... | collective-permute-start | bytes 12296 | tf_op jit(solution)/shard_map/ppermute | solution.py:28
  52.8 10.7 %collective-permute-start.18 = (f32[8,128]{1,0:T(8,128)S(1)}, f32[8,128]{1,0:T(8,128)S(1)}, u32[]{:S(2)}, u32[]{:S(2)}) collective-permute-start(f32[8,128]{1,0:T(8,128)S(1)} %shard_map.114.refs_17_), channel_id=1, source_target_pairs={{0,128},{8,136},{16,144},{24,152},{32,160},{40,168},{48,176},{56,1... | collective-permute-start | bytes 12296 | tf_op jit(solution)/shard_map/ppermute | solution.py:28
  55.5 8.0 %collective-permute-start.19 = (f32[8,128]{1,0:T(8,128)S(1)}, f32[8,128]{1,0:T(8,128)S(1)}, u32[]{:S(2)}, u32[]{:S(2)}) collective-permute-start(f32[8,128]{1,0:T(8,128)S(1)} %shard_map.114.refs_17_), channel_id=1, source_target_pairs={{0,192},{8,200},{16,208},{24,216},{32,224},{40,232},{48,240},{56,2... | collective-permute-start | bytes 12296 | tf_op jit(solution)/shard_map/ppermute | solution.py:28
  64.8 16.1 %collective-permute-start.22 = (bf16[512,384]{1,0:T(8,128)(2,1)S(1)}, bf16[512,384]{1,0:T(8,128)(2,1)S(1)}, u32[]{:S(2)}, u32[]{:S(2)}) collective-permute-start(bf16[512,384]{1,0:T(8,128)(2,1)S(1)} %get-tuple-element.56), channel_id=1, source_target_pairs={{0,2},{1,3},{2,0},{3,1},{4,6},{5,7},{6,4},{7,5},{8,10},{9,11},{10,... | collective-permute-start | bytes 1179656 | tf_op jit(solution)/shard_map/ppermute | solution.py:28
  69.0 12.0 %collective-permute-start.24 = (bf16[48,3072]{1,0:T(8,128)(2,1)S(1)}, bf16[48,3072]{1,0:T(8,128)(2,1)S(1)}, u32[]{:S(2)}, u32[]{:S(2)}) collective-permute-start(bf16[48,3072]{1,0:T(8,128)(2,1)S(1)} %get-tuple-element.54), channel_id=1, source_target_pairs={{0,16},{8,24},{16,0},{24,8},{32,48},{40,56},{48,32},{56,40},{64,80... | collective-permute-start | bytes 884744 | tf_op jit(solution)/shard_map/ppermute | solution.py:28
  70.8 15.4 %collective-permute-start.25 = (bf16[48,3072]{1,0:T(8,128)(2,1)S(1)}, bf16[48,3072]{1,0:T(8,128)(2,1)S(1)}, u32[]{:S(2)}, u32[]{:S(2)}) collective-permute-start(bf16[48,3072]{1,0:T(8,128)(2,1)S(1)} %get-tuple-element.63), channel_id=1, source_target_pairs={{0,32},{8,40},{16,48},{24,56},{32,0},{40,8},{48,16},{56,24},{64,96... | collective-permute-start | bytes 884744 | tf_op jit(solution)/shard_map/ppermute | solution.py:28
  72.6 16.2 %collective-permute-start.26 = (bf16[48,3072]{1,0:T(8,128)(2,1)S(1)}, bf16[48,3072]{1,0:T(8,128)(2,1)S(1)}, u32[]{:S(2)}, u32[]{:S(2)}) collective-permute-start(bf16[48,3072]{1,0:T(8,128)(2,1)S(1)} %get-tuple-element.64), channel_id=1, source_target_pairs={{0,48},{8,56},{16,32},{24,40},{32,16},{40,24},{48,0},{56,8},{64,11... | collective-permute-start | bytes 884744 | tf_op jit(solution)/shard_map/ppermute | solution.py:28
  80.8 8.2 %collective-permute-start.27 = (bf16[1024,384]{1,0:T(8,128)(2,1)S(1)}, bf16[1024,384]{1,0:T(8,128)(2,1)S(1)}, u32[]{:S(2)}, u32[]{:S(2)}) collective-permute-start(bf16[1024,384]{1,0:T(8,128)(2,1)S(1)} %get-tuple-element.61), channel_id=1, source_target_pairs={{0,8},{8,0},{16,24},{24,16},{32,40},{40,32},{48,56},{56,48},{64,72... | collective-permute-start | bytes 2359304 | tf_op jit(solution)/shard_map/ppermute | solution.py:28
  89.3 7.3 %collective-permute-start.28 = (bf16[256,384]{1,0:T(8,128)(2,1)S(1)}, bf16[256,384]{1,0:T(8,128)(2,1)S(1)}, u32[]{:S(2)}, u32[]{:S(2)}) collective-permute-start(bf16[256,384]{1,0:T(8,128)(2,1)S(1)} %get-tuple-element.82), channel_id=1, source_target_pairs={{0,32},{8,40},{16,48},{24,56},{32,0},{40,8},{48,16},{56,24},{64,96... | collective-permute-start | bytes 589832 | tf_op jit(solution)/shard_map/ppermute | solution.py:28
  89.7 8.7 %collective-permute-start.29 = (bf16[256,384]{1,0:T(8,128)(2,1)S(1)}, bf16[256,384]{1,0:T(8,128)(2,1)S(1)}, u32[]{:S(2)}, u32[]{:S(2)}) collective-permute-start(bf16[256,384]{1,0:T(8,128)(2,1)S(1)} %slice.116), channel_id=1, source_target_pairs={{0,1},{1,0},{2,3},{3,2},{4,5},{5,4},{6,7},{7,6},{8,9},{9,8},{10,11... | collective-permute-start | bytes 589832 | tf_op jit(solution)/shard_map/ppermute | solution.py:28
  91.5 15.7 %collective-permute-start.33 = (bf16[24,3072]{1,0:T(8,128)(2,1)S(1)}, bf16[24,3072]{1,0:T(8,128)(2,1)S(1)}, u32[]{:S(2)}, u32[]{:S(2)}) collective-permute-start(bf16[24,3072]{1,0:T(8,128)(2,1)S(1)} %slice.117), channel_id=1, source_target_pairs={{0,128},{8,136},{16,144},{24,152},{32,160},{40,168},{48,176},{56,1... | collective-permute-start | bytes 442376 | tf_op jit(solution)/shard_map/ppermute | solution.py:28
  91.8 20.8 %collective-permute-start.31 = (bf16[768,128]{1,0:T(8,128)(2,1)S(1)}, bf16[768,128]{1,0:T(8,128)(2,1)S(1)}, u32[]{:S(2)}, u32[]{:S(2)}) collective-permute-start(bf16[768,128]{1,0:T(8,128)(2,1)S(1)} %get-tuple-element.70), channel_id=1, source_target_pairs={{0,128},{8,136},{16,144},{24,152},{32,160},{40,168},{48,176},{56,1... | collective-permute-start | bytes 589832 | tf_op jit(solution)/shard_map/ppermute | solution.py:28
  94.6 18.2 %collective-permute-start.34 = (bf16[256,384]{1,0:T(8,128)(2,1)S(1)}, bf16[256,384]{1,0:T(8,128)(2,1)S(1)}, u32[]{:S(2)}, u32[]{:S(2)}) collective-permute-start(bf16[256,384]{1,0:T(8,128)(2,1)S(1)} %get-tuple-element.80), channel_id=1, source_target_pairs={{0,16},{8,24},{16,0},{24,8},{32,48},{40,56},{48,32},{56,40},{64,80... | collective-permute-start | bytes 589832 | tf_op jit(solution)/shard_map/ppermute | solution.py:28
  96.6 16.2 %collective-permute-start.35 = (bf16[256,384]{1,0:T(8,128)(2,1)S(1)}, bf16[256,384]{1,0:T(8,128)(2,1)S(1)}, u32[]{:S(2)}, u32[]{:S(2)}) collective-permute-start(bf16[256,384]{1,0:T(8,128)(2,1)S(1)} %get-tuple-element.81), channel_id=1, source_target_pairs={{0,48},{8,56},{16,32},{24,40},{32,16},{40,24},{48,0},{56,8},{64,11... | collective-permute-start | bytes 589832 | tf_op jit(solution)/shard_map/ppermute | solution.py:28
  98.5 19.7 %collective-permute-start.30 = (bf16[128,384]{1,0:T(8,128)(2,1)S(1)}, bf16[128,384]{1,0:T(8,128)(2,1)S(1)}, u32[]{:S(2)}, u32[]{:S(2)}) collective-permute-start(bf16[128,384]{1,0:T(8,128)(2,1)S(1)} %slice.120), channel_id=1, source_target_pairs={{0,4},{1,5},{2,6},{3,7},{4,0},{5,1},{6,2},{7,3},{8,12},{9,13},{10,... | collective-permute-start | bytes 294920 | tf_op jit(solution)/shard_map/ppermute | solution.py:28
  107.2 7.4 %collective-permute-start.36 = (bf16[12,3072]{1,0:T(8,128)(2,1)S(1)}, bf16[12,3072]{1,0:T(8,128)(2,1)S(1)}, u32[]{:S(2)}, u32[]{:S(2)}) collective-permute-start(bf16[12,3072]{1,0:T(8,128)(2,1)S(1)} %slice.118), channel_id=1, source_target_pairs={{0,64},{8,72},{16,80},{24,88},{32,96},{40,104},{48,112},{56,120},{... | collective-permute-start | bytes 221192 | tf_op jit(solution)/shard_map/ppermute | solution.py:28
  (15 other events, 117.5 us)

commit v5 on v3

--- a/solution.py
+++ b/solution.py
@@ -181,8 +181,8 @@
     col = lax.broadcasted_iota(jnp.int32, (192, COLS), 1)
     source = row * 0
     for jy in range(4):
-        for jt in range(4):
-            low = jy * 48 + jt * 12
+        for place, jt in enumerate((0, 2, 1, 3)):
+            low = jy * 48 + place * 12
             base = (t ^ jt) * 96 + (y ^ jy) * 24 + c * 12 - low
             source = jnp.where((row >= low) & (row < low + 12), row + base, source)
     pick = jnp.where(source == col, 1.0, 0.0).astype(BF)
@@ -228,8 +228,8 @@
             target[place + ROWS : place + 2 * ROWS, cols] = dv.astype(target.dtype)
         dq = dq * SCALE
         for j in range(4):
-            target = dq_own if j < 2 else dq_other
-            start = (j % 2) * COLS + h * HD
+            target = dq_other if j % 2 else dq_own
+            start = (j // 2) * COLS + h * HD
             target[start : start + HD, :] = dq[:, j * ROWS : (j + 1) * ROWS].astype(target.dtype)
 
 
@@ -276,9 +276,8 @@
     d_full = jnp.concatenate([d_full, swap(d_full, "head", 2)], axis=0)
     parts = [parts[0]] + [swap(parts[j], "slab", 8 * j) for j in (1, 2, 3)]
     d_full = after(d_full, *parts[1:])
-    d_other = swap(d_full, "slab", 1)
     grad = call(grad_kernel, [((COLS, ROWS), BF)], ranks, w_out, d_full, flops=3 * 10**8, moved=3 * 10**6)[0]
-    g_near = swap(grad, "slab", 8)
+    g_near = swap(grad, "slab", 16)
     att, logs = call(merge_kernel, [((COLS, ROWS), BF), ((8, ROWS), F32)], *parts, flops=10**8, moved=10**6)
     stats = call(delta_kernel, [((8, ROWS), F32)], logs, att, grad, flops=10**6, moved=10**6)[0]
     stat_all = [stats] + [swap(stats, "slab", 8 * j) for j in (1, 2, 3)]
@@ -294,8 +293,9 @@
         moved=4 * 10**6,
     )
     mix_in = swap(mix[1], "head", 2)
-    g_far = swap(jnp.concatenate([grad, after(g_near, mix[1])], axis=0), "slab", 16)
-    g_all = [grad, g_near, g_far[:COLS], g_far[COLS:]]
+    g_far = swap(jnp.concatenate([grad, after(g_near, mix[1])], axis=0), "slab", 8)
+    g_all = [grad, g_far[:COLS], g_near, g_far[COLS:]]
+    d_other = swap(after(d_full, att), "slab", 1)
     weight = call(
         weight_kernel,
         [((48, WIDE), F32)] + [((48, WIDE), BF)] * 3,
@@ -331,20 +331,20 @@
     pair = (after(own, weight_away) + other.astype(F32)).reshape(4, 2 * ROWS, COLS)
     away = [pair[e].astype(BF) for e in (1, 2, 3)]
     arrived = [swap(away[e - 1], "slab", 2 * e) for e in (1, 2, 3)]
-    dq_in = swap(after(dq_other, other), "slab", 16)
+    dq_in = swap(after(dq_other, other), "slab", 8)
 
     mixed = after(mixed[: 2 * ROWS], arrived[1]) + swap(mixed_away, "head", 1).astype(F32)
     mixed_away = mixed[ROWS:].astype(BF)
-    weight = after(weight[:24], mixed_away) + swap(weight_away, "slab", 16).astype(F32)
+    weight = after(weight[:24], mixed_away) + swap(weight_away, "slab", 8).astype(F32)
     weight_away = weight[12:].astype(BF)
     dq = after(dq_own, mixed_away) + dq_in.astype(F32)
     dq_away = dq[COLS:].astype(BF)
 
     total = after(pair[0], weight_away, mixed_away, dq_away) + sum((a.astype(F32) for a in arrived), 0.0)
     total = total.astype(BF)
-    weight_grad = weight[:12] + swap(weight_away, "slab", 8).astype(F32)
+    weight_grad = weight[:12] + swap(weight_away, "slab", 16).astype(F32)
     mixed = mixed[:ROWS] + swap(mixed_away, "head", 4).astype(F32)
-    dq = dq[:COLS] + swap(dq_away, "slab", 8).astype(F32)
+    dq = dq[:COLS] + swap(dq_away, "slab", 16).astype(F32)
     query_grad = dq.astype(BF).T
     return mixed.astype(BF), query_grad, total[:ROWS], total[ROWS:], weight_grad
 

time: 115 us -> 113 us (0.983); the launches traced: 114 us -> 111 us
  waiting for transfers between devices: 32.6 us -> 28.4 us
    ppermute x37, waiting for transfers between devices: 32.6 us -> 28.4 us  [swap(): return lax.ppermute(block, axis, [(i, i ^ distance) for i in devices])]
  transfers between devices with their start and end apart: 37 -> 37, of which waited for: 13 -> 11; matrix products, arithmetic and copies ran while one was open for 3% -> 3% of each run, Pallas kernels for 13% -> 13%
where the time goes in v5:
time: 113 us; the launch traced here: 111 us
  starting transfers between devices  58 us (51%)
  waiting for transfers between devices  28.4 us (25%)
  Pallas kernels  16.5 us (15%)
  local copies, waits for them, and re-layouts  3.49 us (3%)
  other arithmetic  3.16 us (3%)
    ppermute x37, starting transfers between devices, swap(): return lax.ppermute(block, axis, [(i, i ^ distance) for i in devices])  58 us
    ppermute x37, waiting for transfers between devices, swap(): return lax.ppermute(block, axis, [(i, i ^ distance) for i in devices])  28.4 us
    pallas_call x8, Pallas kernels, call(): pl.pallas_call(kernel, out_shape=[jax.ShapeDtypeStruct(shape, dtype) for...  16.5 us
    unnamed x17, local copies, waits for them, and re-layouts  2.6 us
  transfers between devices with their start and end apart: 37, of which 11 were waited for; matrix products, arithmetic and copies ran while one was open for 3% of the time, Pallas kernels for 13%

profile of v5, /device:TPU:2, one launch (start us, length us, event | category | flops | bytes accessed | tf_op | source)
XLA Modules:
  0.0 110.6 jit_solution(5008242924144624171)
XLA Ops:
  0.6 1.8 %shard_map.110 = (bf16[144,384]{1,0:T(8,128)(2,1)}, bf16[256,384]{1,0:T(8,128)(2,1)}) custom-call(s32[2,4]{1,0:T(2,128)} %ids_hbm.1, s32[2]{0:T(128)} %counts_hbm.1, bf16[128,384]{1,0:T(8,128)(2,1)} %q_hbm.1, bf16[128,384]{1,0:T(8,128)(2,1)} %k_hbm.1, bf16[128,384]{1,0:T(8,128)(2,1)} %v_hbm.1), custom_call_target="tpu_custom_call" | custom-call | flops 1000 | bytes 1000 | tf_op jit(solution)/shard_map/pallas_call | solution.py:39
  2.4 2.0 %collective-permute-start = (bf16[144,384]{1,0:T(8,128)(2,1)}, bf16[144,384]{1,0:T(8,128)(2,1)S(1)}, u32[]{:S(2)}, u32[]{:S(2)}) collective-permute-start(bf16[144,384]{1,0:T(8,128)(2,1)} %get-tuple-element.38.refs_1_), channel_id=1, source_target_pairs={{0,64},{8,72},{16,80},{24,88},{32,96},{40,104},{48,112},{56,120},{... | collective-permute-start | bytes 331784 | tf_op jit(solution)/shard_map/ppermute | solution.py:28
  4.4 2.8 %collective-permute-start.2 = (bf16[144,384]{1,0:T(8,128)(2,1)}, bf16[144,384]{1,0:T(8,128)(2,1)S(1)}, u32[]{:S(2)}, u32[]{:S(2)}) collective-permute-start(bf16[144,384]{1,0:T(8,128)(2,1)} %get-tuple-element.38.refs_1_), channel_id=1, source_target_pairs={{0,192},{8,200},{16,208},{24,216},{32,224},{40,232},{48,240},{56,2... | collective-permute-start | bytes 331784 | tf_op jit(solution)/shard_map/ppermute | solution.py:28
  7.3 3.0 %collective-permute-start.5 = (bf16[256,384]{1,0:T(8,128)(2,1)}, bf16[256,384]{1,0:T(8,128)(2,1)S(1)}, u32[]{:S(2)}, u32[]{:S(2)}) collective-permute-start(bf16[256,384]{1,0:T(8,128)(2,1)} %get-tuple-element.39.refs_5_), channel_id=1, source_target_pairs={{0,48},{8,56},{16,32},{24,40},{32,16},{40,24},{48,0},{56,8},{64,11... | collective-permute-start | bytes 589832 | tf_op jit(solution)/shard_map/ppermute | solution.py:28
  11.4 1.4 %collective-permute-start.1 = (bf16[144,384]{1,0:T(8,128)(2,1)}, bf16[144,384]{1,0:T(8,128)(2,1)S(1)}, u32[]{:S(2)}, u32[]{:S(2)}) collective-permute-start(bf16[144,384]{1,0:T(8,128)(2,1)} %get-tuple-element.38.refs_1_), channel_id=1, source_target_pairs={{0,128},{8,136},{16,144},{24,152},{32,160},{40,168},{48,176},{56,1... | collective-permute-start | bytes 331784 | tf_op jit(solution)/shard_map/ppermute | solution.py:28
  12.9 5.2 %collective-permute-start.13 = (bf16[128,384]{1,0:T(8,128)(2,1)}, bf16[128,384]{1,0:T(8,128)(2,1)S(1)}, u32[]{:S(2)}, u32[]{:S(2)}) collective-permute-start(bf16[128,384]{1,0:T(8,128)(2,1)} %param.11), channel_id=1, source_target_pairs={{0,4},{1,5},{2,6},{3,7},{4,0},{5,1},{6,2},{7,3},{8,12},{9,13},{10,... | collective-permute-start | bytes 294920 | tf_op jit(solution)/shard_map/ppermute | solution.py:28
  18.1 1.6 %collective-permute-done.1.refs_3_ = bf16[144,384]{1,0:T(8,128)(2,1)S(1)} collective-permute-done((bf16[144,384]{1,0:T(8,128)(2,1)}, bf16[144,384]{1,0:T(8,128)(2,1)S(1)}, u32[]{:S(2)}, u32[]{:S(2)}) %collective-permute-start.1) | collective-permute-done | bytes 110624 | tf_op jit(solution)/shard_map/ppermute | solution.py:28
  20.6 1.4 %collective-permute-done.13 = bf16[128,384]{1,0:T(8,128)(2,1)S(1)} collective-permute-done((bf16[128,384]{1,0:T(8,128)(2,1)}, bf16[128,384]{1,0:T(8,128)(2,1)S(1)}, u32[]{:S(2)}, u32[]{:S(2)}) %collective-permute-start.13) | collective-permute-done | bytes 98336 | tf_op jit(solution)/shard_map/ppermute | solution.py:28
  25.5 3.9 %shard_map.111 = (bf16[400,128]{1,0:T(8,128)(2,1)S(1)}, bf16[400,128]{1,0:T(8,128)(2,1)S(1)}, bf16[400,128]{1,0:T(8,128)(2,1)S(1)}, bf16[400,128]{1,0:T(8,128)(2,1)S(1)}) custom-call(s32[4]{0:T(128)S(1)} %pad_add_fusion.refs_0_.rank_ref, bf16[144,384]{1,0:T(8,128)(2,1)S(1)} %copy-done.3, bf16[144,384]{1,0:T(8,128)(2,1)S(1)} %collective-permute-done.refs_2_, ...), custom_call_target="tpu_custom_call" | custom-call | flops 1000 | bytes 1000 | tf_op jit(solution)/shard_map/pallas_call | solution.py:39
  29.5 2.5 %collective-permute-start.15 = (bf16[512,384]{1,0:T(8,128)(2,1)S(1)}, bf16[512,384]{1,0:T(8,128)(2,1)S(1)}, u32[]{:S(2)}, u32[]{:S(2)}) collective-permute-start(bf16[512,384]{1,0:T(8,128)(2,1)S(1)} %pad_maximum_fusion.1), channel_id=1, source_target_pairs={{0,2},{1,3},{2,0},{3,1},{4,6},{5,7},{6,4},{7,5},{8,10},{9,11},{10,... | collective-permute-start | bytes 1179656 | tf_op jit(solution)/shard_map/ppermute | solution.py:28
  32.0 2.7 %collective-permute-start.10 = (bf16[400,128]{1,0:T(8,128)(2,1)S(1)}, bf16[400,128]{1,0:T(8,128)(2,1)S(1)}, u32[]{:S(2)}, u32[]{:S(2)}) collective-permute-start(bf16[400,128]{1,0:T(8,128)(2,1)S(1)} %get-tuple-element.41), channel_id=1, source_target_pairs={{0,64},{8,72},{16,80},{24,88},{32,96},{40,104},{48,112},{56,120},{... | collective-permute-start | bytes 307208 | tf_op jit(solution)/shard_map/ppermute | solution.py:28
  35.6 1.5 %collective-permute-start.12 = (bf16[400,128]{1,0:T(8,128)(2,1)S(1)}, bf16[400,128]{1,0:T(8,128)(2,1)S(1)}, u32[]{:S(2)}, u32[]{:S(2)}) collective-permute-start(bf16[400,128]{1,0:T(8,128)(2,1)S(1)} %get-tuple-element.43), channel_id=1, source_target_pairs={{0,192},{8,200},{16,208},{24,216},{32,224},{40,232},{48,240},{56,2... | collective-permute-start | bytes 307208 | tf_op jit(solution)/shard_map/ppermute | solution.py:28
  37.1 1.3 %collective-permute-done.10.refs_1_ = bf16[400,128]{1,0:T(8,128)(2,1)S(1)} collective-permute-done((bf16[400,128]{1,0:T(8,128)(2,1)S(1)}, bf16[400,128]{1,0:T(8,128)(2,1)S(1)}, u32[]{:S(2)}, u32[]{:S(2)}) %collective-permute-start.10) | collective-permute-done | bytes 102432 | tf_op jit(solution)/shard_map/ppermute | solution.py:28
  38.4 4.0 %collective-permute-done.11.refs_2_ = bf16[400,128]{1,0:T(8,128)(2,1)S(1)} collective-permute-done((bf16[400,128]{1,0:T(8,128)(2,1)S(1)}, bf16[400,128]{1,0:T(8,128)(2,1)S(1)}, u32[]{:S(2)}, u32[]{:S(2)}) %collective-permute-start.11) | collective-permute-done | bytes 102432 | tf_op jit(solution)/shard_map/ppermute | solution.py:28
  42.8 1.3 %shard_map.113.grad_ref.refs_13_ = bf16[384,128]{1,0:T(8,128)(2,1)S(1)} custom-call(s32[4]{0:T(128)S(1)} %pad_add_fusion.refs_0_.rank_ref, bf16[384,3072]{1,0:T(8,128)(2,1)S(1)} %copy-done, bf16[1024,384]{1,0:T(8,128)(2,1)S(1)} %pad_maximum_fusion.d_ref), custom_call_target="tpu_custom_call" | custom-call | flops 1000 | bytes 1000 | tf_op jit(solution)/shard_map/pallas_call | solution.py:39
  44.2 2.3 %collective-permute-start.17 = (bf16[384,128]{1,0:T(8,128)(2,1)S(1)}, bf16[384,128]{1,0:T(8,128)(2,1)S(1)}, u32[]{:S(2)}, u32[]{:S(2)}) collective-permute-start(bf16[384,128]{1,0:T(8,128)(2,1)S(1)} %shard_map.113.grad_ref.refs_13_), channel_id=1, source_target_pairs={{0,128},{8,136},{16,144},{24,152},{32,160},{40,168},{48,176},{56,1... | collective-permute-start | bytes 294920 | tf_op jit(solution)/shard_map/ppermute | solution.py:28
  47.7 4.7 %collective-permute-done.17.refs_15_ = bf16[384,128]{1,0:T(8,128)(2,1)S(1)} collective-permute-done((bf16[384,128]{1,0:T(8,128)(2,1)S(1)}, bf16[384,128]{1,0:T(8,128)(2,1)S(1)}, u32[]{:S(2)}, u32[]{:S(2)}) %collective-permute-start.17) | collective-permute-done | bytes 98336 | tf_op jit(solution)/shard_map/ppermute | solution.py:28
  53.8 2.1 %collective-permute-start.23 = (f32[8,128]{1,0:T(8,128)S(1)}, f32[8,128]{1,0:T(8,128)S(1)}, u32[]{:S(2)}, u32[]{:S(2)}) collective-permute-start(f32[8,128]{1,0:T(8,128)S(1)} %shard_map.115.refs_17_), channel_id=1, source_target_pairs={{0,192},{8,200},{16,208},{24,216},{32,224},{40,232},{48,240},{56,2... | collective-permute-start | bytes 12296 | tf_op jit(solution)/shard_map/ppermute | solution.py:28
  55.9 3.2 %collective-permute-done.18 = bf16[768,128]{1,0:T(8,128)(2,1)S(1)} collective-permute-done((bf16[768,128]{1,0:T(8,128)(2,1)S(1)}, bf16[768,128]{1,0:T(8,128)(2,1)S(1)}, u32[]{:S(2)}, u32[]{:S(2)}) %collective-permute-start.18) | collective-permute-done | bytes 196640 | tf_op jit(solution)/shard_map/ppermute | solution.py:28
  60.0 1.8 %collective-permute-start.21 = (f32[8,128]{1,0:T(8,128)S(1)}, f32[8,128]{1,0:T(8,128)S(1)}, u32[]{:S(2)}, u32[]{:S(2)}) collective-permute-start(f32[8,128]{1,0:T(8,128)S(1)} %shard_map.115.refs_17_), channel_id=1, source_target_pairs={{0,64},{8,72},{16,80},{24,88},{32,96},{40,104},{48,112},{56,120},{... | collective-permute-start | bytes 12296 | tf_op jit(solution)/shard_map/ppermute | solution.py:28
  63.1 3.4 %collective-permute-start.25 = (bf16[48,3072]{1,0:T(8,128)(2,1)S(1)}, bf16[48,3072]{1,0:T(8,128)(2,1)S(1)}, u32[]{:S(2)}, u32[]{:S(2)}) collective-permute-start(bf16[48,3072]{1,0:T(8,128)(2,1)S(1)} %get-tuple-element.61), channel_id=1, source_target_pairs={{0,32},{8,40},{16,48},{24,56},{32,0},{40,8},{48,16},{56,24},{64,96... | collective-permute-start | bytes 884744 | tf_op jit(solution)/shard_map/ppermute | solution.py:28
  67.8 6.8 %shard_map.117 = (f32[768,128]{1,0:T(8,128)S(1)}, bf16[768,128]{1,0:T(8,128)(2,1)S(1)}, f32[1024,384]{1,0:T(8,128)S(1)}, bf16[1024,384]{1,0:T(8,128)(2,1)S(1)}) custom-call(s32[4]{0:T(128)S(1)} %pad_add_fusion.refs_0_.rank_ref, bf16[144,384]{1,0:T(8,128)(2,1)S(1)} %copy-done.4, bf16[144,384]{1,0:T(8,128)(2,1)S(1)} %collective-permute-done.refs_2_, ...), custom_call_target="tpu_custom_call" | custom-call | flops 1000 | bytes 1000 | tf_op jit(solution)/shard_map/pallas_call | solution.py:39
  74.7 3.5 %collective-permute-done.26 = bf16[48,3072]{1,0:T(8,128)(2,1)S(1)} collective-permute-done((bf16[48,3072]{1,0:T(8,128)(2,1)S(1)}, bf16[48,3072]{1,0:T(8,128)(2,1)S(1)}, u32[]{:S(2)}, u32[]{:S(2)}) %collective-permute-start.26) | collective-permute-done | bytes 294944 | tf_op jit(solution)/shard_map/ppermute | solution.py:28
  79.1 2.1 %collective-permute-start.28 = (bf16[256,384]{1,0:T(8,128)(2,1)S(1)}, bf16[256,384]{1,0:T(8,128)(2,1)S(1)}, u32[]{:S(2)}, u32[]{:S(2)}) collective-permute-start(bf16[256,384]{1,0:T(8,128)(2,1)S(1)} %get-tuple-element.80), channel_id=1, source_target_pairs={{0,32},{8,40},{16,48},{24,56},{32,0},{40,8},{48,16},{56,24},{64,96... | collective-permute-start | bytes 589832 | tf_op jit(solution)/shard_map/ppermute | solution.py:28
  81.3 1.8 %collective-permute-start.29 = (bf16[256,384]{1,0:T(8,128)(2,1)S(1)}, bf16[256,384]{1,0:T(8,128)(2,1)S(1)}, u32[]{:S(2)}, u32[]{:S(2)}) collective-permute-start(bf16[256,384]{1,0:T(8,128)(2,1)S(1)} %slice.116), channel_id=1, source_target_pairs={{0,1},{1,0},{2,3},{3,2},{4,5},{5,4},{6,7},{7,6},{8,9},{9,8},{10,11... | collective-permute-start | bytes 589832 | tf_op jit(solution)/shard_map/ppermute | solution.py:28
  83.8 1.4 %collective-permute-start.31 = (bf16[768,128]{1,0:T(8,128)(2,1)S(1)}, bf16[768,128]{1,0:T(8,128)(2,1)S(1)}, u32[]{:S(2)}, u32[]{:S(2)}) collective-permute-start(bf16[768,128]{1,0:T(8,128)(2,1)S(1)} %get-tuple-element.68), channel_id=1, source_target_pairs={{0,64},{8,72},{16,80},{24,88},{32,96},{40,104},{48,112},{56,120},{... | collective-permute-start | bytes 589832 | tf_op jit(solution)/shard_map/ppermute | solution.py:28
  85.2 1.5 %collective-permute-start.34 = (bf16[256,384]{1,0:T(8,128)(2,1)S(1)}, bf16[256,384]{1,0:T(8,128)(2,1)S(1)}, u32[]{:S(2)}, u32[]{:S(2)}) collective-permute-start(bf16[256,384]{1,0:T(8,128)(2,1)S(1)} %get-tuple-element.78), channel_id=1, source_target_pairs={{0,16},{8,24},{16,0},{24,8},{32,48},{40,56},{48,32},{56,40},{64,80... | collective-permute-start | bytes 589832 | tf_op jit(solution)/shard_map/ppermute | solution.py:28
  86.7 4.4 %collective-permute-start.35 = (bf16[256,384]{1,0:T(8,128)(2,1)S(1)}, bf16[256,384]{1,0:T(8,128)(2,1)S(1)}, u32[]{:S(2)}, u32[]{:S(2)}) collective-permute-start(bf16[256,384]{1,0:T(8,128)(2,1)S(1)} %get-tuple-element.79), channel_id=1, source_target_pairs={{0,48},{8,56},{16,32},{24,40},{32,16},{40,24},{48,0},{56,8},{64,11... | collective-permute-start | bytes 589832 | tf_op jit(solution)/shard_map/ppermute | solution.py:28
  91.2 5.4 %collective-permute-start.30 = (bf16[128,384]{1,0:T(8,128)(2,1)S(1)}, bf16[128,384]{1,0:T(8,128)(2,1)S(1)}, u32[]{:S(2)}, u32[]{:S(2)}) collective-permute-start(bf16[128,384]{1,0:T(8,128)(2,1)S(1)} %slice.120), channel_id=1, source_target_pairs={{0,4},{1,5},{2,6},{3,7},{4,0},{5,1},{6,2},{7,3},{8,12},{9,13},{10,... | collective-permute-start | bytes 294920 | tf_op jit(solution)/shard_map/ppermute | solution.py:28
  98.0 1.7 %collective-permute-start.32 = (bf16[384,128]{1,0:T(8,128)(2,1)S(1)}, bf16[384,128]{1,0:T(8,128)(2,1)S(1)}, u32[]{:S(2)}, u32[]{:S(2)}) collective-permute-start(bf16[384,128]{1,0:T(8,128)(2,1)S(1)} %slice.119), channel_id=1, source_target_pairs={{0,128},{8,136},{16,144},{24,152},{32,160},{40,168},{48,176},{56,1... | collective-permute-start | bytes 294920 | tf_op jit(solution)/shard_map/ppermute | solution.py:28
  100.6 6.6 %collective-permute-done.36 = bf16[12,3072]{1,0:T(8,128)(2,1)S(1)} collective-permute-done((bf16[12,3072]{1,0:T(8,128)(2,1)S(1)}, bf16[12,3072]{1,0:T(8,128)(2,1)S(1)}, u32[]{:S(2)}, u32[]{:S(2)}) %collective-permute-start.36) | collective-permute-done | bytes 73760 | tf_op jit(solution)/shard_map/ppermute | solution.py:28
  107.9 1.3 %collective-permute-done.32 = bf16[384,128]{1,0:T(8,128)(2,1)S(1)} collective-permute-done((bf16[384,128]{1,0:T(8,128)(2,1)S(1)}, bf16[384,128]{1,0:T(8,128)(2,1)S(1)}, u32[]{:S(2)}, u32[]{:S(2)}) %collective-permute-start.32) | collective-permute-done | bytes 98336 | tf_op jit(solution)/shard_map/ppermute | solution.py:28
  (95 shorter events, 19.0 us)
Async XLA Ops:
  2.4 8.9 %collective-permute-start = (bf16[144,384]{1,0:T(8,128)(2,1)}, bf16[144,384]{1,0:T(8,128)(2,1)S(1)}, u32[]{:S(2)}, u32[]{:S(2)}) collective-permute-start(bf16[144,384]{1,0:T(8,128)(2,1)} %get-tuple-element.38.refs_1_), channel_id=1, source_target_pairs={{0,64},{8,72},{16,80},{24,88},{32,96},{40,104},{48,112},{56,120},{... | collective-permute-start | bytes 331784 | tf_op jit(solution)/shard_map/ppermute | solution.py:28
  4.4 8.4 %collective-permute-start.2 = (bf16[144,384]{1,0:T(8,128)(2,1)}, bf16[144,384]{1,0:T(8,128)(2,1)S(1)}, u32[]{:S(2)}, u32[]{:S(2)}) collective-permute-start(bf16[144,384]{1,0:T(8,128)(2,1)} %get-tuple-element.38.refs_1_), channel_id=1, source_target_pairs={{0,192},{8,200},{16,208},{24,216},{32,224},{40,232},{48,240},{56,2... | collective-permute-start | bytes 331784 | tf_op jit(solution)/shard_map/ppermute | solution.py:28
  7.3 12.4 %collective-permute-start.5 = (bf16[256,384]{1,0:T(8,128)(2,1)}, bf16[256,384]{1,0:T(8,128)(2,1)S(1)}, u32[]{:S(2)}, u32[]{:S(2)}) collective-permute-start(bf16[256,384]{1,0:T(8,128)(2,1)} %get-tuple-element.39.refs_5_), channel_id=1, source_target_pairs={{0,48},{8,56},{16,32},{24,40},{32,16},{40,24},{48,0},{56,8},{64,11... | collective-permute-start | bytes 589832 | tf_op jit(solution)/shard_map/ppermute | solution.py:28
  10.3 9.9 %collective-permute-start.4 = (bf16[256,384]{1,0:T(8,128)(2,1)}, bf16[256,384]{1,0:T(8,128)(2,1)S(1)}, u32[]{:S(2)}, u32[]{:S(2)}) collective-permute-start(bf16[256,384]{1,0:T(8,128)(2,1)} %get-tuple-element.39.refs_5_), channel_id=1, source_target_pairs={{0,32},{8,40},{16,48},{24,56},{32,0},{40,8},{48,16},{56,24},{64,96... | collective-permute-start | bytes 589832 | tf_op jit(solution)/shard_map/ppermute | solution.py:28
  10.9 9.3 %collective-permute-start.3 = (bf16[256,384]{1,0:T(8,128)(2,1)}, bf16[256,384]{1,0:T(8,128)(2,1)S(1)}, u32[]{:S(2)}, u32[]{:S(2)}) collective-permute-start(bf16[256,384]{1,0:T(8,128)(2,1)} %get-tuple-element.39.refs_5_), channel_id=1, source_target_pairs={{0,16},{8,24},{16,0},{24,8},{32,48},{40,56},{48,32},{56,40},{64,80... | collective-permute-start | bytes 589832 | tf_op jit(solution)/shard_map/ppermute | solution.py:28
  11.4 8.3 %collective-permute-start.1 = (bf16[144,384]{1,0:T(8,128)(2,1)}, bf16[144,384]{1,0:T(8,128)(2,1)S(1)}, u32[]{:S(2)}, u32[]{:S(2)}) collective-permute-start(bf16[144,384]{1,0:T(8,128)(2,1)} %get-tuple-element.38.refs_1_), channel_id=1, source_target_pairs={{0,128},{8,136},{16,144},{24,152},{32,160},{40,168},{48,176},{56,1... | collective-permute-start | bytes 331784 | tf_op jit(solution)/shard_map/ppermute | solution.py:28
  12.9 9.2 %collective-permute-start.13 = (bf16[128,384]{1,0:T(8,128)(2,1)}, bf16[128,384]{1,0:T(8,128)(2,1)S(1)}, u32[]{:S(2)}, u32[]{:S(2)}) collective-permute-start(bf16[128,384]{1,0:T(8,128)(2,1)} %param.11), channel_id=1, source_target_pairs={{0,4},{1,5},{2,6},{3,7},{4,0},{5,1},{6,2},{7,3},{8,12},{9,13},{10,... | collective-permute-start | bytes 294920 | tf_op jit(solution)/shard_map/ppermute | solution.py:28
  23.0 6.4 %collective-permute-start.14 = (bf16[256,384]{1,0:T(8,128)(2,1)S(1)}, bf16[256,384]{1,0:T(8,128)(2,1)S(1)}, u32[]{:S(2)}, u32[]{:S(2)}) collective-permute-start(bf16[256,384]{1,0:T(8,128)(2,1)S(1)} %pad_maximum_fusion.2), channel_id=1, source_target_pairs={{0,1},{1,0},{2,3},{3,2},{4,5},{5,4},{6,7},{7,6},{8,9},{9,8},{10,11... | collective-permute-start | bytes 589832 | tf_op jit(solution)/shard_map/ppermute | solution.py:28
  29.5 13.1 %collective-permute-start.15 = (bf16[512,384]{1,0:T(8,128)(2,1)S(1)}, bf16[512,384]{1,0:T(8,128)(2,1)S(1)}, u32[]{:S(2)}, u32[]{:S(2)}) collective-permute-start(bf16[512,384]{1,0:T(8,128)(2,1)S(1)} %pad_maximum_fusion.1), channel_id=1, source_target_pairs={{0,2},{1,3},{2,0},{3,1},{4,6},{5,7},{6,4},{7,5},{8,10},{9,11},{10,... | collective-permute-start | bytes 1179656 | tf_op jit(solution)/shard_map/ppermute | solution.py:28
  32.0 6.4 %collective-permute-start.10 = (bf16[400,128]{1,0:T(8,128)(2,1)S(1)}, bf16[400,128]{1,0:T(8,128)(2,1)S(1)}, u32[]{:S(2)}, u32[]{:S(2)}) collective-permute-start(bf16[400,128]{1,0:T(8,128)(2,1)S(1)} %get-tuple-element.41), channel_id=1, source_target_pairs={{0,64},{8,72},{16,80},{24,88},{32,96},{40,104},{48,112},{56,120},{... | collective-permute-start | bytes 307208 | tf_op jit(solution)/shard_map/ppermute | solution.py:28
  34.7 7.8 %collective-permute-start.11 = (bf16[400,128]{1,0:T(8,128)(2,1)S(1)}, bf16[400,128]{1,0:T(8,128)(2,1)S(1)}, u32[]{:S(2)}, u32[]{:S(2)}) collective-permute-start(bf16[400,128]{1,0:T(8,128)(2,1)S(1)} %get-tuple-element.42), channel_id=1, source_target_pairs={{0,128},{8,136},{16,144},{24,152},{32,160},{40,168},{48,176},{56,1... | collective-permute-start | bytes 307208 | tf_op jit(solution)/shard_map/ppermute | solution.py:28
  35.6 6.8 %collective-permute-start.12 = (bf16[400,128]{1,0:T(8,128)(2,1)S(1)}, bf16[400,128]{1,0:T(8,128)(2,1)S(1)}, u32[]{:S(2)}, u32[]{:S(2)}) collective-permute-start(bf16[400,128]{1,0:T(8,128)(2,1)S(1)} %get-tuple-element.43), channel_id=1, source_target_pairs={{0,192},{8,200},{16,208},{24,216},{32,224},{40,232},{48,240},{56,2... | collective-permute-start | bytes 307208 | tf_op jit(solution)/shard_map/ppermute | solution.py:28
  42.7 19.1 %collective-permute-start.20 = (bf16[1024,384]{1,0:T(8,128)(2,1)S(1)}, bf16[1024,384]{1,0:T(8,128)(2,1)S(1)}, u32[]{:S(2)}, u32[]{:S(2)}) collective-permute-start(bf16[1024,384]{1,0:T(8,128)(2,1)S(1)} %pad_maximum_fusion.d_ref), channel_id=1, source_target_pairs={{0,8},{8,0},{16,24},{24,16},{32,40},{40,32},{48,56},{56,48},{64,72... | collective-permute-start | bytes 2359304 | tf_op jit(solution)/shard_map/ppermute | solution.py:28
  44.2 8.3 %collective-permute-start.17 = (bf16[384,128]{1,0:T(8,128)(2,1)S(1)}, bf16[384,128]{1,0:T(8,128)(2,1)S(1)}, u32[]{:S(2)}, u32[]{:S(2)}) collective-permute-start(bf16[384,128]{1,0:T(8,128)(2,1)S(1)} %shard_map.113.grad_ref.refs_13_), channel_id=1, source_target_pairs={{0,128},{8,136},{16,144},{24,152},{32,160},{40,168},{48,176},{56,1... | collective-permute-start | bytes 294920 | tf_op jit(solution)/shard_map/ppermute | solution.py:28
  52.5 6.6 %collective-permute-start.18 = (bf16[768,128]{1,0:T(8,128)(2,1)S(1)}, bf16[768,128]{1,0:T(8,128)(2,1)S(1)}, u32[]{:S(2)}, u32[]{:S(2)}) collective-permute-start(bf16[768,128]{1,0:T(8,128)(2,1)S(1)} %pad_maximum_fusion.3), channel_id=1, source_target_pairs={{0,64},{8,72},{16,80},{24,88},{32,96},{40,104},{48,112},{56,120},{... | collective-permute-start | bytes 589832 | tf_op jit(solution)/shard_map/ppermute | solution.py:28
  52.6 15.0 %collective-permute-start.16 = (bf16[512,384]{1,0:T(8,128)(2,1)S(1)}, bf16[512,384]{1,0:T(8,128)(2,1)S(1)}, u32[]{:S(2)}, u32[]{:S(2)}) collective-permute-start(bf16[512,384]{1,0:T(8,128)(2,1)S(1)} %get-tuple-element.51), channel_id=1, source_target_pairs={{0,2},{1,3},{2,0},{3,1},{4,6},{5,7},{6,4},{7,5},{8,10},{9,11},{10,... | collective-permute-start | bytes 1179656 | tf_op jit(solution)/shard_map/ppermute | solution.py:28
  53.7 6.2 %collective-permute-start.19 = (bf16[384,128]{1,0:T(8,128)(2,1)S(1)}, bf16[384,128]{1,0:T(8,128)(2,1)S(1)}, u32[]{:S(2)}, u32[]{:S(2)}) collective-permute-start(bf16[384,128]{1,0:T(8,128)(2,1)S(1)} %get-tuple-element.49.att_ref), channel_id=1, source_target_pairs={{0,8},{8,0},{16,24},{24,16},{32,40},{40,32},{48,56},{56,48},{64,72... | collective-permute-start | bytes 294920 | tf_op jit(solution)/shard_map/ppermute | solution.py:28
  53.8 12.7 %collective-permute-start.23 = (f32[8,128]{1,0:T(8,128)S(1)}, f32[8,128]{1,0:T(8,128)S(1)}, u32[]{:S(2)}, u32[]{:S(2)}) collective-permute-start(f32[8,128]{1,0:T(8,128)S(1)} %shard_map.115.refs_17_), channel_id=1, source_target_pairs={{0,192},{8,200},{16,208},{24,216},{32,224},{40,232},{48,240},{56,2... | collective-permute-start | bytes 12296 | tf_op jit(solution)/shard_map/ppermute | solution.py:28
  59.1 8.6 %collective-permute-start.22 = (f32[8,128]{1,0:T(8,128)S(1)}, f32[8,128]{1,0:T(8,128)S(1)}, u32[]{:S(2)}, u32[]{:S(2)}) collective-permute-start(f32[8,128]{1,0:T(8,128)S(1)} %shard_map.115.refs_17_), channel_id=1, source_target_pairs={{0,128},{8,136},{16,144},{24,152},{32,160},{40,168},{48,176},{56,1... | collective-permute-start | bytes 12296 | tf_op jit(solution)/shard_map/ppermute | solution.py:28
  60.0 7.8 %collective-permute-start.21 = (f32[8,128]{1,0:T(8,128)S(1)}, f32[8,128]{1,0:T(8,128)S(1)}, u32[]{:S(2)}, u32[]{:S(2)}) collective-permute-start(f32[8,128]{1,0:T(8,128)S(1)} %shard_map.115.refs_17_), channel_id=1, source_target_pairs={{0,64},{8,72},{16,80},{24,88},{32,96},{40,104},{48,112},{56,120},{... | collective-permute-start | bytes 12296 | tf_op jit(solution)/shard_map/ppermute | solution.py:28
  63.1 11.6 %collective-permute-start.25 = (bf16[48,3072]{1,0:T(8,128)(2,1)S(1)}, bf16[48,3072]{1,0:T(8,128)(2,1)S(1)}, u32[]{:S(2)}, u32[]{:S(2)}) collective-permute-start(bf16[48,3072]{1,0:T(8,128)(2,1)S(1)} %get-tuple-element.61), channel_id=1, source_target_pairs={{0,32},{8,40},{16,48},{24,56},{32,0},{40,8},{48,16},{56,24},{64,96... | collective-permute-start | bytes 884744 | tf_op jit(solution)/shard_map/ppermute | solution.py:28
  66.5 11.7 %collective-permute-start.26 = (bf16[48,3072]{1,0:T(8,128)(2,1)S(1)}, bf16[48,3072]{1,0:T(8,128)(2,1)S(1)}, u32[]{:S(2)}, u32[]{:S(2)}) collective-permute-start(bf16[48,3072]{1,0:T(8,128)(2,1)S(1)} %get-tuple-element.62), channel_id=1, source_target_pairs={{0,48},{8,56},{16,32},{24,40},{32,16},{40,24},{48,0},{56,8},{64,11... | collective-permute-start | bytes 884744 | tf_op jit(solution)/shard_map/ppermute | solution.py:28
  67.6 11.1 %collective-permute-start.24 = (bf16[48,3072]{1,0:T(8,128)(2,1)S(1)}, bf16[48,3072]{1,0:T(8,128)(2,1)S(1)}, u32[]{:S(2)}, u32[]{:S(2)}) collective-permute-start(bf16[48,3072]{1,0:T(8,128)(2,1)S(1)} %get-tuple-element.55), channel_id=1, source_target_pairs={{0,16},{8,24},{16,0},{24,8},{32,48},{40,56},{48,32},{56,40},{64,80... | collective-permute-start | bytes 884744 | tf_op jit(solution)/shard_map/ppermute | solution.py:28
  79.1 7.5 %collective-permute-start.28 = (bf16[256,384]{1,0:T(8,128)(2,1)S(1)}, bf16[256,384]{1,0:T(8,128)(2,1)S(1)}, u32[]{:S(2)}, u32[]{:S(2)}) collective-permute-start(bf16[256,384]{1,0:T(8,128)(2,1)S(1)} %get-tuple-element.80), channel_id=1, source_target_pairs={{0,32},{8,40},{16,48},{24,56},{32,0},{40,8},{48,16},{56,24},{64,96... | collective-permute-start | bytes 589832 | tf_op jit(solution)/shard_map/ppermute | solution.py:28
  81.3 9.9 %collective-permute-start.29 = (bf16[256,384]{1,0:T(8,128)(2,1)S(1)}, bf16[256,384]{1,0:T(8,128)(2,1)S(1)}, u32[]{:S(2)}, u32[]{:S(2)}) collective-permute-start(bf16[256,384]{1,0:T(8,128)(2,1)S(1)} %slice.116), channel_id=1, source_target_pairs={{0,1},{1,0},{2,3},{3,2},{4,5},{5,4},{6,7},{7,6},{8,9},{9,8},{10,11... | collective-permute-start | bytes 589832 | tf_op jit(solution)/shard_map/ppermute | solution.py:28
  83.1 13.5 %collective-permute-start.33 = (bf16[24,3072]{1,0:T(8,128)(2,1)S(1)}, bf16[24,3072]{1,0:T(8,128)(2,1)S(1)}, u32[]{:S(2)}, u32[]{:S(2)}) collective-permute-start(bf16[24,3072]{1,0:T(8,128)(2,1)S(1)} %slice.117), channel_id=1, source_target_pairs={{0,64},{8,72},{16,80},{24,88},{32,96},{40,104},{48,112},{56,120},{... | collective-permute-start | bytes 442376 | tf_op jit(solution)/shard_map/ppermute | solution.py:28
  83.8 12.9 %collective-permute-start.31 = (bf16[768,128]{1,0:T(8,128)(2,1)S(1)}, bf16[768,128]{1,0:T(8,128)(2,1)S(1)}, u32[]{:S(2)}, u32[]{:S(2)}) collective-permute-start(bf16[768,128]{1,0:T(8,128)(2,1)S(1)} %get-tuple-element.68), channel_id=1, source_target_pairs={{0,64},{8,72},{16,80},{24,88},{32,96},{40,104},{48,112},{56,120},{... | collective-permute-start | bytes 589832 | tf_op jit(solution)/shard_map/ppermute | solution.py:28
  85.2 14.6 %collective-permute-start.34 = (bf16[256,384]{1,0:T(8,128)(2,1)S(1)}, bf16[256,384]{1,0:T(8,128)(2,1)S(1)}, u32[]{:S(2)}, u32[]{:S(2)}) collective-permute-start(bf16[256,384]{1,0:T(8,128)(2,1)S(1)} %get-tuple-element.78), channel_id=1, source_target_pairs={{0,16},{8,24},{16,0},{24,8},{32,48},{40,56},{48,32},{56,40},{64,80... | collective-permute-start | bytes 589832 | tf_op jit(solution)/shard_map/ppermute | solution.py:28
  86.7 13.1 %collective-permute-start.35 = (bf16[256,384]{1,0:T(8,128)(2,1)S(1)}, bf16[256,384]{1,0:T(8,128)(2,1)S(1)}, u32[]{:S(2)}, u32[]{:S(2)}) collective-permute-start(bf16[256,384]{1,0:T(8,128)(2,1)S(1)} %get-tuple-element.79), channel_id=1, source_target_pairs={{0,48},{8,56},{16,32},{24,40},{32,16},{40,24},{48,0},{56,8},{64,11... | collective-permute-start | bytes 589832 | tf_op jit(solution)/shard_map/ppermute | solution.py:28
  91.2 18.7 %collective-permute-start.30 = (bf16[128,384]{1,0:T(8,128)(2,1)S(1)}, bf16[128,384]{1,0:T(8,128)(2,1)S(1)}, u32[]{:S(2)}, u32[]{:S(2)}) collective-permute-start(bf16[128,384]{1,0:T(8,128)(2,1)S(1)} %slice.120), channel_id=1, source_target_pairs={{0,4},{1,5},{2,6},{3,7},{4,0},{5,1},{6,2},{7,3},{8,12},{9,13},{10,... | collective-permute-start | bytes 294920 | tf_op jit(solution)/shard_map/ppermute | solution.py:28
  96.7 10.4 %collective-permute-start.36 = (bf16[12,3072]{1,0:T(8,128)(2,1)S(1)}, bf16[12,3072]{1,0:T(8,128)(2,1)S(1)}, u32[]{:S(2)}, u32[]{:S(2)}) collective-permute-start(bf16[12,3072]{1,0:T(8,128)(2,1)S(1)} %slice.118), channel_id=1, source_target_pairs={{0,128},{8,136},{16,144},{24,152},{32,160},{40,168},{48,176},{56,1... | collective-permute-start | bytes 221192 | tf_op jit(solution)/shard_map/ppermute | solution.py:28
  98.0 11.2 %collective-permute-start.32 = (bf16[384,128]{1,0:T(8,128)(2,1)S(1)}, bf16[384,128]{1,0:T(8,128)(2,1)S(1)}, u32[]{:S(2)}, u32[]{:S(2)}) collective-permute-start(bf16[384,128]{1,0:T(8,128)(2,1)S(1)} %slice.119), channel_id=1, source_target_pairs={{0,128},{8,136},{16,144},{24,152},{32,160},{40,168},{48,176},{56,1... | collective-permute-start | bytes 294920 | tf_op jit(solution)/shard_map/ppermute | solution.py:28
  (15 other events, 114.0 us)

commit v6 on v5

--- a/solution.py
+++ b/solution.py
@@ -283,18 +283,7 @@
     stat_all = [stats] + [swap(stats, "slab", 8 * j) for j in (1, 2, 3)]
     att_other = swap(att, "slab", 1)
 
-    mix = call(
-        mix_kernel,
-        [((4 * ROWS, COLS), F32), ((4 * ROWS, COLS), BF)],
-        ranks,
-        after(att, grad),
-        w_out,
-        flops=3 * 10**8,
-        moved=4 * 10**6,
-    )
-    mix_in = swap(mix[1], "head", 2)
-    g_far = swap(jnp.concatenate([grad, after(g_near, mix[1])], axis=0), "slab", 8)
-    g_all = [grad, g_far[:COLS], g_near, g_far[COLS:]]
+    g_far = swap(jnp.concatenate([grad, after(g_near, *stat_all[1:], att_other)], axis=0), "slab", 8)
     d_other = swap(after(d_full, att), "slab", 1)
     weight = call(
         weight_kernel,
@@ -308,9 +297,21 @@
         moved=4 * 10**6,
     )
     weight_in = [swap(weight[j], "slab", 2 * j) for j in (1, 2, 3)]
+    mix = call(
+        mix_kernel,
+        [((4 * ROWS, COLS), F32), ((4 * ROWS, COLS), BF)],
+        ranks,
+        after(att, weight[1]),
+        w_out,
+        flops=3 * 10**8,
+        moved=4 * 10**6,
+    )
+    mix_in = swap(mix[1], "head", 2)
+    g_far = after(g_far, weight[1])
+    g_all = [grad, g_far[:COLS], g_near, g_far[COLS:]]
     mixed = mix[0] + mix_in.astype(F32)
     mixed_away = mixed[2 * ROWS :].astype(BF)
-    stat_all[0] = after(stat_all[0], weight[1], mixed_away)
+    stat_all[0] = after(stat_all[0], weight[1], mix[1])
 
     dq_own, dq_other, own, other = call(
         backward_kernel,
@@ -328,14 +329,14 @@
     weight_away = weight[24:].astype(BF)
 
     other = swap(other, "slab", 1)
-    pair = (after(own, weight_away) + other.astype(F32)).reshape(4, 2 * ROWS, COLS)
+    pair = (after(own, weight_away, mixed_away) + other.astype(F32)).reshape(4, 2 * ROWS, COLS)
     away = [pair[e].astype(BF) for e in (1, 2, 3)]
     arrived = [swap(away[e - 1], "slab", 2 * e) for e in (1, 2, 3)]
     dq_in = swap(after(dq_other, other), "slab", 8)
 
     mixed = after(mixed[: 2 * ROWS], arrived[1]) + swap(mixed_away, "head", 1).astype(F32)
     mixed_away = mixed[ROWS:].astype(BF)
-    weight = after(weight[:24], mixed_away) + swap(weight_away, "slab", 8).astype(F32)
+    weight = after(weight[:24], arrived[1]) + swap(weight_away, "slab", 8).astype(F32)
     weight_away = weight[12:].astype(BF)
     dq = after(dq_own, mixed_away) + dq_in.astype(F32)
     dq_away = dq[COLS:].astype(BF)

time: 113 us -> 107 us (0.947)
  waiting for transfers between devices: 28.4 us -> 23.6 us
    ppermute x37, waiting for transfers between devices: 28.4 us -> 23.6 us  [swap(): return lax.ppermute(block, axis, [(i, i ^ distance) for i in devices])]
    unnamed x17 -> x15, local copies, waits for them, and re-layouts: 2.6 us -> 2.6 us
  transfers between devices with their start and end apart: 37 -> 37, of which waited for: 11 -> 14; matrix products, arithmetic and copies ran while one was open for 3% -> 4% of each run, Pallas kernels for 13% -> 14%
where the time goes in v6:
time: 107 us; the launch traced here: 105 us
  starting transfers between devices  57.5 us (54%)
  waiting for transfers between devices  23.6 us (22%)
  Pallas kernels  16.5 us (15%)
  local copies, waits for them, and re-layouts  3.51 us (3%)
  other arithmetic  3.09 us (3%)
    ppermute x37, starting transfers between devices, swap(): return lax.ppermute(block, axis, [(i, i ^ distance) for i in devices])  57.5 us
    ppermute x37, waiting for transfers between devices, swap(): return lax.ppermute(block, axis, [(i, i ^ distance) for i in devices])  23.6 us
    pallas_call x8, Pallas kernels, call(): pl.pallas_call(kernel, out_shape=[jax.ShapeDtypeStruct(shape, dtype) for...  16.5 us
    unnamed x15, local copies, waits for them, and re-layouts  2.6 us
  transfers between devices with their start and end apart: 37, of which 14 were waited for; matrix products, arithmetic and copies ran while one was open for 4% of the time, Pallas kernels for 14%

profile of v6, /device:TPU:2, one launch (start us, length us, event | category | flops | bytes accessed | tf_op | source)
XLA Modules:
  0.0 105.2 jit_solution(10565084517334739953)
XLA Ops:
  0.6 1.8 %shard_map.110 = (bf16[144,384]{1,0:T(8,128)(2,1)}, bf16[256,384]{1,0:T(8,128)(2,1)}) custom-call(s32[2,4]{1,0:T(2,128)} %ids_hbm.1, s32[2]{0:T(128)} %counts_hbm.1, bf16[128,384]{1,0:T(8,128)(2,1)} %q_hbm.1, bf16[128,384]{1,0:T(8,128)(2,1)} %k_hbm.1, bf16[128,384]{1,0:T(8,128)(2,1)} %v_hbm.1), custom_call_target="tpu_custom_call" | custom-call | flops 1000 | bytes 1000 | tf_op jit(solution)/shard_map/pallas_call | solution.py:39
  2.4 2.0 %collective-permute-start = (bf16[144,384]{1,0:T(8,128)(2,1)}, bf16[144,384]{1,0:T(8,128)(2,1)S(1)}, u32[]{:S(2)}, u32[]{:S(2)}) collective-permute-start(bf16[144,384]{1,0:T(8,128)(2,1)} %get-tuple-element.39.refs_1_), channel_id=1, source_target_pairs={{0,64},{8,72},{16,80},{24,88},{32,96},{40,104},{48,112},{56,120},{... | collective-permute-start | bytes 331784 | tf_op jit(solution)/shard_map/ppermute | solution.py:28
  4.4 2.8 %collective-permute-start.2 = (bf16[144,384]{1,0:T(8,128)(2,1)}, bf16[144,384]{1,0:T(8,128)(2,1)S(1)}, u32[]{:S(2)}, u32[]{:S(2)}) collective-permute-start(bf16[144,384]{1,0:T(8,128)(2,1)} %get-tuple-element.39.refs_1_), channel_id=1, source_target_pairs={{0,192},{8,200},{16,208},{24,216},{32,224},{40,232},{48,240},{56,2... | collective-permute-start | bytes 331784 | tf_op jit(solution)/shard_map/ppermute | solution.py:28
  7.3 3.0 %collective-permute-start.5 = (bf16[256,384]{1,0:T(8,128)(2,1)}, bf16[256,384]{1,0:T(8,128)(2,1)S(1)}, u32[]{:S(2)}, u32[]{:S(2)}) collective-permute-start(bf16[256,384]{1,0:T(8,128)(2,1)} %get-tuple-element.40.refs_5_), channel_id=1, source_target_pairs={{0,48},{8,56},{16,32},{24,40},{32,16},{40,24},{48,0},{56,8},{64,11... | collective-permute-start | bytes 589832 | tf_op jit(solution)/shard_map/ppermute | solution.py:28
  11.4 1.4 %collective-permute-start.1 = (bf16[144,384]{1,0:T(8,128)(2,1)}, bf16[144,384]{1,0:T(8,128)(2,1)S(1)}, u32[]{:S(2)}, u32[]{:S(2)}) collective-permute-start(bf16[144,384]{1,0:T(8,128)(2,1)} %get-tuple-element.39.refs_1_), channel_id=1, source_target_pairs={{0,128},{8,136},{16,144},{24,152},{32,160},{40,168},{48,176},{56,1... | collective-permute-start | bytes 331784 | tf_op jit(solution)/shard_map/ppermute | solution.py:28
  12.9 5.2 %collective-permute-start.14 = (bf16[128,384]{1,0:T(8,128)(2,1)}, bf16[128,384]{1,0:T(8,128)(2,1)S(1)}, u32[]{:S(2)}, u32[]{:S(2)}) collective-permute-start(bf16[128,384]{1,0:T(8,128)(2,1)} %param.11), channel_id=1, source_target_pairs={{0,4},{1,5},{2,6},{3,7},{4,0},{5,1},{6,2},{7,3},{8,12},{9,13},{10,... | collective-permute-start | bytes 294920 | tf_op jit(solution)/shard_map/ppermute | solution.py:28
  18.1 1.6 %collective-permute-done.1.refs_3_ = bf16[144,384]{1,0:T(8,128)(2,1)S(1)} collective-permute-done((bf16[144,384]{1,0:T(8,128)(2,1)}, bf16[144,384]{1,0:T(8,128)(2,1)S(1)}, u32[]{:S(2)}, u32[]{:S(2)}) %collective-permute-start.1) | collective-permute-done | bytes 110624 | tf_op jit(solution)/shard_map/ppermute | solution.py:28
  20.6 1.4 %collective-permute-done.14 = bf16[128,384]{1,0:T(8,128)(2,1)S(1)} collective-permute-done((bf16[128,384]{1,0:T(8,128)(2,1)}, bf16[128,384]{1,0:T(8,128)(2,1)S(1)}, u32[]{:S(2)}, u32[]{:S(2)}) %collective-permute-start.14) | collective-permute-done | bytes 98336 | tf_op jit(solution)/shard_map/ppermute | solution.py:28
  25.5 3.9 %shard_map.111 = (bf16[400,128]{1,0:T(8,128)(2,1)S(1)}, bf16[400,128]{1,0:T(8,128)(2,1)S(1)}, bf16[400,128]{1,0:T(8,128)(2,1)S(1)}, bf16[400,128]{1,0:T(8,128)(2,1)S(1)}) custom-call(s32[4]{0:T(128)S(1)} %pad_add_fusion.refs_0_.rank_ref, bf16[144,384]{1,0:T(8,128)(2,1)S(1)} %copy-done.3, bf16[144,384]{1,0:T(8,128)(2,1)S(1)} %collective-permute-done.refs_2_, ...), custom_call_target="tpu_custom_call" | custom-call | flops 1000 | bytes 1000 | tf_op jit(solution)/shard_map/pallas_call | solution.py:39
  29.5 2.5 %collective-permute-start.16 = (bf16[512,384]{1,0:T(8,128)(2,1)S(1)}, bf16[512,384]{1,0:T(8,128)(2,1)S(1)}, u32[]{:S(2)}, u32[]{:S(2)}) collective-permute-start(bf16[512,384]{1,0:T(8,128)(2,1)S(1)} %pad_maximum_fusion.1), channel_id=1, source_target_pairs={{0,2},{1,3},{2,0},{3,1},{4,6},{5,7},{6,4},{7,5},{8,10},{9,11},{10,... | collective-permute-start | bytes 1179656 | tf_op jit(solution)/shard_map/ppermute | solution.py:28
  32.0 2.7 %collective-permute-start.10 = (bf16[400,128]{1,0:T(8,128)(2,1)S(1)}, bf16[400,128]{1,0:T(8,128)(2,1)S(1)}, u32[]{:S(2)}, u32[]{:S(2)}) collective-permute-start(bf16[400,128]{1,0:T(8,128)(2,1)S(1)} %get-tuple-element.42), channel_id=1, source_target_pairs={{0,64},{8,72},{16,80},{24,88},{32,96},{40,104},{48,112},{56,120},{... | collective-permute-start | bytes 307208 | tf_op jit(solution)/shard_map/ppermute | solution.py:28
  35.6 1.5 %collective-permute-start.12 = (bf16[400,128]{1,0:T(8,128)(2,1)S(1)}, bf16[400,128]{1,0:T(8,128)(2,1)S(1)}, u32[]{:S(2)}, u32[]{:S(2)}) collective-permute-start(bf16[400,128]{1,0:T(8,128)(2,1)S(1)} %get-tuple-element.44), channel_id=1, source_target_pairs={{0,192},{8,200},{16,208},{24,216},{32,224},{40,232},{48,240},{56,2... | collective-permute-start | bytes 307208 | tf_op jit(solution)/shard_map/ppermute | solution.py:28
  37.1 1.3 %collective-permute-done.10.refs_1_ = bf16[400,128]{1,0:T(8,128)(2,1)S(1)} collective-permute-done((bf16[400,128]{1,0:T(8,128)(2,1)S(1)}, bf16[400,128]{1,0:T(8,128)(2,1)S(1)}, u32[]{:S(2)}, u32[]{:S(2)}) %collective-permute-start.10) | collective-permute-done | bytes 102432 | tf_op jit(solution)/shard_map/ppermute | solution.py:28
  38.4 4.0 %collective-permute-done.11.refs_2_ = bf16[400,128]{1,0:T(8,128)(2,1)S(1)} collective-permute-done((bf16[400,128]{1,0:T(8,128)(2,1)S(1)}, bf16[400,128]{1,0:T(8,128)(2,1)S(1)}, u32[]{:S(2)}, u32[]{:S(2)}) %collective-permute-start.11) | collective-permute-done | bytes 102432 | tf_op jit(solution)/shard_map/ppermute | solution.py:28
  43.3 1.3 %shard_map.115.grad_ref.refs_13_ = bf16[384,128]{1,0:T(8,128)(2,1)S(1)} custom-call(s32[4]{0:T(128)S(1)} %pad_add_fusion.refs_0_.rank_ref, bf16[384,3072]{1,0:T(8,128)(2,1)S(1)} %copy-done, bf16[1024,384]{1,0:T(8,128)(2,1)S(1)} %pad_maximum_fusion.d_ref), custom_call_target="tpu_custom_call" | custom-call | flops 1000 | bytes 1000 | tf_op jit(solution)/shard_map/pallas_call | solution.py:39
  44.6 2.3 %collective-permute-start.19 = (bf16[384,128]{1,0:T(8,128)(2,1)S(1)}, bf16[384,128]{1,0:T(8,128)(2,1)S(1)}, u32[]{:S(2)}, u32[]{:S(2)}) collective-permute-start(bf16[384,128]{1,0:T(8,128)(2,1)S(1)} %shard_map.115.grad_ref.refs_13_), channel_id=1, source_target_pairs={{0,128},{8,136},{16,144},{24,152},{32,160},{40,168},{48,176},{56,1... | collective-permute-start | bytes 294920 | tf_op jit(solution)/shard_map/ppermute | solution.py:28
  47.0 1.9 %collective-permute-start.22 = (f32[8,128]{1,0:T(8,128)S(1)}, f32[8,128]{1,0:T(8,128)S(1)}, u32[]{:S(2)}, u32[]{:S(2)}) collective-permute-start(f32[8,128]{1,0:T(8,128)S(1)} %shard_map.116.refs_17_), channel_id=1, source_target_pairs={{0,192},{8,200},{16,208},{24,216},{32,224},{40,232},{48,240},{56,2... | collective-permute-start | bytes 12296 | tf_op jit(solution)/shard_map/ppermute | solution.py:28
  48.9 2.6 %collective-permute-start.20 = (f32[8,128]{1,0:T(8,128)S(1)}, f32[8,128]{1,0:T(8,128)S(1)}, u32[]{:S(2)}, u32[]{:S(2)}) collective-permute-start(f32[8,128]{1,0:T(8,128)S(1)} %shard_map.116.refs_17_), channel_id=1, source_target_pairs={{0,64},{8,72},{16,80},{24,88},{32,96},{40,104},{48,112},{56,120},{... | collective-permute-start | bytes 12296 | tf_op jit(solution)/shard_map/ppermute | solution.py:28
  53.4 1.8 %collective-permute-start.23 = (bf16[768,128]{1,0:T(8,128)(2,1)S(1)}, bf16[768,128]{1,0:T(8,128)(2,1)S(1)}, u32[]{:S(2)}, u32[]{:S(2)}) collective-permute-start(bf16[768,128]{1,0:T(8,128)(2,1)S(1)} %pad_maximum_fusion.3), channel_id=1, source_target_pairs={{0,64},{8,72},{16,80},{24,88},{32,96},{40,104},{48,112},{56,120},{... | collective-permute-start | bytes 589832 | tf_op jit(solution)/shard_map/ppermute | solution.py:28
  55.2 1.3 %shard_map.113 = (f32[48,3072]{1,0:T(8,128)S(1)}, bf16[48,3072]{1,0:T(8,128)(2,1)S(1)}, bf16[48,3072]{1,0:T(8,128)(2,1)S(1)}, bf16[48,3072]{1,0:T(8,128)(2,1)S(1)}) custom-call(s32[4]{0:T(128)S(1)} %pad_add_fusion.refs_0_.rank_ref, bf16[384,128]{1,0:T(8,128)(2,1)S(1)} %get-tuple-element.52.att_ref, bf16[384,128]{1,0:T(8,128)(2,1)S(1)} %collective-permute-done.13.att2_ref, ...), custom_call_target="tpu_custom_call" | custom-call | flops 1000 | bytes 1000 | tf_op jit(solution)/shard_map/pallas_call | solution.py:39
  56.5 3.4 %collective-permute-start.25 = (bf16[48,3072]{1,0:T(8,128)(2,1)S(1)}, bf16[48,3072]{1,0:T(8,128)(2,1)S(1)}, u32[]{:S(2)}, u32[]{:S(2)}) collective-permute-start(bf16[48,3072]{1,0:T(8,128)(2,1)S(1)} %get-tuple-element.63), channel_id=1, source_target_pairs={{0,32},{8,40},{16,48},{24,56},{32,0},{40,8},{48,16},{56,24},{64,96... | collective-permute-start | bytes 884744 | tf_op jit(solution)/shard_map/ppermute | solution.py:28
  62.2 1.4 %collective-permute-start.18 = (bf16[512,384]{1,0:T(8,128)(2,1)S(1)}, bf16[512,384]{1,0:T(8,128)(2,1)S(1)}, u32[]{:S(2)}, u32[]{:S(2)}) collective-permute-start(bf16[512,384]{1,0:T(8,128)(2,1)S(1)} %get-tuple-element.54), channel_id=1, source_target_pairs={{0,2},{1,3},{2,0},{3,1},{4,6},{5,7},{6,4},{7,5},{8,10},{9,11},{10,... | collective-permute-start | bytes 1179656 | tf_op jit(solution)/shard_map/ppermute | solution.py:28
  63.7 6.8 %shard_map.117 = (f32[768,128]{1,0:T(8,128)S(1)}, bf16[768,128]{1,0:T(8,128)(2,1)S(1)}, f32[1024,384]{1,0:T(8,128)S(1)}, bf16[1024,384]{1,0:T(8,128)(2,1)S(1)}) custom-call(s32[4]{0:T(128)S(1)} %pad_add_fusion.refs_0_.rank_ref, bf16[144,384]{1,0:T(8,128)(2,1)S(1)} %copy-done.4, bf16[144,384]{1,0:T(8,128)(2,1)S(1)} %collective-permute-done.refs_2_, ...), custom_call_target="tpu_custom_call" | custom-call | flops 1000 | bytes 1000 | tf_op jit(solution)/shard_map/pallas_call | solution.py:39
  73.2 3.7 %collective-permute-start.28 = (bf16[256,384]{1,0:T(8,128)(2,1)S(1)}, bf16[256,384]{1,0:T(8,128)(2,1)S(1)}, u32[]{:S(2)}, u32[]{:S(2)}) collective-permute-start(bf16[256,384]{1,0:T(8,128)(2,1)S(1)} %get-tuple-element.82), channel_id=1, source_target_pairs={{0,32},{8,40},{16,48},{24,56},{32,0},{40,8},{48,16},{56,24},{64,96... | collective-permute-start | bytes 589832 | tf_op jit(solution)/shard_map/ppermute | solution.py:28
  76.9 1.5 %collective-permute-start.29 = (bf16[256,384]{1,0:T(8,128)(2,1)S(1)}, bf16[256,384]{1,0:T(8,128)(2,1)S(1)}, u32[]{:S(2)}, u32[]{:S(2)}) collective-permute-start(bf16[256,384]{1,0:T(8,128)(2,1)S(1)} %slice.114), channel_id=1, source_target_pairs={{0,1},{1,0},{2,3},{3,2},{4,5},{5,4},{6,7},{7,6},{8,9},{9,8},{10,11... | collective-permute-start | bytes 589832 | tf_op jit(solution)/shard_map/ppermute | solution.py:28
  79.0 1.6 %collective-permute-start.31 = (bf16[768,128]{1,0:T(8,128)(2,1)S(1)}, bf16[768,128]{1,0:T(8,128)(2,1)S(1)}, u32[]{:S(2)}, u32[]{:S(2)}) collective-permute-start(bf16[768,128]{1,0:T(8,128)(2,1)S(1)} %get-tuple-element.70), channel_id=1, source_target_pairs={{0,64},{8,72},{16,80},{24,88},{32,96},{40,104},{48,112},{56,120},{... | collective-permute-start | bytes 589832 | tf_op jit(solution)/shard_map/ppermute | solution.py:28
  80.6 1.6 %collective-permute-done.28 = bf16[256,384]{1,0:T(8,128)(2,1)S(1)} collective-permute-done((bf16[256,384]{1,0:T(8,128)(2,1)S(1)}, bf16[256,384]{1,0:T(8,128)(2,1)S(1)}, u32[]{:S(2)}, u32[]{:S(2)}) %collective-permute-start.28) | collective-permute-done | bytes 196640 | tf_op jit(solution)/shard_map/ppermute | solution.py:28
  82.2 1.8 %collective-permute-start.35 = (bf16[256,384]{1,0:T(8,128)(2,1)S(1)}, bf16[256,384]{1,0:T(8,128)(2,1)S(1)}, u32[]{:S(2)}, u32[]{:S(2)}) collective-permute-start(bf16[256,384]{1,0:T(8,128)(2,1)S(1)} %get-tuple-element.81), channel_id=1, source_target_pairs={{0,48},{8,56},{16,32},{24,40},{32,16},{40,24},{48,0},{56,8},{64,11... | collective-permute-start | bytes 589832 | tf_op jit(solution)/shard_map/ppermute | solution.py:28
  84.0 5.5 %collective-permute-start.30 = (bf16[128,384]{1,0:T(8,128)(2,1)S(1)}, bf16[128,384]{1,0:T(8,128)(2,1)S(1)}, u32[]{:S(2)}, u32[]{:S(2)}) collective-permute-start(bf16[128,384]{1,0:T(8,128)(2,1)S(1)} %slice.118), channel_id=1, source_target_pairs={{0,4},{1,5},{2,6},{3,7},{4,0},{5,1},{6,2},{7,3},{8,12},{9,13},{10,... | collective-permute-start | bytes 294920 | tf_op jit(solution)/shard_map/ppermute | solution.py:28
  90.7 2.0 %collective-permute-start.32 = (bf16[384,128]{1,0:T(8,128)(2,1)S(1)}, bf16[384,128]{1,0:T(8,128)(2,1)S(1)}, u32[]{:S(2)}, u32[]{:S(2)}) collective-permute-start(bf16[384,128]{1,0:T(8,128)(2,1)S(1)} %slice.117), channel_id=1, source_target_pairs={{0,128},{8,136},{16,144},{24,152},{32,160},{40,168},{48,176},{56,1... | collective-permute-start | bytes 294920 | tf_op jit(solution)/shard_map/ppermute | solution.py:28
  93.5 8.2 %collective-permute-done.36 = bf16[12,3072]{1,0:T(8,128)(2,1)S(1)} collective-permute-done((bf16[12,3072]{1,0:T(8,128)(2,1)S(1)}, bf16[12,3072]{1,0:T(8,128)(2,1)S(1)}, u32[]{:S(2)}, u32[]{:S(2)}) %collective-permute-start.36) | collective-permute-done | bytes 73760 | tf_op jit(solution)/shard_map/ppermute | solution.py:28
  102.4 1.3 %collective-permute-done.32 = bf16[384,128]{1,0:T(8,128)(2,1)S(1)} collective-permute-done((bf16[384,128]{1,0:T(8,128)(2,1)S(1)}, bf16[384,128]{1,0:T(8,128)(2,1)S(1)}, u32[]{:S(2)}, u32[]{:S(2)}) %collective-permute-start.32) | collective-permute-done | bytes 98336 | tf_op jit(solution)/shard_map/ppermute | solution.py:28
  (92 shorter events, 19.1 us)
Async XLA Ops:
  2.4 8.9 %collective-permute-start = (bf16[144,384]{1,0:T(8,128)(2,1)}, bf16[144,384]{1,0:T(8,128)(2,1)S(1)}, u32[]{:S(2)}, u32[]{:S(2)}) collective-permute-start(bf16[144,384]{1,0:T(8,128)(2,1)} %get-tuple-element.39.refs_1_), channel_id=1, source_target_pairs={{0,64},{8,72},{16,80},{24,88},{32,96},{40,104},{48,112},{56,120},{... | collective-permute-start | bytes 331784 | tf_op jit(solution)/shard_map/ppermute | solution.py:28
  4.4 8.4 %collective-permute-start.2 = (bf16[144,384]{1,0:T(8,128)(2,1)}, bf16[144,384]{1,0:T(8,128)(2,1)S(1)}, u32[]{:S(2)}, u32[]{:S(2)}) collective-permute-start(bf16[144,384]{1,0:T(8,128)(2,1)} %get-tuple-element.39.refs_1_), channel_id=1, source_target_pairs={{0,192},{8,200},{16,208},{24,216},{32,224},{40,232},{48,240},{56,2... | collective-permute-start | bytes 331784 | tf_op jit(solution)/shard_map/ppermute | solution.py:28
  7.3 12.4 %collective-permute-start.5 = (bf16[256,384]{1,0:T(8,128)(2,1)}, bf16[256,384]{1,0:T(8,128)(2,1)S(1)}, u32[]{:S(2)}, u32[]{:S(2)}) collective-permute-start(bf16[256,384]{1,0:T(8,128)(2,1)} %get-tuple-element.40.refs_5_), channel_id=1, source_target_pairs={{0,48},{8,56},{16,32},{24,40},{32,16},{40,24},{48,0},{56,8},{64,11... | collective-permute-start | bytes 589832 | tf_op jit(solution)/shard_map/ppermute | solution.py:28
  10.3 9.9 %collective-permute-start.4 = (bf16[256,384]{1,0:T(8,128)(2,1)}, bf16[256,384]{1,0:T(8,128)(2,1)S(1)}, u32[]{:S(2)}, u32[]{:S(2)}) collective-permute-start(bf16[256,384]{1,0:T(8,128)(2,1)} %get-tuple-element.40.refs_5_), channel_id=1, source_target_pairs={{0,32},{8,40},{16,48},{24,56},{32,0},{40,8},{48,16},{56,24},{64,96... | collective-permute-start | bytes 589832 | tf_op jit(solution)/shard_map/ppermute | solution.py:28
  10.9 9.3 %collective-permute-start.3 = (bf16[256,384]{1,0:T(8,128)(2,1)}, bf16[256,384]{1,0:T(8,128)(2,1)S(1)}, u32[]{:S(2)}, u32[]{:S(2)}) collective-permute-start(bf16[256,384]{1,0:T(8,128)(2,1)} %get-tuple-element.40.refs_5_), channel_id=1, source_target_pairs={{0,16},{8,24},{16,0},{24,8},{32,48},{40,56},{48,32},{56,40},{64,80... | collective-permute-start | bytes 589832 | tf_op jit(solution)/shard_map/ppermute | solution.py:28
  11.4 8.3 %collective-permute-start.1 = (bf16[144,384]{1,0:T(8,128)(2,1)}, bf16[144,384]{1,0:T(8,128)(2,1)S(1)}, u32[]{:S(2)}, u32[]{:S(2)}) collective-permute-start(bf16[144,384]{1,0:T(8,128)(2,1)} %get-tuple-element.39.refs_1_), channel_id=1, source_target_pairs={{0,128},{8,136},{16,144},{24,152},{32,160},{40,168},{48,176},{56,1... | collective-permute-start | bytes 331784 | tf_op jit(solution)/shard_map/ppermute | solution.py:28
  12.9 9.2 %collective-permute-start.14 = (bf16[128,384]{1,0:T(8,128)(2,1)}, bf16[128,384]{1,0:T(8,128)(2,1)S(1)}, u32[]{:S(2)}, u32[]{:S(2)}) collective-permute-start(bf16[128,384]{1,0:T(8,128)(2,1)} %param.11), channel_id=1, source_target_pairs={{0,4},{1,5},{2,6},{3,7},{4,0},{5,1},{6,2},{7,3},{8,12},{9,13},{10,... | collective-permute-start | bytes 294920 | tf_op jit(solution)/shard_map/ppermute | solution.py:28
  23.0 6.4 %collective-permute-start.15 = (bf16[256,384]{1,0:T(8,128)(2,1)S(1)}, bf16[256,384]{1,0:T(8,128)(2,1)S(1)}, u32[]{:S(2)}, u32[]{:S(2)}) collective-permute-start(bf16[256,384]{1,0:T(8,128)(2,1)S(1)} %pad_maximum_fusion.2), channel_id=1, source_target_pairs={{0,1},{1,0},{2,3},{3,2},{4,5},{5,4},{6,7},{7,6},{8,9},{9,8},{10,11... | collective-permute-start | bytes 589832 | tf_op jit(solution)/shard_map/ppermute | solution.py:28
  29.5 13.1 %collective-permute-start.16 = (bf16[512,384]{1,0:T(8,128)(2,1)S(1)}, bf16[512,384]{1,0:T(8,128)(2,1)S(1)}, u32[]{:S(2)}, u32[]{:S(2)}) collective-permute-start(bf16[512,384]{1,0:T(8,128)(2,1)S(1)} %pad_maximum_fusion.1), channel_id=1, source_target_pairs={{0,2},{1,3},{2,0},{3,1},{4,6},{5,7},{6,4},{7,5},{8,10},{9,11},{10,... | collective-permute-start | bytes 1179656 | tf_op jit(solution)/shard_map/ppermute | solution.py:28
  32.0 6.4 %collective-permute-start.10 = (bf16[400,128]{1,0:T(8,128)(2,1)S(1)}, bf16[400,128]{1,0:T(8,128)(2,1)S(1)}, u32[]{:S(2)}, u32[]{:S(2)}) collective-permute-start(bf16[400,128]{1,0:T(8,128)(2,1)S(1)} %get-tuple-element.42), channel_id=1, source_target_pairs={{0,64},{8,72},{16,80},{24,88},{32,96},{40,104},{48,112},{56,120},{... | collective-permute-start | bytes 307208 | tf_op jit(solution)/shard_map/ppermute | solution.py:28
  34.7 7.8 %collective-permute-start.11 = (bf16[400,128]{1,0:T(8,128)(2,1)S(1)}, bf16[400,128]{1,0:T(8,128)(2,1)S(1)}, u32[]{:S(2)}, u32[]{:S(2)}) collective-permute-start(bf16[400,128]{1,0:T(8,128)(2,1)S(1)} %get-tuple-element.43), channel_id=1, source_target_pairs={{0,128},{8,136},{16,144},{24,152},{32,160},{40,168},{48,176},{56,1... | collective-permute-start | bytes 307208 | tf_op jit(solution)/shard_map/ppermute | solution.py:28
  35.6 6.8 %collective-permute-start.12 = (bf16[400,128]{1,0:T(8,128)(2,1)S(1)}, bf16[400,128]{1,0:T(8,128)(2,1)S(1)}, u32[]{:S(2)}, u32[]{:S(2)}) collective-permute-start(bf16[400,128]{1,0:T(8,128)(2,1)S(1)} %get-tuple-element.44), channel_id=1, source_target_pairs={{0,192},{8,200},{16,208},{24,216},{32,224},{40,232},{48,240},{56,2... | collective-permute-start | bytes 307208 | tf_op jit(solution)/shard_map/ppermute | solution.py:28
  42.7 12.5 %collective-permute-start.17 = (bf16[1024,384]{1,0:T(8,128)(2,1)S(1)}, bf16[1024,384]{1,0:T(8,128)(2,1)S(1)}, u32[]{:S(2)}, u32[]{:S(2)}) collective-permute-start(bf16[1024,384]{1,0:T(8,128)(2,1)S(1)} %pad_maximum_fusion.d_ref), channel_id=1, source_target_pairs={{0,8},{8,0},{16,24},{24,16},{32,40},{40,32},{48,56},{56,48},{64,72... | collective-permute-start | bytes 2359304 | tf_op jit(solution)/shard_map/ppermute | solution.py:28
  42.8 6.1 %collective-permute-start.13 = (bf16[384,128]{1,0:T(8,128)(2,1)S(1)}, bf16[384,128]{1,0:T(8,128)(2,1)S(1)}, u32[]{:S(2)}, u32[]{:S(2)}) collective-permute-start(bf16[384,128]{1,0:T(8,128)(2,1)S(1)} %get-tuple-element.52.att_ref), channel_id=1, source_target_pairs={{0,8},{8,0},{16,24},{24,16},{32,40},{40,32},{48,56},{56,48},{64,72... | collective-permute-start | bytes 294920 | tf_op jit(solution)/shard_map/ppermute | solution.py:28
  44.6 8.7 %collective-permute-start.19 = (bf16[384,128]{1,0:T(8,128)(2,1)S(1)}, bf16[384,128]{1,0:T(8,128)(2,1)S(1)}, u32[]{:S(2)}, u32[]{:S(2)}) collective-permute-start(bf16[384,128]{1,0:T(8,128)(2,1)S(1)} %shard_map.115.grad_ref.refs_13_), channel_id=1, source_target_pairs={{0,128},{8,136},{16,144},{24,152},{32,160},{40,168},{48,176},{56,1... | collective-permute-start | bytes 294920 | tf_op jit(solution)/shard_map/ppermute | solution.py:28
  47.0 5.6 %collective-permute-start.22 = (f32[8,128]{1,0:T(8,128)S(1)}, f32[8,128]{1,0:T(8,128)S(1)}, u32[]{:S(2)}, u32[]{:S(2)}) collective-permute-start(f32[8,128]{1,0:T(8,128)S(1)} %shard_map.116.refs_17_), channel_id=1, source_target_pairs={{0,192},{8,200},{16,208},{24,216},{32,224},{40,232},{48,240},{56,2... | collective-permute-start | bytes 12296 | tf_op jit(solution)/shard_map/ppermute | solution.py:28
  48.9 4.5 %collective-permute-start.21 = (f32[8,128]{1,0:T(8,128)S(1)}, f32[8,128]{1,0:T(8,128)S(1)}, u32[]{:S(2)}, u32[]{:S(2)}) collective-permute-start(f32[8,128]{1,0:T(8,128)S(1)} %shard_map.116.refs_17_), channel_id=1, source_target_pairs={{0,128},{8,136},{16,144},{24,152},{32,160},{40,168},{48,176},{56,1... | collective-permute-start | bytes 12296 | tf_op jit(solution)/shard_map/ppermute | solution.py:28
  48.9 4.5 %collective-permute-start.20 = (f32[8,128]{1,0:T(8,128)S(1)}, f32[8,128]{1,0:T(8,128)S(1)}, u32[]{:S(2)}, u32[]{:S(2)}) collective-permute-start(f32[8,128]{1,0:T(8,128)S(1)} %shard_map.116.refs_17_), channel_id=1, source_target_pairs={{0,64},{8,72},{16,80},{24,88},{32,96},{40,104},{48,112},{56,120},{... | collective-permute-start | bytes 12296 | tf_op jit(solution)/shard_map/ppermute | solution.py:28
  53.4 10.2 %collective-permute-start.23 = (bf16[768,128]{1,0:T(8,128)(2,1)S(1)}, bf16[768,128]{1,0:T(8,128)(2,1)S(1)}, u32[]{:S(2)}, u32[]{:S(2)}) collective-permute-start(bf16[768,128]{1,0:T(8,128)(2,1)S(1)} %pad_maximum_fusion.3), channel_id=1, source_target_pairs={{0,64},{8,72},{16,80},{24,88},{32,96},{40,104},{48,112},{56,120},{... | collective-permute-start | bytes 589832 | tf_op jit(solution)/shard_map/ppermute | solution.py:28
  56.5 14.1 %collective-permute-start.25 = (bf16[48,3072]{1,0:T(8,128)(2,1)S(1)}, bf16[48,3072]{1,0:T(8,128)(2,1)S(1)}, u32[]{:S(2)}, u32[]{:S(2)}) collective-permute-start(bf16[48,3072]{1,0:T(8,128)(2,1)S(1)} %get-tuple-element.63), channel_id=1, source_target_pairs={{0,32},{8,40},{16,48},{24,56},{32,0},{40,8},{48,16},{56,24},{64,96... | collective-permute-start | bytes 884744 | tf_op jit(solution)/shard_map/ppermute | solution.py:28
  59.9 11.3 %collective-permute-start.26 = (bf16[48,3072]{1,0:T(8,128)(2,1)S(1)}, bf16[48,3072]{1,0:T(8,128)(2,1)S(1)}, u32[]{:S(2)}, u32[]{:S(2)}) collective-permute-start(bf16[48,3072]{1,0:T(8,128)(2,1)S(1)} %get-tuple-element.64), channel_id=1, source_target_pairs={{0,48},{8,56},{16,32},{24,40},{32,16},{40,24},{48,0},{56,8},{64,11... | collective-permute-start | bytes 884744 | tf_op jit(solution)/shard_map/ppermute | solution.py:28
  61.0 10.7 %collective-permute-start.24 = (bf16[48,3072]{1,0:T(8,128)(2,1)S(1)}, bf16[48,3072]{1,0:T(8,128)(2,1)S(1)}, u32[]{:S(2)}, u32[]{:S(2)}) collective-permute-start(bf16[48,3072]{1,0:T(8,128)(2,1)S(1)} %get-tuple-element.51), channel_id=1, source_target_pairs={{0,16},{8,24},{16,0},{24,8},{32,48},{40,56},{48,32},{56,40},{64,80... | collective-permute-start | bytes 884744 | tf_op jit(solution)/shard_map/ppermute | solution.py:28
  62.2 10.1 %collective-permute-start.18 = (bf16[512,384]{1,0:T(8,128)(2,1)S(1)}, bf16[512,384]{1,0:T(8,128)(2,1)S(1)}, u32[]{:S(2)}, u32[]{:S(2)}) collective-permute-start(bf16[512,384]{1,0:T(8,128)(2,1)S(1)} %get-tuple-element.54), channel_id=1, source_target_pairs={{0,2},{1,3},{2,0},{3,1},{4,6},{5,7},{6,4},{7,5},{8,10},{9,11},{10,... | collective-permute-start | bytes 1179656 | tf_op jit(solution)/shard_map/ppermute | solution.py:28
  73.2 9.0 %collective-permute-start.28 = (bf16[256,384]{1,0:T(8,128)(2,1)S(1)}, bf16[256,384]{1,0:T(8,128)(2,1)S(1)}, u32[]{:S(2)}, u32[]{:S(2)}) collective-permute-start(bf16[256,384]{1,0:T(8,128)(2,1)S(1)} %get-tuple-element.82), channel_id=1, source_target_pairs={{0,32},{8,40},{16,48},{24,56},{32,0},{40,8},{48,16},{56,24},{64,96... | collective-permute-start | bytes 589832 | tf_op jit(solution)/shard_map/ppermute | solution.py:28
  76.9 7.0 %collective-permute-start.29 = (bf16[256,384]{1,0:T(8,128)(2,1)S(1)}, bf16[256,384]{1,0:T(8,128)(2,1)S(1)}, u32[]{:S(2)}, u32[]{:S(2)}) collective-permute-start(bf16[256,384]{1,0:T(8,128)(2,1)S(1)} %slice.114), channel_id=1, source_target_pairs={{0,1},{1,0},{2,3},{3,2},{4,5},{5,4},{6,7},{7,6},{8,9},{9,8},{10,11... | collective-permute-start | bytes 589832 | tf_op jit(solution)/shard_map/ppermute | solution.py:28
  78.4 11.2 %collective-permute-start.33 = (bf16[24,3072]{1,0:T(8,128)(2,1)S(1)}, bf16[24,3072]{1,0:T(8,128)(2,1)S(1)}, u32[]{:S(2)}, u32[]{:S(2)}) collective-permute-start(bf16[24,3072]{1,0:T(8,128)(2,1)S(1)} %slice.115), channel_id=1, source_target_pairs={{0,64},{8,72},{16,80},{24,88},{32,96},{40,104},{48,112},{56,120},{... | collective-permute-start | bytes 442376 | tf_op jit(solution)/shard_map/ppermute | solution.py:28
  79.0 10.6 %collective-permute-start.31 = (bf16[768,128]{1,0:T(8,128)(2,1)S(1)}, bf16[768,128]{1,0:T(8,128)(2,1)S(1)}, u32[]{:S(2)}, u32[]{:S(2)}) collective-permute-start(bf16[768,128]{1,0:T(8,128)(2,1)S(1)} %get-tuple-element.70), channel_id=1, source_target_pairs={{0,64},{8,72},{16,80},{24,88},{32,96},{40,104},{48,112},{56,120},{... | collective-permute-start | bytes 589832 | tf_op jit(solution)/shard_map/ppermute | solution.py:28
  80.5 12.2 %collective-permute-start.34 = (bf16[256,384]{1,0:T(8,128)(2,1)S(1)}, bf16[256,384]{1,0:T(8,128)(2,1)S(1)}, u32[]{:S(2)}, u32[]{:S(2)}) collective-permute-start(bf16[256,384]{1,0:T(8,128)(2,1)S(1)} %get-tuple-element.80), channel_id=1, source_target_pairs={{0,16},{8,24},{16,0},{24,8},{32,48},{40,56},{48,32},{56,40},{64,80... | collective-permute-start | bytes 589832 | tf_op jit(solution)/shard_map/ppermute | solution.py:28
  82.2 10.6 %collective-permute-start.35 = (bf16[256,384]{1,0:T(8,128)(2,1)S(1)}, bf16[256,384]{1,0:T(8,128)(2,1)S(1)}, u32[]{:S(2)}, u32[]{:S(2)}) collective-permute-start(bf16[256,384]{1,0:T(8,128)(2,1)S(1)} %get-tuple-element.81), channel_id=1, source_target_pairs={{0,48},{8,56},{16,32},{24,40},{32,16},{40,24},{48,0},{56,8},{64,11... | collective-permute-start | bytes 589832 | tf_op jit(solution)/shard_map/ppermute | solution.py:28
  84.0 20.5 %collective-permute-start.30 = (bf16[128,384]{1,0:T(8,128)(2,1)S(1)}, bf16[128,384]{1,0:T(8,128)(2,1)S(1)}, u32[]{:S(2)}, u32[]{:S(2)}) collective-permute-start(bf16[128,384]{1,0:T(8,128)(2,1)S(1)} %slice.118), channel_id=1, source_target_pairs={{0,4},{1,5},{2,6},{3,7},{4,0},{5,1},{6,2},{7,3},{8,12},{9,13},{10,... | collective-permute-start | bytes 294920 | tf_op jit(solution)/shard_map/ppermute | solution.py:28
  89.7 12.0 %collective-permute-start.36 = (bf16[12,3072]{1,0:T(8,128)(2,1)S(1)}, bf16[12,3072]{1,0:T(8,128)(2,1)S(1)}, u32[]{:S(2)}, u32[]{:S(2)}) collective-permute-start(bf16[12,3072]{1,0:T(8,128)(2,1)S(1)} %slice.116), channel_id=1, source_target_pairs={{0,128},{8,136},{16,144},{24,152},{32,160},{40,168},{48,176},{56,1... | collective-permute-start | bytes 221192 | tf_op jit(solution)/shard_map/ppermute | solution.py:28
  90.7 13.0 %collective-permute-start.32 = (bf16[384,128]{1,0:T(8,128)(2,1)S(1)}, bf16[384,128]{1,0:T(8,128)(2,1)S(1)}, u32[]{:S(2)}, u32[]{:S(2)}) collective-permute-start(bf16[384,128]{1,0:T(8,128)(2,1)S(1)} %slice.117), channel_id=1, source_target_pairs={{0,128},{8,136},{16,144},{24,152},{32,160},{40,168},{48,176},{56,1... | collective-permute-start | bytes 294920 | tf_op jit(solution)/shard_map/ppermute | solution.py:28
  (13 other events, 94.3 us)

commit v7 on v5

--- a/solution.py
+++ b/solution.py
@@ -283,18 +283,18 @@
     stat_all = [stats] + [swap(stats, "slab", 8 * j) for j in (1, 2, 3)]
     att_other = swap(att, "slab", 1)
 
+    g_pair = jnp.concatenate([grad, after(g_near, *stat_all[1:], att_other)], axis=0)
+    g_far = swap(g_pair, "slab", 8)
     mix = call(
         mix_kernel,
         [((4 * ROWS, COLS), F32), ((4 * ROWS, COLS), BF)],
         ranks,
-        after(att, grad),
+        after(att, g_pair),
         w_out,
         flops=3 * 10**8,
         moved=4 * 10**6,
     )
     mix_in = swap(mix[1], "head", 2)
-    g_far = swap(jnp.concatenate([grad, after(g_near, mix[1])], axis=0), "slab", 8)
-    g_all = [grad, g_far[:COLS], g_near, g_far[COLS:]]
     d_other = swap(after(d_full, att), "slab", 1)
     weight = call(
         weight_kernel,
@@ -308,8 +308,11 @@
         moved=4 * 10**6,
     )
     weight_in = [swap(weight[j], "slab", 2 * j) for j in (1, 2, 3)]
+    g_far = after(g_far, weight[1])
+    g_all = [grad, g_far[:COLS], g_near, g_far[COLS:]]
     mixed = mix[0] + mix_in.astype(F32)
     mixed_away = mixed[2 * ROWS :].astype(BF)
+    mix_near = swap(mixed_away, "head", 1)
     stat_all[0] = after(stat_all[0], weight[1], mixed_away)
 
     dq_own, dq_other, own, other = call(
@@ -328,16 +331,16 @@
     weight_away = weight[24:].astype(BF)
 
     other = swap(other, "slab", 1)
-    pair = (after(own, weight_away) + other.astype(F32)).reshape(4, 2 * ROWS, COLS)
+    pair = (after(own, weight_away, mix_near) + other.astype(F32)).reshape(4, 2 * ROWS, COLS)
     away = [pair[e].astype(BF) for e in (1, 2, 3)]
     arrived = [swap(away[e - 1], "slab", 2 * e) for e in (1, 2, 3)]
     dq_in = swap(after(dq_other, other), "slab", 8)
 
-    mixed = after(mixed[: 2 * ROWS], arrived[1]) + swap(mixed_away, "head", 1).astype(F32)
+    mixed = after(mixed[: 2 * ROWS], arrived[1]) + mix_near.astype(F32)
     mixed_away = mixed[ROWS:].astype(BF)
-    weight = after(weight[:24], mixed_away) + swap(weight_away, "slab", 8).astype(F32)
+    weight = after(weight[:24], arrived[1]) + swap(weight_away, "slab", 8).astype(F32)
     weight_away = weight[12:].astype(BF)
-    dq = after(dq_own, mixed_away) + dq_in.astype(F32)
+    dq = after(dq_own, arrived[1]) + dq_in.astype(F32)
     dq_away = dq[COLS:].astype(BF)
 
     total = after(pair[0], weight_away, mixed_away, dq_away) + sum((a.astype(F32) for a in arrived), 0.0)

time: 113 us -> 112 us (level)
  starting transfers between devices: 58 us -> 56.5 us
    ppermute x37, starting transfers between devices: 58 us -> 56.5 us  [swap(): return lax.ppermute(block, axis, [(i, i ^ distance) for i in devices])]
    unnamed x17 -> x15, local copies, waits for them, and re-layouts: 2.6 us -> 2.6 us
  transfers between devices with their start and end apart: 37 -> 37, of which waited for: 11 -> 14; matrix products, arithmetic and copies ran while one was open for 3% -> 3% of each run, Pallas kernels for 13% -> 13%
where the time goes in v7:
time: 112 us; the launch traced here: 110 us
  starting transfers between devices  56.5 us (50%)
  waiting for transfers between devices  29.3 us (26%)
  Pallas kernels  16.5 us (15%)
  local copies, waits for them, and re-layouts  3.51 us (3%)
  other arithmetic  3.12 us (3%)
    ppermute x37, starting transfers between devices, swap(): return lax.ppermute(block, axis, [(i, i ^ distance) for i in devices])  56.5 us
    ppermute x37, waiting for transfers between devices, swap(): return lax.ppermute(block, axis, [(i, i ^ distance) for i in devices])  29.3 us
    pallas_call x8, Pallas kernels, call(): pl.pallas_call(kernel, out_shape=[jax.ShapeDtypeStruct(shape, dtype) for...  16.5 us
    unnamed x15, local copies, waits for them, and re-layouts  2.6 us
  transfers between devices with their start and end apart: 37, of which 14 were waited for; matrix products, arithmetic and copies ran while one was open for 3% of the time, Pallas kernels for 13%

profile of v7, /device:TPU:2, one launch (start us, length us, event | category | flops | bytes accessed | tf_op | source)
XLA Modules:
  0.0 109.9 jit_solution(12694966451375979555)
XLA Ops:
  0.6 1.8 %shard_map.110 = (bf16[144,384]{1,0:T(8,128)(2,1)}, bf16[256,384]{1,0:T(8,128)(2,1)}) custom-call(s32[2,4]{1,0:T(2,128)} %ids_hbm.1, s32[2]{0:T(128)} %counts_hbm.1, bf16[128,384]{1,0:T(8,128)(2,1)} %q_hbm.1, bf16[128,384]{1,0:T(8,128)(2,1)} %k_hbm.1, bf16[128,384]{1,0:T(8,128)(2,1)} %v_hbm.1), custom_call_target="tpu_custom_call" | custom-call | flops 1000 | bytes 1000 | tf_op jit(solution)/shard_map/pallas_call | solution.py:39
  2.4 2.0 %collective-permute-start = (bf16[144,384]{1,0:T(8,128)(2,1)}, bf16[144,384]{1,0:T(8,128)(2,1)S(1)}, u32[]{:S(2)}, u32[]{:S(2)}) collective-permute-start(bf16[144,384]{1,0:T(8,128)(2,1)} %get-tuple-element.39.refs_1_), channel_id=1, source_target_pairs={{0,64},{8,72},{16,80},{24,88},{32,96},{40,104},{48,112},{56,120},{... | collective-permute-start | bytes 331784 | tf_op jit(solution)/shard_map/ppermute | solution.py:28
  4.4 2.8 %collective-permute-start.2 = (bf16[144,384]{1,0:T(8,128)(2,1)}, bf16[144,384]{1,0:T(8,128)(2,1)S(1)}, u32[]{:S(2)}, u32[]{:S(2)}) collective-permute-start(bf16[144,384]{1,0:T(8,128)(2,1)} %get-tuple-element.39.refs_1_), channel_id=1, source_target_pairs={{0,192},{8,200},{16,208},{24,216},{32,224},{40,232},{48,240},{56,2... | collective-permute-start | bytes 331784 | tf_op jit(solution)/shard_map/ppermute | solution.py:28
  7.3 3.0 %collective-permute-start.5 = (bf16[256,384]{1,0:T(8,128)(2,1)}, bf16[256,384]{1,0:T(8,128)(2,1)S(1)}, u32[]{:S(2)}, u32[]{:S(2)}) collective-permute-start(bf16[256,384]{1,0:T(8,128)(2,1)} %get-tuple-element.40.refs_5_), channel_id=1, source_target_pairs={{0,48},{8,56},{16,32},{24,40},{32,16},{40,24},{48,0},{56,8},{64,11... | collective-permute-start | bytes 589832 | tf_op jit(solution)/shard_map/ppermute | solution.py:28
  11.4 1.4 %collective-permute-start.1 = (bf16[144,384]{1,0:T(8,128)(2,1)}, bf16[144,384]{1,0:T(8,128)(2,1)S(1)}, u32[]{:S(2)}, u32[]{:S(2)}) collective-permute-start(bf16[144,384]{1,0:T(8,128)(2,1)} %get-tuple-element.39.refs_1_), channel_id=1, source_target_pairs={{0,128},{8,136},{16,144},{24,152},{32,160},{40,168},{48,176},{56,1... | collective-permute-start | bytes 331784 | tf_op jit(solution)/shard_map/ppermute | solution.py:28
  12.9 5.2 %collective-permute-start.13 = (bf16[128,384]{1,0:T(8,128)(2,1)}, bf16[128,384]{1,0:T(8,128)(2,1)S(1)}, u32[]{:S(2)}, u32[]{:S(2)}) collective-permute-start(bf16[128,384]{1,0:T(8,128)(2,1)} %param.11), channel_id=1, source_target_pairs={{0,4},{1,5},{2,6},{3,7},{4,0},{5,1},{6,2},{7,3},{8,12},{9,13},{10,... | collective-permute-start | bytes 294920 | tf_op jit(solution)/shard_map/ppermute | solution.py:28
  18.1 1.6 %collective-permute-done.1.refs_3_ = bf16[144,384]{1,0:T(8,128)(2,1)S(1)} collective-permute-done((bf16[144,384]{1,0:T(8,128)(2,1)}, bf16[144,384]{1,0:T(8,128)(2,1)S(1)}, u32[]{:S(2)}, u32[]{:S(2)}) %collective-permute-start.1) | collective-permute-done | bytes 110624 | tf_op jit(solution)/shard_map/ppermute | solution.py:28
  20.6 1.4 %collective-permute-done.13 = bf16[128,384]{1,0:T(8,128)(2,1)S(1)} collective-permute-done((bf16[128,384]{1,0:T(8,128)(2,1)}, bf16[128,384]{1,0:T(8,128)(2,1)S(1)}, u32[]{:S(2)}, u32[]{:S(2)}) %collective-permute-start.13) | collective-permute-done | bytes 98336 | tf_op jit(solution)/shard_map/ppermute | solution.py:28
  25.5 3.9 %shard_map.111 = (bf16[400,128]{1,0:T(8,128)(2,1)S(1)}, bf16[400,128]{1,0:T(8,128)(2,1)S(1)}, bf16[400,128]{1,0:T(8,128)(2,1)S(1)}, bf16[400,128]{1,0:T(8,128)(2,1)S(1)}) custom-call(s32[4]{0:T(128)S(1)} %pad_add_fusion.refs_0_.rank_ref, bf16[144,384]{1,0:T(8,128)(2,1)S(1)} %copy-done.3, bf16[144,384]{1,0:T(8,128)(2,1)S(1)} %collective-permute-done.refs_2_, ...), custom_call_target="tpu_custom_call" | custom-call | flops 1000 | bytes 1000 | tf_op jit(solution)/shard_map/pallas_call | solution.py:39
  29.5 2.5 %collective-permute-start.15 = (bf16[512,384]{1,0:T(8,128)(2,1)S(1)}, bf16[512,384]{1,0:T(8,128)(2,1)S(1)}, u32[]{:S(2)}, u32[]{:S(2)}) collective-permute-start(bf16[512,384]{1,0:T(8,128)(2,1)S(1)} %pad_maximum_fusion.1), channel_id=1, source_target_pairs={{0,2},{1,3},{2,0},{3,1},{4,6},{5,7},{6,4},{7,5},{8,10},{9,11},{10,... | collective-permute-start | bytes 1179656 | tf_op jit(solution)/shard_map/ppermute | solution.py:28
  32.0 2.7 %collective-permute-start.10 = (bf16[400,128]{1,0:T(8,128)(2,1)S(1)}, bf16[400,128]{1,0:T(8,128)(2,1)S(1)}, u32[]{:S(2)}, u32[]{:S(2)}) collective-permute-start(bf16[400,128]{1,0:T(8,128)(2,1)S(1)} %get-tuple-element.42), channel_id=1, source_target_pairs={{0,64},{8,72},{16,80},{24,88},{32,96},{40,104},{48,112},{56,120},{... | collective-permute-start | bytes 307208 | tf_op jit(solution)/shard_map/ppermute | solution.py:28
  35.6 1.5 %collective-permute-start.12 = (bf16[400,128]{1,0:T(8,128)(2,1)S(1)}, bf16[400,128]{1,0:T(8,128)(2,1)S(1)}, u32[]{:S(2)}, u32[]{:S(2)}) collective-permute-start(bf16[400,128]{1,0:T(8,128)(2,1)S(1)} %get-tuple-element.44), channel_id=1, source_target_pairs={{0,192},{8,200},{16,208},{24,216},{32,224},{40,232},{48,240},{56,2... | collective-permute-start | bytes 307208 | tf_op jit(solution)/shard_map/ppermute | solution.py:28
  37.1 1.3 %collective-permute-done.10.refs_1_ = bf16[400,128]{1,0:T(8,128)(2,1)S(1)} collective-permute-done((bf16[400,128]{1,0:T(8,128)(2,1)S(1)}, bf16[400,128]{1,0:T(8,128)(2,1)S(1)}, u32[]{:S(2)}, u32[]{:S(2)}) %collective-permute-start.10) | collective-permute-done | bytes 102432 | tf_op jit(solution)/shard_map/ppermute | solution.py:28
  38.4 4.0 %collective-permute-done.11.refs_2_ = bf16[400,128]{1,0:T(8,128)(2,1)S(1)} collective-permute-done((bf16[400,128]{1,0:T(8,128)(2,1)S(1)}, bf16[400,128]{1,0:T(8,128)(2,1)S(1)}, u32[]{:S(2)}, u32[]{:S(2)}) %collective-permute-start.11) | collective-permute-done | bytes 102432 | tf_op jit(solution)/shard_map/ppermute | solution.py:28
  44.6 2.3 %collective-permute-start.16 = (bf16[384,128]{1,0:T(8,128)(2,1)S(1)}, bf16[384,128]{1,0:T(8,128)(2,1)S(1)}, u32[]{:S(2)}, u32[]{:S(2)}) collective-permute-start(bf16[384,128]{1,0:T(8,128)(2,1)S(1)} %shard_map.113.grad_ref.refs_13_), channel_id=1, source_target_pairs={{0,128},{8,136},{16,144},{24,152},{32,160},{40,168},{48,176},{56,1... | collective-permute-start | bytes 294920 | tf_op jit(solution)/shard_map/ppermute | solution.py:28
  47.0 1.9 %collective-permute-start.19 = (f32[8,128]{1,0:T(8,128)S(1)}, f32[8,128]{1,0:T(8,128)S(1)}, u32[]{:S(2)}, u32[]{:S(2)}) collective-permute-start(f32[8,128]{1,0:T(8,128)S(1)} %shard_map.114.refs_17_), channel_id=1, source_target_pairs={{0,192},{8,200},{16,208},{24,216},{32,224},{40,232},{48,240},{56,2... | collective-permute-start | bytes 12296 | tf_op jit(solution)/shard_map/ppermute | solution.py:28
  48.9 2.6 %collective-permute-start.17 = (f32[8,128]{1,0:T(8,128)S(1)}, f32[8,128]{1,0:T(8,128)S(1)}, u32[]{:S(2)}, u32[]{:S(2)}) collective-permute-start(f32[8,128]{1,0:T(8,128)S(1)} %shard_map.114.refs_17_), channel_id=1, source_target_pairs={{0,64},{8,72},{16,80},{24,88},{32,96},{40,104},{48,112},{56,120},{... | collective-permute-start | bytes 12296 | tf_op jit(solution)/shard_map/ppermute | solution.py:28
  55.9 1.7 %collective-permute-start.22 = (bf16[768,128]{1,0:T(8,128)(2,1)S(1)}, bf16[768,128]{1,0:T(8,128)(2,1)S(1)}, u32[]{:S(2)}, u32[]{:S(2)}) collective-permute-start(bf16[768,128]{1,0:T(8,128)(2,1)S(1)} %pad_maximum_fusion.3), channel_id=1, source_target_pairs={{0,64},{8,72},{16,80},{24,88},{32,96},{40,104},{48,112},{56,120},{... | collective-permute-start | bytes 589832 | tf_op jit(solution)/shard_map/ppermute | solution.py:28
  58.9 3.4 %collective-permute-start.25 = (bf16[48,3072]{1,0:T(8,128)(2,1)S(1)}, bf16[48,3072]{1,0:T(8,128)(2,1)S(1)}, u32[]{:S(2)}, u32[]{:S(2)}) collective-permute-start(bf16[48,3072]{1,0:T(8,128)(2,1)S(1)} %get-tuple-element.63), channel_id=1, source_target_pairs={{0,32},{8,40},{16,48},{24,56},{32,0},{40,8},{48,16},{56,24},{64,96... | collective-permute-start | bytes 884744 | tf_op jit(solution)/shard_map/ppermute | solution.py:28
  63.3 2.7 %collective-permute-done.21 = bf16[512,384]{1,0:T(8,128)(2,1)S(1)} collective-permute-done((bf16[512,384]{1,0:T(8,128)(2,1)S(1)}, bf16[512,384]{1,0:T(8,128)(2,1)S(1)}, u32[]{:S(2)}, u32[]{:S(2)}) %collective-permute-start.21) | collective-permute-done | bytes 393248 | tf_op jit(solution)/shard_map/ppermute | solution.py:28
  66.2 6.8 %shard_map.117 = (f32[768,128]{1,0:T(8,128)S(1)}, bf16[768,128]{1,0:T(8,128)(2,1)S(1)}, f32[1024,384]{1,0:T(8,128)S(1)}, bf16[1024,384]{1,0:T(8,128)(2,1)S(1)}) custom-call(s32[4]{0:T(128)S(1)} %pad_add_fusion.refs_0_.rank_ref, bf16[144,384]{1,0:T(8,128)(2,1)S(1)} %copy-done.4, bf16[144,384]{1,0:T(8,128)(2,1)S(1)} %collective-permute-done.refs_2_, ...), custom_call_target="tpu_custom_call" | custom-call | flops 1000 | bytes 1000 | tf_op jit(solution)/shard_map/pallas_call | solution.py:39
  73.1 1.9 %collective-permute-start.27 = (bf16[256,384]{1,0:T(8,128)(2,1)S(1)}, bf16[256,384]{1,0:T(8,128)(2,1)S(1)}, u32[]{:S(2)}, u32[]{:S(2)}) collective-permute-start(bf16[256,384]{1,0:T(8,128)(2,1)S(1)} %slice.114), channel_id=1, source_target_pairs={{0,1},{1,0},{2,3},{3,2},{4,5},{5,4},{6,7},{7,6},{8,9},{9,8},{10,11... | collective-permute-start | bytes 589832 | tf_op jit(solution)/shard_map/ppermute | solution.py:28
  75.2 5.3 %collective-permute-done.27 = bf16[256,384]{1,0:T(8,128)(2,1)S(1)} collective-permute-done((bf16[256,384]{1,0:T(8,128)(2,1)S(1)}, bf16[256,384]{1,0:T(8,128)(2,1)S(1)}, u32[]{:S(2)}, u32[]{:S(2)}) %collective-permute-start.27) | collective-permute-done | bytes 196640 | tf_op jit(solution)/shard_map/ppermute | solution.py:28
  80.8 3.4 %collective-permute-start.29 = (bf16[256,384]{1,0:T(8,128)(2,1)S(1)}, bf16[256,384]{1,0:T(8,128)(2,1)S(1)}, u32[]{:S(2)}, u32[]{:S(2)}) collective-permute-start(bf16[256,384]{1,0:T(8,128)(2,1)S(1)} %get-tuple-element.82), channel_id=1, source_target_pairs={{0,32},{8,40},{16,48},{24,56},{32,0},{40,8},{48,16},{56,24},{64,96... | collective-permute-start | bytes 589832 | tf_op jit(solution)/shard_map/ppermute | solution.py:28
  87.5 2.1 %collective-permute-done.29 = bf16[256,384]{1,0:T(8,128)(2,1)S(1)} collective-permute-done((bf16[256,384]{1,0:T(8,128)(2,1)S(1)}, bf16[256,384]{1,0:T(8,128)(2,1)S(1)}, u32[]{:S(2)}, u32[]{:S(2)}) %collective-permute-start.29) | collective-permute-done | bytes 196640 | tf_op jit(solution)/shard_map/ppermute | solution.py:28
  89.6 1.4 %collective-permute-done.33 = bf16[24,3072]{1,0:T(8,128)(2,1)S(1)} collective-permute-done((bf16[24,3072]{1,0:T(8,128)(2,1)S(1)}, bf16[24,3072]{1,0:T(8,128)(2,1)S(1)}, u32[]{:S(2)}, u32[]{:S(2)}) %collective-permute-start.33) | collective-permute-done | bytes 147488 | tf_op jit(solution)/shard_map/ppermute | solution.py:28
  91.1 2.5 %collective-permute-done.31 = bf16[768,128]{1,0:T(8,128)(2,1)S(1)} collective-permute-done((bf16[768,128]{1,0:T(8,128)(2,1)S(1)}, bf16[768,128]{1,0:T(8,128)(2,1)S(1)}, u32[]{:S(2)}, u32[]{:S(2)}) %collective-permute-start.31) | collective-permute-done | bytes 196640 | tf_op jit(solution)/shard_map/ppermute | solution.py:28
  93.7 1.5 %collective-permute-start.36 = (bf16[12,3072]{1,0:T(8,128)(2,1)S(1)}, bf16[12,3072]{1,0:T(8,128)(2,1)S(1)}, u32[]{:S(2)}, u32[]{:S(2)}) collective-permute-start(bf16[12,3072]{1,0:T(8,128)(2,1)S(1)} %slice.116), channel_id=1, source_target_pairs={{0,128},{8,136},{16,144},{24,152},{32,160},{40,168},{48,176},{56,1... | collective-permute-start | bytes 221192 | tf_op jit(solution)/shard_map/ppermute | solution.py:28
  95.2 1.5 %collective-permute-start.32 = (bf16[384,128]{1,0:T(8,128)(2,1)S(1)}, bf16[384,128]{1,0:T(8,128)(2,1)S(1)}, u32[]{:S(2)}, u32[]{:S(2)}) collective-permute-start(bf16[384,128]{1,0:T(8,128)(2,1)S(1)} %slice.117), channel_id=1, source_target_pairs={{0,128},{8,136},{16,144},{24,152},{32,160},{40,168},{48,176},{56,1... | collective-permute-start | bytes 294920 | tf_op jit(solution)/shard_map/ppermute | solution.py:28
  96.7 5.5 %collective-permute-start.30 = (bf16[128,384]{1,0:T(8,128)(2,1)S(1)}, bf16[128,384]{1,0:T(8,128)(2,1)S(1)}, u32[]{:S(2)}, u32[]{:S(2)}) collective-permute-start(bf16[128,384]{1,0:T(8,128)(2,1)S(1)} %slice.118), channel_id=1, source_target_pairs={{0,4},{1,5},{2,6},{3,7},{4,0},{5,1},{6,2},{7,3},{8,12},{9,13},{10,... | collective-permute-start | bytes 294920 | tf_op jit(solution)/shard_map/ppermute | solution.py:28
  103.0 2.2 %collective-permute-done.36 = bf16[12,3072]{1,0:T(8,128)(2,1)S(1)} collective-permute-done((bf16[12,3072]{1,0:T(8,128)(2,1)S(1)}, bf16[12,3072]{1,0:T(8,128)(2,1)S(1)}, u32[]{:S(2)}, u32[]{:S(2)}) %collective-permute-start.36) | collective-permute-done | bytes 73760 | tf_op jit(solution)/shard_map/ppermute | solution.py:28
  105.9 2.6 %collective-permute-done.32 = bf16[384,128]{1,0:T(8,128)(2,1)S(1)} collective-permute-done((bf16[384,128]{1,0:T(8,128)(2,1)S(1)}, bf16[384,128]{1,0:T(8,128)(2,1)S(1)}, u32[]{:S(2)}, u32[]{:S(2)}) %collective-permute-start.32) | collective-permute-done | bytes 98336 | tf_op jit(solution)/shard_map/ppermute | solution.py:28
  (92 shorter events, 22.6 us)
Async XLA Ops:
  2.4 8.9 %collective-permute-start = (bf16[144,384]{1,0:T(8,128)(2,1)}, bf16[144,384]{1,0:T(8,128)(2,1)S(1)}, u32[]{:S(2)}, u32[]{:S(2)}) collective-permute-start(bf16[144,384]{1,0:T(8,128)(2,1)} %get-tuple-element.39.refs_1_), channel_id=1, source_target_pairs={{0,64},{8,72},{16,80},{24,88},{32,96},{40,104},{48,112},{56,120},{... | collective-permute-start | bytes 331784 | tf_op jit(solution)/shard_map/ppermute | solution.py:28
  4.4 8.4 %collective-permute-start.2 = (bf16[144,384]{1,0:T(8,128)(2,1)}, bf16[144,384]{1,0:T(8,128)(2,1)S(1)}, u32[]{:S(2)}, u32[]{:S(2)}) collective-permute-start(bf16[144,384]{1,0:T(8,128)(2,1)} %get-tuple-element.39.refs_1_), channel_id=1, source_target_pairs={{0,192},{8,200},{16,208},{24,216},{32,224},{40,232},{48,240},{56,2... | collective-permute-start | bytes 331784 | tf_op jit(solution)/shard_map/ppermute | solution.py:28
  7.3 12.4 %collective-permute-start.5 = (bf16[256,384]{1,0:T(8,128)(2,1)}, bf16[256,384]{1,0:T(8,128)(2,1)S(1)}, u32[]{:S(2)}, u32[]{:S(2)}) collective-permute-start(bf16[256,384]{1,0:T(8,128)(2,1)} %get-tuple-element.40.refs_5_), channel_id=1, source_target_pairs={{0,48},{8,56},{16,32},{24,40},{32,16},{40,24},{48,0},{56,8},{64,11... | collective-permute-start | bytes 589832 | tf_op jit(solution)/shard_map/ppermute | solution.py:28
  10.3 9.9 %collective-permute-start.4 = (bf16[256,384]{1,0:T(8,128)(2,1)}, bf16[256,384]{1,0:T(8,128)(2,1)S(1)}, u32[]{:S(2)}, u32[]{:S(2)}) collective-permute-start(bf16[256,384]{1,0:T(8,128)(2,1)} %get-tuple-element.40.refs_5_), channel_id=1, source_target_pairs={{0,32},{8,40},{16,48},{24,56},{32,0},{40,8},{48,16},{56,24},{64,96... | collective-permute-start | bytes 589832 | tf_op jit(solution)/shard_map/ppermute | solution.py:28
  10.9 9.3 %collective-permute-start.3 = (bf16[256,384]{1,0:T(8,128)(2,1)}, bf16[256,384]{1,0:T(8,128)(2,1)S(1)}, u32[]{:S(2)}, u32[]{:S(2)}) collective-permute-start(bf16[256,384]{1,0:T(8,128)(2,1)} %get-tuple-element.40.refs_5_), channel_id=1, source_target_pairs={{0,16},{8,24},{16,0},{24,8},{32,48},{40,56},{48,32},{56,40},{64,80... | collective-permute-start | bytes 589832 | tf_op jit(solution)/shard_map/ppermute | solution.py:28
  11.4 8.3 %collective-permute-start.1 = (bf16[144,384]{1,0:T(8,128)(2,1)}, bf16[144,384]{1,0:T(8,128)(2,1)S(1)}, u32[]{:S(2)}, u32[]{:S(2)}) collective-permute-start(bf16[144,384]{1,0:T(8,128)(2,1)} %get-tuple-element.39.refs_1_), channel_id=1, source_target_pairs={{0,128},{8,136},{16,144},{24,152},{32,160},{40,168},{48,176},{56,1... | collective-permute-start | bytes 331784 | tf_op jit(solution)/shard_map/ppermute | solution.py:28
  12.9 9.2 %collective-permute-start.13 = (bf16[128,384]{1,0:T(8,128)(2,1)}, bf16[128,384]{1,0:T(8,128)(2,1)S(1)}, u32[]{:S(2)}, u32[]{:S(2)}) collective-permute-start(bf16[128,384]{1,0:T(8,128)(2,1)} %param.11), channel_id=1, source_target_pairs={{0,4},{1,5},{2,6},{3,7},{4,0},{5,1},{6,2},{7,3},{8,12},{9,13},{10,... | collective-permute-start | bytes 294920 | tf_op jit(solution)/shard_map/ppermute | solution.py:28
  23.0 6.4 %collective-permute-start.14 = (bf16[256,384]{1,0:T(8,128)(2,1)S(1)}, bf16[256,384]{1,0:T(8,128)(2,1)S(1)}, u32[]{:S(2)}, u32[]{:S(2)}) collective-permute-start(bf16[256,384]{1,0:T(8,128)(2,1)S(1)} %pad_maximum_fusion.2), channel_id=1, source_target_pairs={{0,1},{1,0},{2,3},{3,2},{4,5},{5,4},{6,7},{7,6},{8,9},{9,8},{10,11... | collective-permute-start | bytes 589832 | tf_op jit(solution)/shard_map/ppermute | solution.py:28
  29.5 13.1 %collective-permute-start.15 = (bf16[512,384]{1,0:T(8,128)(2,1)S(1)}, bf16[512,384]{1,0:T(8,128)(2,1)S(1)}, u32[]{:S(2)}, u32[]{:S(2)}) collective-permute-start(bf16[512,384]{1,0:T(8,128)(2,1)S(1)} %pad_maximum_fusion.1), channel_id=1, source_target_pairs={{0,2},{1,3},{2,0},{3,1},{4,6},{5,7},{6,4},{7,5},{8,10},{9,11},{10,... | collective-permute-start | bytes 1179656 | tf_op jit(solution)/shard_map/ppermute | solution.py:28
  32.0 6.4 %collective-permute-start.10 = (bf16[400,128]{1,0:T(8,128)(2,1)S(1)}, bf16[400,128]{1,0:T(8,128)(2,1)S(1)}, u32[]{:S(2)}, u32[]{:S(2)}) collective-permute-start(bf16[400,128]{1,0:T(8,128)(2,1)S(1)} %get-tuple-element.42), channel_id=1, source_target_pairs={{0,64},{8,72},{16,80},{24,88},{32,96},{40,104},{48,112},{56,120},{... | collective-permute-start | bytes 307208 | tf_op jit(solution)/shard_map/ppermute | solution.py:28
  34.7 7.8 %collective-permute-start.11 = (bf16[400,128]{1,0:T(8,128)(2,1)S(1)}, bf16[400,128]{1,0:T(8,128)(2,1)S(1)}, u32[]{:S(2)}, u32[]{:S(2)}) collective-permute-start(bf16[400,128]{1,0:T(8,128)(2,1)S(1)} %get-tuple-element.43), channel_id=1, source_target_pairs={{0,128},{8,136},{16,144},{24,152},{32,160},{40,168},{48,176},{56,1... | collective-permute-start | bytes 307208 | tf_op jit(solution)/shard_map/ppermute | solution.py:28
  35.6 6.8 %collective-permute-start.12 = (bf16[400,128]{1,0:T(8,128)(2,1)S(1)}, bf16[400,128]{1,0:T(8,128)(2,1)S(1)}, u32[]{:S(2)}, u32[]{:S(2)}) collective-permute-start(bf16[400,128]{1,0:T(8,128)(2,1)S(1)} %get-tuple-element.44), channel_id=1, source_target_pairs={{0,192},{8,200},{16,208},{24,216},{32,224},{40,232},{48,240},{56,2... | collective-permute-start | bytes 307208 | tf_op jit(solution)/shard_map/ppermute | solution.py:28
  42.7 14.9 %collective-permute-start.23 = (bf16[1024,384]{1,0:T(8,128)(2,1)S(1)}, bf16[1024,384]{1,0:T(8,128)(2,1)S(1)}, u32[]{:S(2)}, u32[]{:S(2)}) collective-permute-start(bf16[1024,384]{1,0:T(8,128)(2,1)S(1)} %pad_maximum_fusion.d_ref), channel_id=1, source_target_pairs={{0,8},{8,0},{16,24},{24,16},{32,40},{40,32},{48,56},{56,48},{64,72... | collective-permute-start | bytes 2359304 | tf_op jit(solution)/shard_map/ppermute | solution.py:28
  42.8 6.1 %collective-permute-start.20 = (bf16[384,128]{1,0:T(8,128)(2,1)S(1)}, bf16[384,128]{1,0:T(8,128)(2,1)S(1)}, u32[]{:S(2)}, u32[]{:S(2)}) collective-permute-start(bf16[384,128]{1,0:T(8,128)(2,1)S(1)} %get-tuple-element.52.att_ref), channel_id=1, source_target_pairs={{0,8},{8,0},{16,24},{24,16},{32,40},{40,32},{48,56},{56,48},{64,72... | collective-permute-start | bytes 294920 | tf_op jit(solution)/shard_map/ppermute | solution.py:28
  44.6 8.7 %collective-permute-start.16 = (bf16[384,128]{1,0:T(8,128)(2,1)S(1)}, bf16[384,128]{1,0:T(8,128)(2,1)S(1)}, u32[]{:S(2)}, u32[]{:S(2)}) collective-permute-start(bf16[384,128]{1,0:T(8,128)(2,1)S(1)} %shard_map.113.grad_ref.refs_13_), channel_id=1, source_target_pairs={{0,128},{8,136},{16,144},{24,152},{32,160},{40,168},{48,176},{56,1... | collective-permute-start | bytes 294920 | tf_op jit(solution)/shard_map/ppermute | solution.py:28
  47.0 5.6 %collective-permute-start.19 = (f32[8,128]{1,0:T(8,128)S(1)}, f32[8,128]{1,0:T(8,128)S(1)}, u32[]{:S(2)}, u32[]{:S(2)}) collective-permute-start(f32[8,128]{1,0:T(8,128)S(1)} %shard_map.114.refs_17_), channel_id=1, source_target_pairs={{0,192},{8,200},{16,208},{24,216},{32,224},{40,232},{48,240},{56,2... | collective-permute-start | bytes 12296 | tf_op jit(solution)/shard_map/ppermute | solution.py:28
  48.9 4.5 %collective-permute-start.18 = (f32[8,128]{1,0:T(8,128)S(1)}, f32[8,128]{1,0:T(8,128)S(1)}, u32[]{:S(2)}, u32[]{:S(2)}) collective-permute-start(f32[8,128]{1,0:T(8,128)S(1)} %shard_map.114.refs_17_), channel_id=1, source_target_pairs={{0,128},{8,136},{16,144},{24,152},{32,160},{40,168},{48,176},{56,1... | collective-permute-start | bytes 12296 | tf_op jit(solution)/shard_map/ppermute | solution.py:28
  54.7 11.3 %collective-permute-start.21 = (bf16[512,384]{1,0:T(8,128)(2,1)S(1)}, bf16[512,384]{1,0:T(8,128)(2,1)S(1)}, u32[]{:S(2)}, u32[]{:S(2)}) collective-permute-start(bf16[512,384]{1,0:T(8,128)(2,1)S(1)} %get-tuple-element.54), channel_id=1, source_target_pairs={{0,2},{1,3},{2,0},{3,1},{4,6},{5,7},{6,4},{7,5},{8,10},{9,11},{10,... | collective-permute-start | bytes 1179656 | tf_op jit(solution)/shard_map/ppermute | solution.py:28
  55.9 10.3 %collective-permute-start.22 = (bf16[768,128]{1,0:T(8,128)(2,1)S(1)}, bf16[768,128]{1,0:T(8,128)(2,1)S(1)}, u32[]{:S(2)}, u32[]{:S(2)}) collective-permute-start(bf16[768,128]{1,0:T(8,128)(2,1)S(1)} %pad_maximum_fusion.3), channel_id=1, source_target_pairs={{0,64},{8,72},{16,80},{24,88},{32,96},{40,104},{48,112},{56,120},{... | collective-permute-start | bytes 589832 | tf_op jit(solution)/shard_map/ppermute | solution.py:28
  58.9 16.1 %collective-permute-start.25 = (bf16[48,3072]{1,0:T(8,128)(2,1)S(1)}, bf16[48,3072]{1,0:T(8,128)(2,1)S(1)}, u32[]{:S(2)}, u32[]{:S(2)}) collective-permute-start(bf16[48,3072]{1,0:T(8,128)(2,1)S(1)} %get-tuple-element.63), channel_id=1, source_target_pairs={{0,32},{8,40},{16,48},{24,56},{32,0},{40,8},{48,16},{56,24},{64,96... | collective-permute-start | bytes 884744 | tf_op jit(solution)/shard_map/ppermute | solution.py:28
  62.3 12.7 %collective-permute-start.26 = (bf16[48,3072]{1,0:T(8,128)(2,1)S(1)}, bf16[48,3072]{1,0:T(8,128)(2,1)S(1)}, u32[]{:S(2)}, u32[]{:S(2)}) collective-permute-start(bf16[48,3072]{1,0:T(8,128)(2,1)S(1)} %get-tuple-element.64), channel_id=1, source_target_pairs={{0,48},{8,56},{16,32},{24,40},{32,16},{40,24},{48,0},{56,8},{64,11... | collective-permute-start | bytes 884744 | tf_op jit(solution)/shard_map/ppermute | solution.py:28
  63.3 11.7 %collective-permute-start.24 = (bf16[48,3072]{1,0:T(8,128)(2,1)S(1)}, bf16[48,3072]{1,0:T(8,128)(2,1)S(1)}, u32[]{:S(2)}, u32[]{:S(2)}) collective-permute-start(bf16[48,3072]{1,0:T(8,128)(2,1)S(1)} %get-tuple-element.56), channel_id=1, source_target_pairs={{0,16},{8,24},{16,0},{24,8},{32,48},{40,56},{48,32},{56,40},{64,80... | collective-permute-start | bytes 884744 | tf_op jit(solution)/shard_map/ppermute | solution.py:28
  73.0 7.5 %collective-permute-start.28 = (bf16[1024,384]{1,0:T(8,128)(2,1)S(1)}, bf16[1024,384]{1,0:T(8,128)(2,1)S(1)}, u32[]{:S(2)}, u32[]{:S(2)}) collective-permute-start(bf16[1024,384]{1,0:T(8,128)(2,1)S(1)} %get-tuple-element.61), channel_id=1, source_target_pairs={{0,8},{8,0},{16,24},{24,16},{32,40},{40,32},{48,56},{56,48},{64,72... | collective-permute-start | bytes 2359304 | tf_op jit(solution)/shard_map/ppermute | solution.py:28
  73.1 7.4 %collective-permute-start.27 = (bf16[256,384]{1,0:T(8,128)(2,1)S(1)}, bf16[256,384]{1,0:T(8,128)(2,1)S(1)}, u32[]{:S(2)}, u32[]{:S(2)}) collective-permute-start(bf16[256,384]{1,0:T(8,128)(2,1)S(1)} %slice.114), channel_id=1, source_target_pairs={{0,1},{1,0},{2,3},{3,2},{4,5},{5,4},{6,7},{7,6},{8,9},{9,8},{10,11... | collective-permute-start | bytes 589832 | tf_op jit(solution)/shard_map/ppermute | solution.py:28
  80.8 8.8 %collective-permute-start.29 = (bf16[256,384]{1,0:T(8,128)(2,1)S(1)}, bf16[256,384]{1,0:T(8,128)(2,1)S(1)}, u32[]{:S(2)}, u32[]{:S(2)}) collective-permute-start(bf16[256,384]{1,0:T(8,128)(2,1)S(1)} %get-tuple-element.82), channel_id=1, source_target_pairs={{0,32},{8,40},{16,48},{24,56},{32,0},{40,8},{48,16},{56,24},{64,96... | collective-permute-start | bytes 589832 | tf_op jit(solution)/shard_map/ppermute | solution.py:28
  84.2 6.8 %collective-permute-start.33 = (bf16[24,3072]{1,0:T(8,128)(2,1)S(1)}, bf16[24,3072]{1,0:T(8,128)(2,1)S(1)}, u32[]{:S(2)}, u32[]{:S(2)}) collective-permute-start(bf16[24,3072]{1,0:T(8,128)(2,1)S(1)} %slice.115), channel_id=1, source_target_pairs={{0,64},{8,72},{16,80},{24,88},{32,96},{40,104},{48,112},{56,120},{... | collective-permute-start | bytes 442376 | tf_op jit(solution)/shard_map/ppermute | solution.py:28
  85.3 8.3 %collective-permute-start.31 = (bf16[768,128]{1,0:T(8,128)(2,1)S(1)}, bf16[768,128]{1,0:T(8,128)(2,1)S(1)}, u32[]{:S(2)}, u32[]{:S(2)}) collective-permute-start(bf16[768,128]{1,0:T(8,128)(2,1)S(1)} %get-tuple-element.70), channel_id=1, source_target_pairs={{0,64},{8,72},{16,80},{24,88},{32,96},{40,104},{48,112},{56,120},{... | collective-permute-start | bytes 589832 | tf_op jit(solution)/shard_map/ppermute | solution.py:28
  86.4 15.8 %collective-permute-start.34 = (bf16[256,384]{1,0:T(8,128)(2,1)S(1)}, bf16[256,384]{1,0:T(8,128)(2,1)S(1)}, u32[]{:S(2)}, u32[]{:S(2)}) collective-permute-start(bf16[256,384]{1,0:T(8,128)(2,1)S(1)} %get-tuple-element.80), channel_id=1, source_target_pairs={{0,16},{8,24},{16,0},{24,8},{32,48},{40,56},{48,32},{56,40},{64,80... | collective-permute-start | bytes 589832 | tf_op jit(solution)/shard_map/ppermute | solution.py:28
  87.0 15.1 %collective-permute-start.35 = (bf16[256,384]{1,0:T(8,128)(2,1)S(1)}, bf16[256,384]{1,0:T(8,128)(2,1)S(1)}, u32[]{:S(2)}, u32[]{:S(2)}) collective-permute-start(bf16[256,384]{1,0:T(8,128)(2,1)S(1)} %get-tuple-element.81), channel_id=1, source_target_pairs={{0,48},{8,56},{16,32},{24,40},{32,16},{40,24},{48,0},{56,8},{64,11... | collective-permute-start | bytes 589832 | tf_op jit(solution)/shard_map/ppermute | solution.py:28
  93.7 11.5 %collective-permute-start.36 = (bf16[12,3072]{1,0:T(8,128)(2,1)S(1)}, bf16[12,3072]{1,0:T(8,128)(2,1)S(1)}, u32[]{:S(2)}, u32[]{:S(2)}) collective-permute-start(bf16[12,3072]{1,0:T(8,128)(2,1)S(1)} %slice.116), channel_id=1, source_target_pairs={{0,128},{8,136},{16,144},{24,152},{32,160},{40,168},{48,176},{56,1... | collective-permute-start | bytes 221192 | tf_op jit(solution)/shard_map/ppermute | solution.py:28
  95.2 13.2 %collective-permute-start.32 = (bf16[384,128]{1,0:T(8,128)(2,1)S(1)}, bf16[384,128]{1,0:T(8,128)(2,1)S(1)}, u32[]{:S(2)}, u32[]{:S(2)}) collective-permute-start(bf16[384,128]{1,0:T(8,128)(2,1)S(1)} %slice.117), channel_id=1, source_target_pairs={{0,128},{8,136},{16,144},{24,152},{32,160},{40,168},{48,176},{56,1... | collective-permute-start | bytes 294920 | tf_op jit(solution)/shard_map/ppermute | solution.py:28
  96.7 12.5 %collective-permute-start.30 = (bf16[128,384]{1,0:T(8,128)(2,1)S(1)}, bf16[128,384]{1,0:T(8,128)(2,1)S(1)}, u32[]{:S(2)}, u32[]{:S(2)}) collective-permute-start(bf16[128,384]{1,0:T(8,128)(2,1)S(1)} %slice.118), channel_id=1, source_target_pairs={{0,4},{1,5},{2,6},{3,7},{4,0},{5,1},{6,2},{7,3},{8,12},{9,13},{10,... | collective-permute-start | bytes 294920 | tf_op jit(solution)/shard_map/ppermute | solution.py:28
  (13 other events, 103.8 us)

commit v8 on v6

--- a/solution.py
+++ b/solution.py
@@ -334,12 +334,12 @@
     arrived = [swap(away[e - 1], "slab", 2 * e) for e in (1, 2, 3)]
     dq_in = swap(after(dq_other, other), "slab", 8)
 
-    mixed = after(mixed[: 2 * ROWS], arrived[1]) + swap(mixed_away, "head", 1).astype(F32)
-    mixed_away = mixed[ROWS:].astype(BF)
     weight = after(weight[:24], arrived[1]) + swap(weight_away, "slab", 8).astype(F32)
     weight_away = weight[12:].astype(BF)
-    dq = after(dq_own, mixed_away) + dq_in.astype(F32)
+    dq = after(dq_own, arrived[1]) + dq_in.astype(F32)
     dq_away = dq[COLS:].astype(BF)
+    mixed = after(mixed[: 2 * ROWS], weight_away, dq_away) + swap(mixed_away, "head", 1).astype(F32)
+    mixed_away = mixed[ROWS:].astype(BF)
 
     total = after(pair[0], weight_away, mixed_away, dq_away) + sum((a.astype(F32) for a in arrived), 0.0)
     total = total.astype(BF)

time: 107 us -> 105 us (0.981)
  waiting for transfers between devices: 23.6 us -> 22.4 us
    ppermute x37, waiting for transfers between devices: 23.6 us -> 22.4 us  [swap(): return lax.ppermute(block, axis, [(i, i ^ distance) for i in devices])]
    unnamed x15 -> x17, local copies, waits for them, and re-layouts: 2.6 us -> 2.6 us
where the time goes in v8:
time: 105 us; the launch traced here: 104 us
  starting transfers between devices  57.5 us (55%)
  waiting for transfers between devices  22.4 us (21%)
  Pallas kernels  16.5 us (16%)
  local copies, waits for them, and re-layouts  3.49 us (3%)
  other arithmetic  3.1 us (3%)
    ppermute x37, starting transfers between devices, swap(): return lax.ppermute(block, axis, [(i, i ^ distance) for i in devices])  57.5 us
    ppermute x37, waiting for transfers between devices, swap(): return lax.ppermute(block, axis, [(i, i ^ distance) for i in devices])  22.4 us
    pallas_call x8, Pallas kernels, call(): pl.pallas_call(kernel, out_shape=[jax.ShapeDtypeStruct(shape, dtype) for...  16.5 us
    unnamed x17, local copies, waits for them, and re-layouts  2.6 us
  transfers between devices with their start and end apart: 37, of which 14 were waited for; matrix products, arithmetic and copies ran while one was open for 4% of the time, Pallas kernels for 14%

profile of v8, /device:TPU:2, one launch (start us, length us, event | category | flops | bytes accessed | tf_op | source)
XLA Modules:
  0.0 103.9 jit_solution(1595284167781484020)
XLA Ops:
  0.6 1.8 %shard_map.110 = (bf16[144,384]{1,0:T(8,128)(2,1)}, bf16[256,384]{1,0:T(8,128)(2,1)}) custom-call(s32[2,4]{1,0:T(2,128)} %ids_hbm.1, s32[2]{0:T(128)} %counts_hbm.1, bf16[128,384]{1,0:T(8,128)(2,1)} %q_hbm.1, bf16[128,384]{1,0:T(8,128)(2,1)} %k_hbm.1, bf16[128,384]{1,0:T(8,128)(2,1)} %v_hbm.1), custom_call_target="tpu_custom_call" | custom-call | flops 1000 | bytes 1000 | tf_op jit(solution)/shard_map/pallas_call | solution.py:39
  2.4 2.0 %collective-permute-start = (bf16[144,384]{1,0:T(8,128)(2,1)}, bf16[144,384]{1,0:T(8,128)(2,1)S(1)}, u32[]{:S(2)}, u32[]{:S(2)}) collective-permute-start(bf16[144,384]{1,0:T(8,128)(2,1)} %get-tuple-element.39.refs_1_), channel_id=1, source_target_pairs={{0,64},{8,72},{16,80},{24,88},{32,96},{40,104},{48,112},{56,120},{... | collective-permute-start | bytes 331784 | tf_op jit(solution)/shard_map/ppermute | solution.py:28
  4.4 2.8 %collective-permute-start.2 = (bf16[144,384]{1,0:T(8,128)(2,1)}, bf16[144,384]{1,0:T(8,128)(2,1)S(1)}, u32[]{:S(2)}, u32[]{:S(2)}) collective-permute-start(bf16[144,384]{1,0:T(8,128)(2,1)} %get-tuple-element.39.refs_1_), channel_id=1, source_target_pairs={{0,192},{8,200},{16,208},{24,216},{32,224},{40,232},{48,240},{56,2... | collective-permute-start | bytes 331784 | tf_op jit(solution)/shard_map/ppermute | solution.py:28
  7.3 3.0 %collective-permute-start.5 = (bf16[256,384]{1,0:T(8,128)(2,1)}, bf16[256,384]{1,0:T(8,128)(2,1)S(1)}, u32[]{:S(2)}, u32[]{:S(2)}) collective-permute-start(bf16[256,384]{1,0:T(8,128)(2,1)} %get-tuple-element.40.refs_5_), channel_id=1, source_target_pairs={{0,48},{8,56},{16,32},{24,40},{32,16},{40,24},{48,0},{56,8},{64,11... | collective-permute-start | bytes 589832 | tf_op jit(solution)/shard_map/ppermute | solution.py:28
  11.4 1.4 %collective-permute-start.1 = (bf16[144,384]{1,0:T(8,128)(2,1)}, bf16[144,384]{1,0:T(8,128)(2,1)S(1)}, u32[]{:S(2)}, u32[]{:S(2)}) collective-permute-start(bf16[144,384]{1,0:T(8,128)(2,1)} %get-tuple-element.39.refs_1_), channel_id=1, source_target_pairs={{0,128},{8,136},{16,144},{24,152},{32,160},{40,168},{48,176},{56,1... | collective-permute-start | bytes 331784 | tf_op jit(solution)/shard_map/ppermute | solution.py:28
  12.9 5.2 %collective-permute-start.14 = (bf16[128,384]{1,0:T(8,128)(2,1)}, bf16[128,384]{1,0:T(8,128)(2,1)S(1)}, u32[]{:S(2)}, u32[]{:S(2)}) collective-permute-start(bf16[128,384]{1,0:T(8,128)(2,1)} %param.11), channel_id=1, source_target_pairs={{0,4},{1,5},{2,6},{3,7},{4,0},{5,1},{6,2},{7,3},{8,12},{9,13},{10,... | collective-permute-start | bytes 294920 | tf_op jit(solution)/shard_map/ppermute | solution.py:28
  18.1 1.6 %collective-permute-done.1.refs_3_ = bf16[144,384]{1,0:T(8,128)(2,1)S(1)} collective-permute-done((bf16[144,384]{1,0:T(8,128)(2,1)}, bf16[144,384]{1,0:T(8,128)(2,1)S(1)}, u32[]{:S(2)}, u32[]{:S(2)}) %collective-permute-start.1) | collective-permute-done | bytes 110624 | tf_op jit(solution)/shard_map/ppermute | solution.py:28
  20.6 1.4 %collective-permute-done.14 = bf16[128,384]{1,0:T(8,128)(2,1)S(1)} collective-permute-done((bf16[128,384]{1,0:T(8,128)(2,1)}, bf16[128,384]{1,0:T(8,128)(2,1)S(1)}, u32[]{:S(2)}, u32[]{:S(2)}) %collective-permute-start.14) | collective-permute-done | bytes 98336 | tf_op jit(solution)/shard_map/ppermute | solution.py:28
  25.5 3.9 %shard_map.111 = (bf16[400,128]{1,0:T(8,128)(2,1)S(1)}, bf16[400,128]{1,0:T(8,128)(2,1)S(1)}, bf16[400,128]{1,0:T(8,128)(2,1)S(1)}, bf16[400,128]{1,0:T(8,128)(2,1)S(1)}) custom-call(s32[4]{0:T(128)S(1)} %pad_add_fusion.refs_0_.rank_ref, bf16[144,384]{1,0:T(8,128)(2,1)S(1)} %copy-done.3, bf16[144,384]{1,0:T(8,128)(2,1)S(1)} %collective-permute-done.refs_2_, ...), custom_call_target="tpu_custom_call" | custom-call | flops 1000 | bytes 1000 | tf_op jit(solution)/shard_map/pallas_call | solution.py:39
  29.5 2.5 %collective-permute-start.16 = (bf16[512,384]{1,0:T(8,128)(2,1)S(1)}, bf16[512,384]{1,0:T(8,128)(2,1)S(1)}, u32[]{:S(2)}, u32[]{:S(2)}) collective-permute-start(bf16[512,384]{1,0:T(8,128)(2,1)S(1)} %pad_maximum_fusion.1), channel_id=1, source_target_pairs={{0,2},{1,3},{2,0},{3,1},{4,6},{5,7},{6,4},{7,5},{8,10},{9,11},{10,... | collective-permute-start | bytes 1179656 | tf_op jit(solution)/shard_map/ppermute | solution.py:28
  32.0 2.7 %collective-permute-start.10 = (bf16[400,128]{1,0:T(8,128)(2,1)S(1)}, bf16[400,128]{1,0:T(8,128)(2,1)S(1)}, u32[]{:S(2)}, u32[]{:S(2)}) collective-permute-start(bf16[400,128]{1,0:T(8,128)(2,1)S(1)} %get-tuple-element.42), channel_id=1, source_target_pairs={{0,64},{8,72},{16,80},{24,88},{32,96},{40,104},{48,112},{56,120},{... | collective-permute-start | bytes 307208 | tf_op jit(solution)/shard_map/ppermute | solution.py:28
  35.6 1.5 %collective-permute-start.12 = (bf16[400,128]{1,0:T(8,128)(2,1)S(1)}, bf16[400,128]{1,0:T(8,128)(2,1)S(1)}, u32[]{:S(2)}, u32[]{:S(2)}) collective-permute-start(bf16[400,128]{1,0:T(8,128)(2,1)S(1)} %get-tuple-element.44), channel_id=1, source_target_pairs={{0,192},{8,200},{16,208},{24,216},{32,224},{40,232},{48,240},{56,2... | collective-permute-start | bytes 307208 | tf_op jit(solution)/shard_map/ppermute | solution.py:28
  37.1 1.3 %collective-permute-done.10.refs_1_ = bf16[400,128]{1,0:T(8,128)(2,1)S(1)} collective-permute-done((bf16[400,128]{1,0:T(8,128)(2,1)S(1)}, bf16[400,128]{1,0:T(8,128)(2,1)S(1)}, u32[]{:S(2)}, u32[]{:S(2)}) %collective-permute-start.10) | collective-permute-done | bytes 102432 | tf_op jit(solution)/shard_map/ppermute | solution.py:28
  38.4 4.0 %collective-permute-done.11.refs_2_ = bf16[400,128]{1,0:T(8,128)(2,1)S(1)} collective-permute-done((bf16[400,128]{1,0:T(8,128)(2,1)S(1)}, bf16[400,128]{1,0:T(8,128)(2,1)S(1)}, u32[]{:S(2)}, u32[]{:S(2)}) %collective-permute-start.11) | collective-permute-done | bytes 102432 | tf_op jit(solution)/shard_map/ppermute | solution.py:28
  43.3 1.3 %shard_map.115.grad_ref.refs_13_ = bf16[384,128]{1,0:T(8,128)(2,1)S(1)} custom-call(s32[4]{0:T(128)S(1)} %pad_add_fusion.refs_0_.rank_ref, bf16[384,3072]{1,0:T(8,128)(2,1)S(1)} %copy-done, bf16[1024,384]{1,0:T(8,128)(2,1)S(1)} %pad_maximum_fusion.d_ref), custom_call_target="tpu_custom_call" | custom-call | flops 1000 | bytes 1000 | tf_op jit(solution)/shard_map/pallas_call | solution.py:39
  44.6 2.3 %collective-permute-start.19 = (bf16[384,128]{1,0:T(8,128)(2,1)S(1)}, bf16[384,128]{1,0:T(8,128)(2,1)S(1)}, u32[]{:S(2)}, u32[]{:S(2)}) collective-permute-start(bf16[384,128]{1,0:T(8,128)(2,1)S(1)} %shard_map.115.grad_ref.refs_13_), channel_id=1, source_target_pairs={{0,128},{8,136},{16,144},{24,152},{32,160},{40,168},{48,176},{56,1... | collective-permute-start | bytes 294920 | tf_op jit(solution)/shard_map/ppermute | solution.py:28
  47.0 1.9 %collective-permute-start.22 = (f32[8,128]{1,0:T(8,128)S(1)}, f32[8,128]{1,0:T(8,128)S(1)}, u32[]{:S(2)}, u32[]{:S(2)}) collective-permute-start(f32[8,128]{1,0:T(8,128)S(1)} %shard_map.116.refs_17_), channel_id=1, source_target_pairs={{0,192},{8,200},{16,208},{24,216},{32,224},{40,232},{48,240},{56,2... | collective-permute-start | bytes 12296 | tf_op jit(solution)/shard_map/ppermute | solution.py:28
  48.9 2.6 %collective-permute-start.20 = (f32[8,128]{1,0:T(8,128)S(1)}, f32[8,128]{1,0:T(8,128)S(1)}, u32[]{:S(2)}, u32[]{:S(2)}) collective-permute-start(f32[8,128]{1,0:T(8,128)S(1)} %shard_map.116.refs_17_), channel_id=1, source_target_pairs={{0,64},{8,72},{16,80},{24,88},{32,96},{40,104},{48,112},{56,120},{... | collective-permute-start | bytes 12296 | tf_op jit(solution)/shard_map/ppermute | solution.py:28
  53.4 1.8 %collective-permute-start.23 = (bf16[768,128]{1,0:T(8,128)(2,1)S(1)}, bf16[768,128]{1,0:T(8,128)(2,1)S(1)}, u32[]{:S(2)}, u32[]{:S(2)}) collective-permute-start(bf16[768,128]{1,0:T(8,128)(2,1)S(1)} %pad_maximum_fusion.3), channel_id=1, source_target_pairs={{0,64},{8,72},{16,80},{24,88},{32,96},{40,104},{48,112},{56,120},{... | collective-permute-start | bytes 589832 | tf_op jit(solution)/shard_map/ppermute | solution.py:28
  55.2 1.3 %shard_map.113 = (f32[48,3072]{1,0:T(8,128)S(1)}, bf16[48,3072]{1,0:T(8,128)(2,1)S(1)}, bf16[48,3072]{1,0:T(8,128)(2,1)S(1)}, bf16[48,3072]{1,0:T(8,128)(2,1)S(1)}) custom-call(s32[4]{0:T(128)S(1)} %pad_add_fusion.refs_0_.rank_ref, bf16[384,128]{1,0:T(8,128)(2,1)S(1)} %get-tuple-element.52.att_ref, bf16[384,128]{1,0:T(8,128)(2,1)S(1)} %collective-permute-done.13.att2_ref, ...), custom_call_target="tpu_custom_call" | custom-call | flops 1000 | bytes 1000 | tf_op jit(solution)/shard_map/pallas_call | solution.py:39
  56.5 3.4 %collective-permute-start.25 = (bf16[48,3072]{1,0:T(8,128)(2,1)S(1)}, bf16[48,3072]{1,0:T(8,128)(2,1)S(1)}, u32[]{:S(2)}, u32[]{:S(2)}) collective-permute-start(bf16[48,3072]{1,0:T(8,128)(2,1)S(1)} %get-tuple-element.62), channel_id=1, source_target_pairs={{0,32},{8,40},{16,48},{24,56},{32,0},{40,8},{48,16},{56,24},{64,96... | collective-permute-start | bytes 884744 | tf_op jit(solution)/shard_map/ppermute | solution.py:28
  62.2 1.4 %collective-permute-start.18 = (bf16[512,384]{1,0:T(8,128)(2,1)S(1)}, bf16[512,384]{1,0:T(8,128)(2,1)S(1)}, u32[]{:S(2)}, u32[]{:S(2)}) collective-permute-start(bf16[512,384]{1,0:T(8,128)(2,1)S(1)} %get-tuple-element.54), channel_id=1, source_target_pairs={{0,2},{1,3},{2,0},{3,1},{4,6},{5,7},{6,4},{7,5},{8,10},{9,11},{10,... | collective-permute-start | bytes 1179656 | tf_op jit(solution)/shard_map/ppermute | solution.py:28
  63.7 6.8 %shard_map.117 = (f32[768,128]{1,0:T(8,128)S(1)}, bf16[768,128]{1,0:T(8,128)(2,1)S(1)}, f32[1024,384]{1,0:T(8,128)S(1)}, bf16[1024,384]{1,0:T(8,128)(2,1)S(1)}) custom-call(s32[4]{0:T(128)S(1)} %pad_add_fusion.refs_0_.rank_ref, bf16[144,384]{1,0:T(8,128)(2,1)S(1)} %copy-done.4, bf16[144,384]{1,0:T(8,128)(2,1)S(1)} %collective-permute-done.refs_2_, ...), custom_call_target="tpu_custom_call" | custom-call | flops 1000 | bytes 1000 | tf_op jit(solution)/shard_map/pallas_call | solution.py:39
  73.2 3.7 %collective-permute-start.28 = (bf16[256,384]{1,0:T(8,128)(2,1)S(1)}, bf16[256,384]{1,0:T(8,128)(2,1)S(1)}, u32[]{:S(2)}, u32[]{:S(2)}) collective-permute-start(bf16[256,384]{1,0:T(8,128)(2,1)S(1)} %get-tuple-element.82), channel_id=1, source_target_pairs={{0,32},{8,40},{16,48},{24,56},{32,0},{40,8},{48,16},{56,24},{64,96... | collective-permute-start | bytes 589832 | tf_op jit(solution)/shard_map/ppermute | solution.py:28
  77.3 1.8 %collective-permute-start.31 = (bf16[256,384]{1,0:T(8,128)(2,1)S(1)}, bf16[256,384]{1,0:T(8,128)(2,1)S(1)}, u32[]{:S(2)}, u32[]{:S(2)}) collective-permute-start(bf16[256,384]{1,0:T(8,128)(2,1)S(1)} %slice.114), channel_id=1, source_target_pairs={{0,1},{1,0},{2,3},{3,2},{4,5},{5,4},{6,7},{7,6},{8,9},{9,8},{10,11... | collective-permute-start | bytes 589832 | tf_op jit(solution)/shard_map/ppermute | solution.py:28
  79.1 1.5 %collective-permute-start.30 = (bf16[768,128]{1,0:T(8,128)(2,1)S(1)}, bf16[768,128]{1,0:T(8,128)(2,1)S(1)}, u32[]{:S(2)}, u32[]{:S(2)}) collective-permute-start(bf16[768,128]{1,0:T(8,128)(2,1)S(1)} %get-tuple-element.70), channel_id=1, source_target_pairs={{0,64},{8,72},{16,80},{24,88},{32,96},{40,104},{48,112},{56,120},{... | collective-permute-start | bytes 589832 | tf_op jit(solution)/shard_map/ppermute | solution.py:28
  80.6 1.6 %collective-permute-done.28 = bf16[256,384]{1,0:T(8,128)(2,1)S(1)} collective-permute-done((bf16[256,384]{1,0:T(8,128)(2,1)S(1)}, bf16[256,384]{1,0:T(8,128)(2,1)S(1)}, u32[]{:S(2)}, u32[]{:S(2)}) %collective-permute-start.28) | collective-permute-done | bytes 196640 | tf_op jit(solution)/shard_map/ppermute | solution.py:28
  82.2 1.8 %collective-permute-start.35 = (bf16[256,384]{1,0:T(8,128)(2,1)S(1)}, bf16[256,384]{1,0:T(8,128)(2,1)S(1)}, u32[]{:S(2)}, u32[]{:S(2)}) collective-permute-start(bf16[256,384]{1,0:T(8,128)(2,1)S(1)} %get-tuple-element.81), channel_id=1, source_target_pairs={{0,48},{8,56},{16,32},{24,40},{32,16},{40,24},{48,0},{56,8},{64,11... | collective-permute-start | bytes 589832 | tf_op jit(solution)/shard_map/ppermute | solution.py:28
  84.0 2.7 %collective-permute-done.30 = bf16[768,128]{1,0:T(8,128)(2,1)S(1)} collective-permute-done((bf16[768,128]{1,0:T(8,128)(2,1)S(1)}, bf16[768,128]{1,0:T(8,128)(2,1)S(1)}, u32[]{:S(2)}, u32[]{:S(2)}) %collective-permute-start.30) | collective-permute-done | bytes 196640 | tf_op jit(solution)/shard_map/ppermute | solution.py:28
  87.8 2.0 %collective-permute-start.36 = (bf16[12,3072]{1,0:T(8,128)(2,1)S(1)}, bf16[12,3072]{1,0:T(8,128)(2,1)S(1)}, u32[]{:S(2)}, u32[]{:S(2)}) collective-permute-start(bf16[12,3072]{1,0:T(8,128)(2,1)S(1)} %slice.118), channel_id=1, source_target_pairs={{0,128},{8,136},{16,144},{24,152},{32,160},{40,168},{48,176},{56,1... | collective-permute-start | bytes 221192 | tf_op jit(solution)/shard_map/ppermute | solution.py:28
  89.9 5.5 %collective-permute-start.32 = (bf16[128,384]{1,0:T(8,128)(2,1)S(1)}, bf16[128,384]{1,0:T(8,128)(2,1)S(1)}, u32[]{:S(2)}, u32[]{:S(2)}) collective-permute-start(bf16[128,384]{1,0:T(8,128)(2,1)S(1)} %slice.116), channel_id=1, source_target_pairs={{0,4},{1,5},{2,6},{3,7},{4,0},{5,1},{6,2},{7,3},{8,12},{9,13},{10,... | collective-permute-start | bytes 294920 | tf_op jit(solution)/shard_map/ppermute | solution.py:28
  96.2 5.5 %collective-permute-done.36 = bf16[12,3072]{1,0:T(8,128)(2,1)S(1)} collective-permute-done((bf16[12,3072]{1,0:T(8,128)(2,1)S(1)}, bf16[12,3072]{1,0:T(8,128)(2,1)S(1)}, u32[]{:S(2)}, u32[]{:S(2)}) %collective-permute-start.36) | collective-permute-done | bytes 73760 | tf_op jit(solution)/shard_map/ppermute | solution.py:28
  (95 shorter events, 18.9 us)
Async XLA Ops:
  2.4 8.9 %collective-permute-start = (bf16[144,384]{1,0:T(8,128)(2,1)}, bf16[144,384]{1,0:T(8,128)(2,1)S(1)}, u32[]{:S(2)}, u32[]{:S(2)}) collective-permute-start(bf16[144,384]{1,0:T(8,128)(2,1)} %get-tuple-element.39.refs_1_), channel_id=1, source_target_pairs={{0,64},{8,72},{16,80},{24,88},{32,96},{40,104},{48,112},{56,120},{... | collective-permute-start | bytes 331784 | tf_op jit(solution)/shard_map/ppermute | solution.py:28
  4.4 8.4 %collective-permute-start.2 = (bf16[144,384]{1,0:T(8,128)(2,1)}, bf16[144,384]{1,0:T(8,128)(2,1)S(1)}, u32[]{:S(2)}, u32[]{:S(2)}) collective-permute-start(bf16[144,384]{1,0:T(8,128)(2,1)} %get-tuple-element.39.refs_1_), channel_id=1, source_target_pairs={{0,192},{8,200},{16,208},{24,216},{32,224},{40,232},{48,240},{56,2... | collective-permute-start | bytes 331784 | tf_op jit(solution)/shard_map/ppermute | solution.py:28
  7.3 12.4 %collective-permute-start.5 = (bf16[256,384]{1,0:T(8,128)(2,1)}, bf16[256,384]{1,0:T(8,128)(2,1)S(1)}, u32[]{:S(2)}, u32[]{:S(2)}) collective-permute-start(bf16[256,384]{1,0:T(8,128)(2,1)} %get-tuple-element.40.refs_5_), channel_id=1, source_target_pairs={{0,48},{8,56},{16,32},{24,40},{32,16},{40,24},{48,0},{56,8},{64,11... | collective-permute-start | bytes 589832 | tf_op jit(solution)/shard_map/ppermute | solution.py:28
  10.3 9.9 %collective-permute-start.4 = (bf16[256,384]{1,0:T(8,128)(2,1)}, bf16[256,384]{1,0:T(8,128)(2,1)S(1)}, u32[]{:S(2)}, u32[]{:S(2)}) collective-permute-start(bf16[256,384]{1,0:T(8,128)(2,1)} %get-tuple-element.40.refs_5_), channel_id=1, source_target_pairs={{0,32},{8,40},{16,48},{24,56},{32,0},{40,8},{48,16},{56,24},{64,96... | collective-permute-start | bytes 589832 | tf_op jit(solution)/shard_map/ppermute | solution.py:28
  10.9 9.3 %collective-permute-start.3 = (bf16[256,384]{1,0:T(8,128)(2,1)}, bf16[256,384]{1,0:T(8,128)(2,1)S(1)}, u32[]{:S(2)}, u32[]{:S(2)}) collective-permute-start(bf16[256,384]{1,0:T(8,128)(2,1)} %get-tuple-element.40.refs_5_), channel_id=1, source_target_pairs={{0,16},{8,24},{16,0},{24,8},{32,48},{40,56},{48,32},{56,40},{64,80... | collective-permute-start | bytes 589832 | tf_op jit(solution)/shard_map/ppermute | solution.py:28
  11.4 8.3 %collective-permute-start.1 = (bf16[144,384]{1,0:T(8,128)(2,1)}, bf16[144,384]{1,0:T(8,128)(2,1)S(1)}, u32[]{:S(2)}, u32[]{:S(2)}) collective-permute-start(bf16[144,384]{1,0:T(8,128)(2,1)} %get-tuple-element.39.refs_1_), channel_id=1, source_target_pairs={{0,128},{8,136},{16,144},{24,152},{32,160},{40,168},{48,176},{56,1... | collective-permute-start | bytes 331784 | tf_op jit(solution)/shard_map/ppermute | solution.py:28
  12.9 9.2 %collective-permute-start.14 = (bf16[128,384]{1,0:T(8,128)(2,1)}, bf16[128,384]{1,0:T(8,128)(2,1)S(1)}, u32[]{:S(2)}, u32[]{:S(2)}) collective-permute-start(bf16[128,384]{1,0:T(8,128)(2,1)} %param.11), channel_id=1, source_target_pairs={{0,4},{1,5},{2,6},{3,7},{4,0},{5,1},{6,2},{7,3},{8,12},{9,13},{10,... | collective-permute-start | bytes 294920 | tf_op jit(solution)/shard_map/ppermute | solution.py:28
  23.0 6.4 %collective-permute-start.15 = (bf16[256,384]{1,0:T(8,128)(2,1)S(1)}, bf16[256,384]{1,0:T(8,128)(2,1)S(1)}, u32[]{:S(2)}, u32[]{:S(2)}) collective-permute-start(bf16[256,384]{1,0:T(8,128)(2,1)S(1)} %pad_maximum_fusion.2), channel_id=1, source_target_pairs={{0,1},{1,0},{2,3},{3,2},{4,5},{5,4},{6,7},{7,6},{8,9},{9,8},{10,11... | collective-permute-start | bytes 589832 | tf_op jit(solution)/shard_map/ppermute | solution.py:28
  29.5 13.1 %collective-permute-start.16 = (bf16[512,384]{1,0:T(8,128)(2,1)S(1)}, bf16[512,384]{1,0:T(8,128)(2,1)S(1)}, u32[]{:S(2)}, u32[]{:S(2)}) collective-permute-start(bf16[512,384]{1,0:T(8,128)(2,1)S(1)} %pad_maximum_fusion.1), channel_id=1, source_target_pairs={{0,2},{1,3},{2,0},{3,1},{4,6},{5,7},{6,4},{7,5},{8,10},{9,11},{10,... | collective-permute-start | bytes 1179656 | tf_op jit(solution)/shard_map/ppermute | solution.py:28
  32.0 6.4 %collective-permute-start.10 = (bf16[400,128]{1,0:T(8,128)(2,1)S(1)}, bf16[400,128]{1,0:T(8,128)(2,1)S(1)}, u32[]{:S(2)}, u32[]{:S(2)}) collective-permute-start(bf16[400,128]{1,0:T(8,128)(2,1)S(1)} %get-tuple-element.42), channel_id=1, source_target_pairs={{0,64},{8,72},{16,80},{24,88},{32,96},{40,104},{48,112},{56,120},{... | collective-permute-start | bytes 307208 | tf_op jit(solution)/shard_map/ppermute | solution.py:28
  34.7 7.8 %collective-permute-start.11 = (bf16[400,128]{1,0:T(8,128)(2,1)S(1)}, bf16[400,128]{1,0:T(8,128)(2,1)S(1)}, u32[]{:S(2)}, u32[]{:S(2)}) collective-permute-start(bf16[400,128]{1,0:T(8,128)(2,1)S(1)} %get-tuple-element.43), channel_id=1, source_target_pairs={{0,128},{8,136},{16,144},{24,152},{32,160},{40,168},{48,176},{56,1... | collective-permute-start | bytes 307208 | tf_op jit(solution)/shard_map/ppermute | solution.py:28
  35.6 6.8 %collective-permute-start.12 = (bf16[400,128]{1,0:T(8,128)(2,1)S(1)}, bf16[400,128]{1,0:T(8,128)(2,1)S(1)}, u32[]{:S(2)}, u32[]{:S(2)}) collective-permute-start(bf16[400,128]{1,0:T(8,128)(2,1)S(1)} %get-tuple-element.44), channel_id=1, source_target_pairs={{0,192},{8,200},{16,208},{24,216},{32,224},{40,232},{48,240},{56,2... | collective-permute-start | bytes 307208 | tf_op jit(solution)/shard_map/ppermute | solution.py:28
  42.7 12.5 %collective-permute-start.17 = (bf16[1024,384]{1,0:T(8,128)(2,1)S(1)}, bf16[1024,384]{1,0:T(8,128)(2,1)S(1)}, u32[]{:S(2)}, u32[]{:S(2)}) collective-permute-start(bf16[1024,384]{1,0:T(8,128)(2,1)S(1)} %pad_maximum_fusion.d_ref), channel_id=1, source_target_pairs={{0,8},{8,0},{16,24},{24,16},{32,40},{40,32},{48,56},{56,48},{64,72... | collective-permute-start | bytes 2359304 | tf_op jit(solution)/shard_map/ppermute | solution.py:28
  42.8 6.1 %collective-permute-start.13 = (bf16[384,128]{1,0:T(8,128)(2,1)S(1)}, bf16[384,128]{1,0:T(8,128)(2,1)S(1)}, u32[]{:S(2)}, u32[]{:S(2)}) collective-permute-start(bf16[384,128]{1,0:T(8,128)(2,1)S(1)} %get-tuple-element.52.att_ref), channel_id=1, source_target_pairs={{0,8},{8,0},{16,24},{24,16},{32,40},{40,32},{48,56},{56,48},{64,72... | collective-permute-start | bytes 294920 | tf_op jit(solution)/shard_map/ppermute | solution.py:28
  44.6 8.7 %collective-permute-start.19 = (bf16[384,128]{1,0:T(8,128)(2,1)S(1)}, bf16[384,128]{1,0:T(8,128)(2,1)S(1)}, u32[]{:S(2)}, u32[]{:S(2)}) collective-permute-start(bf16[384,128]{1,0:T(8,128)(2,1)S(1)} %shard_map.115.grad_ref.refs_13_), channel_id=1, source_target_pairs={{0,128},{8,136},{16,144},{24,152},{32,160},{40,168},{48,176},{56,1... | collective-permute-start | bytes 294920 | tf_op jit(solution)/shard_map/ppermute | solution.py:28
  47.0 5.6 %collective-permute-start.22 = (f32[8,128]{1,0:T(8,128)S(1)}, f32[8,128]{1,0:T(8,128)S(1)}, u32[]{:S(2)}, u32[]{:S(2)}) collective-permute-start(f32[8,128]{1,0:T(8,128)S(1)} %shard_map.116.refs_17_), channel_id=1, source_target_pairs={{0,192},{8,200},{16,208},{24,216},{32,224},{40,232},{48,240},{56,2... | collective-permute-start | bytes 12296 | tf_op jit(solution)/shard_map/ppermute | solution.py:28
  48.9 4.5 %collective-permute-start.21 = (f32[8,128]{1,0:T(8,128)S(1)}, f32[8,128]{1,0:T(8,128)S(1)}, u32[]{:S(2)}, u32[]{:S(2)}) collective-permute-start(f32[8,128]{1,0:T(8,128)S(1)} %shard_map.116.refs_17_), channel_id=1, source_target_pairs={{0,128},{8,136},{16,144},{24,152},{32,160},{40,168},{48,176},{56,1... | collective-permute-start | bytes 12296 | tf_op jit(solution)/shard_map/ppermute | solution.py:28
  48.9 4.5 %collective-permute-start.20 = (f32[8,128]{1,0:T(8,128)S(1)}, f32[8,128]{1,0:T(8,128)S(1)}, u32[]{:S(2)}, u32[]{:S(2)}) collective-permute-start(f32[8,128]{1,0:T(8,128)S(1)} %shard_map.116.refs_17_), channel_id=1, source_target_pairs={{0,64},{8,72},{16,80},{24,88},{32,96},{40,104},{48,112},{56,120},{... | collective-permute-start | bytes 12296 | tf_op jit(solution)/shard_map/ppermute | solution.py:28
  53.4 10.2 %collective-permute-start.23 = (bf16[768,128]{1,0:T(8,128)(2,1)S(1)}, bf16[768,128]{1,0:T(8,128)(2,1)S(1)}, u32[]{:S(2)}, u32[]{:S(2)}) collective-permute-start(bf16[768,128]{1,0:T(8,128)(2,1)S(1)} %pad_maximum_fusion.3), channel_id=1, source_target_pairs={{0,64},{8,72},{16,80},{24,88},{32,96},{40,104},{48,112},{56,120},{... | collective-permute-start | bytes 589832 | tf_op jit(solution)/shard_map/ppermute | solution.py:28
  56.5 14.1 %collective-permute-start.25 = (bf16[48,3072]{1,0:T(8,128)(2,1)S(1)}, bf16[48,3072]{1,0:T(8,128)(2,1)S(1)}, u32[]{:S(2)}, u32[]{:S(2)}) collective-permute-start(bf16[48,3072]{1,0:T(8,128)(2,1)S(1)} %get-tuple-element.62), channel_id=1, source_target_pairs={{0,32},{8,40},{16,48},{24,56},{32,0},{40,8},{48,16},{56,24},{64,96... | collective-permute-start | bytes 884744 | tf_op jit(solution)/shard_map/ppermute | solution.py:28
  59.9 11.3 %collective-permute-start.26 = (bf16[48,3072]{1,0:T(8,128)(2,1)S(1)}, bf16[48,3072]{1,0:T(8,128)(2,1)S(1)}, u32[]{:S(2)}, u32[]{:S(2)}) collective-permute-start(bf16[48,3072]{1,0:T(8,128)(2,1)S(1)} %get-tuple-element.63), channel_id=1, source_target_pairs={{0,48},{8,56},{16,32},{24,40},{32,16},{40,24},{48,0},{56,8},{64,11... | collective-permute-start | bytes 884744 | tf_op jit(solution)/shard_map/ppermute | solution.py:28
  61.0 10.7 %collective-permute-start.24 = (bf16[48,3072]{1,0:T(8,128)(2,1)S(1)}, bf16[48,3072]{1,0:T(8,128)(2,1)S(1)}, u32[]{:S(2)}, u32[]{:S(2)}) collective-permute-start(bf16[48,3072]{1,0:T(8,128)(2,1)S(1)} %get-tuple-element.51), channel_id=1, source_target_pairs={{0,16},{8,24},{16,0},{24,8},{32,48},{40,56},{48,32},{56,40},{64,80... | collective-permute-start | bytes 884744 | tf_op jit(solution)/shard_map/ppermute | solution.py:28
  62.2 10.1 %collective-permute-start.18 = (bf16[512,384]{1,0:T(8,128)(2,1)S(1)}, bf16[512,384]{1,0:T(8,128)(2,1)S(1)}, u32[]{:S(2)}, u32[]{:S(2)}) collective-permute-start(bf16[512,384]{1,0:T(8,128)(2,1)S(1)} %get-tuple-element.54), channel_id=1, source_target_pairs={{0,2},{1,3},{2,0},{3,1},{4,6},{5,7},{6,4},{7,5},{8,10},{9,11},{10,... | collective-permute-start | bytes 1179656 | tf_op jit(solution)/shard_map/ppermute | solution.py:28
  73.2 9.0 %collective-permute-start.28 = (bf16[256,384]{1,0:T(8,128)(2,1)S(1)}, bf16[256,384]{1,0:T(8,128)(2,1)S(1)}, u32[]{:S(2)}, u32[]{:S(2)}) collective-permute-start(bf16[256,384]{1,0:T(8,128)(2,1)S(1)} %get-tuple-element.82), channel_id=1, source_target_pairs={{0,32},{8,40},{16,48},{24,56},{32,0},{40,8},{48,16},{56,24},{64,96... | collective-permute-start | bytes 589832 | tf_op jit(solution)/shard_map/ppermute | solution.py:28
  76.9 7.0 %collective-permute-start.29 = (bf16[24,3072]{1,0:T(8,128)(2,1)S(1)}, bf16[24,3072]{1,0:T(8,128)(2,1)S(1)}, u32[]{:S(2)}, u32[]{:S(2)}) collective-permute-start(bf16[24,3072]{1,0:T(8,128)(2,1)S(1)} %slice.115), channel_id=1, source_target_pairs={{0,64},{8,72},{16,80},{24,88},{32,96},{40,104},{48,112},{56,120},{... | collective-permute-start | bytes 442376 | tf_op jit(solution)/shard_map/ppermute | solution.py:28
  77.3 12.5 %collective-permute-start.31 = (bf16[256,384]{1,0:T(8,128)(2,1)S(1)}, bf16[256,384]{1,0:T(8,128)(2,1)S(1)}, u32[]{:S(2)}, u32[]{:S(2)}) collective-permute-start(bf16[256,384]{1,0:T(8,128)(2,1)S(1)} %slice.114), channel_id=1, source_target_pairs={{0,1},{1,0},{2,3},{3,2},{4,5},{5,4},{6,7},{7,6},{8,9},{9,8},{10,11... | collective-permute-start | bytes 589832 | tf_op jit(solution)/shard_map/ppermute | solution.py:28
  79.1 7.7 %collective-permute-start.30 = (bf16[768,128]{1,0:T(8,128)(2,1)S(1)}, bf16[768,128]{1,0:T(8,128)(2,1)S(1)}, u32[]{:S(2)}, u32[]{:S(2)}) collective-permute-start(bf16[768,128]{1,0:T(8,128)(2,1)S(1)} %get-tuple-element.70), channel_id=1, source_target_pairs={{0,64},{8,72},{16,80},{24,88},{32,96},{40,104},{48,112},{56,120},{... | collective-permute-start | bytes 589832 | tf_op jit(solution)/shard_map/ppermute | solution.py:28
  80.5 14.9 %collective-permute-start.34 = (bf16[256,384]{1,0:T(8,128)(2,1)S(1)}, bf16[256,384]{1,0:T(8,128)(2,1)S(1)}, u32[]{:S(2)}, u32[]{:S(2)}) collective-permute-start(bf16[256,384]{1,0:T(8,128)(2,1)S(1)} %get-tuple-element.80), channel_id=1, source_target_pairs={{0,16},{8,24},{16,0},{24,8},{32,48},{40,56},{48,32},{56,40},{64,80... | collective-permute-start | bytes 589832 | tf_op jit(solution)/shard_map/ppermute | solution.py:28
  82.2 13.3 %collective-permute-start.35 = (bf16[256,384]{1,0:T(8,128)(2,1)S(1)}, bf16[256,384]{1,0:T(8,128)(2,1)S(1)}, u32[]{:S(2)}, u32[]{:S(2)}) collective-permute-start(bf16[256,384]{1,0:T(8,128)(2,1)S(1)} %get-tuple-element.81), channel_id=1, source_target_pairs={{0,48},{8,56},{16,32},{24,40},{32,16},{40,24},{48,0},{56,8},{64,11... | collective-permute-start | bytes 589832 | tf_op jit(solution)/shard_map/ppermute | solution.py:28
  86.8 15.7 %collective-permute-start.33 = (bf16[384,128]{1,0:T(8,128)(2,1)S(1)}, bf16[384,128]{1,0:T(8,128)(2,1)S(1)}, u32[]{:S(2)}, u32[]{:S(2)}) collective-permute-start(bf16[384,128]{1,0:T(8,128)(2,1)S(1)} %slice.117), channel_id=1, source_target_pairs={{0,128},{8,136},{16,144},{24,152},{32,160},{40,168},{48,176},{56,1... | collective-permute-start | bytes 294920 | tf_op jit(solution)/shard_map/ppermute | solution.py:28
  87.8 14.0 %collective-permute-start.36 = (bf16[12,3072]{1,0:T(8,128)(2,1)S(1)}, bf16[12,3072]{1,0:T(8,128)(2,1)S(1)}, u32[]{:S(2)}, u32[]{:S(2)}) collective-permute-start(bf16[12,3072]{1,0:T(8,128)(2,1)S(1)} %slice.118), channel_id=1, source_target_pairs={{0,128},{8,136},{16,144},{24,152},{32,160},{40,168},{48,176},{56,1... | collective-permute-start | bytes 221192 | tf_op jit(solution)/shard_map/ppermute | solution.py:28
  89.9 13.4 %collective-permute-start.32 = (bf16[128,384]{1,0:T(8,128)(2,1)S(1)}, bf16[128,384]{1,0:T(8,128)(2,1)S(1)}, u32[]{:S(2)}, u32[]{:S(2)}) collective-permute-start(bf16[128,384]{1,0:T(8,128)(2,1)S(1)} %slice.116), channel_id=1, source_target_pairs={{0,4},{1,5},{2,6},{3,7},{4,0},{5,1},{6,2},{7,3},{8,12},{9,13},{10,... | collective-permute-start | bytes 294920 | tf_op jit(solution)/shard_map/ppermute | solution.py:28
  (15 other events, 106.1 us)
